TPU v7x, 32 devices: a whole 2x2x4 slice. The times are simulated.
32 devices in a mesh: blk: 8 (over z, y), rep: 4 (over x, core).
Axes of the slice: x: 2, y: 2, z: 4, core: 2. Of those that a mesh axis runs over, the one named last changes fastest.
Arguments:
- dense: bfloat16 [32768, 1024], P(('blk', 'rep')), may hold values from -6 to 6
- labels: int32 [32768], P(('blk', 'rep')), may hold values 0 or 1
- tile_values: bfloat16 [1024, 64, 128], P(('blk', 'rep')), may hold values from -1.1953125 to 1.1953125
- tile_block: int32 [1024, 64], P(('blk', 'rep')), may hold values from 0 to 1023
- tile_example: int32 [1024, 64], P(('blk', 'rep')), may hold values from 0 to 1023
- tile_count: int32 [1024], P(('blk', 'rep')), may hold values from 16 to 64, as said below
- z_state: float32 [32768, 128], P(('blk', 'rep')), may hold values from -6 to 6
- n_state: float32 [32768, 128], P(('blk', 'rep')), may hold values from 0.01 to 4
- w_one: bfloat16 [1024, 512], replicated, may hold values from -0.1875 to 0.1875
- b_one: float32 [512], replicated, may hold values from -3 to 3
- w_two: bfloat16 [512, 256], replicated, may hold values from -0.25 to 0.25
- b_two: float32 [256], replicated, may hold values from -3 to 3
- head: bfloat16 [256], replicated, may hold values from -0.375 to 0.375
Outputs:
- probability: float32 [32768], P(('blk', 'rep'))
- z_new: float32 [32768, 128], P(('blk', 'rep'))
- n_new: float32 [32768, 128], P(('blk', 'rep'))
- grad_w_one: float32 [1024, 512], replicated
- grad_b_one: float32 [512], replicated
- grad_w_two: float32 [512, 256], replicated
- grad_b_two: float32 [256], replicated
- grad_head: float32 [256], replicated
Inputs may be any that keep to these rules, and one draw needn't show every extreme that they name: `tile_count`: slots at or beyond a list's count are padding; in every draw some owners receive 64 live slots from every device.
All inputs are finite; a program needn't handle non-finite values. No bound on the sum of `labels` on one device may be relied on, other than what follows from the above.
Results may differ from a plain program's by a relative error of at most 0.013.
Values may be sent and summed in bfloat16 or wider, within the bound.
No kernel may reach another device: no remote copies, remote signals or barrier semaphores. Data moves between devices by JAX's collectives and lax.ppermute only.
A program may use at most 64 MiB of HBM per device.

v0:
```python
import jax
import jax.numpy as jnp
from jax import lax
from jax.sharding import PartitionSpec as P

alpha_rate = 0.5
beta_shift = 1.0
lasso_term = 0.5
ridge_term = 0.1


def wide_weight(z_state, n_state):
    shrunk = z_state - jnp.sign(z_state) * lasso_term
    denominator = (beta_shift + jnp.sqrt(n_state)) / alpha_rate + ridge_term
    return jnp.where(jnp.abs(z_state) > lasso_term, -shrunk / denominator, jnp.zeros_like(z_state))


def silu_slope(pre):
    gate = jax.nn.sigmoid(pre)
    return gate * (1.0 + pre * (1.0 - gate))


def per_device(
    dense,
    labels,
    tile_values,
    tile_block,
    tile_example,
    tile_count,
    z_state,
    n_state,
    w_one,
    b_one,
    w_two,
    b_two,
    head,
):
    owners, capacity, width = tile_values.shape
    slots = jnp.arange(capacity, dtype=jnp.int32)
    live = slots[None, :] < tile_count[:, None]
    masked = jnp.where(live[:, :, None], tile_values, jnp.zeros_like(tile_values))
    got_values, got_block = (
        lax.all_to_all(masked, ("blk", "rep"), split_axis=0, concat_axis=0, tiled=True),
        lax.all_to_all(tile_block, ("blk", "rep"), split_axis=0, concat_axis=0, tiled=True),
    )
    weight = wide_weight(z_state, n_state)
    flat_block = got_block.reshape(-1)
    flat_values = got_values.reshape(-1, width)
    picked = jnp.take(weight, flat_block, axis=0)
    tile_logit = jnp.sum(flat_values.astype(jnp.float32) * picked, axis=1).reshape(owners, capacity)
    returned = lax.all_to_all(tile_logit, ("blk", "rep"), split_axis=0, concat_axis=0, tiled=True)
    flat_example = tile_example.reshape(-1)
    wide = jnp.zeros((dense.shape[0],), jnp.float32).at[flat_example].add(returned.reshape(-1))
    pre_one = jnp.dot(dense, w_one, preferred_element_type=jnp.float32) + b_one
    hid_one = jax.nn.silu(pre_one).astype(jnp.bfloat16)
    pre_two = jnp.dot(hid_one, w_two, preferred_element_type=jnp.float32) + b_two
    hid_two = jax.nn.silu(pre_two).astype(jnp.bfloat16)
    deep = jnp.dot(hid_two, head, preferred_element_type=jnp.float32)
    probability = jax.nn.sigmoid(wide + deep)
    residual = probability - labels.astype(jnp.float32)
    tile_residual = jnp.take(residual, flat_example).reshape(owners, capacity)
    got_residual = lax.all_to_all(
        tile_residual, ("blk", "rep"), split_axis=0, concat_axis=0, tiled=True
    )
    contrib = flat_values.astype(jnp.float32) * got_residual.reshape(-1)[:, None]
    grad_block = jnp.zeros_like(z_state).at[flat_block].add(contrib)
    n_new = n_state + grad_block * grad_block
    sigma = (jnp.sqrt(n_new) - jnp.sqrt(n_state)) / alpha_rate
    z_new = z_state + grad_block - sigma * weight
    dlogit = residual.astype(jnp.bfloat16)
    grad_head = jnp.dot(dlogit, hid_two, preferred_element_type=jnp.float32)
    d_two = (
        dlogit.astype(jnp.float32)[:, None]
        * head.astype(jnp.float32)[None, :]
        * silu_slope(pre_two)
    ).astype(jnp.bfloat16)
    grad_w_two = lax.dot_general(
        hid_one, d_two, (((0,), (0,)), ((), ())), preferred_element_type=jnp.float32
    )
    grad_b_two = jnp.sum(d_two.astype(jnp.float32), axis=0)
    back_one = lax.dot_general(
        d_two, w_two, (((1,), (1,)), ((), ())), preferred_element_type=jnp.float32
    )
    d_one = (back_one * silu_slope(pre_one)).astype(jnp.bfloat16)
    grad_w_one = lax.dot_general(
        dense, d_one, (((0,), (0,)), ((), ())), preferred_element_type=jnp.float32
    )
    grad_b_one = jnp.sum(d_one.astype(jnp.float32), axis=0)
    grad_head, grad_w_two, grad_b_two, grad_w_one, grad_b_one = lax.psum(
        (grad_head, grad_w_two, grad_b_two, grad_w_one, grad_b_one), ("blk", "rep")
    )
    return (probability, z_new, n_new, grad_w_one, grad_b_one, grad_w_two, grad_b_two, grad_head)


def solution(mesh):
    placed = (
        P(("blk", "rep"), None),
        P(("blk", "rep")),
        P(("blk", "rep"), None, None),
        P(("blk", "rep"), None),
        P(("blk", "rep"), None),
        P(("blk", "rep")),
        P(("blk", "rep"), None),
        P(("blk", "rep"), None),
        P(),
        P(),
        P(),
        P(),
        P(),
    )
    return jax.shard_map(
        per_device,
        mesh=mesh,
        in_specs=placed,
        out_specs=(
            P(("blk", "rep")),
            P(("blk", "rep"), None),
            P(("blk", "rep"), None),
            P(),
            P(),
            P(),
            P(),
            P(),
        ),
        check_vma=False,
    )
```

profile of v0, /device:TPU:0, one launch (start us, length us, event | category | flops | bytes accessed | tf_op | source)
XLA Modules:
  0.0 224.7 jit_solution(4188646832370213735)
XLA Ops:
  7.2 7.3 %all-to-all-start.1 = ((s32[32,1,64]{2,1,0:T(1,128)}), s32[32,1,64]{2,1,0:T(1,128)S(1)}, u32[]{:S(2)}, u32[]{:S(2)}) async-start(s32[32,1,64]{2,1,0:T(1,128)} %bitcast.36), calls=%async_computation.1 | async-start | bytes 32768 | tf_op jit(solution)/shard_map/all_to_all | solution.py:44
  14.5 0.7 iota_compare_fusion
  15.2 0.8 reshape.146
  16.1 4.0 %multiply_convert_fusion.1 = (bf16[1024,512]{1,0:T(8,128)(2,1)S(1)}, f32[1024,512]{1,0:T(8,128)}) fusion(f32[512]{0:T(512)} %param.22, bf16[1024,1024]{1,0:T(8,128)(2,1)S(1)} %copy-done, bf16[1024,512]{1,0:T(8,128)(2,1)} %param.21), kind=kOutput, calls=%fused_computation.6 | convolution fusion | flops 1076887552 | bytes 6293504 | tf_op jit(solution)/shard_map/dot_general | solution.py:54
  20.1 1.6 multiply_convert_fusion.3
  21.7 1.1 broadcast_select_fusion
  22.9 5.8 %all-to-all-start = ((bf16[32,64,128]{2,1,0:T(8,128)(2,1)}), bf16[32,64,128]{2,1,0:T(8,128)(2,1)S(1)}, u32[]{:S(2)}, u32[]{:S(2)}) async-start(bf16[32,64,128]{2,1,0:T(8,128)(2,1)} %broadcast_select_fusion), calls=%async_computation | async-start | bytes 1048576 | tf_op jit(solution)/shard_map/all_to_all | solution.py:43
  28.7 1.6 divide_select_fusion
  30.9 0.7 reduce.10
  31.7 7.6 %gather_fusion = f32[2048,128]{1,0:T(8,128)} fusion(f32[1024,128]{1,0:T(8,128)S(1)} %divide_select_fusion, s32[2048]{0:T(1024)S(1)} %broadcast_clamp_fusion.1), kind=kCustom, calls=%fused_computation | custom fusion | bytes 2105344 | tf_op jit(solution)/shard_map/jit(_take)/gather | solution.py:49
  39.3 4.9 %all-to-all-done = bf16[32,64,128]{2,1,0:T(8,128)(2,1)S(1)} async-done(((bf16[32,64,128]{2,1,0:T(8,128)(2,1)}), bf16[32,64,128]{2,1,0:T(8,128)(2,1)S(1)}, u32[]{:S(2)}, u32[]{:S(2)}) %all-to-all-start) | async-done | bytes 524320 | tf_op jit(solution)/shard_map/all_to_all | solution.py:43
  44.2 2.5 %multiply_reduce_fusion = f32[32,64]{1,0:T(8,128)} fusion(f32[32,64,128]{2,1,0:T(8,128)} %bitcast.30, pred[32,64]{1,0:T(8,128)(4,1)S(1)} %compare_and_fusion, bf16[32,64,128]{2,1,0:T(8,128)(2,1)S(1)} %all-to-all-done), kind=kLoop, calls=%fused_computation.13 | loop fusion | flops 1046528 | bytes 1583104 | tf_op jit(solution)/shard_map/reduce_sum | solution.py:50
  46.7 3.1 %all-to-all-start.2 = ((f32[32,1,64]{2,1,0:T(1,128)}), f32[32,1,64]{2,1,0:T(1,128)S(1)}, u32[]{:S(2)}, u32[]{:S(2)}) async-start(f32[32,1,64]{2,1,0:T(1,128)} %bitcast.6), calls=%async_computation.2 | async-start | bytes 32768 | tf_op jit(solution)/shard_map/all_to_all | solution.py:51
  49.9 1.3 fusion.3
  51.1 5.7 %all-to-all-done.2 = f32[32,1,64]{2,1,0:T(1,128)S(1)} async-done(((f32[32,1,64]{2,1,0:T(1,128)}), f32[32,1,64]{2,1,0:T(1,128)S(1)}, u32[]{:S(2)}, u32[]{:S(2)}) %all-to-all-start.2) | async-done | bytes 8224 | tf_op jit(solution)/shard_map/all_to_all | solution.py:51
  57.4 0.7 reduce.11
  58.2 14.7 %scatter_fusion = f32[1024]{0:T(1024)S(1)} fusion(f32[1024]{0:T(1024)S(1)} %bitcast.29, s32[2048]{0:T(1024)S(1)} %bitcast.32, f32[2048]{0:T(1024)S(1)} %reshape.171), kind=kCustom, calls=%fused_computation.2 | custom fusion | flops 2048 | bytes 32768 | tf_op jit(solution)/shard_map/scatter-add | solution.py:53
  73.5 1.7 convert_reduce_fusion.1
  75.2 2.5 %fusion.4 = f32[512,256]{1,0:T(8,128)} fusion(bf16[1024,512]{1,0:T(8,128)(2,1)} %copy-done.10, bf16[1024,256]{1,0:T(8,128)(2,1)S(1)} %get-tuple-element.38), kind=kOutput, calls=%fused_computation.36 | convolution fusion | flops 268435456 | bytes 2097152 | tf_op jit(solution)/shard_map/dot_general | solution.py:77
  77.7 1.0 convert_reduce_fusion
  78.7 2.6 %convolution_bitcast_fusion = f32[1024,512]{0,1:T(8,128)} fusion(bf16[1024,512]{1,0:T(8,128)(2,1)S(1)} %get-tuple-element.50, bf16[1024,1024]{1,0:T(8,128)(2,1)S(1)} %copy-done), kind=kOutput, calls=%fused_computation.8 | convolution fusion | flops 1073741824 | bytes 5242880 | tf_op jit(solution)/shard_map/dot_general | solution.py:85
  81.4 8.6 %gather_fusion.1 = f32[2048]{0:T(1024)S(1)} fusion(f32[1024]{0:T(1024)S(1)} %get-tuple-element.41, s32[2048]{0:T(1024)S(1)} %broadcast_clamp_fusion), kind=kCustom, calls=%fused_computation.1 | custom fusion | bytes 24576 | tf_op jit(solution)/shard_map/jit(_take)/gather | solution.py:61
  90.7 2.5 %all-to-all-start.3 = ((f32[32,1,64]{2,1,0:T(1,128)}), f32[32,1,64]{2,1,0:T(1,128)S(1)}, u32[]{:S(2)}, u32[]{:S(2)}) async-start(f32[32,1,64]{2,1,0:T(1,128)} %bitcast.9), calls=%async_computation.3 | async-start | bytes 32768 | tf_op jit(solution)/shard_map/all_to_all | solution.py:62
  93.2 1.2 fusion.5
  94.5 40.7 %all-reduce = (f32[512]{0:T(512)}, f32[256]{0:T(256)}, f32[256]{0:T(256)}) all-reduce(f32[512]{0:T(512)S(1)} %get-tuple-element.49, f32[256]{0:T(256)S(1)} %get-tuple-element.37, f32[256]{0:T(256)S(1)} %bitcast.37), channel_id=1, replica_groups=mesh['blk'=8,'rep'=4] {'blk','rep'}, use_global_device_ids=true, to_apply=%region_5.6 | all-reduce | flops 1024 | bytes 8192 | tf_op jit(solution)/shard_map/psum | solution.py:89
  135.2 0.7 reduce.12
  136.0 1.3 bitcast_multiply_fusion
  137.3 12.0 %scatter_custom_fusion.1 = f32[1024,128]{1,0:T(8,128)S(1)} fusion(s32[2048]{0:T(1024)S(1)} %bitcast.35, f32[2048,128]{1,0:T(8,128)} %bitcast_multiply_fusion, f32[]{:T(128)} %constant.32.clone.1), kind=kCustom, calls=%fused_computation.21 | custom fusion | flops 262144 | bytes 524800 | tf_op jit(solution)/shard_map/scatter-add | solution.py:66
  149.3 2.7 %multiply_subtract_fusion = (f32[1024,128]{1,0:T(8,128)}, f32[1024,128]{1,0:T(8,128)}) fusion(f32[1024,128]{1,0:T(8,128)S(1)} %copy-done.1, f32[1024,128]{1,0:T(8,128)S(1)} %scatter_custom_fusion.1, f32[1024,128]{1,0:T(8,128)} %param.20), kind=kLoop, calls=%fused_computation.16 | loop fusion | flops 2359296 | bytes 2621440 | tf_op jit(solution)/shard_map/sub | solution.py:69
  152.0 62.1 %all-reduce.4.cloned.1.call-done = (f32[1024,512]{0,1:T(8,128)}, f32[512,256]{1,0:T(8,128)}) async-done(((f32[1024,512]{0,1:T(8,128)}, f32[512,256]{1,0:T(8,128)}), (f32[1024,512]{0,1:T(8,128)}, f32[512,256]{1,0:T(8,128)})) %all-reduce.4.cloned.1.call-update) | async-done | bytes 2621456 | tf_op jit(solution)/shard_map/psum | solution.py:89
  214.1 2.9 %copy.24 = f32[1024,512]{1,0:T(8,128)} copy(f32[1024,512]{0,1:T(8,128)} %get-tuple-element.35) | data formatting | bytes 4194304
  217.0 0.8 copy.28
  (44 shorter events, 2.7 us)
Async XLA Ops:
  7.2 8.9 %copy-start = (bf16[1024,1024]{1,0:T(8,128)(2,1)S(1)}, bf16[1024,1024]{1,0:T(8,128)(2,1)}, u32[]{:S(2)}) copy-start(bf16[1024,1024]{1,0:T(8,128)(2,1)} %param.13) | copy-start | bytes 6291460
  7.2 15.7 %all-to-all-start.1 = ((s32[32,1,64]{2,1,0:T(1,128)}), s32[32,1,64]{2,1,0:T(1,128)S(1)}, u32[]{:S(2)}, u32[]{:S(2)}) async-start(s32[32,1,64]{2,1,0:T(1,128)} %bitcast.36), calls=%async_computation.1 | async-start | bytes 32768 | tf_op jit(solution)/shard_map/all_to_all | solution.py:44
  16.0 4.1 %copy-start.6 = (bf16[512,256]{1,0:T(8,128)(2,1)S(1)}, bf16[512,256]{1,0:T(8,128)(2,1)}, u32[]{:S(2)}) copy-start(bf16[512,256]{1,0:T(8,128)(2,1)} %param.23) | copy-start | bytes 786436
  16.1 4.1 %copy-start.8 = (f32[256]{0:T(256)S(1)}, f32[256]{0:T(256)}, u32[]{:S(2)}) copy-start(f32[256]{0:T(256)} %param.24) | copy-start | bytes 3076
  20.1 1.6 copy-start.10
  20.1 1.6 copy-start.2
  21.7 8.6 %copy-start.9 = (bf16[256]{0:T(256)(128)(2,1)S(1)}, bf16[256]{0:T(256)(128)(2,1)}, u32[]{:S(2)}) copy-start(bf16[256]{0:T(256)(128)(2,1)} %param.25) | copy-start | bytes 1540
  22.9 21.4 %all-to-all-start = ((bf16[32,64,128]{2,1,0:T(8,128)(2,1)}), bf16[32,64,128]{2,1,0:T(8,128)(2,1)S(1)}, u32[]{:S(2)}, u32[]{:S(2)}) async-start(bf16[32,64,128]{2,1,0:T(8,128)(2,1)} %broadcast_select_fusion), calls=%async_computation | async-start | bytes 1048576 | tf_op jit(solution)/shard_map/all_to_all | solution.py:43
  46.7 10.2 %all-to-all-start.2 = ((f32[32,1,64]{2,1,0:T(1,128)}), f32[32,1,64]{2,1,0:T(1,128)S(1)}, u32[]{:S(2)}, u32[]{:S(2)}) async-start(f32[32,1,64]{2,1,0:T(1,128)} %bitcast.6), calls=%async_computation.2 | async-start | bytes 32768 | tf_op jit(solution)/shard_map/all_to_all | solution.py:51
  49.8 164.3 %all-reduce.4.cloned.1.call-start = ((), (), s32[]{:S(2)}) async-start(), calls=%async_computation.4 | async-start | bytes 5242880 | tf_op jit(solution)/shard_map/psum | solution.py:89
  58.2 14.7 %copy-start.5 = (s32[1024]{0:T(1024)S(1)}, s32[1024]{0:T(1024)}, u32[]{:S(2)}) copy-start(s32[1024]{0:T(1024)} %param.14) | copy-start | bytes 12292
  72.9 4.8 %copy-start.7 = (f32[512]{0:T(512)S(1)}, f32[512]{0:T(512)}, u32[]{:S(2)}) copy-start(f32[512]{0:T(512)} %param.22) | copy-start | bytes 6148
  72.9 4.8 %copy-start.11 = (f32[1024,512]{1,0:T(8,128)S(1)}, f32[1024,512]{1,0:T(8,128)}, u32[]{:S(2)}) copy-start(f32[1024,512]{1,0:T(8,128)} %get-tuple-element.46) | copy-start | bytes 6291460
  81.4 8.7 %copy-start.4 = (s32[32,64]{1,0:T(8,128)S(1)}, s32[32,64]{1,0:T(8,128)}, u32[]{:S(2)}) copy-start(s32[32,64]{1,0:T(8,128)} %param.17) | copy-start | bytes 24580
  90.0 59.3 %copy-start.1 = (f32[1024,128]{1,0:T(8,128)S(1)}, f32[1024,128]{1,0:T(8,128)}, u32[]{:S(2)}) copy-start(f32[1024,128]{1,0:T(8,128)} %param.19) | copy-start | bytes 1572868
  90.7 44.5 %all-to-all-start.3 = ((f32[32,1,64]{2,1,0:T(1,128)}), f32[32,1,64]{2,1,0:T(1,128)S(1)}, u32[]{:S(2)}, u32[]{:S(2)}) async-start(f32[32,1,64]{2,1,0:T(1,128)} %bitcast.9), calls=%async_computation.3 | async-start | bytes 32768 | tf_op jit(solution)/shard_map/all_to_all | solution.py:62
  214.1 2.9 %copy-start.3 = (f32[512,256]{1,0:T(8,128)S(1)}, f32[512,256]{1,0:T(8,128)}, u32[]{:S(2)}) copy-start(f32[512,256]{1,0:T(8,128)} %get-tuple-element.56) | copy-start | bytes 1572868
Sparse Core Ops, SparseCore 0:
  81.5 132.5 all-reduce.3
where the time goes:
time: 225 us
  waiting for transfers between devices  72.9 us (32%)
  other arithmetic  41.6 us (18%)
  blocking collectives  40.7 us (18%)
  local copies, waits for them, and re-layouts  22.1 us (10%)
  starting transfers between devices  18.8 us (8%)
  matrix products  14.3 us (6%)
  between operations  14.3 us (6%)
    psum x1, waiting for transfers between devices, per_device(): lax.psum((grad_head, grad_w_two, grad_b_two, grad_w_one, grad_b_one), ('b...  62.1 us
    psum x1, blocking collectives, per_device(): lax.psum((grad_head, grad_w_two, grad_b_two, grad_w_one, grad_b_one), ('b...  40.7 us
    scatter-add x1, other arithmetic, per_device(): jnp.zeros((dense.shape[0],), jnp.float32).at[flat_example]  14.7 us
    scatter-add x1, other arithmetic, per_device(): grad_block = jnp.zeros_like(z_state).at[flat_block].add(contrib)  12 us
    gather x2, local copies, waits for them, and re-layouts, per_device(): tile_residual = jnp.take(residual, flat_example).reshape(owners, capacity)  8.66 us
    gather x1, local copies, waits for them, and re-layouts, per_device(): picked = jnp.take(weight, flat_block, axis=0)  7.62 us
    all_to_all x1, starting transfers between devices, per_device(): lax.all_to_all(tile_block, ('blk', 'rep'), split_axis=0, concat_axis=0, t...  7.3 us
    all_to_all x1, starting transfers between devices, per_device(): lax.all_to_all(masked, ('blk', 'rep'), split_axis=0, concat_axis=0, tiled...  5.83 us
  transfers between devices with their start and end apart: 5, of which 3 were waited for; matrix products, arithmetic and copies ran while one was open for 21% of the time, Pallas kernels for 0%

commit v1 on v0

v1 whole, which is shorter than its diff:
```python
import functools
import jax
import jax.numpy as jnp
from jax import lax
from jax.experimental import pallas as pl
from jax.experimental.pallas import tpu as pltpu
from jax.sharding import PartitionSpec as P

alpha_rate = 0.5
beta_shift = 1.0
lasso_term = 0.5
ridge_term = 0.1

AXES = ("blk", "rep")
LANES = 128
f32 = jnp.float32
bf16 = jnp.bfloat16
NT = (((1,), (1,)), ((), ()))
NN = (((1,), (0,)), ((), ()))


def dot(a, b, dims=NN):
    return lax.dot_general(a, b, dims, preferred_element_type=f32)


def iota(shape, axis):
    return lax.broadcasted_iota(jnp.int32, shape, axis)


def split_two(x):
    top = x.astype(bf16)
    return top, (x - top.astype(f32)).astype(bf16)


def wide_weight(z, n):
    sign = jnp.where(z > 0, 1.0, jnp.where(z < 0, -1.0, 0.0))
    shrunk = z - sign * lasso_term
    denominator = (beta_shift + jnp.sqrt(n)) / alpha_rate + ridge_term
    return jnp.where(jnp.abs(z) > lasso_term, -shrunk / denominator, jnp.zeros_like(z))


def params(megabytes=40):
    return pltpu.CompilerParams(vmem_limit_bytes=megabytes << 20)


VM = pl.BlockSpec(memory_space=pltpu.VMEM)
ANY = pl.BlockSpec(memory_space=pl.ANY)


def pack_kernel(values_ref, block_ref, count_ref, out_ref):
    lists, cap = block_ref.shape
    dead_index = 64
    counts = jnp.sum(
        jnp.where(iota((lists, lists), 0) == iota((lists, lists), 1), count_ref[...], 0),
        axis=1,
        keepdims=True,
    )
    block = block_ref[...]
    high = jnp.where(iota((lists, cap), 1) < counts, block >> 5, dead_index)
    low = block & 31
    high = jnp.concatenate([high, high], axis=1).astype(f32)
    low = jnp.concatenate([low, low], axis=1).astype(f32)
    row = iota((8, LANES), 0)
    for k in range(lists):
        out_ref[k, 0:cap, :] = values_ref[k]
        tail = jnp.where(row == 0, high[k : k + 1], jnp.where(row == 1, low[k : k + 1], 0.0))
        out_ref[k, cap : cap + 8, :] = tail.astype(bf16)


def pack(values, block, count):
    lists, cap, width = values.shape
    return pl.pallas_call(
        pack_kernel,
        out_shape=jax.ShapeDtypeStruct((lists, cap + 8, width), bf16),
        in_specs=[VM, VM, VM],
        out_specs=VM,
        compiler_params=params(),
        name="pack",
    )(values, block, count.reshape(1, lists))


def to_column(row):
    return jnp.transpose(jnp.broadcast_to(row, (8, row.shape[1])))[:, 0:1]


def tower_kernel(
    dense_ref, w1_ref, b1_ref, w2_ref, b2_ref, head_ref, z_ref, n_ref,
    dense_t_ref, h1_ref, h2_ref, s2_ref, q_ref, deep_ref, wcat_ref,
    w1t, w2t,
):
    @pl.when(pl.program_id(0) == 0)
    def _():
        w1t[...] = jnp.transpose(w1_ref[...])
        w2t[...] = jnp.transpose(w2_ref[...])

    dense_t = jnp.transpose(dense_ref[...])
    dense_t_ref[...] = dense_t
    pre1 = dot(w1t[...], dense_t) + to_column(b1_ref[...])
    gate1 = jax.nn.sigmoid(pre1)
    h1 = (pre1 * gate1).astype(bf16)
    h1_ref[...] = h1
    slope1 = gate1 * (1.0 + pre1 * (1.0 - gate1))
    pre2 = dot(w2t[...], h1) + to_column(b2_ref[...])
    gate2 = jax.nn.sigmoid(pre2)
    h2 = (pre2 * gate2).astype(bf16)
    h2_ref[...] = h2
    head = head_ref[...]
    deep_ref[...] = dot(jnp.broadcast_to(head, (16, head.shape[1])), h2)[0:1]
    s2 = to_column(head.astype(f32)) * (gate2 * (1.0 + pre2 * (1.0 - gate2)))
    s2_ref[...] = s2
    q_ref[...] = dot(w2_ref[...], s2.astype(bf16)) * slope1
    wcat_ref[...] = jnp.concatenate(split_two(wide_weight(z_ref[...], n_ref[...])), axis=1)


def tower(dense, w1, b1, w2, b2, head, z, n):
    ex, din = dense.shape
    h1, h2 = w2.shape
    blocks, width = z.shape
    steps = 4
    be, bb = ex // steps, blocks // steps
    whole = lambda a: pl.BlockSpec(a.shape, lambda i: (0, 0))
    cols = lambda rows: pl.BlockSpec((rows, be), lambda i: (0, i))
    b1, b2, head = b1.reshape(1, h1), b2.reshape(1, h2), head.reshape(1, h2)
    return pl.pallas_call(
        tower_kernel,
        grid=(steps,),
        out_shape=(
            jax.ShapeDtypeStruct((din, ex), bf16),
            jax.ShapeDtypeStruct((h1, ex), bf16),
            jax.ShapeDtypeStruct((h2, ex), bf16),
            jax.ShapeDtypeStruct((h2, ex), f32),
            jax.ShapeDtypeStruct((h1, ex), f32),
            jax.ShapeDtypeStruct((1, ex), f32),
            jax.ShapeDtypeStruct((blocks, 2 * width), bf16),
        ),
        in_specs=[
            pl.BlockSpec((be, din), lambda i: (i, 0)),
            whole(w1), whole(b1), whole(w2), whole(b2), whole(head),
            pl.BlockSpec((bb, width), lambda i: (i, 0)),
            pl.BlockSpec((bb, width), lambda i: (i, 0)),
        ],
        out_specs=(
            cols(din), cols(h1), cols(h2), cols(h2), cols(h1), cols(1),
            pl.BlockSpec((bb, 2 * width), lambda i: (i, 0)),
        ),
        scratch_shapes=[pltpu.VMEM((h1, din), bf16), pltpu.VMEM((h2, h1), bf16)],
        compiler_params=params(),
        cost_estimate=pl.CostEstimate(
            flops=2 * ex * (din * h1 + 2 * h1 * h2), bytes_accessed=12 << 20, transcendentals=ex * (h1 + h2)
        ),
        name="tower",
    )(dense, w1, b1, w2, b2, head, z, n)


def four_lists(got_ref, at, cap):
    planes = [got_ref[at + k] for k in range(4)]
    values = jnp.concatenate([p[0:cap] for p in planes], axis=0)
    index = [p[cap : cap + 1].astype(f32) * 32.0 + p[cap + 1 : cap + 2].astype(f32) for p in planes]
    left = iota((1, LANES), 1) < cap
    pairs = [jnp.where(left, index[0], index[1]), jnp.where(left, index[2], index[3])]
    return values, jnp.concatenate(pairs, axis=1).astype(jnp.int32)


def logit_kernel(got_ref, wcat_ref, out_ref):
    lists = got_ref.shape[0]
    cap = got_ref.shape[1] - 8
    blocks = wcat_ref.shape[0]
    for at in range(0, lists, 4):
        values, index = four_lists(got_ref, at, cap)
        every = dot(wcat_ref[...], jnp.concatenate([values, values], axis=1), NT)
        picked = jnp.where(iota((blocks, 4 * cap), 0) == index, every, 0.0)
        logit = jnp.sum(picked, axis=0, keepdims=True)
        for k in range(4):
            out_ref[at + k] = logit[:, (k // 2) * LANES : (k // 2 + 1) * LANES]


def slot_logits(got, wcat):
    lists = got.shape[0]
    return pl.pallas_call(
        logit_kernel,
        out_shape=jax.ShapeDtypeStruct((lists, 1, LANES), f32),
        in_specs=[VM, VM],
        out_specs=VM,
        compiler_params=params(),
        name="slot_logits",
    )(got, wcat)


def step_kernel(
    logit_ref, example_ref, deep_ref, label_ref, dense_any, h1_any, h2_any, s2_any, q_any,
    prob_ref, out_ref, send_ref, keep_ref,
    marks, spread, dense_t, h1, h2, s2, q, sems,
):
    lists, cap = example_ref.shape
    ex = deep_ref.shape[1]
    rows = ex // LANES
    core = lax.axis_index("rep") & 1
    copies = [
        pltpu.make_async_copy(src, dst, sems.at[k])
        for k, (src, dst) in enumerate(
            ((q_any, q), (s2_any, s2), (h2_any, h2), (dense_any, dense_t), (h1_any, h1))
        )
    ]
    for copy in copies:
        copy.start()
    example = jnp.concatenate([example_ref[...], example_ref[...]], axis=1)
    high, low = example >> 7, example & (LANES - 1)
    mine = (iota((lists, LANES), 1) >= cap) == (core == 1)
    high_mine = jnp.where(mine, high, -1)
    down = iota((rows, LANES), 0)
    down_all = iota((LANES, LANES), 0)
    for k in range(lists):
        at = slice(k * LANES, (k + 1) * LANES)
        part = jnp.where(high_mine[k : k + 1] == down, logit_ref[k], 0.0)
        spread[:, at] = jnp.concatenate(split_two(part), axis=0)
        marks[:, at] = jnp.where(low[k : k + 1] == down_all, 1.0, 0.0).astype(bf16)
    wide = dot(spread[...], marks[...], NT)
    wide = wide[0:rows] + wide[rows:]
    deep = jnp.concatenate([deep_ref[:, k * LANES : (k + 1) * LANES] for k in range(rows)], axis=0)
    prob = jax.nn.sigmoid(wide + deep)
    prob_ref[...] = prob
    residual = prob - label_ref[...].astype(f32)
    found = dot(jnp.concatenate(split_two(residual), axis=0), marks[...])
    found = found[0:rows] + found[rows:]
    for k in range(lists):
        part = found[:, k * LANES : (k + 1) * LANES]
        out_ref[k, 0:8, :] = jnp.broadcast_to(
            jnp.sum(jnp.where(high[k : k + 1] == down, part, 0.0), axis=0, keepdims=True), (8, LANES)
        )
    dlogit = jnp.concatenate([residual[k : k + 1] for k in range(rows)], axis=1)
    dlogit = dlogit.astype(bf16).astype(f32)
    for copy in copies[0:3]:
        copy.wait()
    d_one = (q[...] * dlogit).astype(bf16)
    d_two = (s2[...] * dlogit).astype(bf16)
    head_part = h2[...].astype(f32) * dlogit
    fold = lambda a: functools.reduce(
        jnp.add, [a[:, k * LANES : (k + 1) * LANES].astype(f32) for k in range(rows)]
    )
    small = jnp.concatenate([fold(d_one), fold(d_two), fold(head_part)], axis=0)
    ones = jnp.ones((16, 2 * LANES), bf16)
    sums = dot(ones, jnp.concatenate(split_two(small), axis=1), NT)[0:1]
    count = sums.shape[1] // LANES
    sums = jnp.concatenate([sums[:, k * LANES : (k + 1) * LANES] for k in range(count)], axis=0)
    for k in range(lists):
        out_ref[k, 8 : 8 + count, :] = sums
    for copy in copies[3:]:
        copy.wait()
    big, packed = dense_t.shape[0] // 2, h1.shape[0] // 4
    width = d_two.shape[0]
    for half, target in ((1 - core, send_ref), (core, keep_ref)):
        part = dense_t[pl.ds(pl.multiple_of(half * big, big), big), :]
        target[0:big, :] = dot(part, d_one, NT).astype(bf16)
        for side in range(2):
            at = pl.multiple_of(half * packed + side * 2 * packed, packed)
            target[big:, side * width : (side + 1) * width] = dot(h1[pl.ds(at, packed), :], d_two, NT).astype(bf16)


def step(logits, example, deep, labels, dense_t, h1, h2, s2, q):
    lists, cap = example.shape
    ex = deep.shape[1]
    rows = ex // LANES
    n1, n2 = h1.shape[0], h2.shape[0]
    half = dense_t.shape[0] // 2 + n1 // 4
    count = (n1 + 2 * n2) // LANES
    big = (dense_t, h1, h2, s2, q)
    return pl.pallas_call(
        step_kernel,
        out_shape=(
            jax.ShapeDtypeStruct((rows, LANES), f32),
            jax.ShapeDtypeStruct((lists, 8 + count, LANES), f32),
            jax.ShapeDtypeStruct((half, n1), bf16),
            jax.ShapeDtypeStruct((half, n1), bf16),
        ),
        in_specs=[VM, VM, VM, VM] + [ANY] * 5,
        out_specs=(VM, VM, VM, VM),
        scratch_shapes=[
            pltpu.VMEM((LANES, lists * LANES), bf16),
            pltpu.VMEM((2 * rows, lists * LANES), bf16),
        ]
        + [pltpu.VMEM(a.shape, a.dtype) for a in big]
        + [pltpu.SemaphoreType.DMA((5,))],
        compiler_params=params(),
        name="step",
    )(logits, example, deep, labels.reshape(rows, LANES), *big)


def state_kernel(got_ref, res_ref, z_ref, n_ref, z_out, n_out, small_ref):
    lists = got_ref.shape[0]
    cap = got_ref.shape[1] - 8
    blocks, width = z_ref.shape
    left = iota((1, LANES), 1) < cap
    grad = jnp.zeros((blocks, width), f32)
    for at in range(0, lists, 4):
        values, index = four_lists(got_ref, at, cap)
        res = [res_ref[at + k, 0:1, :] for k in range(4)]
        res = jnp.concatenate([jnp.where(left, res[0], res[1]), jnp.where(left, res[2], res[3])], axis=1)
        top, rest = split_two(jnp.where(iota((blocks, 4 * cap), 0) == index, res, 0.0))
        grad = grad + dot(jnp.concatenate([top, rest], axis=1), jnp.concatenate([values, values], axis=0))
    z, n = z_ref[...], n_ref[...]
    n_new = n + grad * grad
    sigma = (jnp.sqrt(n_new) - jnp.sqrt(n)) / alpha_rate
    n_out[...] = n_new
    z_out[...] = z + grad - sigma * wide_weight(z, n)
    small_ref[...] = functools.reduce(jnp.add, [res_ref[k, 8:, :] for k in range(lists)])


def new_states(got, res, z, n):
    count = res.shape[1] - 8
    return pl.pallas_call(
        state_kernel,
        out_shape=(
            jax.ShapeDtypeStruct(z.shape, f32),
            jax.ShapeDtypeStruct(z.shape, f32),
            jax.ShapeDtypeStruct((count, LANES), f32),
        ),
        in_specs=[VM] * 4,
        out_specs=(VM, VM, VM),
        compiler_params=params(),
        name="new_states",
    )(got, res, z, n)


def every_to_every(x):
    return lax.all_to_all(x, AXES, split_axis=0, concat_axis=0, tiled=True)


def swap(x, bit, devices):
    return lax.ppermute(x, AXES, [(i, i ^ bit) for i in range(devices)])


def add(a, b):
    return (a.astype(f32) + b.astype(f32)).astype(bf16)


def halves(x, side):
    rows = x.shape[0] // 2
    return lax.dynamic_slice_in_dim(x, side * rows, rows, 0)


def sum_everywhere(pieces, me, devices):
    bits = [1 << k for k in range(1, devices.bit_length() - 1)]
    inner, last = bits[:-1], bits[-1]
    orders = [inner, inner[-1:] + inner[:-1]]
    pieces = list(pieces)
    for k in range(len(inner)):
        got = []
        for p, order in zip(pieces, orders):
            side = (me // order[k]) % 2
            got.append(swap(halves(p, 1 - side), order[k], devices))
        pieces = [
            add(halves(p, (me // order[k]) % 2), g) for p, order, g in zip(pieces, orders, got)
        ]
    pieces = [add(p, g) for p, g in zip(pieces, [swap(p, last, devices) for p in pieces])]
    for k in reversed(range(len(inner))):
        got = [swap(p, order[k], devices) for p, order in zip(pieces, orders)]
        joined = []
        for p, order, g in zip(pieces, orders, got):
            side = (me // order[k]) % 2
            joined.append(jnp.concatenate([jnp.where(side == 0, p, g), jnp.where(side == 0, g, p)], axis=0))
        pieces = joined
    return pieces


def per_device(
    devices,
    dense,
    labels,
    tile_values,
    tile_block,
    tile_example,
    tile_count,
    z_state,
    n_state,
    w_one,
    b_one,
    w_two,
    b_two,
    head,
):
    n1, n2 = w_two.shape
    din = dense.shape[1]
    me = lax.axis_index(AXES)
    core = me % 2
    got = every_to_every(pack(tile_values, tile_block, tile_count))
    dense_t, h1, h2, s2, q, deep, wcat = tower(dense, w_one, b_one, w_two, b_two, head, z_state, n_state)
    logits = every_to_every(slot_logits(got, wcat))
    prob, res, send, keep = step(logits, tile_example, deep, labels, dense_t, h1, h2, s2, q)
    own = add(keep, swap(send, 1, devices))
    got_res = every_to_every(res)
    z_new, n_new, small = new_states(got, got_res, z_state, n_state)
    cut = own.shape[0] // 2
    own = jnp.concatenate(sum_everywhere((own[:cut], own[cut:]), me, devices), axis=0)
    other = swap(own, 1, devices)
    first, second = jnp.where(core == 0, own, other), jnp.where(core == 0, other, own)
    big = din // 2
    grad_w_one = jnp.concatenate([first[:big], second[:big]], axis=0).astype(f32)
    packed = jnp.concatenate([first[big:], second[big:]], axis=0).astype(f32)
    grad_w_two = jnp.concatenate([packed[:, :n2], packed[:, n2:]], axis=0)
    small = small.reshape(-1)
    return (
        prob.reshape(-1),
        z_new,
        n_new,
        grad_w_one,
        small[:n1],
        grad_w_two,
        small[n1 : n1 + n2],
        small[n1 + n2 :],
    )


def solution(mesh):
    placed = (
        P(AXES, None),
        P(AXES),
        P(AXES, None, None),
        P(AXES, None),
        P(AXES, None),
        P(AXES),
        P(AXES, None),
        P(AXES, None),
        P(),
        P(),
        P(),
        P(),
        P(),
    )
    devices = mesh.shape["blk"] * mesh.shape["rep"]
    return jax.shard_map(
        functools.partial(per_device, devices),
        mesh=mesh,
        in_specs=placed,
        out_specs=(P(AXES), P(AXES, None), P(AXES, None), P(), P(), P(), P(), P()),
        check_vma=False,
    )
```

time: 225 us -> 105 us (0.47)
  waiting for transfers between devices: 72.9 us -> 20 us
  other arithmetic: 41.6 us -> 4.46 us
  blocking collectives: 40.7 us -> 12.8 us
  Pallas kernels: 0 us -> 18.4 us
  matrix products: 14.3 us -> 0 us
  between operations: 14.3 us -> 1.1 us
  starting transfers between devices: 18.8 us -> 30.1 us
  local copies, waits for them, and re-layouts: 22.1 us -> 17.6 us
    psum x1 -> x0, waiting for transfers between devices: 62.1 us -> none  [per_device(): lax.psum((grad_head, grad_w_two, grad_b_two, grad_w_one, grad_b_one), ('b...]
    psum x1 -> x0, blocking collectives: 40.7 us -> none  [per_device(): lax.psum((grad_head, grad_w_two, grad_b_two, grad_w_one, grad_b_one), ('b...]
    scatter-add x2 -> x0, other arithmetic: 26.6 us -> none  [the longest x1 14.7 us: per_device(): jnp.zeros((dense.shape[0],), jnp.float32).at[flat_example]]
    ppermute x0 -> x16, starting transfers between devices: none -> 20.1 us  [swap(): return lax.ppermute(x, AXES, [(i, i ^ bit) for i in range(devices)])]
    ppermute x0 -> x16, waiting for transfers between devices: none -> 20 us  [swap(): return lax.ppermute(x, AXES, [(i, i ^ bit) for i in range(devices)])]
    pallas_call x0 -> x5, Pallas kernels: none -> 18.4 us  [the longest x1 6.77 us: tower(): pl.pallas_call(tower_kernel, grid=(steps,), out_shape=(jax.ShapeDtypeStru...]
    gather x3 -> x0, local copies, waits for them, and re-layouts: 16.3 us -> none  [the longest x2 8.66 us: per_device(): tile_residual = jnp.take(residual, flat_example).reshape(owners, capacity)]
    dot_general x7 -> x0, matrix products: 14.3 us -> none  [the longest x1 4.04 us: per_device(): pre_one = jnp.dot(dense, w_one, preferred_element_type=jnp.float32) + b_one]
  transfers between devices with their start and end apart: 5 -> 18, of which waited for: 3 -> 12; matrix products, arithmetic and copies ran while one was open for 21% -> 2% of each run, Pallas kernels for 0% -> 11%
where the time goes in v1:
time: 105 us; the launch traced here: 104 us
  starting transfers between devices  30.1 us (29%)
  waiting for transfers between devices  20 us (19%)
  Pallas kernels  18.4 us (18%)
  local copies, waits for them, and re-layouts  17.6 us (17%)
  blocking collectives  12.8 us (12%)
  other arithmetic  4.46 us (4%)
  between operations  1.1 us (1%)
    ppermute x16, starting transfers between devices, swap(): return lax.ppermute(x, AXES, [(i, i ^ bit) for i in range(devices)])  20.1 us
    ppermute x16, waiting for transfers between devices, swap(): return lax.ppermute(x, AXES, [(i, i ^ bit) for i in range(devices)])  20 us
    unnamed x46, local copies, waits for them, and re-layouts  16.2 us
    all_to_all x1, blocking collectives, every_to_every(): return lax.all_to_all(x, AXES, split_axis=0, concat_axis=0, tiled=True)  12.8 us
    all_to_all x2, starting transfers between devices, every_to_every(): return lax.all_to_all(x, AXES, split_axis=0, concat_axis=0, tiled=True)  10.1 us
    pallas_call x1, Pallas kernels, tower(): pl.pallas_call(tower_kernel, grid=(steps,), out_shape=(jax.ShapeDtypeStru...  6.77 us
    pallas_call x1, Pallas kernels, step(): pl.pallas_call(step_kernel, out_shape=(jax.ShapeDtypeStruct((rows, LANES)...  4.94 us
    pallas_call x1, Pallas kernels, new_states(): pl.pallas_call(state_kernel, out_shape=(jax.ShapeDtypeStruct(z.shape, f32...  4.32 us
  transfers between devices with their start and end apart: 18, of which 12 were waited for; matrix products, arithmetic and copies ran while one was open for 2% of the time, Pallas kernels for 11%

profile of v1, /device:TPU:0, one launch (start us, length us, event | category | flops | bytes accessed | tf_op | source)
XLA Modules:
  0.0 104.5 jit_solution(16242337790359348734)
XLA Ops:
  0.7 1.0 copy-done.6
  4.1 7.3 %all-to-all-start = ((bf16[32,72,128]{2,1,0:T(8,128)(2,1)}), bf16[32,72,128]{2,1,0:T(8,128)(2,1)S(1)}, u32[]{:S(2)}, u32[]{:S(2)}) async-start(bf16[32,72,128]{2,1,0:T(8,128)(2,1)} %pack.1), calls=%async_computation | async-start | bytes 1179648 | tf_op jit(solution)/shard_map/all_to_all | solution.py:325
  13.5 1.6 %copy-done.17 = bf16[1024,1024]{1,0:T(8,128)(2,1)S(1)} copy-done((bf16[1024,1024]{1,0:T(8,128)(2,1)S(1)}, bf16[1024,1024]{1,0:T(8,128)(2,1)}, u32[]{:S(2)}) %copy-start.17) | copy-done | bytes 2097176
  15.1 1.2 %copy-done.18 = bf16[1024,512]{1,0:T(8,128)(2,1)S(1)} copy-done((bf16[1024,512]{1,0:T(8,128)(2,1)S(1)}, bf16[1024,512]{1,0:T(8,128)(2,1)}, u32[]{:S(2)}) %copy-start.18) | copy-done | bytes 1048600
  17.3 6.8 %tower.1 = (bf16[1024,1024]{1,0:T(8,128)(2,1)S(1)}, bf16[512,1024]{1,0:T(8,128)(2,1)S(1)}, bf16[256,1024]{1,0:T(8,128)(2,1)S(1)}, f32[256,1024]{1,0:T(8,128)S(1)...) custom-call(bf16[1024,1024]{1,0:T(8,128)(2,1)S(1)} %copy-done.17, ...), custom_call_target="tpu_custom_call" | custom-call | flops 1610612736 | bytes 12582912 | tf_op jit(solution)/shard_map/tower/pallas_call | solution.py:124
  24.1 1.3 %copy-done = f32[512,1024]{1,0:T(8,128)} copy-done((f32[512,1024]{1,0:T(8,128)}, f32[512,1024]{1,0:T(8,128)S(1)}, u32[]{:S(2)}) %copy-start) | copy-done | bytes 2097176
  28.1 1.3 %slot_logits.1 = f32[32,1,128]{2,1,0:T(1,128)S(1)} custom-call(bf16[32,72,128]{2,1,0:T(8,128)(2,1)S(1)} %all-to-all-done.got_ref, bf16[1024,256]{1,0:T(8,128)(2,1)S(1)} %get-tuple-element.22.wcat_ref), custom_call_target="tpu_custom_call" | custom-call | tf_op jit(solution)/shard_map/slot_logits/pallas_call | solution.py:179
  29.5 12.8 %all_to_all.15.logit_ref = f32[32,1,128]{2,1,0:T(1,128)S(1)} all-to-all(f32[32,1,128]{2,1,0:T(1,128)S(1)} %slot_logits.1), channel_id=1, replica_groups=mesh['blk'=8,'rep'=4] {'blk','rep'}, dimensions={0} | all-to-all | bytes 32768 | tf_op jit(solution)/shard_map/all_to_all | solution.py:325
  42.3 1.6 %copy-done.1 = f32[512,1024]{1,0:T(8,128)S(1)} copy-done((f32[512,1024]{1,0:T(8,128)S(1)}, f32[512,1024]{1,0:T(8,128)}, u32[]{:S(2)}) %copy-start.1) | copy-done | bytes 2097176
  43.9 1.2 %copy-done.5 = f32[256,1024]{1,0:T(8,128)S(1)} copy-done((f32[256,1024]{1,0:T(8,128)S(1)}, f32[256,1024]{1,0:T(8,128)}, u32[]{:S(2)}) %copy-start.5) | copy-done | bytes 1048600
  46.2 4.9 %step.1 = (f32[8,128]{1,0:T(8,128)}, f32[32,16,128]{2,1,0:T(8,128)}, bf16[640,512]{1,0:T(8,128)(2,1)}, bf16[640,512]{1,0:T(8,128)(2,1)S(1)}) custom-call(f32[32,1,128]{2,1,0:T(1,128)S(1)} %all_to_all.15.logit_ref, s32[32,64]{1,0:T(8,128)S(1)} %copy-done.14, f32[1,1024]{1,0:T(1,128)S(1)} %get-tuple-element.23.deep_ref, s32[8,128]{1,0:T(8,128)S(1)} %bitcast.11, ...), custom_call_target="tpu_custom_call" | custom-call | tf_op jit(solution)/shard_map/step/pallas_call | solution.py:267
  51.2 2.3 %collective-permute-done = bf16[640,512]{1,0:T(8,128)(2,1)S(1)} collective-permute-done((bf16[640,512]{1,0:T(8,128)(2,1)}, bf16[640,512]{1,0:T(8,128)(2,1)S(1)}, u32[]{:S(2)}, u32[]{:S(2)}) %collective-permute-start) | collective-permute-done | bytes 655392 | tf_op jit(solution)/shard_map/ppermute | solution.py:329
  54.4 2.8 %all-to-all-start.2 = ((f32[32,16,128]{2,1,0:T(8,128)}), f32[32,16,128]{2,1,0:T(8,128)S(1)}, u32[]{:S(2)}, u32[]{:S(2)}) async-start(f32[32,16,128]{2,1,0:T(8,128)} %get-tuple-element.30), calls=%async_computation.2 | async-start | bytes 524288 | tf_op jit(solution)/shard_map/all_to_all | solution.py:325
  57.2 1.5 %collective-permute-start.1 = (bf16[160,512]{1,0:T(8,128)(2,1)S(1)}, bf16[160,512]{1,0:T(8,128)(2,1)S(1)}, u32[]{:S(2)}, u32[]{:S(2)}) collective-permute-start(bf16[160,512]{1,0:T(8,128)(2,1)S(1)} %constant_dynamic-slice_fusion.5), channel_id=1, source_target_pairs={{0,2},{1,3},{2,0},{3,1},{4,6},{5,7},{6,4},{7,5},{8,10},{9,11},{10,... | collective-permute-start | bytes 491528 | tf_op jit(solution)/shard_map/ppermute | solution.py:329
  58.7 1.6 %collective-permute-done.8 = bf16[160,512]{1,0:T(8,128)(2,1)S(1)} collective-permute-done((bf16[160,512]{1,0:T(8,128)(2,1)S(1)}, bf16[160,512]{1,0:T(8,128)(2,1)S(1)}, u32[]{:S(2)}, u32[]{:S(2)}) %collective-permute-start.8) | collective-permute-done | bytes 163872 | tf_op jit(solution)/shard_map/ppermute | solution.py:329
  60.7 5.7 %collective-permute-done.1 = bf16[160,512]{1,0:T(8,128)(2,1)S(1)} collective-permute-done((bf16[160,512]{1,0:T(8,128)(2,1)S(1)}, bf16[160,512]{1,0:T(8,128)(2,1)S(1)}, u32[]{:S(2)}, u32[]{:S(2)}) %collective-permute-start.1) | collective-permute-done | bytes 163872 | tf_op jit(solution)/shard_map/ppermute | solution.py:329
  66.5 1.5 %collective-permute-start.2 = (bf16[80,512]{1,0:T(8,128)(2,1)S(1)}, bf16[80,512]{1,0:T(8,128)(2,1)S(1)}, u32[]{:S(2)}, u32[]{:S(2)}) collective-permute-start(bf16[80,512]{1,0:T(8,128)(2,1)S(1)} %constant_dynamic-slice_fusion.4), channel_id=1, source_target_pairs={{0,4},{1,5},{2,6},{3,7},{4,0},{5,1},{6,2},{7,3},{8,12},{9,13},{10,... | collective-permute-start | bytes 245768 | tf_op jit(solution)/shard_map/ppermute | solution.py:329
  68.0 1.4 %collective-permute-start.10 = (bf16[40,512]{1,0:T(8,128)(2,1)S(1)}, bf16[40,512]{1,0:T(8,128)(2,1)S(1)}, u32[]{:S(2)}, u32[]{:S(2)}) collective-permute-start(bf16[40,512]{1,0:T(8,128)(2,1)S(1)} %constant_dynamic-slice_fusion), channel_id=1, source_target_pairs={{0,4},{1,5},{2,6},{3,7},{4,0},{5,1},{6,2},{7,3},{8,12},{9,13},{10,... | collective-permute-start | bytes 122888 | tf_op jit(solution)/shard_map/ppermute | solution.py:329
  69.4 2.0 %collective-permute-done.2 = bf16[80,512]{1,0:T(8,128)(2,1)S(1)} collective-permute-done((bf16[80,512]{1,0:T(8,128)(2,1)S(1)}, bf16[80,512]{1,0:T(8,128)(2,1)S(1)}, u32[]{:S(2)}, u32[]{:S(2)}) %collective-permute-start.2) | collective-permute-done | bytes 81952 | tf_op jit(solution)/shard_map/ppermute | solution.py:329
  71.5 1.6 %collective-permute-start.3 = (bf16[40,512]{1,0:T(8,128)(2,1)S(1)}, bf16[40,512]{1,0:T(8,128)(2,1)S(1)}, u32[]{:S(2)}, u32[]{:S(2)}) collective-permute-start(bf16[40,512]{1,0:T(8,128)(2,1)S(1)} %constant_dynamic-slice_fusion.3), channel_id=1, source_target_pairs={{0,8},{1,9},{2,10},{3,11},{4,12},{5,13},{6,14},{7,15},{8,0},{9,1},... | collective-permute-start | bytes 122888 | tf_op jit(solution)/shard_map/ppermute | solution.py:329
  73.1 2.5 %collective-permute-start.11 = (bf16[40,512]{1,0:T(8,128)(2,1)S(1)}, bf16[40,512]{1,0:T(8,128)(2,1)S(1)}, u32[]{:S(2)}, u32[]{:S(2)}) collective-permute-start(bf16[40,512]{1,0:T(8,128)(2,1)S(1)} %add_convert_fusion.6), channel_id=1, source_target_pairs={{0,16},{1,17},{2,18},{3,19},{4,20},{5,21},{6,22},{7,23},{8,24},{9,... | collective-permute-start | bytes 122888 | tf_op jit(solution)/shard_map/ppermute | solution.py:329
  75.6 2.4 %collective-permute-start.4 = (bf16[40,512]{1,0:T(8,128)(2,1)S(1)}, bf16[40,512]{1,0:T(8,128)(2,1)S(1)}, u32[]{:S(2)}, u32[]{:S(2)}) collective-permute-start(bf16[40,512]{1,0:T(8,128)(2,1)S(1)} %add_convert_fusion.8), channel_id=1, source_target_pairs={{0,16},{1,17},{2,18},{3,19},{4,20},{5,21},{6,22},{7,23},{8,24},{9,... | collective-permute-start | bytes 122888 | tf_op jit(solution)/shard_map/ppermute | solution.py:329
  78.9 1.6 %collective-permute-start.12 = (bf16[40,512]{1,0:T(8,128)(2,1)S(1)}, bf16[40,512]{1,0:T(8,128)(2,1)S(1)}, u32[]{:S(2)}, u32[]{:S(2)}) collective-permute-start(bf16[40,512]{1,0:T(8,128)(2,1)S(1)} %add_convert_fusion.5), channel_id=1, source_target_pairs={{0,4},{1,5},{2,6},{3,7},{4,0},{5,1},{6,2},{7,3},{8,12},{9,13},{10,... | collective-permute-start | bytes 122888 | tf_op jit(solution)/shard_map/ppermute | solution.py:329
  80.7 2.1 %collective-permute-start.5 = (bf16[40,512]{1,0:T(8,128)(2,1)S(1)}, bf16[40,512]{1,0:T(8,128)(2,1)S(1)}, u32[]{:S(2)}, u32[]{:S(2)}) collective-permute-start(bf16[40,512]{1,0:T(8,128)(2,1)S(1)} %add_convert_fusion.7), channel_id=1, source_target_pairs={{0,8},{1,9},{2,10},{3,11},{4,12},{5,13},{6,14},{7,15},{8,0},{9,1},... | collective-permute-start | bytes 122888 | tf_op jit(solution)/shard_map/ppermute | solution.py:329
  84.8 1.5 %collective-permute-start.6 = (bf16[80,512]{1,0:T(8,128)(2,1)S(1)}, bf16[80,512]{1,0:T(8,128)(2,1)S(1)}, u32[]{:S(2)}, u32[]{:S(2)}) collective-permute-start(bf16[80,512]{1,0:T(8,128)(2,1)S(1)} %pad_maximum_fusion.4), channel_id=1, source_target_pairs={{0,4},{1,5},{2,6},{3,7},{4,0},{5,1},{6,2},{7,3},{8,12},{9,13},{10,... | collective-permute-start | bytes 245768 | tf_op jit(solution)/shard_map/ppermute | solution.py:329
  86.3 1.2 %collective-permute-done.13 = bf16[80,512]{1,0:T(8,128)(2,1)S(1)} collective-permute-done((bf16[80,512]{1,0:T(8,128)(2,1)S(1)}, bf16[80,512]{1,0:T(8,128)(2,1)S(1)}, u32[]{:S(2)}, u32[]{:S(2)}) %collective-permute-start.13) | collective-permute-done | bytes 81952 | tf_op jit(solution)/shard_map/ppermute | solution.py:329
  87.6 1.1 %collective-permute-start.14 = (bf16[160,512]{1,0:T(8,128)(2,1)S(1)}, bf16[160,512]{1,0:T(8,128)(2,1)S(1)}, u32[]{:S(2)}, u32[]{:S(2)}) collective-permute-start(bf16[160,512]{1,0:T(8,128)(2,1)S(1)} %pad_maximum_fusion.3), channel_id=1, source_target_pairs={{0,8},{1,9},{2,10},{3,11},{4,12},{5,13},{6,14},{7,15},{8,0},{9,1},... | collective-permute-start | bytes 491528 | tf_op jit(solution)/shard_map/ppermute | solution.py:329
  90.3 2.7 %collective-permute-done.14 = bf16[160,512]{1,0:T(8,128)(2,1)S(1)} collective-permute-done((bf16[160,512]{1,0:T(8,128)(2,1)S(1)}, bf16[160,512]{1,0:T(8,128)(2,1)S(1)}, u32[]{:S(2)}, u32[]{:S(2)}) %collective-permute-start.14) | collective-permute-done | bytes 163872 | tf_op jit(solution)/shard_map/ppermute | solution.py:329
  93.0 1.8 %collective-permute-done.7 = bf16[160,512]{1,0:T(8,128)(2,1)S(1)} collective-permute-done((bf16[160,512]{1,0:T(8,128)(2,1)S(1)}, bf16[160,512]{1,0:T(8,128)(2,1)S(1)}, u32[]{:S(2)}, u32[]{:S(2)}) %collective-permute-start.7) | collective-permute-done | bytes 163872 | tf_op jit(solution)/shard_map/ppermute | solution.py:329
  95.0 4.3 %new_states.1 = (f32[1024,128]{1,0:T(8,128)}, f32[1024,128]{1,0:T(8,128)}, f32[8,128]{1,0:T(8,128)S(1)}) custom-call(bf16[32,72,128]{2,1,0:T(8,128)(2,1)S(1)} %all-to-all-done.got_ref, f32[32,16,128]{2,1,0:T(8,128)S(1)} %all-to-all-done.2.res_ref, f32[1024,128]{1,0:T(8,128)S(1)} %copy-done.8, f32[1024,128]{1,0:T(8,128)S(1)} %copy-done.10), custom_call_target="tpu_custom_call" | custom-call | tf_op jit(solution)/shard_map/new_states/pallas_call | solution.py:310
  100.5 1.3 %broadcast_select_fusion.1 = (bf16[640,512]{1,0:T(8,128)(2,1)S(1)}, bf16[640,512]{1,0:T(8,128)(2,1)S(1)}) fusion(bf16[640,512]{1,0:T(8,128)(2,1)} %collective-permute-done.15, pred[]{:T(512)S(6)} %eq.42, bf16[160,512]{1,0:T(8,128)(2,1)S(1)} %get-tuple-element.45, bf16[160,512]{1,0:T(8,128)(2,1)S(1)} %get-tuple-element.44, ...), kind=kLoop, calls=%fused_computation.4 | loop fusion | flops 3276800 | bytes 2621441 | tf_op jit(solution)/shard_map/jit(_where)/select_n | solution.py:395
  102.0 1.6 %maximum_convert_fusion = f32[1024,512]{1,0:T(8,128)} fusion(bf16[512,512]{1,0:T(8,128)(2,1)S(1)} %slice.59, bf16[512,512]{1,0:T(8,128)(2,1)S(1)} %slice.58), kind=kLoop, calls=%fused_computation.1 | loop fusion | flops 2097152 | bytes 3145728 | tf_op jit(solution)/shard_map/convert_element_type | solution.py:397
  (95 shorter events, 17.9 us)
Async XLA Ops:
  0.6 10.7 %copy-start.22 = (bf16[256]{0:T(256)(128)(2,1)S(1)}, bf16[256]{0:T(256)(128)(2,1)}, u32[]{:S(2)}) copy-start(bf16[256]{0:T(256)(128)(2,1)} %param.25) | copy-start | bytes 1540
  0.6 10.8 %copy-start.21 = (f32[256]{0:T(256)S(1)}, f32[256]{0:T(256)}, u32[]{:S(2)}) copy-start(f32[256]{0:T(256)} %param.24) | copy-start | bytes 3076
  0.7 1.1 %copy-start.6 = (bf16[32,64,128]{2,1,0:T(8,128)(2,1)S(1)}, bf16[32,64,128]{2,1,0:T(8,128)(2,1)}, u32[]{:S(2)}) copy-start(bf16[32,64,128]{2,1,0:T(8,128)(2,1)} %values_ref.1) | copy-start | bytes 1572868
  3.1 8.3 %copy-start.20 = (f32[512]{0:T(512)S(1)}, f32[512]{0:T(512)}, u32[]{:S(2)}) copy-start(f32[512]{0:T(512)} %param.22) | copy-start | bytes 6148
  4.1 24.1 %all-to-all-start = ((bf16[32,72,128]{2,1,0:T(8,128)(2,1)}), bf16[32,72,128]{2,1,0:T(8,128)(2,1)S(1)}, u32[]{:S(2)}, u32[]{:S(2)}) async-start(bf16[32,72,128]{2,1,0:T(8,128)(2,1)} %pack.1), calls=%async_computation | async-start | bytes 1179648 | tf_op jit(solution)/shard_map/all_to_all | solution.py:325
  13.5 1.6 %copy-start.17 = (bf16[1024,1024]{1,0:T(8,128)(2,1)S(1)}, bf16[1024,1024]{1,0:T(8,128)(2,1)}, u32[]{:S(2)}) copy-start(bf16[1024,1024]{1,0:T(8,128)(2,1)} %dense_ref.1) | copy-start | bytes 6291460
  15.1 1.2 %copy-start.18 = (bf16[1024,512]{1,0:T(8,128)(2,1)S(1)}, bf16[1024,512]{1,0:T(8,128)(2,1)}, u32[]{:S(2)}) copy-start(bf16[1024,512]{1,0:T(8,128)(2,1)} %w1_ref.1) | copy-start | bytes 3145732
  17.3 25.0 %copy-start.14 = (s32[32,64]{1,0:T(8,128)S(1)}, s32[32,64]{1,0:T(8,128)}, u32[]{:S(2)}) copy-start(s32[32,64]{1,0:T(8,128)} %example_ref.1) | copy-start | bytes 24580
  17.3 25.0 %copy-start.15 = (s32[1024]{0:T(1024)S(1)}, s32[1024]{0:T(1024)}, u32[]{:S(2)}) copy-start(s32[1024]{0:T(1024)} %param.14) | copy-start | bytes 12292
  24.1 1.3 %copy-start = (f32[512,1024]{1,0:T(8,128)}, f32[512,1024]{1,0:T(8,128)S(1)}, u32[]{:S(2)}) copy-start(f32[512,1024]{1,0:T(8,128)S(1)} %get-tuple-element.28.q_any) | copy-start | bytes 6291460
  28.1 14.1 %copy-start.3 = (bf16[512,1024]{1,0:T(8,128)(2,1)S(1)}, bf16[512,1024]{1,0:T(8,128)(2,1)}, u32[]{:S(2)}) copy-start(bf16[512,1024]{1,0:T(8,128)(2,1)} %copy-done.2) | copy-start | bytes 3145732
  42.3 1.6 %copy-start.1 = (f32[512,1024]{1,0:T(8,128)S(1)}, f32[512,1024]{1,0:T(8,128)}, u32[]{:S(2)}) copy-start(f32[512,1024]{1,0:T(8,128)} %copy-done) | copy-start | bytes 6291460
  43.9 1.2 %copy-start.5 = (f32[256,1024]{1,0:T(8,128)S(1)}, f32[256,1024]{1,0:T(8,128)}, u32[]{:S(2)}) copy-start(f32[256,1024]{1,0:T(8,128)} %copy-done.4) | copy-start | bytes 3145732
  51.1 2.4 %collective-permute-start = (bf16[640,512]{1,0:T(8,128)(2,1)}, bf16[640,512]{1,0:T(8,128)(2,1)S(1)}, u32[]{:S(2)}, u32[]{:S(2)}) collective-permute-start(bf16[640,512]{1,0:T(8,128)(2,1)} %get-tuple-element.34), channel_id=1, source_target_pairs={{0,1},{1,0},{2,3},{3,2},{4,5},{5,4},{6,7},{7,6},{8,9},{9,8},{10,11... | collective-permute-start | bytes 1966088 | tf_op jit(solution)/shard_map/ppermute | solution.py:329
  53.7 6.5 %collective-permute-start.8 = (bf16[160,512]{1,0:T(8,128)(2,1)S(1)}, bf16[160,512]{1,0:T(8,128)(2,1)S(1)}, u32[]{:S(2)}, u32[]{:S(2)}) collective-permute-start(bf16[160,512]{1,0:T(8,128)(2,1)S(1)} %constant_dynamic-slice_fusion.2), channel_id=1, source_target_pairs={{0,8},{1,9},{2,10},{3,11},{4,12},{5,13},{6,14},{7,15},{8,0},{9,1},... | collective-permute-start | bytes 491528 | tf_op jit(solution)/shard_map/ppermute | solution.py:329
  54.4 40.6 %all-to-all-start.2 = ((f32[32,16,128]{2,1,0:T(8,128)}), f32[32,16,128]{2,1,0:T(8,128)S(1)}, u32[]{:S(2)}, u32[]{:S(2)}) async-start(f32[32,16,128]{2,1,0:T(8,128)} %get-tuple-element.30), calls=%async_computation.2 | async-start | bytes 524288 | tf_op jit(solution)/shard_map/all_to_all | solution.py:325
  57.2 9.2 %collective-permute-start.1 = (bf16[160,512]{1,0:T(8,128)(2,1)S(1)}, bf16[160,512]{1,0:T(8,128)(2,1)S(1)}, u32[]{:S(2)}, u32[]{:S(2)}) collective-permute-start(bf16[160,512]{1,0:T(8,128)(2,1)S(1)} %constant_dynamic-slice_fusion.5), channel_id=1, source_target_pairs={{0,2},{1,3},{2,0},{3,1},{4,6},{5,7},{6,4},{7,5},{8,10},{9,11},{10,... | collective-permute-start | bytes 491528 | tf_op jit(solution)/shard_map/ppermute | solution.py:329
  60.3 7.6 %collective-permute-start.9 = (bf16[80,512]{1,0:T(8,128)(2,1)S(1)}, bf16[80,512]{1,0:T(8,128)(2,1)S(1)}, u32[]{:S(2)}, u32[]{:S(2)}) collective-permute-start(bf16[80,512]{1,0:T(8,128)(2,1)S(1)} %constant_dynamic-slice_fusion.1), channel_id=1, source_target_pairs={{0,2},{1,3},{2,0},{3,1},{4,6},{5,7},{6,4},{7,5},{8,10},{9,11},{10,... | collective-permute-start | bytes 245768 | tf_op jit(solution)/shard_map/ppermute | solution.py:329
  66.5 4.9 %collective-permute-start.2 = (bf16[80,512]{1,0:T(8,128)(2,1)S(1)}, bf16[80,512]{1,0:T(8,128)(2,1)S(1)}, u32[]{:S(2)}, u32[]{:S(2)}) collective-permute-start(bf16[80,512]{1,0:T(8,128)(2,1)S(1)} %constant_dynamic-slice_fusion.4), channel_id=1, source_target_pairs={{0,4},{1,5},{2,6},{3,7},{4,0},{5,1},{6,2},{7,3},{8,12},{9,13},{10,... | collective-permute-start | bytes 245768 | tf_op jit(solution)/shard_map/ppermute | solution.py:329
  68.0 5.0 %collective-permute-start.10 = (bf16[40,512]{1,0:T(8,128)(2,1)S(1)}, bf16[40,512]{1,0:T(8,128)(2,1)S(1)}, u32[]{:S(2)}, u32[]{:S(2)}) collective-permute-start(bf16[40,512]{1,0:T(8,128)(2,1)S(1)} %constant_dynamic-slice_fusion), channel_id=1, source_target_pairs={{0,4},{1,5},{2,6},{3,7},{4,0},{5,1},{6,2},{7,3},{8,12},{9,13},{10,... | collective-permute-start | bytes 122888 | tf_op jit(solution)/shard_map/ppermute | solution.py:329
  71.5 4.1 %collective-permute-start.3 = (bf16[40,512]{1,0:T(8,128)(2,1)S(1)}, bf16[40,512]{1,0:T(8,128)(2,1)S(1)}, u32[]{:S(2)}, u32[]{:S(2)}) collective-permute-start(bf16[40,512]{1,0:T(8,128)(2,1)S(1)} %constant_dynamic-slice_fusion.3), channel_id=1, source_target_pairs={{0,8},{1,9},{2,10},{3,11},{4,12},{5,13},{6,14},{7,15},{8,0},{9,1},... | collective-permute-start | bytes 122888 | tf_op jit(solution)/shard_map/ppermute | solution.py:329
  73.1 5.8 %collective-permute-start.11 = (bf16[40,512]{1,0:T(8,128)(2,1)S(1)}, bf16[40,512]{1,0:T(8,128)(2,1)S(1)}, u32[]{:S(2)}, u32[]{:S(2)}) collective-permute-start(bf16[40,512]{1,0:T(8,128)(2,1)S(1)} %add_convert_fusion.6), channel_id=1, source_target_pairs={{0,16},{1,17},{2,18},{3,19},{4,20},{5,21},{6,22},{7,23},{8,24},{9,... | collective-permute-start | bytes 122888 | tf_op jit(solution)/shard_map/ppermute | solution.py:329
  75.6 5.1 %collective-permute-start.4 = (bf16[40,512]{1,0:T(8,128)(2,1)S(1)}, bf16[40,512]{1,0:T(8,128)(2,1)S(1)}, u32[]{:S(2)}, u32[]{:S(2)}) collective-permute-start(bf16[40,512]{1,0:T(8,128)(2,1)S(1)} %add_convert_fusion.8), channel_id=1, source_target_pairs={{0,16},{1,17},{2,18},{3,19},{4,20},{5,21},{6,22},{7,23},{8,24},{9,... | collective-permute-start | bytes 122888 | tf_op jit(solution)/shard_map/ppermute | solution.py:329
  78.9 4.1 %collective-permute-start.12 = (bf16[40,512]{1,0:T(8,128)(2,1)S(1)}, bf16[40,512]{1,0:T(8,128)(2,1)S(1)}, u32[]{:S(2)}, u32[]{:S(2)}) collective-permute-start(bf16[40,512]{1,0:T(8,128)(2,1)S(1)} %add_convert_fusion.5), channel_id=1, source_target_pairs={{0,4},{1,5},{2,6},{3,7},{4,0},{5,1},{6,2},{7,3},{8,12},{9,13},{10,... | collective-permute-start | bytes 122888 | tf_op jit(solution)/shard_map/ppermute | solution.py:329
  80.7 4.1 %collective-permute-start.5 = (bf16[40,512]{1,0:T(8,128)(2,1)S(1)}, bf16[40,512]{1,0:T(8,128)(2,1)S(1)}, u32[]{:S(2)}, u32[]{:S(2)}) collective-permute-start(bf16[40,512]{1,0:T(8,128)(2,1)S(1)} %add_convert_fusion.7), channel_id=1, source_target_pairs={{0,8},{1,9},{2,10},{3,11},{4,12},{5,13},{6,14},{7,15},{8,0},{9,1},... | collective-permute-start | bytes 122888 | tf_op jit(solution)/shard_map/ppermute | solution.py:329
  83.0 4.5 %collective-permute-start.13 = (bf16[80,512]{1,0:T(8,128)(2,1)S(1)}, bf16[80,512]{1,0:T(8,128)(2,1)S(1)}, u32[]{:S(2)}, u32[]{:S(2)}) collective-permute-start(bf16[80,512]{1,0:T(8,128)(2,1)S(1)} %pad_maximum_fusion.5), channel_id=1, source_target_pairs={{0,2},{1,3},{2,0},{3,1},{4,6},{5,7},{6,4},{7,5},{8,10},{9,11},{10,... | collective-permute-start | bytes 245768 | tf_op jit(solution)/shard_map/ppermute | solution.py:329
  84.8 4.5 %collective-permute-start.6 = (bf16[80,512]{1,0:T(8,128)(2,1)S(1)}, bf16[80,512]{1,0:T(8,128)(2,1)S(1)}, u32[]{:S(2)}, u32[]{:S(2)}) collective-permute-start(bf16[80,512]{1,0:T(8,128)(2,1)S(1)} %pad_maximum_fusion.4), channel_id=1, source_target_pairs={{0,4},{1,5},{2,6},{3,7},{4,0},{5,1},{6,2},{7,3},{8,12},{9,13},{10,... | collective-permute-start | bytes 245768 | tf_op jit(solution)/shard_map/ppermute | solution.py:329
  87.6 5.4 %collective-permute-start.14 = (bf16[160,512]{1,0:T(8,128)(2,1)S(1)}, bf16[160,512]{1,0:T(8,128)(2,1)S(1)}, u32[]{:S(2)}, u32[]{:S(2)}) collective-permute-start(bf16[160,512]{1,0:T(8,128)(2,1)S(1)} %pad_maximum_fusion.3), channel_id=1, source_target_pairs={{0,8},{1,9},{2,10},{3,11},{4,12},{5,13},{6,14},{7,15},{8,0},{9,1},... | collective-permute-start | bytes 491528 | tf_op jit(solution)/shard_map/ppermute | solution.py:329
  89.4 5.6 %copy-start.8 = (f32[1024,128]{1,0:T(8,128)S(1)}, f32[1024,128]{1,0:T(8,128)}, u32[]{:S(2)}) copy-start(f32[1024,128]{1,0:T(8,128)} %z_ref.3) | copy-start | bytes 1572868
  89.4 5.6 %copy-start.10 = (f32[1024,128]{1,0:T(8,128)S(1)}, f32[1024,128]{1,0:T(8,128)}, u32[]{:S(2)}) copy-start(f32[1024,128]{1,0:T(8,128)} %n_ref.3) | copy-start | bytes 1572868
  89.4 5.4 %collective-permute-start.7 = (bf16[160,512]{1,0:T(8,128)(2,1)S(1)}, bf16[160,512]{1,0:T(8,128)(2,1)S(1)}, u32[]{:S(2)}, u32[]{:S(2)}) collective-permute-start(bf16[160,512]{1,0:T(8,128)(2,1)S(1)} %pad_maximum_fusion.2), channel_id=1, source_target_pairs={{0,2},{1,3},{2,0},{3,1},{4,6},{5,7},{6,4},{7,5},{8,10},{9,11},{10,... | collective-permute-start | bytes 491528 | tf_op jit(solution)/shard_map/ppermute | solution.py:329
  94.9 5.6 %collective-permute-start.15 = (bf16[640,512]{1,0:T(8,128)(2,1)S(1)}, bf16[640,512]{1,0:T(8,128)(2,1)}, u32[]{:S(2)}, u32[]{:S(2)}) collective-permute-start(bf16[640,512]{1,0:T(8,128)(2,1)S(1)} %pad_maximum_fusion), channel_id=1, source_target_pairs={{0,1},{1,0},{2,3},{3,2},{4,5},{5,4},{6,7},{7,6},{8,9},{9,8},{10,11... | collective-permute-start | bytes 1966088 | tf_op jit(solution)/shard_map/ppermute | solution.py:329
  (9 other events, 8.2 us)

commit v2 on v1

v2 whole, which is shorter than its diff:
```python
import functools
import jax
import jax.numpy as jnp
from jax import lax
from jax.experimental import pallas as pl
from jax.experimental.pallas import tpu as pltpu
from jax.sharding import PartitionSpec as P

alpha_rate = 0.5
beta_shift = 1.0
lasso_term = 0.5
ridge_term = 0.1

AXES = ("blk", "rep")
LANES = 128
f32 = jnp.float32
bf16 = jnp.bfloat16
NT = (((1,), (1,)), ((), ()))
NN = (((1,), (0,)), ((), ()))


def dot(a, b, dims=NN):
    return lax.dot_general(a, b, dims, preferred_element_type=f32)


def iota(shape, axis):
    return lax.broadcasted_iota(jnp.int32, shape, axis)


def split_two(x):
    top = x.astype(bf16)
    return top, (x - top.astype(f32)).astype(bf16)


def wide_weight(z, n):
    sign = jnp.where(z > 0, 1.0, jnp.where(z < 0, -1.0, 0.0))
    shrunk = z - sign * lasso_term
    denominator = (beta_shift + jnp.sqrt(n)) / alpha_rate + ridge_term
    return jnp.where(jnp.abs(z) > lasso_term, -shrunk / denominator, jnp.zeros_like(z))


def params(megabytes=40):
    return pltpu.CompilerParams(vmem_limit_bytes=megabytes << 20)


VM = pl.BlockSpec(memory_space=pltpu.VMEM)
ANY = pl.BlockSpec(memory_space=pl.ANY)
HBM = pl.BlockSpec(memory_space=pltpu.HBM)


def pack_kernel(values_any, block_any, count_any, out_any, block_ref, count_ref, buf, sems):
    lists, cap = block_ref.shape
    dead_index = 64
    parts = 4
    each = lists // parts
    small = [
        pltpu.make_async_copy(block_any, block_ref, sems.at[2 * parts]),
        pltpu.make_async_copy(count_any, count_ref, sems.at[2 * parts + 1]),
    ]
    spans = [pl.ds(k * each, each) for k in range(parts)]
    loads = [
        pltpu.make_async_copy(values_any.at[at], buf.at[at, pl.ds(0, cap)], sems.at[k])
        for k, at in enumerate(spans)
    ]
    stores = [
        pltpu.make_async_copy(buf.at[at], out_any.at[at], sems.at[parts + k]) for k, at in enumerate(spans)
    ]
    for copy in small + loads:
        copy.start()
    for copy in small:
        copy.wait()
    counts = jnp.sum(
        jnp.where(iota((lists, lists), 0) == iota((lists, lists), 1), count_ref[...], 0),
        axis=1,
        keepdims=True,
    )
    block = block_ref[...]
    high = jnp.where(iota((lists, cap), 1) < counts, block >> 5, dead_index)
    low = block & 31
    high = jnp.concatenate([high, high], axis=1).astype(f32)
    low = jnp.concatenate([low, low], axis=1).astype(f32)
    row = iota((8, LANES), 0)
    for k in range(lists):
        tail = jnp.where(row == 0, high[k : k + 1], jnp.where(row == 1, low[k : k + 1], 0.0))
        buf[k, cap : cap + 8, :] = tail.astype(bf16)
    for load, store in zip(loads, stores):
        load.wait()
        store.start()
    for store in stores:
        store.wait()


def pack(values, block, count):
    lists, cap, width = values.shape
    shape = (lists, cap + 8, width)
    return pl.pallas_call(
        pack_kernel,
        out_shape=jax.ShapeDtypeStruct(shape, bf16),
        in_specs=[ANY, ANY, ANY],
        out_specs=ANY,
        scratch_shapes=[
            pltpu.VMEM((lists, cap), jnp.int32),
            pltpu.VMEM((1, lists), jnp.int32),
            pltpu.VMEM(shape, bf16),
            pltpu.SemaphoreType.DMA((10,)),
        ],
        compiler_params=params(60),
        name="pack",
    )(values, block, count.reshape(1, lists))


def to_column(row):
    return jnp.transpose(jnp.broadcast_to(row, (8, row.shape[1])))[:, 0:1]


def tower_kernel(
    dense_ref, w1_ref, b1_ref, w2_ref, b2_ref, head_ref,
    big_ref, s2_ref, q_ref, deep_ref,
    w1t, w2t,
):
    @pl.when(pl.program_id(0) == 0)
    def _():
        w1t[...] = jnp.transpose(w1_ref[...])
        w2t[...] = jnp.transpose(w2_ref[...])

    din, n1, n2 = dense_ref.shape[1], w1t.shape[0], w2t.shape[0]
    dense_t = jnp.transpose(dense_ref[...])
    big_ref[0:din, :] = dense_t
    pre1 = dot(w1t[...], dense_t) + to_column(b1_ref[...])
    gate1 = jax.nn.sigmoid(pre1)
    h1 = (pre1 * gate1).astype(bf16)
    big_ref[din : din + n1, :] = h1
    slope1 = gate1 * (1.0 + pre1 * (1.0 - gate1))
    pre2 = dot(w2t[...], h1) + to_column(b2_ref[...])
    gate2 = jax.nn.sigmoid(pre2)
    h2 = (pre2 * gate2).astype(bf16)
    big_ref[din + n1 : din + n1 + n2, :] = h2
    head = head_ref[...]
    deep_ref[...] = dot(jnp.broadcast_to(head, (16, head.shape[1])), h2)[0:1]
    s2 = to_column(head.astype(f32)) * (gate2 * (1.0 + pre2 * (1.0 - gate2)))
    s2 = s2.astype(bf16)
    s2_ref[...] = s2
    q_ref[...] = (dot(w2_ref[...], s2) * slope1).astype(bf16)


def tower(dense, w1, b1, w2, b2, head):
    ex, din = dense.shape
    h1, h2 = w2.shape
    steps = 4
    be = ex // steps
    whole = lambda a: pl.BlockSpec(a.shape, lambda i: (0, 0))
    cols = lambda rows: pl.BlockSpec((rows, be), lambda i: (0, i))
    b1, b2, head = b1.reshape(1, h1), b2.reshape(1, h2), head.reshape(1, h2)
    return pl.pallas_call(
        tower_kernel,
        grid=(steps,),
        out_shape=(
            jax.ShapeDtypeStruct((din + h1 + h2, ex), bf16),
            jax.ShapeDtypeStruct((h2, ex), bf16),
            jax.ShapeDtypeStruct((h1, ex), bf16),
            jax.ShapeDtypeStruct((1, ex), f32),
        ),
        in_specs=[
            pl.BlockSpec((be, din), lambda i: (i, 0)),
            whole(w1), whole(b1), whole(w2), whole(b2), whole(head),
        ],
        out_specs=(cols(din + h1 + h2), cols(h2), cols(h1), cols(1)),
        scratch_shapes=[pltpu.VMEM((h1, din), bf16), pltpu.VMEM((h2, h1), bf16)],
        compiler_params=params(62),
        cost_estimate=pl.CostEstimate(
            flops=2 * ex * (din * h1 + 2 * h1 * h2), bytes_accessed=12 << 20, transcendentals=ex * (h1 + h2)
        ),
        name="tower",
    )(dense, w1, b1, w2, b2, head)


def weight_kernel(z_ref, n_ref, out_ref):
    out_ref[...] = jnp.concatenate(split_two(wide_weight(z_ref[...], n_ref[...])), axis=1)


def weights(z, n):
    blocks, width = z.shape
    return pl.pallas_call(
        weight_kernel,
        out_shape=jax.ShapeDtypeStruct((blocks, 2 * width), bf16),
        in_specs=[VM, VM],
        out_specs=VM,
        compiler_params=params(6),
        cost_estimate=pl.CostEstimate(flops=10 * z.size, bytes_accessed=12 * z.size, transcendentals=2 * z.size),
        name="weights",
    )(z, n)


def four_lists(got_ref, at, cap):
    planes = [got_ref[at + k] for k in range(4)]
    values = jnp.concatenate([p[0:cap] for p in planes], axis=0)
    index = [p[cap : cap + 1].astype(f32) * 32.0 + p[cap + 1 : cap + 2].astype(f32) for p in planes]
    left = iota((1, LANES), 1) < cap
    pairs = [jnp.where(left, index[0], index[1]), jnp.where(left, index[2], index[3])]
    return values, jnp.concatenate(pairs, axis=1).astype(jnp.int32)


def logit_kernel(got_ref, wcat_ref, out_ref):
    lists = got_ref.shape[0]
    cap = got_ref.shape[1] - 8
    blocks = wcat_ref.shape[0]
    for at in range(0, lists, 4):
        values, index = four_lists(got_ref, at, cap)
        every = dot(wcat_ref[...], jnp.concatenate([values, values], axis=1), NT)
        picked = jnp.where(iota((blocks, 4 * cap), 0) == index, every, 0.0)
        logit = jnp.sum(picked, axis=0, keepdims=True)
        for k in range(4):
            out_ref[at + k] = logit[:, (k // 2) * LANES : (k // 2 + 1) * LANES]


def slot_logits(got, wcat):
    lists = got.shape[0]
    return pl.pallas_call(
        logit_kernel,
        out_shape=jax.ShapeDtypeStruct((lists, 1, LANES), f32),
        in_specs=[VM, VM],
        out_specs=VM,
        compiler_params=params(16),
        name="slot_logits",
    )(got, wcat)


def doubled(example_ref):
    example = jnp.concatenate([example_ref[...], example_ref[...]], axis=1)
    return example >> 7, example & (LANES - 1)


def mark(low, marks):
    down = iota((LANES, LANES), 0)
    for k in range(low.shape[0]):
        marks[:, k * LANES : (k + 1) * LANES] = jnp.where(low[k : k + 1] == down, 1.0, 0.0).astype(bf16)


def marks_kernel(example_ref, marks_ref):
    mark(doubled(example_ref)[1], marks_ref)


def example_marks(example):
    lists = example.shape[0]
    return pl.pallas_call(
        marks_kernel,
        out_shape=jax.ShapeDtypeStruct((LANES, lists * LANES), bf16),
        in_specs=[VM],
        out_specs=VM,
        compiler_params=params(8),
        cost_estimate=pl.CostEstimate(flops=2 << 20, bytes_accessed=4 << 20, transcendentals=0),
        name="example_marks",
    )(example)


def half_copies(half, big_any, dense_t, h1, sems):
    each, packed = dense_t.shape[0], h1.shape[0] // 2
    copies = [
        pltpu.make_async_copy(big_any.at[pl.ds(pl.multiple_of(half * each, each), each)], dense_t, sems.at[0])
    ]
    for side in range(2):
        start = pl.multiple_of(2 * each + half * packed + side * 2 * packed, packed)
        copies.append(
            pltpu.make_async_copy(
                big_any.at[pl.ds(start, packed)], h1.at[pl.ds(side * packed, packed)], sems.at[1 + side]
            )
        )
    return copies


def half_gradients(residual, copies, s2, q, dense_t, h1, target):
    rows, half = residual.shape[0], dense_t.shape[0]
    packed, width = h1.shape[0] // 2, s2.shape[0]
    dlogit = jnp.concatenate([residual[k : k + 1] for k in range(rows)], axis=1)
    dlogit = dlogit.astype(bf16).astype(f32)
    d_two = (s2[...].astype(f32) * dlogit).astype(bf16)
    copies[1].wait()
    copies[2].wait()
    second = dot(h1[...], d_two, NT).astype(bf16)
    target[half:, 0:width] = second[0:packed]
    target[half:, width:] = second[packed:]
    d_one = (q[...].astype(f32) * dlogit).astype(bf16)
    copies[0].wait()
    target[0:half, :] = dot(dense_t[...], d_one, NT).astype(bf16)


def half_scratch(big, n1):
    half = (big.shape[0] - n1 - n1 // 2) // 2
    return [
        pltpu.VMEM((half, big.shape[1]), bf16),
        pltpu.VMEM((n1 // 2, big.shape[1]), bf16),
        pltpu.SemaphoreType.DMA((4,)),
    ]


def residual_kernel(
    logit_any, example_ref, deep_ref, label_ref, marks, s2, q, big_any,
    prob_ref, residual_ref, send_ref,
    spread, logit_ref, dense_t, h1, sems,
):
    lists, cap = example_ref.shape
    rows = label_ref.shape[0]
    core = lax.axis_index("rep") & 1
    first = pltpu.make_async_copy(logit_any, logit_ref, sems.at[3])
    first.start()
    copies = half_copies(1 - core, big_any, dense_t, h1, sems)
    for copy in copies:
        copy.start()
    high = doubled(example_ref)[0]
    mine = (iota((lists, LANES), 1) >= cap) == (core == 1)
    high = jnp.where(mine, high, -1)
    down = iota((rows, LANES), 0)
    first.wait()
    for k in range(lists):
        part = jnp.where(high[k : k + 1] == down, logit_ref[k], 0.0)
        spread[:, k * LANES : (k + 1) * LANES] = jnp.concatenate(split_two(part), axis=0)
    wide = dot(spread[...], marks[...], NT)
    wide = wide[0:rows] + wide[rows:]
    deep = jnp.concatenate([deep_ref[:, k * LANES : (k + 1) * LANES] for k in range(rows)], axis=0)
    prob = jax.nn.sigmoid(wide + deep)
    prob_ref[...] = prob
    residual = prob - label_ref[...].astype(f32)
    residual_ref[...] = residual
    half_gradients(residual, copies, s2, q, dense_t, h1, send_ref)


def residuals(logits, example, deep, labels, marks, s2, q, big):
    lists = example.shape[0]
    rows = deep.shape[1] // LANES
    n1 = q.shape[0]
    half = (big.shape[0] - n1 - s2.shape[0]) // 2 + n1 // 4
    return pl.pallas_call(
        residual_kernel,
        out_shape=(
            jax.ShapeDtypeStruct((rows, LANES), f32),
            jax.ShapeDtypeStruct((rows, LANES), f32),
            jax.ShapeDtypeStruct((half, n1), bf16),
        ),
        in_specs=[ANY] + [VM] * 6 + [HBM],
        out_specs=[VM, VM, VM],
        scratch_shapes=[pltpu.VMEM((2 * rows, lists * LANES), bf16), pltpu.VMEM(logits.shape, f32)]
        + half_scratch(big, n1),
        compiler_params=params(49),
        name="residuals",
    )(logits, example, deep, labels.reshape(rows, LANES), marks, s2, q, big)


def gradient_kernel(residual_ref, s2, q, big_any, keep_ref, dense_t, h1, sems):
    core = lax.axis_index("rep") & 1
    copies = half_copies(core, big_any, dense_t, h1, sems)
    for copy in copies:
        copy.start()
    half_gradients(residual_ref[...], copies, s2, q, dense_t, h1, keep_ref)


def gradients(residual, s2, q, big):
    n1, ex = q.shape
    half = (big.shape[0] - n1 - s2.shape[0]) // 2 + n1 // 4
    return pl.pallas_call(
        gradient_kernel,
        out_shape=jax.ShapeDtypeStruct((half, n1), bf16),
        in_specs=[VM] * 3 + [HBM],
        out_specs=VM,
        scratch_shapes=half_scratch(big, n1),
        compiler_params=params(49),
        cost_estimate=pl.CostEstimate(flops=2 * half * n1 * ex, bytes_accessed=6 << 20, transcendentals=0),
        name="gradients",
    )(residual, s2, q, big)


def slot_kernel(residual_ref, example_ref, s2_any, q_any, big_any, out_ref, marks, s2, q, h2, sems):
    h2_any = big_any.at[pl.ds(big_any.shape[0] - h2.shape[0], h2.shape[0])]
    copies = [
        pltpu.make_async_copy(src, dst, sems.at[k])
        for k, (src, dst) in enumerate(((q_any, q), (s2_any, s2), (h2_any, h2)))
    ]
    for copy in copies:
        copy.start()
    lists = example_ref.shape[0]
    rows = residual_ref.shape[0]
    high, low = doubled(example_ref)
    mark(low, marks)
    down = iota((rows, LANES), 0)
    residual = residual_ref[...]
    found = dot(jnp.concatenate(split_two(residual), axis=0), marks[...])
    found = found[0:rows] + found[rows:]
    for k in range(lists):
        part = found[:, k * LANES : (k + 1) * LANES]
        out_ref[k, 0:8, :] = jnp.broadcast_to(
            jnp.sum(jnp.where(high[k : k + 1] == down, part, 0.0), axis=0, keepdims=True), (8, LANES)
        )
    dlogit = jnp.concatenate([residual[k : k + 1] for k in range(rows)], axis=1)
    dlogit = dlogit.astype(bf16).astype(f32)

    def fold(a):
        return functools.reduce(
            jnp.add, [a[:, k * LANES : (k + 1) * LANES].astype(f32) for k in range(rows)]
        )

    for copy in copies:
        copy.wait()
    small = jnp.concatenate(
        [
            fold((q[...].astype(f32) * dlogit).astype(bf16)),
            fold((s2[...].astype(f32) * dlogit).astype(bf16)),
            fold(h2[...].astype(f32) * dlogit),
        ],
        axis=0,
    )
    ones = jnp.ones((16, 2 * LANES), bf16)
    sums = dot(ones, jnp.concatenate(split_two(small), axis=1), NT)[0:1]
    count = sums.shape[1] // LANES
    sums = jnp.concatenate([sums[:, k * LANES : (k + 1) * LANES] for k in range(count)], axis=0)
    for k in range(lists):
        out_ref[k, 8 : 8 + count, :] = sums


def slot_residuals(residual, example, s2, q, big):
    lists = example.shape[0]
    count = (q.shape[0] + 2 * s2.shape[0]) // LANES
    return pl.pallas_call(
        slot_kernel,
        out_shape=jax.ShapeDtypeStruct((lists, 8 + count, LANES), f32),
        in_specs=[VM] * 2 + [HBM] * 3,
        out_specs=VM,
        scratch_shapes=[
            pltpu.VMEM((LANES, lists * LANES), bf16),
            pltpu.VMEM(s2.shape, bf16),
            pltpu.VMEM(q.shape, bf16),
            pltpu.VMEM(s2.shape, bf16),
            pltpu.SemaphoreType.DMA((3,)),
        ],
        compiler_params=params(60),
        cost_estimate=pl.CostEstimate(flops=2 * q.size + (lists << 20), bytes_accessed=3 << 20, transcendentals=0),
        name="slot_residuals",
    )(residual, example, s2, q, big)


def state_kernel(got_ref, res_ref, z_ref, n_ref, z_out, n_out, small_ref):
    lists = got_ref.shape[0]
    cap = got_ref.shape[1] - 8
    blocks, width = z_ref.shape
    left = iota((1, LANES), 1) < cap
    grad = jnp.zeros((blocks, 2 * width), f32)
    for at in range(0, lists, 4):
        values, index = four_lists(got_ref, at, cap)
        res = [res_ref[at + k, 0:1, :] for k in range(4)]
        res = jnp.concatenate([jnp.where(left, res[0], res[1]), jnp.where(left, res[2], res[3])], axis=1)
        scaled = jnp.concatenate(split_two(values.astype(f32) * to_column(res)), axis=1)
        hit = jnp.where(iota((blocks, 4 * cap), 0) == index, 1.0, 0.0).astype(bf16)
        grad = grad + dot(hit, scaled)
    grad = grad[:, :width] + grad[:, width:]
    z, n = z_ref[...], n_ref[...]
    n_new = n + grad * grad
    sigma = (jnp.sqrt(n_new) - jnp.sqrt(n)) / alpha_rate
    n_out[...] = n_new
    z_out[...] = z + grad - sigma * wide_weight(z, n)
    small_ref[...] = functools.reduce(jnp.add, [res_ref[k, 8:, :] for k in range(lists)])


def new_states(got, res, z, n):
    count = res.shape[1] - 8
    return pl.pallas_call(
        state_kernel,
        out_shape=(
            jax.ShapeDtypeStruct(z.shape, f32),
            jax.ShapeDtypeStruct(z.shape, f32),
            jax.ShapeDtypeStruct((count, LANES), f32),
        ),
        in_specs=[VM] * 4,
        out_specs=(VM, VM, VM),
        compiler_params=params(16),
        cost_estimate=pl.CostEstimate(
            flops=4 * got.shape[0] * (got.shape[1] - 8) * z.size, bytes_accessed=4 << 20, transcendentals=2 * z.size
        ),
        name="new_states",
    )(got, res, z, n)


def every_to_every(x):
    return lax.all_to_all(x, AXES, split_axis=0, concat_axis=0, tiled=True)


def swap(x, bit, devices):
    return lax.ppermute(x, AXES, [(i, i ^ bit) for i in range(devices)])


def add(*terms):
    return functools.reduce(jnp.add, [t.astype(f32) for t in terms]).astype(bf16)


def halves(x, side):
    rows = x.shape[0] // 2
    return lax.dynamic_slice_in_dim(x, side * rows, rows, 0)


def hold(*values):
    return lax.optimization_barrier(values)


def sum_everywhere(x, me, devices, slots, states):
    bits = [1 << k for k in range(1, devices.bit_length() - 1)]
    quad, inner, last = bits[:2], bits[2:-1], bits[-1]
    at = (me // quad[0]) % 4
    others = [(3, quad[0] + quad[1]), (1, quad[0]), (2, quad[1])]
    rows = x.shape[0] // 4
    quarter = lambda k: lax.dynamic_slice_in_dim(x, (at ^ k) * rows, rows, 0)
    res = slots(x)
    x = add(quarter(0), *[swap(quarter(k), bit, devices) for k, bit in others])
    x, res = hold(x, res)
    res = every_to_every(res)
    for bit in inner:
        side = (me // bit) % 2
        x = add(halves(x, side), swap(halves(x, 1 - side), bit, devices))
    x, res = hold(x, res)
    made = states(res)
    x = add(x, swap(x, last, devices))
    x, *made = hold(x, *made)
    for bit in reversed(inner):
        side = (me // bit) % 2
        other = swap(x, bit, devices)
        x = jnp.concatenate([jnp.where(side == 0, x, other), jnp.where(side == 0, other, x)], axis=0)
    parts = [(0, x)] + [(k, swap(x, bit, devices)) for k, bit in others]
    whole = jnp.zeros((4 * x.shape[0], x.shape[1]), x.dtype)
    for k, part in parts:
        whole = lax.dynamic_update_slice_in_dim(whole, part, (at ^ k) * x.shape[0], 0)
    return whole, made


def per_device(
    devices,
    dense,
    labels,
    tile_values,
    tile_block,
    tile_example,
    tile_count,
    z_state,
    n_state,
    w_one,
    b_one,
    w_two,
    b_two,
    head,
):
    n1, n2 = w_two.shape
    din = dense.shape[1]
    me = lax.axis_index(AXES)
    core = me % 2
    got = every_to_every(pack(tile_values, tile_block, tile_count))
    big, s2, q, deep = tower(dense, w_one, b_one, w_two, b_two, head)
    wcat = weights(z_state, n_state)
    got, deep = lax.optimization_barrier((got, deep))
    logits = slot_logits(got, wcat)
    logits, example = hold(logits, tile_example)
    marks = example_marks(example)
    logits = every_to_every(logits)
    prob, residual, send = residuals(logits, tile_example, deep, labels, marks, s2, q, big)
    keep = gradients(residual, s2, q, big)
    own = add(keep, swap(send, 1, devices))

    def slots(x):
        seen = hold(x, residual)[1]
        return slot_residuals(seen, tile_example, s2, q, big)

    def states(res):
        return new_states(got, res, z_state, n_state)

    own, (z_new, n_new, small) = sum_everywhere(own, me, devices, slots, states)
    other = swap(own, 1, devices)
    first, second = jnp.where(core == 0, own, other), jnp.where(core == 0, other, own)
    big = din // 2
    grad_w_one = jnp.concatenate([first[:big], second[:big]], axis=0).astype(f32)
    packed = jnp.concatenate([first[big:], second[big:]], axis=0).astype(f32)
    grad_w_two = jnp.concatenate([packed[:, :n2], packed[:, n2:]], axis=0)
    small = small.reshape(-1)
    return (
        prob.reshape(-1),
        z_new,
        n_new,
        grad_w_one,
        small[:n1],
        grad_w_two,
        small[n1 : n1 + n2],
        small[n1 + n2 :],
    )


def solution(mesh):
    placed = (
        P(AXES, None),
        P(AXES),
        P(AXES, None, None),
        P(AXES, None),
        P(AXES, None),
        P(AXES),
        P(AXES, None),
        P(AXES, None),
        P(),
        P(),
        P(),
        P(),
        P(),
    )
    devices = mesh.shape["blk"] * mesh.shape["rep"]
    return jax.shard_map(
        functools.partial(per_device, devices),
        mesh=mesh,
        in_specs=placed,
        out_specs=(P(AXES), P(AXES, None), P(AXES, None), P(), P(), P(), P(), P()),
        check_vma=False,
    )
```

time: 105 us -> 96.4 us (0.918)
  waiting for transfers between devices: 20 us -> 40.6 us
  local copies, waits for them, and re-layouts: 17.6 us -> 2.05 us
  blocking collectives: 12.8 us -> 0 us
  Pallas kernels: 18.4 us -> 26.1 us
  starting transfers between devices: 30.1 us -> 23.2 us
  other arithmetic: 4.46 us -> 2.93 us
    all_to_all x2 -> x3, waiting for transfers between devices: 0.01 us -> 16.8 us  [every_to_every(): return lax.all_to_all(x, AXES, split_axis=0, concat_axis=0, tiled=True)]
    unnamed x46 -> x22, local copies, waits for them, and re-layouts: 16.2 us -> 0.06 us
    all_to_all x1 -> x0, blocking collectives: 12.8 us -> none  [every_to_every(): return lax.all_to_all(x, AXES, split_axis=0, concat_axis=0, tiled=True)]
    ppermute x16 -> x11, starting transfers between devices: 20.1 us -> 9.78 us  [swap(): return lax.ppermute(x, AXES, [(i, i ^ bit) for i in range(devices)])]
    pallas_call x2 -> x6, Pallas kernels: 5.93 us -> 13.3 us  [the longest x1 3.81 us: residuals(): pl.pallas_call(residual_kernel, out_shape=(jax.ShapeDtypeStruct((rows, LA...]
    ppermute x16 -> x11, waiting for transfers between devices: 20 us -> 23.9 us  [swap(): return lax.ppermute(x, AXES, [(i, i ^ bit) for i in range(devices)])]
    all_to_all x2 -> x3, starting transfers between devices: 10.1 us -> 13.4 us  [every_to_every(): return lax.all_to_all(x, AXES, split_axis=0, concat_axis=0, tiled=True)]
    pallas_call x1, Pallas kernels: 4.32 us -> 2.92 us  [new_states(): pl.pallas_call(state_kernel, out_shape=(jax.ShapeDtypeStruct(z.shape, f32...]
  transfers between devices with their start and end apart: 18 -> 14, of which waited for: 12 -> 12; matrix products, arithmetic and copies ran while one was open for 2% -> 2% of each run, Pallas kernels for 11% -> 19%
where the time goes in v2:
time: 96.4 us; the launch traced here: 95.9 us
  waiting for transfers between devices  40.6 us (42%)
  Pallas kernels  26.1 us (27%)
  starting transfers between devices  23.2 us (24%)
  other arithmetic  2.93 us (3%)
  local copies, waits for them, and re-layouts  2.05 us (2%)
  between operations  1.08 us (1%)
    ppermute x11, waiting for transfers between devices, swap(): return lax.ppermute(x, AXES, [(i, i ^ bit) for i in range(devices)])  23.9 us
    all_to_all x3, waiting for transfers between devices, every_to_every(): return lax.all_to_all(x, AXES, split_axis=0, concat_axis=0, tiled=True)  16.8 us
    all_to_all x3, starting transfers between devices, every_to_every(): return lax.all_to_all(x, AXES, split_axis=0, concat_axis=0, tiled=True)  13.4 us
    ppermute x11, starting transfers between devices, swap(): return lax.ppermute(x, AXES, [(i, i ^ bit) for i in range(devices)])  9.78 us
    pallas_call x1, Pallas kernels, tower(): pl.pallas_call(tower_kernel, grid=(steps,), out_shape=(jax.ShapeDtypeStru...  7.89 us
    pallas_call x1, Pallas kernels, residuals(): pl.pallas_call(residual_kernel, out_shape=(jax.ShapeDtypeStruct((rows, LA...  3.81 us
    pallas_call x1, Pallas kernels, slot_residuals(): pl.pallas_call(slot_kernel, out_shape=jax.ShapeDtypeStruct((lists, 8 + co...  3.79 us
    pallas_call x1, Pallas kernels, gradients(): pl.pallas_call(gradient_kernel, out_shape=jax.ShapeDtypeStruct((half, n1)...  2.96 us
  transfers between devices with their start and end apart: 14, of which 12 were waited for; matrix products, arithmetic and copies ran while one was open for 2% of the time, Pallas kernels for 19%

profile of v2, /device:TPU:0, one launch (start us, length us, event | category | flops | bytes accessed | tf_op | source)
XLA Modules:
  0.0 95.9 jit_solution(11215075797526390239)
XLA Ops:
  0.7 2.0 %pack.1 = bf16[32,72,128]{2,1,0:T(8,128)(2,1)} custom-call(bf16[32,64,128]{2,1,0:T(8,128)(2,1)} %values_any.1, s32[32,64]{1,0:T(8,128)} %block_any.1, s32[1,32]{1,0:T(1,128)} %bitcast.12), custom_call_target="tpu_custom_call" | custom-call | tf_op jit(solution)/shard_map/pack/pallas_call | solution.py:96
  2.6 7.3 %all-to-all-start = ((bf16[32,72,128]{2,1,0:T(8,128)(2,1)}), bf16[32,72,128]{2,1,0:T(8,128)(2,1)S(1)}, u32[]{:S(2)}, u32[]{:S(2)}) async-start(bf16[32,72,128]{2,1,0:T(8,128)(2,1)} %pack.1), calls=%async_computation | async-start | bytes 1179648 | tf_op jit(solution)/shard_map/all_to_all | solution.py:481
  11.0 7.9 %tower.1 = (bf16[1792,1024]{1,0:T(8,128)(2,1)}, bf16[256,1024]{1,0:T(8,128)(2,1)}, bf16[512,1024]{1,0:T(8,128)(2,1)}, f32[1,1024]{1,0:T(1,128)}) custom-call(bf16[1024,1024]{1,0:T(8,128)(2,1)} %dense_ref.1, bf16[1024,512]{1,0:T(8,128)(2,1)} %w1_ref.1, f32[1,512]{1,0:T(1,128)} %bitcast.14, bf16[512,256]{1,0:T(8,128)(2,1)} %w2_ref.1, f32[1,256]{1,0:T(1,128)} %bitcast.15, ...), custom_call_target="tpu_custom_call" | custom-call | flops 1610612736 | bytes 12582912 | tf_op jit(solution)/shard_map/tower/pallas_call | solution.py:154
  18.9 7.8 %all-to-all-done.got_ref = bf16[32,72,128]{2,1,0:T(8,128)(2,1)S(1)} async-done(((bf16[32,72,128]{2,1,0:T(8,128)(2,1)}), bf16[32,72,128]{2,1,0:T(8,128)(2,1)S(1)}, u32[]{:S(2)}, u32[]{:S(2)}) %all-to-all-start) | async-done | bytes 589856 | tf_op jit(solution)/shard_map/all_to_all | solution.py:481
  26.7 2.0 %slot_logits.1 = f32[32,1,128]{2,1,0:T(1,128)} custom-call(bf16[32,72,128]{2,1,0:T(8,128)(2,1)S(1)} %all-to-all-done.got_ref, bf16[1024,256]{1,0:T(8,128)(2,1)S(1)} %weights.1.wcat_ref), custom_call_target="tpu_custom_call" | custom-call | tf_op jit(solution)/shard_map/slot_logits/pallas_call | solution.py:218
  28.6 3.3 %all-to-all-start.1 = ((f32[32,1,128]{2,1,0:T(1,128)}), f32[32,1,128]{2,1,0:T(1,128)S(1)}, u32[]{:S(2)}, u32[]{:S(2)}) async-start(f32[32,1,128]{2,1,0:T(1,128)} %slot_logits.1), calls=%async_computation.1 | async-start | bytes 32768 | tf_op jit(solution)/shard_map/all_to_all | solution.py:481
  32.3 6.7 %all-to-all-done.1.logit_any = f32[32,1,128]{2,1,0:T(1,128)S(1)} async-done(((f32[32,1,128]{2,1,0:T(1,128)}), f32[32,1,128]{2,1,0:T(1,128)S(1)}, u32[]{:S(2)}, u32[]{:S(2)}) %all-to-all-start.1) | async-done | bytes 16416 | tf_op jit(solution)/shard_map/all_to_all | solution.py:481
  39.0 3.8 %residuals.1 = (f32[8,128]{1,0:T(8,128)}, f32[8,128]{1,0:T(8,128)S(1)}, bf16[640,512]{1,0:T(8,128)(2,1)}) custom-call(f32[32,1,128]{2,1,0:T(1,128)S(1)} %all-to-all-done.1.logit_any, s32[32,64]{1,0:T(8,128)S(1)} %copy-done.6, f32[1,1024]{1,0:T(1,128)S(1)} %copy-done.9, s32[8,128]{1,0:T(8,128)S(1)} %bitcast.11, bf16[128,4096]{1,0:T(8,128)(2,1)S(1)} %example_marks.1.marks, ...), custom_call_target="tpu_custom_call" | custom-call | tf_op jit(solution)/shard_map/residuals/pallas_call | solution.py:332
  43.0 3.0 %gradients.1 = bf16[640,512]{1,0:T(8,128)(2,1)S(1)} custom-call(f32[8,128]{1,0:T(8,128)S(1)} %get-tuple-element.42.residual_ref, bf16[256,1024]{1,0:T(8,128)(2,1)S(1)} %copy-done.1, bf16[512,1024]{1,0:T(8,128)(2,1)S(1)} %copy-done, bf16[1792,1024]{1,0:T(8,128)(2,1)} %get-tuple-element.38.big_any), custom_call_target="tpu_custom_call" | custom-call | flops 671088640 | bytes 6291456 | tf_op jit(solution)/shard_map/gradients/pallas_call | solution.py:359
  46.2 0.6 collective-permute-start.3
  46.8 0.6 collective-permute-start.2
  47.5 2.3 %collective-permute-start.1 = (bf16[160,512]{1,0:T(8,128)(2,1)S(1)}, bf16[160,512]{1,0:T(8,128)(2,1)S(1)}, u32[]{:S(2)}, u32[]{:S(2)}) collective-permute-start(bf16[160,512]{1,0:T(8,128)(2,1)S(1)} %get-tuple-element.56), channel_id=1, source_target_pairs={{0,6},{1,7},{2,4},{3,5},{4,2},{5,3},{6,0},{7,1},{8,14},{9,15},{10,... | collective-permute-start | bytes 491528 | tf_op jit(solution)/shard_map/ppermute | solution.py:485
  49.8 3.8 %slot_residuals.1 = f32[32,16,128]{2,1,0:T(8,128)} custom-call(f32[8,128]{1,0:T(8,128)} %copy-done.7, s32[32,64]{1,0:T(8,128)} %example_ref.4, bf16[256,1024]{1,0:T(8,128)(2,1)} %get-tuple-element.36.s2.s2_any, bf16[512,1024]{1,0:T(8,128)(2,1)} %get-tuple-element.37.q.q_any, bf16[1792,1024]{1,0:T(8,128)(2,1)} %get-tuple-element.38.big_any), custom_call_target="tpu_custom_call" | custom-call | flops 34603008 | bytes 3145728 | tf_op jit(solution)/shard_map/slot_residuals/pallas_call | solution.py:421
  53.9 3.6 %collective-permute-done.1 = bf16[160,512]{1,0:T(8,128)(2,1)S(1)} collective-permute-done((bf16[160,512]{1,0:T(8,128)(2,1)S(1)}, bf16[160,512]{1,0:T(8,128)(2,1)S(1)}, u32[]{:S(2)}, u32[]{:S(2)}) %collective-permute-start.1) | collective-permute-done | bytes 163872 | tf_op jit(solution)/shard_map/ppermute | solution.py:485
  57.6 2.8 %all-to-all-start.2 = ((f32[32,16,128]{2,1,0:T(8,128)}), f32[32,16,128]{2,1,0:T(8,128)S(1)}, u32[]{:S(2)}, u32[]{:S(2)}) async-start(f32[32,16,128]{2,1,0:T(8,128)} %slot_residuals.1), calls=%async_computation.2 | async-start | bytes 524288 | tf_op jit(solution)/shard_map/all_to_all | solution.py:481
  60.5 1.6 %collective-permute-start.4 = (bf16[80,512]{1,0:T(8,128)(2,1)S(1)}, bf16[80,512]{1,0:T(8,128)(2,1)S(1)}, u32[]{:S(2)}, u32[]{:S(2)}) collective-permute-start(bf16[80,512]{1,0:T(8,128)(2,1)S(1)} %constant_dynamic-slice_fusion), channel_id=1, source_target_pairs={{0,8},{1,9},{2,10},{3,11},{4,12},{5,13},{6,14},{7,15},{8,0},{9,1},... | collective-permute-start | bytes 245768 | tf_op jit(solution)/shard_map/ppermute | solution.py:485
  62.1 6.3 %collective-permute-done.4 = bf16[80,512]{1,0:T(8,128)(2,1)S(1)} collective-permute-done((bf16[80,512]{1,0:T(8,128)(2,1)S(1)}, bf16[80,512]{1,0:T(8,128)(2,1)S(1)}, u32[]{:S(2)}, u32[]{:S(2)}) %collective-permute-start.4) | collective-permute-done | bytes 81952 | tf_op jit(solution)/shard_map/ppermute | solution.py:485
  68.4 2.3 %all-to-all-done.2.res_ref = f32[32,16,128]{2,1,0:T(8,128)S(1)} async-done(((f32[32,16,128]{2,1,0:T(8,128)}), f32[32,16,128]{2,1,0:T(8,128)S(1)}, u32[]{:S(2)}, u32[]{:S(2)}) %all-to-all-start.2) | async-done | bytes 262176 | tf_op jit(solution)/shard_map/all_to_all | solution.py:481
  70.7 0.9 collective-permute-start.5
  71.6 2.9 %new_states.1 = (f32[1024,128]{1,0:T(8,128)}, f32[1024,128]{1,0:T(8,128)}, f32[8,128]{1,0:T(8,128)S(1)}) custom-call(bf16[32,72,128]{2,1,0:T(8,128)(2,1)S(1)} %all-to-all-done.got_ref, f32[32,16,128]{2,1,0:T(8,128)S(1)} %all-to-all-done.2.res_ref, f32[1024,128]{1,0:T(8,128)S(1)} %copy-done.3, f32[1024,128]{1,0:T(8,128)S(1)} %copy-done.5), custom_call_target="tpu_custom_call" | custom-call | flops 1073741824 | bytes 4194304 | tf_op jit(solution)/shard_map/new_states/pallas_call | solution.py:463
  74.5 2.8 %collective-permute-done.5 = bf16[80,512]{1,0:T(8,128)(2,1)S(1)} collective-permute-done((bf16[80,512]{1,0:T(8,128)(2,1)S(1)}, bf16[80,512]{1,0:T(8,128)(2,1)S(1)}, u32[]{:S(2)}, u32[]{:S(2)}) %collective-permute-start.5) | collective-permute-done | bytes 81952 | tf_op jit(solution)/shard_map/ppermute | solution.py:485
  77.4 4.4 %collective-permute-done.6 = bf16[80,512]{1,0:T(8,128)(2,1)S(1)} collective-permute-done((bf16[80,512]{1,0:T(8,128)(2,1)S(1)}, bf16[80,512]{1,0:T(8,128)(2,1)S(1)}, u32[]{:S(2)}, u32[]{:S(2)}) %collective-permute-start.6) | collective-permute-done | bytes 81952 | tf_op jit(solution)/shard_map/ppermute | solution.py:485
  81.9 1.4 %collective-permute-start.7 = (bf16[160,512]{1,0:T(8,128)(2,1)S(1)}, bf16[160,512]{1,0:T(8,128)(2,1)S(1)}, u32[]{:S(2)}, u32[]{:S(2)}) collective-permute-start(bf16[160,512]{1,0:T(8,128)(2,1)S(1)} %get-tuple-element.61), channel_id=1, source_target_pairs={{0,6},{1,7},{2,4},{3,5},{4,2},{5,3},{6,0},{7,1},{8,14},{9,15},{10,... | collective-permute-start | bytes 491528 | tf_op jit(solution)/shard_map/ppermute | solution.py:485
  83.3 1.0 %collective-permute-start.8 = (bf16[160,512]{1,0:T(8,128)(2,1)S(1)}, bf16[160,512]{1,0:T(8,128)(2,1)S(1)}, u32[]{:S(2)}, u32[]{:S(2)}) collective-permute-start(bf16[160,512]{1,0:T(8,128)(2,1)S(1)} %get-tuple-element.61), channel_id=1, source_target_pairs={{0,2},{1,3},{2,0},{3,1},{4,6},{5,7},{6,4},{7,5},{8,10},{9,11},{10,... | collective-permute-start | bytes 491528 | tf_op jit(solution)/shard_map/ppermute | solution.py:485
  84.3 1.1 %collective-permute-start.9 = (bf16[160,512]{1,0:T(8,128)(2,1)S(1)}, bf16[160,512]{1,0:T(8,128)(2,1)S(1)}, u32[]{:S(2)}, u32[]{:S(2)}) collective-permute-start(bf16[160,512]{1,0:T(8,128)(2,1)S(1)} %get-tuple-element.61), channel_id=1, source_target_pairs={{0,4},{1,5},{2,6},{3,7},{4,0},{5,1},{6,2},{7,3},{8,12},{9,13},{10,... | collective-permute-start | bytes 491528 | tf_op jit(solution)/shard_map/ppermute | solution.py:485
  85.5 3.9 %collective-permute-done.7 = bf16[160,512]{1,0:T(8,128)(2,1)S(1)} collective-permute-done((bf16[160,512]{1,0:T(8,128)(2,1)S(1)}, bf16[160,512]{1,0:T(8,128)(2,1)S(1)}, u32[]{:S(2)}, u32[]{:S(2)}) %collective-permute-start.7) | collective-permute-done | bytes 163872 | tf_op jit(solution)/shard_map/ppermute | solution.py:485
  89.4 1.0 %collective-permute-done.8 = bf16[160,512]{1,0:T(8,128)(2,1)S(1)} collective-permute-done((bf16[160,512]{1,0:T(8,128)(2,1)S(1)}, bf16[160,512]{1,0:T(8,128)(2,1)S(1)}, u32[]{:S(2)}, u32[]{:S(2)}) %collective-permute-start.8) | collective-permute-done | bytes 163872 | tf_op jit(solution)/shard_map/ppermute | solution.py:485
  90.4 0.6 collective-permute-done.9
  91.1 0.6 slice_bitcast_fusion
  92.3 0.9 collective-permute-done.10
  93.5 1.6 %maximum_convert_fusion = f32[1024,512]{1,0:T(8,128)} fusion(bf16[512,512]{1,0:T(8,128)(2,1)S(1)} %slice.49, bf16[512,512]{1,0:T(8,128)(2,1)S(1)} %slice.48), kind=kLoop, calls=%fused_computation.1 | loop fusion | flops 2097152 | bytes 3145728 | tf_op jit(solution)/shard_map/convert_element_type | solution.py:573
  95.1 0.8 pad_maximum_fusion
  (51 shorter events, 3.3 us)
Async XLA Ops:
  0.6 9.3 %copy-start.10 = (bf16[256]{0:T(256)(128)(2,1)S(1)}, bf16[256]{0:T(256)(128)(2,1)}, u32[]{:S(2)}) copy-start(bf16[256]{0:T(256)(128)(2,1)} %param.25) | copy-start | bytes 1540
  0.6 9.9 %copy-start.2 = (f32[1024,128]{1,0:T(8,128)S(1)}, f32[1024,128]{1,0:T(8,128)}, u32[]{:S(2)}) copy-start(f32[1024,128]{1,0:T(8,128)} %z_ref.3) | copy-start | bytes 1572868
  0.7 9.9 %copy-start.4 = (f32[1024,128]{1,0:T(8,128)S(1)}, f32[1024,128]{1,0:T(8,128)}, u32[]{:S(2)}) copy-start(f32[1024,128]{1,0:T(8,128)} %n_ref.3) | copy-start | bytes 1572868
  2.6 24.0 %all-to-all-start = ((bf16[32,72,128]{2,1,0:T(8,128)(2,1)}), bf16[32,72,128]{2,1,0:T(8,128)(2,1)S(1)}, u32[]{:S(2)}, u32[]{:S(2)}) async-start(bf16[32,72,128]{2,1,0:T(8,128)(2,1)} %pack.1), calls=%async_computation | async-start | bytes 1179648 | tf_op jit(solution)/shard_map/all_to_all | solution.py:481
  11.0 21.0 %copy-start.6 = (s32[32,64]{1,0:T(8,128)S(1)}, s32[32,64]{1,0:T(8,128)}, u32[]{:S(2)}) copy-start(s32[32,64]{1,0:T(8,128)} %example_ref.4) | copy-start | bytes 24580
  18.9 20.1 %copy-start = (bf16[512,1024]{1,0:T(8,128)(2,1)S(1)}, bf16[512,1024]{1,0:T(8,128)(2,1)}, u32[]{:S(2)}) copy-start(bf16[512,1024]{1,0:T(8,128)(2,1)} %get-tuple-element.37.q.q_any) | copy-start | bytes 3145732
  18.9 20.1 %copy-start.1 = (bf16[256,1024]{1,0:T(8,128)(2,1)S(1)}, bf16[256,1024]{1,0:T(8,128)(2,1)}, u32[]{:S(2)}) copy-start(bf16[256,1024]{1,0:T(8,128)(2,1)} %get-tuple-element.36.s2.s2_any) | copy-start | bytes 1572868
  18.9 20.1 %copy-start.8 = (s32[1024]{0:T(1024)S(1)}, s32[1024]{0:T(1024)}, u32[]{:S(2)}) copy-start(s32[1024]{0:T(1024)} %param.14) | copy-start | bytes 12292
  18.9 20.1 %copy-start.9 = (f32[1,1024]{1,0:T(1,128)S(1)}, f32[1,1024]{1,0:T(1,128)}, u32[]{:S(2)}) copy-start(f32[1,1024]{1,0:T(1,128)} %get-tuple-element.34.deep_ref) | copy-start | bytes 12292
  28.6 10.4 %all-to-all-start.1 = ((f32[32,1,128]{2,1,0:T(1,128)}), f32[32,1,128]{2,1,0:T(1,128)S(1)}, u32[]{:S(2)}, u32[]{:S(2)}) async-start(f32[32,1,128]{2,1,0:T(1,128)} %slot_logits.1), calls=%async_computation.1 | async-start | bytes 32768 | tf_op jit(solution)/shard_map/all_to_all | solution.py:481
  42.9 3.1 %copy-start.7 = (f32[8,128]{1,0:T(8,128)}, f32[8,128]{1,0:T(8,128)S(1)}, u32[]{:S(2)}) copy-start(f32[8,128]{1,0:T(8,128)S(1)} %get-tuple-element.42.residual_ref) | copy-start | bytes 12292
  42.9 3.1 %collective-permute-start = (bf16[640,512]{1,0:T(8,128)(2,1)}, bf16[640,512]{1,0:T(8,128)(2,1)S(1)}, u32[]{:S(2)}, u32[]{:S(2)}) collective-permute-start(bf16[640,512]{1,0:T(8,128)(2,1)} %get-tuple-element.41), channel_id=1, source_target_pairs={{0,1},{1,0},{2,3},{3,2},{4,5},{5,4},{6,7},{7,6},{8,9},{9,8},{10,11... | collective-permute-start | bytes 1966088 | tf_op jit(solution)/shard_map/ppermute | solution.py:485
  46.2 7.4 %collective-permute-start.3 = (bf16[160,512]{1,0:T(8,128)(2,1)S(1)}, bf16[160,512]{1,0:T(8,128)(2,1)S(1)}, u32[]{:S(2)}, u32[]{:S(2)}) collective-permute-start(bf16[160,512]{1,0:T(8,128)(2,1)S(1)} %get-tuple-element.57), channel_id=1, source_target_pairs={{0,4},{1,5},{2,6},{3,7},{4,0},{5,1},{6,2},{7,3},{8,12},{9,13},{10,... | collective-permute-start | bytes 491528 | tf_op jit(solution)/shard_map/ppermute | solution.py:485
  46.8 7.0 %collective-permute-start.2 = (bf16[160,512]{1,0:T(8,128)(2,1)S(1)}, bf16[160,512]{1,0:T(8,128)(2,1)S(1)}, u32[]{:S(2)}, u32[]{:S(2)}) collective-permute-start(bf16[160,512]{1,0:T(8,128)(2,1)S(1)} %get-tuple-element.58), channel_id=1, source_target_pairs={{0,2},{1,3},{2,0},{3,1},{4,6},{5,7},{6,4},{7,5},{8,10},{9,11},{10,... | collective-permute-start | bytes 491528 | tf_op jit(solution)/shard_map/ppermute | solution.py:485
  47.5 10.1 %collective-permute-start.1 = (bf16[160,512]{1,0:T(8,128)(2,1)S(1)}, bf16[160,512]{1,0:T(8,128)(2,1)S(1)}, u32[]{:S(2)}, u32[]{:S(2)}) collective-permute-start(bf16[160,512]{1,0:T(8,128)(2,1)S(1)} %get-tuple-element.56), channel_id=1, source_target_pairs={{0,6},{1,7},{2,4},{3,5},{4,2},{5,3},{6,0},{7,1},{8,14},{9,15},{10,... | collective-permute-start | bytes 491528 | tf_op jit(solution)/shard_map/ppermute | solution.py:485
  49.8 21.8 %copy-start.3 = (f32[1024,128]{1,0:T(8,128)S(1)}, f32[1024,128]{1,0:T(8,128)}, u32[]{:S(2)}) copy-start(f32[1024,128]{1,0:T(8,128)} %z_ref.3) | copy-start | bytes 1572868
  49.8 21.8 %copy-start.5 = (f32[1024,128]{1,0:T(8,128)S(1)}, f32[1024,128]{1,0:T(8,128)}, u32[]{:S(2)}) copy-start(f32[1024,128]{1,0:T(8,128)} %n_ref.3) | copy-start | bytes 1572868
  57.6 13.1 %all-to-all-start.2 = ((f32[32,16,128]{2,1,0:T(8,128)}), f32[32,16,128]{2,1,0:T(8,128)S(1)}, u32[]{:S(2)}, u32[]{:S(2)}) async-start(f32[32,16,128]{2,1,0:T(8,128)} %slot_residuals.1), calls=%async_computation.2 | async-start | bytes 524288 | tf_op jit(solution)/shard_map/all_to_all | solution.py:481
  60.5 7.9 %collective-permute-start.4 = (bf16[80,512]{1,0:T(8,128)(2,1)S(1)}, bf16[80,512]{1,0:T(8,128)(2,1)S(1)}, u32[]{:S(2)}, u32[]{:S(2)}) collective-permute-start(bf16[80,512]{1,0:T(8,128)(2,1)S(1)} %constant_dynamic-slice_fusion), channel_id=1, source_target_pairs={{0,8},{1,9},{2,10},{3,11},{4,12},{5,13},{6,14},{7,15},{8,0},{9,1},... | collective-permute-start | bytes 245768 | tf_op jit(solution)/shard_map/ppermute | solution.py:485
  70.7 6.6 %collective-permute-start.5 = (bf16[80,512]{1,0:T(8,128)(2,1)S(1)}, bf16[80,512]{1,0:T(8,128)(2,1)S(1)}, u32[]{:S(2)}, u32[]{:S(2)}) collective-permute-start(bf16[80,512]{1,0:T(8,128)(2,1)S(1)} %add_convert_fusion.3), channel_id=1, source_target_pairs={{0,16},{1,17},{2,18},{3,19},{4,20},{5,21},{6,22},{7,23},{8,24},{9,... | collective-permute-start | bytes 245768 | tf_op jit(solution)/shard_map/ppermute | solution.py:485
  77.3 4.5 %collective-permute-start.6 = (bf16[80,512]{1,0:T(8,128)(2,1)S(1)}, bf16[80,512]{1,0:T(8,128)(2,1)S(1)}, u32[]{:S(2)}, u32[]{:S(2)}) collective-permute-start(bf16[80,512]{1,0:T(8,128)(2,1)S(1)} %add_convert_fusion.2), channel_id=1, source_target_pairs={{0,8},{1,9},{2,10},{3,11},{4,12},{5,13},{6,14},{7,15},{8,0},{9,1},... | collective-permute-start | bytes 245768 | tf_op jit(solution)/shard_map/ppermute | solution.py:485
  81.9 7.4 %collective-permute-start.7 = (bf16[160,512]{1,0:T(8,128)(2,1)S(1)}, bf16[160,512]{1,0:T(8,128)(2,1)S(1)}, u32[]{:S(2)}, u32[]{:S(2)}) collective-permute-start(bf16[160,512]{1,0:T(8,128)(2,1)S(1)} %get-tuple-element.61), channel_id=1, source_target_pairs={{0,6},{1,7},{2,4},{3,5},{4,2},{5,3},{6,0},{7,1},{8,14},{9,15},{10,... | collective-permute-start | bytes 491528 | tf_op jit(solution)/shard_map/ppermute | solution.py:485
  83.3 7.0 %collective-permute-start.8 = (bf16[160,512]{1,0:T(8,128)(2,1)S(1)}, bf16[160,512]{1,0:T(8,128)(2,1)S(1)}, u32[]{:S(2)}, u32[]{:S(2)}) collective-permute-start(bf16[160,512]{1,0:T(8,128)(2,1)S(1)} %get-tuple-element.61), channel_id=1, source_target_pairs={{0,2},{1,3},{2,0},{3,1},{4,6},{5,7},{6,4},{7,5},{8,10},{9,11},{10,... | collective-permute-start | bytes 491528 | tf_op jit(solution)/shard_map/ppermute | solution.py:485
  84.3 6.7 %collective-permute-start.9 = (bf16[160,512]{1,0:T(8,128)(2,1)S(1)}, bf16[160,512]{1,0:T(8,128)(2,1)S(1)}, u32[]{:S(2)}, u32[]{:S(2)}) collective-permute-start(bf16[160,512]{1,0:T(8,128)(2,1)S(1)} %get-tuple-element.61), channel_id=1, source_target_pairs={{0,4},{1,5},{2,6},{3,7},{4,0},{5,1},{6,2},{7,3},{8,12},{9,13},{10,... | collective-permute-start | bytes 491528 | tf_op jit(solution)/shard_map/ppermute | solution.py:485
  91.0 2.2 %collective-permute-start.10 = (bf16[640,512]{1,0:T(8,128)(2,1)S(1)}, bf16[640,512]{1,0:T(8,128)(2,1)S(1)}, u32[]{:S(2)}, u32[]{:S(2)}) collective-permute-start(bf16[640,512]{1,0:T(8,128)(2,1)S(1)} %constant_dynamic-update-slice_fusion), channel_id=1, source_target_pairs={{0,1},{1,0},{2,3},{3,2},{4,5},{5,4},{6,7},{7,6},{8,9},{9,8},{10,11... | collective-permute-start | bytes 1966088 | tf_op jit(solution)/shard_map/ppermute | solution.py:485

commit v3 on v2

--- a/solution.py
+++ b/solution.py
@@ -269,19 +269,24 @@
 
 
 def half_gradients(residual, copies, s2, q, dense_t, h1, target):
-    rows, half = residual.shape[0], dense_t.shape[0]
-    packed, width = h1.shape[0] // 2, s2.shape[0]
+    rows, first = residual.shape[0], dense_t.shape[0] // 4
+    packed, width = h1.shape[0] // 8, s2.shape[0]
+    each = first + packed
     dlogit = jnp.concatenate([residual[k : k + 1] for k in range(rows)], axis=1)
     dlogit = dlogit.astype(bf16).astype(f32)
     d_two = (s2[...].astype(f32) * dlogit).astype(bf16)
     copies[1].wait()
     copies[2].wait()
     second = dot(h1[...], d_two, NT).astype(bf16)
-    target[half:, 0:width] = second[0:packed]
-    target[half:, width:] = second[packed:]
+    for k in range(4):
+        at = k * packed
+        target[k * each + first : (k + 1) * each, 0:width] = second[at : at + packed]
+        target[k * each + first : (k + 1) * each, width:] = second[4 * packed + at : 5 * packed + at]
     d_one = (q[...].astype(f32) * dlogit).astype(bf16)
     copies[0].wait()
-    target[0:half, :] = dot(dense_t[...], d_one, NT).astype(bf16)
+    made = dot(dense_t[...], d_one, NT).astype(bf16)
+    for k in range(4):
+        target[k * each : k * each + first, :] = made[k * first : (k + 1) * first]
 
 
 def half_scratch(big, n1):
@@ -293,14 +298,19 @@
     ]
 
 
+def position():
+    return lax.axis_index("blk") * lax.axis_size("rep") + lax.axis_index("rep")
+
+
 def residual_kernel(
     logit_any, example_ref, deep_ref, label_ref, marks, s2, q, big_any,
-    prob_ref, residual_ref, send_ref,
-    spread, logit_ref, dense_t, h1, sems,
+    prob_ref, residual_ref, send_ref, slot_ref,
+    spread, logit_ref, apart, dense_t, h1, sems,
 ):
     lists, cap = example_ref.shape
     rows = label_ref.shape[0]
-    core = lax.axis_index("rep") & 1
+    me = position()
+    core = me & 1
     first = pltpu.make_async_copy(logit_any, logit_ref, sems.at[3])
     first.start()
     copies = half_copies(1 - core, big_any, dense_t, h1, sems)
@@ -308,11 +318,11 @@
         copy.start()
     high = doubled(example_ref)[0]
     mine = (iota((lists, LANES), 1) >= cap) == (core == 1)
-    high = jnp.where(mine, high, -1)
+    high_mine = jnp.where(mine, high, -1)
     down = iota((rows, LANES), 0)
     first.wait()
     for k in range(lists):
-        part = jnp.where(high[k : k + 1] == down, logit_ref[k], 0.0)
+        part = jnp.where(high_mine[k : k + 1] == down, logit_ref[k], 0.0)
         spread[:, k * LANES : (k + 1) * LANES] = jnp.concatenate(split_two(part), axis=0)
     wide = dot(spread[...], marks[...], NT)
     wide = wide[0:rows] + wide[rows:]
@@ -322,6 +332,16 @@
     residual = prob - label_ref[...].astype(f32)
     residual_ref[...] = residual
     half_gradients(residual, copies, s2, q, dense_t, h1, send_ref)
+    found = dot(jnp.concatenate(split_two(residual), axis=0), marks[...])
+    found = found[0:rows] + found[rows:]
+    for k in range(lists):
+        part = jnp.where(high[k : k + 1] == down, found[:, k * LANES : (k + 1) * LANES], 0.0)
+        top, rest = split_two(jnp.sum(part, axis=0, keepdims=True))
+        apart[me ^ k] = jnp.concatenate([top.astype(f32), rest.astype(f32)], axis=0)
+    for k in range(lists):
+        for side in range(2):
+            at = (k % 2) * 2 * LANES + side * LANES
+            slot_ref[k // 2 : k // 2 + 1, at : at + LANES] = apart[k, side : side + 1, :]
 
 
 def residuals(logits, example, deep, labels, marks, s2, q, big):
@@ -335,10 +355,11 @@
             jax.ShapeDtypeStruct((rows, LANES), f32),
             jax.ShapeDtypeStruct((rows, LANES), f32),
             jax.ShapeDtypeStruct((half, n1), bf16),
+            jax.ShapeDtypeStruct((lists // 2, 4 * LANES), f32),
         ),
         in_specs=[ANY] + [VM] * 6 + [HBM],
-        out_specs=[VM, VM, VM],
-        scratch_shapes=[pltpu.VMEM((2 * rows, lists * LANES), bf16), pltpu.VMEM(logits.shape, f32)]
+        out_specs=[VM, VM, VM, VM],
+        scratch_shapes=[pltpu.VMEM((2 * rows, lists * LANES), bf16), pltpu.VMEM(logits.shape, f32), pltpu.VMEM((lists, 2, LANES), f32)]
         + half_scratch(big, n1),
         compiler_params=params(49),
         name="residuals",
@@ -368,7 +389,7 @@
     )(residual, s2, q, big)
 
 
-def slot_kernel(residual_ref, example_ref, s2_any, q_any, big_any, out_ref, marks, s2, q, h2, sems):
+def small_kernel(residual_ref, s2_any, q_any, big_any, out_ref, s2, q, h2, sems):
     h2_any = big_any.at[pl.ds(big_any.shape[0] - h2.shape[0], h2.shape[0])]
     copies = [
         pltpu.make_async_copy(src, dst, sems.at[k])
@@ -376,19 +397,8 @@
     ]
     for copy in copies:
         copy.start()
-    lists = example_ref.shape[0]
-    rows = residual_ref.shape[0]
-    high, low = doubled(example_ref)
-    mark(low, marks)
-    down = iota((rows, LANES), 0)
     residual = residual_ref[...]
-    found = dot(jnp.concatenate(split_two(residual), axis=0), marks[...])
-    found = found[0:rows] + found[rows:]
-    for k in range(lists):
-        part = found[:, k * LANES : (k + 1) * LANES]
-        out_ref[k, 0:8, :] = jnp.broadcast_to(
-            jnp.sum(jnp.where(high[k : k + 1] == down, part, 0.0), axis=0, keepdims=True), (8, LANES)
-        )
+    rows = residual.shape[0]
     dlogit = jnp.concatenate([residual[k : k + 1] for k in range(rows)], axis=1)
     dlogit = dlogit.astype(bf16).astype(f32)
 
@@ -409,42 +419,41 @@
     )
     ones = jnp.ones((16, 2 * LANES), bf16)
     sums = dot(ones, jnp.concatenate(split_two(small), axis=1), NT)[0:1]
-    count = sums.shape[1] // LANES
-    sums = jnp.concatenate([sums[:, k * LANES : (k + 1) * LANES] for k in range(count)], axis=0)
-    for k in range(lists):
-        out_ref[k, 8 : 8 + count, :] = sums
-
-
-def slot_residuals(residual, example, s2, q, big):
-    lists = example.shape[0]
-    count = (q.shape[0] + 2 * s2.shape[0]) // LANES
-    return pl.pallas_call(
-        slot_kernel,
-        out_shape=jax.ShapeDtypeStruct((lists, 8 + count, LANES), f32),
-        in_specs=[VM] * 2 + [HBM] * 3,
+    width = out_ref.shape[1]
+    sums = jnp.concatenate([sums[:, k * width : (k + 1) * width] for k in range(sums.shape[1] // width)], axis=0)
+    out_ref[...] = jnp.concatenate(split_two(sums), axis=0).astype(f32)
+
+
+def small_gradients(residual, s2, q, big):
+    count = (q.shape[0] + 2 * s2.shape[0]) // q.shape[0]
+    return pl.pallas_call(
+        small_kernel,
+        out_shape=jax.ShapeDtypeStruct((2 * count, q.shape[0]), f32),
+        in_specs=[VM] + [HBM] * 3,
         out_specs=VM,
         scratch_shapes=[
-            pltpu.VMEM((LANES, lists * LANES), bf16),
             pltpu.VMEM(s2.shape, bf16),
             pltpu.VMEM(q.shape, bf16),
             pltpu.VMEM(s2.shape, bf16),
             pltpu.SemaphoreType.DMA((3,)),
         ],
         compiler_params=params(60),
-        cost_estimate=pl.CostEstimate(flops=2 * q.size + (lists << 20), bytes_accessed=3 << 20, transcendentals=0),
-        name="slot_residuals",
-    )(residual, example, s2, q, big)
-
-
-def state_kernel(got_ref, res_ref, z_ref, n_ref, z_out, n_out, small_ref):
+        cost_estimate=pl.CostEstimate(flops=8 * q.size, bytes_accessed=8 << 20, transcendentals=0),
+        name="small_gradients",
+    )(residual, s2, q, big)
+
+
+def state_kernel(got_ref, res_ref, z_ref, n_ref, z_out, n_out):
     lists = got_ref.shape[0]
+    me = position()
     cap = got_ref.shape[1] - 8
     blocks, width = z_ref.shape
     left = iota((1, LANES), 1) < cap
     grad = jnp.zeros((blocks, 2 * width), f32)
     for at in range(0, lists, 4):
         values, index = four_lists(got_ref, at, cap)
-        res = [res_ref[at + k, 0:1, :] for k in range(4)]
+        apart = [me ^ (at + k) for k in range(4)]
+        res = [res_ref[pl.ds((a & 1) * (lists // 2) + (a >> 1), 1), :] for a in apart]
         res = jnp.concatenate([jnp.where(left, res[0], res[1]), jnp.where(left, res[2], res[3])], axis=1)
         scaled = jnp.concatenate(split_two(values.astype(f32) * to_column(res)), axis=1)
         hit = jnp.where(iota((blocks, 4 * cap), 0) == index, 1.0, 0.0).astype(bf16)
@@ -455,20 +464,14 @@
     sigma = (jnp.sqrt(n_new) - jnp.sqrt(n)) / alpha_rate
     n_out[...] = n_new
     z_out[...] = z + grad - sigma * wide_weight(z, n)
-    small_ref[...] = functools.reduce(jnp.add, [res_ref[k, 8:, :] for k in range(lists)])
 
 
 def new_states(got, res, z, n):
-    count = res.shape[1] - 8
     return pl.pallas_call(
         state_kernel,
-        out_shape=(
-            jax.ShapeDtypeStruct(z.shape, f32),
-            jax.ShapeDtypeStruct(z.shape, f32),
-            jax.ShapeDtypeStruct((count, LANES), f32),
-        ),
+        out_shape=(jax.ShapeDtypeStruct(z.shape, f32), jax.ShapeDtypeStruct(z.shape, f32)),
         in_specs=[VM] * 4,
-        out_specs=(VM, VM, VM),
+        out_specs=(VM, VM),
         compiler_params=params(16),
         cost_estimate=pl.CostEstimate(
             flops=4 * got.shape[0] * (got.shape[1] - 8) * z.size, bytes_accessed=4 << 20, transcendentals=2 * z.size
@@ -477,6 +480,58 @@
     )(got, res, z, n)
 
 
+def place_half(half, quad, parts, w1_any, w2_any, wide, narrow, sems):
+    each, width = parts[0].shape
+    first, packed = wide.shape[0] // 4, narrow.shape[1] // 4
+    copies = []
+    for k, part in enumerate(parts):
+        quarter = quad ^ k
+        span = pl.ds(k * first, first)
+        wide[span, :] = part[0:first, :].astype(f32)
+        start = pl.multiple_of((half * 4 + quarter) * first, first)
+        copies.append(pltpu.make_async_copy(wide.at[span], w1_any.at[pl.ds(start, first)], sems.at[3 * k]))
+        copies[-1].start()
+        for side in range(2):
+            span = pl.ds(k * packed, packed)
+            narrow[side, span, :] = part[first:each, side * (width // 2) : (side + 1) * (width // 2)].astype(f32)
+            start = pl.multiple_of((side * 8 + half * 4 + quarter) * packed, packed)
+            copies.append(
+                pltpu.make_async_copy(narrow.at[side, span], w2_any.at[pl.ds(start, packed)], sems.at[3 * k + 1 + side])
+            )
+            copies[-1].start()
+    for copy in copies:
+        copy.wait()
+
+
+def place_kernel(swapped, *refs):
+    parts, (w1_any, w2_any, wide, narrow, sems) = refs[:4], refs[-5:]
+    me = position()
+    place_half((me & 1) ^ swapped, (me >> 1) & 3, parts, w1_any, w2_any, wide, narrow, sems)
+
+
+def place(swapped, parts, first, packed, before=()):
+    width = parts[0].shape[1]
+    shapes = (
+        jax.ShapeDtypeStruct((8 * first, width), f32),
+        jax.ShapeDtypeStruct((16 * packed, width // 2), f32),
+    )
+    return pl.pallas_call(
+        functools.partial(place_kernel, swapped),
+        out_shape=shapes,
+        in_specs=[VM] * 4 + [ANY] * len(before),
+        out_specs=[ANY, ANY],
+        input_output_aliases={4 + k: k for k in range(len(before))},
+        scratch_shapes=[
+            pltpu.VMEM((4 * first, width), f32),
+            pltpu.VMEM((2, 4 * packed, width // 2), f32),
+            pltpu.SemaphoreType.DMA((12,)),
+        ],
+        compiler_params=params(16),
+        cost_estimate=pl.CostEstimate(flops=first * width, bytes_accessed=40 * first * width, transcendentals=0),
+        name="place_other" if swapped else "place_own",
+    )(*parts, *before)
+
+
 def every_to_every(x):
     return lax.all_to_all(x, AXES, split_axis=0, concat_axis=0, tiled=True)
 
@@ -498,33 +553,57 @@
     return lax.optimization_barrier(values)
 
 
-def sum_everywhere(x, me, devices, slots, states):
+def pair(x):
+    top = lax.reduce_precision(x, 8, 7)
+    return jnp.concatenate([top, x - top], axis=0).astype(bf16)
+
+
+def whole(p):
+    rows = p.shape[0] // 2
+    return p[:rows].astype(f32) + p[rows:].astype(f32)
+
+
+def sum_everywhere(x, slots, me, devices, small, states):
     bits = [1 << k for k in range(1, devices.bit_length() - 1)]
     quad, inner, last = bits[:2], bits[2:-1], bits[-1]
     at = (me // quad[0]) % 4
     others = [(3, quad[0] + quad[1]), (1, quad[0]), (2, quad[1])]
+    join = lambda *parts: jnp.concatenate(parts, axis=0)
+    wide = x.shape[1]
+    slots = slots.astype(bf16).reshape(-1, 4, wide)
     rows = x.shape[0] // 4
     quarter = lambda k: lax.dynamic_slice_in_dim(x, (at ^ k) * rows, rows, 0)
-    res = slots(x)
-    x = add(quarter(0), *[swap(quarter(k), bit, devices) for k, bit in others])
-    x, res = hold(x, res)
-    res = every_to_every(res)
-    for bit in inner:
+    sums = small(x)
+    got = {k: swap(join(quarter(k), slots[:, k]), bit, devices) for k, bit in others}
+    slots = jnp.stack([slots[:, 0]] + [got[k][rows:] for k in (1, 2, 3)], axis=1)
+    x = add(quarter(0), *[got[k][:rows] for k in (1, 2, 3)])
+    x, sums = hold(x, sums)
+    sums = whole(sums)
+    for bit in inner + [last]:
         side = (me // bit) % 2
-        x = add(halves(x, side), swap(halves(x, 1 - side), bit, devices))
-    x, res = hold(x, res)
-    made = states(res)
-    x = add(x, swap(x, last, devices))
-    x, *made = hold(x, *made)
+        mine, theirs = (x, x) if bit == last else (halves(x, side), halves(x, 1 - side))
+        slots = slots.reshape(slots.shape[0] // 2, 2, -1, wide)
+        ride, extra = slots[:, 1].reshape(-1, wide), pair(sums)
+        got = swap(join(theirs, ride, extra), bit, devices)
+        n, m = theirs.shape[0], ride.shape[0]
+        x = add(mine, got[:n])
+        slots = jnp.stack([slots[:, 0], got[n : n + m].reshape(slots[:, 0].shape)], axis=1)
+        slots = slots.reshape(slots.shape[0], -1, wide)
+        sums = sums + whole(got[n + m :])
+    slots = slots.reshape(-1, 2, wide // 2)
+    far = swap(slots[:, 1], 1, devices)
+    made = states(whole(jnp.stack([*jnp.split(join(slots[:, 0], far), 2, axis=1)]).reshape(-1, wide // 4)))
     for bit in reversed(inner):
         side = (me // bit) % 2
         other = swap(x, bit, devices)
-        x = jnp.concatenate([jnp.where(side == 0, x, other), jnp.where(side == 0, other, x)], axis=0)
-    parts = [(0, x)] + [(k, swap(x, bit, devices)) for k, bit in others]
-    whole = jnp.zeros((4 * x.shape[0], x.shape[1]), x.dtype)
-    for k, part in parts:
-        whole = lax.dynamic_update_slice_in_dim(whole, part, (at ^ k) * x.shape[0], 0)
-    return whole, made
+        x = join(jnp.where(side == 0, x, other), jnp.where(side == 0, other, x))
+    n = x.shape[0]
+    message = join(x, pair(sums))
+    got = {k: swap(message, bit, devices) for k, bit in others}
+    parts = [x] + [got[k][:n] for k in (1, 2, 3)]
+    sums = sums + sum(whole(got[k][n:]) for k in (1, 2, 3))
+    parts[0], *made = hold(parts[0], *made)
+    return parts, sums, made
 
 
 def per_device(
@@ -546,7 +625,6 @@
     n1, n2 = w_two.shape
     din = dense.shape[1]
     me = lax.axis_index(AXES)
-    core = me % 2
     got = every_to_every(pack(tile_values, tile_block, tile_count))
     big, s2, q, deep = tower(dense, w_one, b_one, w_two, b_two, head)
     wcat = weights(z_state, n_state)
@@ -555,34 +633,35 @@
     logits, example = hold(logits, tile_example)
     marks = example_marks(example)
     logits = every_to_every(logits)
-    prob, residual, send = residuals(logits, tile_example, deep, labels, marks, s2, q, big)
+    prob, residual, send, slots = residuals(logits, tile_example, deep, labels, marks, s2, q, big)
     keep = gradients(residual, s2, q, big)
     own = add(keep, swap(send, 1, devices))
 
-    def slots(x):
-        seen = hold(x, residual)[1]
-        return slot_residuals(seen, tile_example, s2, q, big)
+    def small(x):
+        return small_gradients(hold(x, residual)[1], s2, q, big)
 
     def states(res):
         return new_states(got, res, z_state, n_state)
 
-    own, (z_new, n_new, small) = sum_everywhere(own, me, devices, slots, states)
-    other = swap(own, 1, devices)
-    first, second = jnp.where(core == 0, own, other), jnp.where(core == 0, other, own)
-    big = din // 2
-    grad_w_one = jnp.concatenate([first[:big], second[:big]], axis=0).astype(f32)
-    packed = jnp.concatenate([first[big:], second[big:]], axis=0).astype(f32)
-    grad_w_two = jnp.concatenate([packed[:, :n2], packed[:, n2:]], axis=0)
-    small = small.reshape(-1)
+    parts, sums, (z_new, n_new) = sum_everywhere(own, slots, me, devices, small, states)
+    first, packed = din // 8, n1 // 16
+    order = (3, 1, 2, 0)
+    others = {k: swap(parts[k], 1, devices) for k in order[:-1]}
+    rows = parts[0].shape[0]
+    final = swap(jnp.concatenate([parts[0], pair(sums)], axis=0), 1, devices)
+    sums = (sums + whole(final[rows:])).reshape(-1)
+    others[0] = final[:rows]
+    placed = place(0, parts, first, packed)
+    grad_w_one, grad_w_two = place(1, [others[k] for k in range(4)], first, packed, placed)
     return (
         prob.reshape(-1),
         z_new,
         n_new,
         grad_w_one,
-        small[:n1],
+        sums[:n1],
         grad_w_two,
-        small[n1 : n1 + n2],
-        small[n1 + n2 :],
+        sums[n1 : n1 + n2],
+        sums[n1 + n2 :],
     )
 
 

time: 96.4 us -> 89.9 us (0.933)
  waiting for transfers between devices: 40.6 us -> 34.6 us
  starting transfers between devices: 23.2 us -> 20.8 us
  Pallas kernels: 26.1 us -> 28.2 us
    ppermute x11 -> x15, waiting for transfers between devices: 23.9 us -> 20.4 us  [swap(): return lax.ppermute(x, AXES, [(i, i ^ bit) for i in range(devices)])]
    all_to_all x3 -> x2, starting transfers between devices: 13.4 us -> 10.8 us  [every_to_every(): return lax.all_to_all(x, AXES, split_axis=0, concat_axis=0, tiled=True)]
    all_to_all x3 -> x2, waiting for transfers between devices: 16.8 us -> 14.3 us  [every_to_every(): return lax.all_to_all(x, AXES, split_axis=0, concat_axis=0, tiled=True)]
    pallas_call x1 -> x3, Pallas kernels: 3.79 us -> 5.86 us  [the longest x1 3.55 us: small_gradients(): pl.pallas_call(small_kernel, out_shape=jax.ShapeDtypeStruct((2 * count, q...]
    another operation x0 -> x9, other arithmetic: none -> 1.66 us
    convert_element_type x2 -> x1, other arithmetic: 1.66 us -> 0.01 us  [sum_everywhere(): slots = slots.astype(bf16).reshape(-1, 4, wide)]
    ppermute x11 -> x15, starting transfers between devices: 9.78 us -> 9.98 us  [swap(): return lax.ppermute(x, AXES, [(i, i ^ bit) for i in range(devices)])]
  transfers between devices with their start and end apart: 14 -> 17, of which waited for: 12 -> 11; matrix products, arithmetic and copies ran while one was open for 2% -> 2% of each run, Pallas kernels for 19% -> 22%
where the time goes in v3:
time: 89.9 us; the launch traced here: 89.4 us
  waiting for transfers between devices  34.6 us (38%)
  Pallas kernels  28.2 us (31%)
  starting transfers between devices  20.8 us (23%)
  local copies, waits for them, and re-layouts  2.22 us (2%)
  other arithmetic  2.13 us (2%)
  between operations  1.44 us (2%)
    ppermute x15, waiting for transfers between devices, swap(): return lax.ppermute(x, AXES, [(i, i ^ bit) for i in range(devices)])  20.4 us
    all_to_all x2, waiting for transfers between devices, every_to_every(): return lax.all_to_all(x, AXES, split_axis=0, concat_axis=0, tiled=True)  14.3 us
    all_to_all x2, starting transfers between devices, every_to_every(): return lax.all_to_all(x, AXES, split_axis=0, concat_axis=0, tiled=True)  10.8 us
    ppermute x15, starting transfers between devices, swap(): return lax.ppermute(x, AXES, [(i, i ^ bit) for i in range(devices)])  9.98 us
    pallas_call x1, Pallas kernels, tower(): pl.pallas_call(tower_kernel, grid=(steps,), out_shape=(jax.ShapeDtypeStru...  7.89 us
    pallas_call x1, Pallas kernels, residuals(): pl.pallas_call(residual_kernel, out_shape=(jax.ShapeDtypeStruct((rows, LA...  3.84 us
    pallas_call x1, Pallas kernels, small_gradients(): pl.pallas_call(small_kernel, out_shape=jax.ShapeDtypeStruct((2 * count, q...  3.55 us
    pallas_call x1, Pallas kernels, gradients(): pl.pallas_call(gradient_kernel, out_shape=jax.ShapeDtypeStruct((half, n1)...  2.96 us
  transfers between devices with their start and end apart: 17, of which 11 were waited for; matrix products, arithmetic and copies ran while one was open for 2% of the time, Pallas kernels for 22%

profile of v3, /device:TPU:0, one launch (start us, length us, event | category | flops | bytes accessed | tf_op | source)
XLA Modules:
  0.0 89.4 jit_solution(1548217235798351238)
XLA Ops:
  0.7 2.0 %pack.1 = bf16[32,72,128]{2,1,0:T(8,128)(2,1)} custom-call(bf16[32,64,128]{2,1,0:T(8,128)(2,1)} %values_any.1, s32[32,64]{1,0:T(8,128)} %block_any.1, s32[1,32]{1,0:T(1,128)} %bitcast.40), custom_call_target="tpu_custom_call" | custom-call | tf_op jit(solution)/shard_map/pack/pallas_call | solution.py:96
  2.6 7.3 %all-to-all-start = ((bf16[32,72,128]{2,1,0:T(8,128)(2,1)}), bf16[32,72,128]{2,1,0:T(8,128)(2,1)S(1)}, u32[]{:S(2)}, u32[]{:S(2)}) async-start(bf16[32,72,128]{2,1,0:T(8,128)(2,1)} %pack.1), calls=%async_computation | async-start | bytes 1179648 | tf_op jit(solution)/shard_map/all_to_all | solution.py:536
  11.0 7.9 %tower.1 = (bf16[1792,1024]{1,0:T(8,128)(2,1)}, bf16[256,1024]{1,0:T(8,128)(2,1)}, bf16[512,1024]{1,0:T(8,128)(2,1)}, f32[1,1024]{1,0:T(1,128)}) custom-call(bf16[1024,1024]{1,0:T(8,128)(2,1)} %dense_ref.1, bf16[1024,512]{1,0:T(8,128)(2,1)} %w1_ref.1, f32[1,512]{1,0:T(1,128)} %bitcast.42, bf16[512,256]{1,0:T(8,128)(2,1)} %w2_ref.1, f32[1,256]{1,0:T(1,128)} %bitcast.43, ...), custom_call_target="tpu_custom_call" | custom-call | flops 1610612736 | bytes 12582912 | tf_op jit(solution)/shard_map/tower/pallas_call | solution.py:154
  18.9 7.8 %all-to-all-done.got_ref = bf16[32,72,128]{2,1,0:T(8,128)(2,1)S(1)} async-done(((bf16[32,72,128]{2,1,0:T(8,128)(2,1)}), bf16[32,72,128]{2,1,0:T(8,128)(2,1)S(1)}, u32[]{:S(2)}, u32[]{:S(2)}) %all-to-all-start) | async-done | bytes 589856 | tf_op jit(solution)/shard_map/all_to_all | solution.py:536
  26.7 2.0 %slot_logits.1 = f32[32,1,128]{2,1,0:T(1,128)} custom-call(bf16[32,72,128]{2,1,0:T(8,128)(2,1)S(1)} %all-to-all-done.got_ref, bf16[1024,256]{1,0:T(8,128)(2,1)S(1)} %weights.1.wcat_ref), custom_call_target="tpu_custom_call" | custom-call | tf_op jit(solution)/shard_map/slot_logits/pallas_call | solution.py:218
  28.6 3.5 %all-to-all-start.1 = ((f32[32,1,128]{2,1,0:T(1,128)}), f32[32,1,128]{2,1,0:T(1,128)S(1)}, u32[]{:S(2)}, u32[]{:S(2)}) async-start(f32[32,1,128]{2,1,0:T(1,128)} %slot_logits.1), calls=%async_computation.1 | async-start | bytes 32768 | tf_op jit(solution)/shard_map/all_to_all | solution.py:536
  32.5 6.5 %all-to-all-done.1.logit_any = f32[32,1,128]{2,1,0:T(1,128)S(1)} async-done(((f32[32,1,128]{2,1,0:T(1,128)}), f32[32,1,128]{2,1,0:T(1,128)S(1)}, u32[]{:S(2)}, u32[]{:S(2)}) %all-to-all-start.1) | async-done | bytes 16416 | tf_op jit(solution)/shard_map/all_to_all | solution.py:536
  39.0 3.8 %residuals.1 = (f32[8,128]{1,0:T(8,128)}, f32[8,128]{1,0:T(8,128)S(1)}, bf16[640,512]{1,0:T(8,128)(2,1)}, f32[16,512]{1,0:T(8,128)S(1)}) custom-call(f32[32,1,128]{2,1,0:T(1,128)S(1)} %all-to-all-done.1.logit_any, s32[32,64]{1,0:T(8,128)S(1)} %copy-done.6, f32[1,1024]{1,0:T(1,128)S(1)} %copy-done.9, s32[8,128]{1,0:T(8,128)S(1)} %bitcast.31, ...), custom_call_target="tpu_custom_call" | custom-call | tf_op jit(solution)/shard_map/residuals/pallas_call | solution.py:352
  43.1 3.0 %gradients.1 = bf16[640,512]{1,0:T(8,128)(2,1)S(1)} custom-call(f32[8,128]{1,0:T(8,128)S(1)} %get-tuple-element.44.residual_ref, bf16[256,1024]{1,0:T(8,128)(2,1)S(1)} %copy-done.1, bf16[512,1024]{1,0:T(8,128)(2,1)S(1)} %copy-done, bf16[1792,1024]{1,0:T(8,128)(2,1)} %get-tuple-element.39.big_any), custom_call_target="tpu_custom_call" | custom-call | flops 671088640 | bytes 6291456 | tf_op jit(solution)/shard_map/gradients/pallas_call | solution.py:380
  46.4 0.7 collective-permute-start.3
  47.1 1.5 %collective-permute-start.2 = (bf16[164,512]{1,0:T(8,128)(2,1)S(1)}, bf16[164,512]{1,0:T(8,128)(2,1)S(1)}, u32[]{:S(2)}, u32[]{:S(2)}) collective-permute-start(bf16[164,512]{1,0:T(8,128)(2,1)S(1)} %pad_maximum_fusion.1), channel_id=1, source_target_pairs={{0,4},{1,5},{2,6},{3,7},{4,0},{5,1},{6,2},{7,3},{8,12},{9,13},{10,... | collective-permute-start | bytes 503816 | tf_op jit(solution)/shard_map/ppermute | solution.py:540
  48.5 1.6 %collective-permute-start.1 = (bf16[164,512]{1,0:T(8,128)(2,1)S(1)}, bf16[164,512]{1,0:T(8,128)(2,1)S(1)}, u32[]{:S(2)}, u32[]{:S(2)}) collective-permute-start(bf16[164,512]{1,0:T(8,128)(2,1)S(1)} %pad_maximum_fusion), channel_id=1, source_target_pairs={{0,2},{1,3},{2,0},{3,1},{4,6},{5,7},{6,4},{7,5},{8,10},{9,11},{10,... | collective-permute-start | bytes 503816 | tf_op jit(solution)/shard_map/ppermute | solution.py:540
  50.1 3.5 %small_gradients.1 = f32[4,512]{1,0:T(4,128)} custom-call(f32[8,128]{1,0:T(8,128)} %copy-done.7, bf16[256,1024]{1,0:T(8,128)(2,1)} %get-tuple-element.37.s2.s2_any, bf16[512,1024]{1,0:T(8,128)(2,1)} %get-tuple-element.38.q.q_any, bf16[1792,1024]{1,0:T(8,128)(2,1)} %get-tuple-element.39.big_any), custom_call_target="tpu_custom_call" | custom-call | flops 4194304 | bytes 8388608 | tf_op jit(solution)/shard_map/small_gradients/pallas_call | solution.py:429
  53.7 0.9 collective-permute-done.3
  54.6 2.7 %collective-permute-done.2 = bf16[164,512]{1,0:T(8,128)(2,1)S(1)} collective-permute-done((bf16[164,512]{1,0:T(8,128)(2,1)S(1)}, bf16[164,512]{1,0:T(8,128)(2,1)S(1)}, u32[]{:S(2)}, u32[]{:S(2)}) %collective-permute-start.2) | collective-permute-done | bytes 167968 | tf_op jit(solution)/shard_map/ppermute | solution.py:540
  57.4 0.8 reduce-precision_convert_fusion.3
  58.4 0.7 collective-permute-start.4
  59.0 4.0 %collective-permute-done.4 = bf16[92,512]{1,0:T(8,128)(2,1)S(1)} collective-permute-done((bf16[92,512]{1,0:T(8,128)(2,1)S(1)}, bf16[92,512]{1,0:T(8,128)(2,1)S(1)}, u32[]{:S(2)}, u32[]{:S(2)}) %collective-permute-start.4) | collective-permute-done | bytes 94240 | tf_op jit(solution)/shard_map/ppermute | solution.py:540
  63.1 0.8 reduce-precision_convert_fusion.2
  64.1 0.6 collective-permute-start.5
  64.7 6.0 %collective-permute-done.5 = bf16[92,512]{1,0:T(8,128)(2,1)S(1)} collective-permute-done((bf16[92,512]{1,0:T(8,128)(2,1)S(1)}, bf16[92,512]{1,0:T(8,128)(2,1)S(1)}, u32[]{:S(2)}, u32[]{:S(2)}) %collective-permute-start.5) | collective-permute-done | bytes 94240 | tf_op jit(solution)/shard_map/ppermute | solution.py:540
  71.0 1.1 %collective-permute-done.7 = bf16[16,256]{1,0:T(8,128)(2,1)S(1)} collective-permute-done((bf16[16,256]{1,0:T(8,128)(2,1)S(1)}, bf16[16,256]{1,0:T(8,128)(2,1)S(1)}, u32[]{:S(2)}, u32[]{:S(2)}) %collective-permute-start.7) | collective-permute-done | bytes 8224 | tf_op jit(solution)/shard_map/ppermute | solution.py:540
  72.1 3.1 %collective-permute-done.6 = bf16[80,512]{1,0:T(8,128)(2,1)S(1)} collective-permute-done((bf16[80,512]{1,0:T(8,128)(2,1)S(1)}, bf16[80,512]{1,0:T(8,128)(2,1)S(1)}, u32[]{:S(2)}, u32[]{:S(2)}) %collective-permute-start.6) | collective-permute-done | bytes 81952 | tf_op jit(solution)/shard_map/ppermute | solution.py:540
  75.3 1.6 %collective-permute-start.10 = (bf16[164,512]{1,0:T(8,128)(2,1)S(1)}, bf16[164,512]{1,0:T(8,128)(2,1)S(1)}, u32[]{:S(2)}, u32[]{:S(2)}) collective-permute-start(bf16[164,512]{1,0:T(8,128)(2,1)S(1)} %pad_maximum_fusion.3), channel_id=1, source_target_pairs={{0,6},{1,7},{2,4},{3,5},{4,2},{5,3},{6,0},{7,1},{8,14},{9,15},{10,... | collective-permute-start | bytes 503816 | tf_op jit(solution)/shard_map/ppermute | solution.py:540
  76.9 1.4 %collective-permute-start.9 = (bf16[164,512]{1,0:T(8,128)(2,1)S(1)}, bf16[164,512]{1,0:T(8,128)(2,1)S(1)}, u32[]{:S(2)}, u32[]{:S(2)}) collective-permute-start(bf16[164,512]{1,0:T(8,128)(2,1)S(1)} %pad_maximum_fusion.3), channel_id=1, source_target_pairs={{0,4},{1,5},{2,6},{3,7},{4,0},{5,1},{6,2},{7,3},{8,12},{9,13},{10,... | collective-permute-start | bytes 503816 | tf_op jit(solution)/shard_map/ppermute | solution.py:540
  78.8 2.9 %new_states.1 = (f32[1024,128]{1,0:T(8,128)}, f32[1024,128]{1,0:T(8,128)}) custom-call(bf16[32,72,128]{2,1,0:T(8,128)(2,1)S(1)} %all-to-all-done.got_ref, f32[32,128]{1,0:T(8,128)S(1)} %convert_add_fusion.res_ref, f32[1024,128]{1,0:T(8,128)S(1)} %copy-done.3, f32[1024,128]{1,0:T(8,128)S(1)} %copy-done.5), custom_call_target="tpu_custom_call" | custom-call | flops 1073741824 | bytes 4194304 | tf_op jit(solution)/shard_map/new_states/pallas_call | solution.py:470
  81.8 0.6 collective-permute-done.10
  82.4 1.5 %collective-permute-done.9 = bf16[164,512]{1,0:T(8,128)(2,1)S(1)} collective-permute-done((bf16[164,512]{1,0:T(8,128)(2,1)S(1)}, bf16[164,512]{1,0:T(8,128)(2,1)S(1)}, u32[]{:S(2)}, u32[]{:S(2)}) %collective-permute-start.9) | collective-permute-done | bytes 167968 | tf_op jit(solution)/shard_map/ppermute | solution.py:540
  85.7 1.2 %place_own.1 = (f32[1024,512]{1,0:T(8,128)}, f32[512,256]{1,0:T(8,128)}) custom-call(bf16[160,512]{1,0:T(8,128)(2,1)S(1)} %pad_maximum_fusion.5.refs_0_, bf16[160,512]{1,0:T(8,128)(2,1)S(1)} %slice.221.refs_1_, bf16[160,512]{1,0:T(8,128)(2,1)S(1)} %slice.222.refs_2_, bf16[160,512]{1,0:T(8,128)(2,1)S(1)} %slice.223.refs_3_), custom_call_target="tpu_custom_call" | custom-call | flops 65536 | bytes 2621440 | tf_op jit(solution)/shard_map/place_own/pallas_call | solution.py:518
  86.9 0.6 slice.226
  87.5 0.6 fusion.8
  88.0 1.2 %place_other.1 = (f32[1024,512]{1,0:T(8,128)}, f32[512,256]{1,0:T(8,128)}) custom-call(bf16[160,512]{1,0:T(8,128)(2,1)S(1)} %slice.220.refs_0_, bf16[160,512]{1,0:T(8,128)(2,1)S(1)} %collective-permute-done.12.refs_1_, bf16[160,512]{1,0:T(8,128)(2,1)S(1)} %collective-permute-done.13.refs_2_, ...), custom_call_target="tpu_custom_call", output_to_operand_aliasing={{0}: (4, {}), {1}: (5, {})} | custom-call | flops 65536 | bytes 2621440 | tf_op jit(solution)/shard_map/place_other/pallas_call | solution.py:518
  (100 shorter events, 4.9 us)
Async XLA Ops:
  0.6 9.3 %copy-start.10 = (bf16[256]{0:T(256)(128)(2,1)S(1)}, bf16[256]{0:T(256)(128)(2,1)}, u32[]{:S(2)}) copy-start(bf16[256]{0:T(256)(128)(2,1)} %param.25) | copy-start | bytes 1540
  0.6 9.9 %copy-start.2 = (f32[1024,128]{1,0:T(8,128)S(1)}, f32[1024,128]{1,0:T(8,128)}, u32[]{:S(2)}) copy-start(f32[1024,128]{1,0:T(8,128)} %z_ref.3) | copy-start | bytes 1572868
  0.7 9.9 %copy-start.4 = (f32[1024,128]{1,0:T(8,128)S(1)}, f32[1024,128]{1,0:T(8,128)}, u32[]{:S(2)}) copy-start(f32[1024,128]{1,0:T(8,128)} %n_ref.3) | copy-start | bytes 1572868
  2.6 24.0 %all-to-all-start = ((bf16[32,72,128]{2,1,0:T(8,128)(2,1)}), bf16[32,72,128]{2,1,0:T(8,128)(2,1)S(1)}, u32[]{:S(2)}, u32[]{:S(2)}) async-start(bf16[32,72,128]{2,1,0:T(8,128)(2,1)} %pack.1), calls=%async_computation | async-start | bytes 1179648 | tf_op jit(solution)/shard_map/all_to_all | solution.py:536
  11.0 21.1 %copy-start.6 = (s32[32,64]{1,0:T(8,128)S(1)}, s32[32,64]{1,0:T(8,128)}, u32[]{:S(2)}) copy-start(s32[32,64]{1,0:T(8,128)} %example_ref.2) | copy-start | bytes 24580
  18.9 20.1 %copy-start = (bf16[512,1024]{1,0:T(8,128)(2,1)S(1)}, bf16[512,1024]{1,0:T(8,128)(2,1)}, u32[]{:S(2)}) copy-start(bf16[512,1024]{1,0:T(8,128)(2,1)} %get-tuple-element.38.q.q_any) | copy-start | bytes 3145732
  18.9 20.1 %copy-start.1 = (bf16[256,1024]{1,0:T(8,128)(2,1)S(1)}, bf16[256,1024]{1,0:T(8,128)(2,1)}, u32[]{:S(2)}) copy-start(bf16[256,1024]{1,0:T(8,128)(2,1)} %get-tuple-element.37.s2.s2_any) | copy-start | bytes 1572868
  18.9 20.1 %copy-start.8 = (s32[1024]{0:T(1024)S(1)}, s32[1024]{0:T(1024)}, u32[]{:S(2)}) copy-start(s32[1024]{0:T(1024)} %param.14) | copy-start | bytes 12292
  18.9 20.1 %copy-start.9 = (f32[1,1024]{1,0:T(1,128)S(1)}, f32[1,1024]{1,0:T(1,128)}, u32[]{:S(2)}) copy-start(f32[1,1024]{1,0:T(1,128)} %get-tuple-element.35.deep_ref) | copy-start | bytes 12292
  28.6 10.4 %all-to-all-start.1 = ((f32[32,1,128]{2,1,0:T(1,128)}), f32[32,1,128]{2,1,0:T(1,128)S(1)}, u32[]{:S(2)}, u32[]{:S(2)}) async-start(f32[32,1,128]{2,1,0:T(1,128)} %slot_logits.1), calls=%async_computation.1 | async-start | bytes 32768 | tf_op jit(solution)/shard_map/all_to_all | solution.py:536
  42.9 3.2 %copy-start.7 = (f32[8,128]{1,0:T(8,128)}, f32[8,128]{1,0:T(8,128)S(1)}, u32[]{:S(2)}) copy-start(f32[8,128]{1,0:T(8,128)S(1)} %get-tuple-element.44.residual_ref) | copy-start | bytes 12292
  42.9 3.2 %collective-permute-start = (bf16[640,512]{1,0:T(8,128)(2,1)}, bf16[640,512]{1,0:T(8,128)(2,1)S(1)}, u32[]{:S(2)}, u32[]{:S(2)}) collective-permute-start(bf16[640,512]{1,0:T(8,128)(2,1)} %get-tuple-element.42), channel_id=1, source_target_pairs={{0,1},{1,0},{2,3},{3,2},{4,5},{5,4},{6,7},{7,6},{8,9},{9,8},{10,11... | collective-permute-start | bytes 1966088 | tf_op jit(solution)/shard_map/ppermute | solution.py:540
  46.4 8.2 %collective-permute-start.3 = (bf16[164,512]{1,0:T(8,128)(2,1)S(1)}, bf16[164,512]{1,0:T(8,128)(2,1)S(1)}, u32[]{:S(2)}, u32[]{:S(2)}) collective-permute-start(bf16[164,512]{1,0:T(8,128)(2,1)S(1)} %pad_maximum_fusion.2), channel_id=1, source_target_pairs={{0,6},{1,7},{2,4},{3,5},{4,2},{5,3},{6,0},{7,1},{8,14},{9,15},{10,... | collective-permute-start | bytes 503816 | tf_op jit(solution)/shard_map/ppermute | solution.py:540
  47.1 10.2 %collective-permute-start.2 = (bf16[164,512]{1,0:T(8,128)(2,1)S(1)}, bf16[164,512]{1,0:T(8,128)(2,1)S(1)}, u32[]{:S(2)}, u32[]{:S(2)}) collective-permute-start(bf16[164,512]{1,0:T(8,128)(2,1)S(1)} %pad_maximum_fusion.1), channel_id=1, source_target_pairs={{0,4},{1,5},{2,6},{3,7},{4,0},{5,1},{6,2},{7,3},{8,12},{9,13},{10,... | collective-permute-start | bytes 503816 | tf_op jit(solution)/shard_map/ppermute | solution.py:540
  48.5 8.7 %collective-permute-start.1 = (bf16[164,512]{1,0:T(8,128)(2,1)S(1)}, bf16[164,512]{1,0:T(8,128)(2,1)S(1)}, u32[]{:S(2)}, u32[]{:S(2)}) collective-permute-start(bf16[164,512]{1,0:T(8,128)(2,1)S(1)} %pad_maximum_fusion), channel_id=1, source_target_pairs={{0,2},{1,3},{2,0},{3,1},{4,6},{5,7},{6,4},{7,5},{8,10},{9,11},{10,... | collective-permute-start | bytes 503816 | tf_op jit(solution)/shard_map/ppermute | solution.py:540
  53.7 25.2 %copy-start.3 = (f32[1024,128]{1,0:T(8,128)S(1)}, f32[1024,128]{1,0:T(8,128)}, u32[]{:S(2)}) copy-start(f32[1024,128]{1,0:T(8,128)} %z_ref.3) | copy-start | bytes 1572868
  53.7 25.2 %copy-start.5 = (f32[1024,128]{1,0:T(8,128)S(1)}, f32[1024,128]{1,0:T(8,128)}, u32[]{:S(2)}) copy-start(f32[1024,128]{1,0:T(8,128)} %n_ref.3) | copy-start | bytes 1572868
  58.4 4.7 %collective-permute-start.4 = (bf16[92,512]{1,0:T(8,128)(2,1)S(1)}, bf16[92,512]{1,0:T(8,128)(2,1)S(1)}, u32[]{:S(2)}, u32[]{:S(2)}) collective-permute-start(bf16[92,512]{1,0:T(8,128)(2,1)S(1)} %pad_maximum_fusion.6), channel_id=1, source_target_pairs={{0,8},{1,9},{2,10},{3,11},{4,12},{5,13},{6,14},{7,15},{8,0},{9,1},... | collective-permute-start | bytes 282632 | tf_op jit(solution)/shard_map/ppermute | solution.py:540
  64.1 6.6 %collective-permute-start.5 = (bf16[92,512]{1,0:T(8,128)(2,1)S(1)}, bf16[92,512]{1,0:T(8,128)(2,1)S(1)}, u32[]{:S(2)}, u32[]{:S(2)}) collective-permute-start(bf16[92,512]{1,0:T(8,128)(2,1)S(1)} %pad_maximum_fusion.7), channel_id=1, source_target_pairs={{0,16},{1,17},{2,18},{3,19},{4,20},{5,21},{6,22},{7,23},{8,24},{9,... | collective-permute-start | bytes 282632 | tf_op jit(solution)/shard_map/ppermute | solution.py:540
  70.7 4.5 %collective-permute-start.6 = (bf16[80,512]{1,0:T(8,128)(2,1)S(1)}, bf16[80,512]{1,0:T(8,128)(2,1)S(1)}, u32[]{:S(2)}, u32[]{:S(2)}) collective-permute-start(bf16[80,512]{1,0:T(8,128)(2,1)S(1)} %add_convert_fusion.2), channel_id=1, source_target_pairs={{0,8},{1,9},{2,10},{3,11},{4,12},{5,13},{6,14},{7,15},{8,0},{9,1},... | collective-permute-start | bytes 245768 | tf_op jit(solution)/shard_map/ppermute | solution.py:540
  70.9 1.2 %collective-permute-start.7 = (bf16[16,256]{1,0:T(8,128)(2,1)S(1)}, bf16[16,256]{1,0:T(8,128)(2,1)S(1)}, u32[]{:S(2)}, u32[]{:S(2)}) collective-permute-start(bf16[16,256]{1,0:T(8,128)(2,1)S(1)} %bitcast.38), channel_id=1, source_target_pairs={{0,1},{1,0},{2,3},{3,2},{4,5},{5,4},{6,7},{7,6},{8,9},{9,8},{10,11... | collective-permute-start | bytes 24584 | tf_op jit(solution)/shard_map/ppermute | solution.py:540
  75.3 7.1 %collective-permute-start.10 = (bf16[164,512]{1,0:T(8,128)(2,1)S(1)}, bf16[164,512]{1,0:T(8,128)(2,1)S(1)}, u32[]{:S(2)}, u32[]{:S(2)}) collective-permute-start(bf16[164,512]{1,0:T(8,128)(2,1)S(1)} %pad_maximum_fusion.3), channel_id=1, source_target_pairs={{0,6},{1,7},{2,4},{3,5},{4,2},{5,3},{6,0},{7,1},{8,14},{9,15},{10,... | collective-permute-start | bytes 503816 | tf_op jit(solution)/shard_map/ppermute | solution.py:540
  76.9 6.9 %collective-permute-start.9 = (bf16[164,512]{1,0:T(8,128)(2,1)S(1)}, bf16[164,512]{1,0:T(8,128)(2,1)S(1)}, u32[]{:S(2)}, u32[]{:S(2)}) collective-permute-start(bf16[164,512]{1,0:T(8,128)(2,1)S(1)} %pad_maximum_fusion.3), channel_id=1, source_target_pairs={{0,4},{1,5},{2,6},{3,7},{4,0},{5,1},{6,2},{7,3},{8,12},{9,13},{10,... | collective-permute-start | bytes 503816 | tf_op jit(solution)/shard_map/ppermute | solution.py:540
  78.3 6.0 %collective-permute-start.8 = (bf16[164,512]{1,0:T(8,128)(2,1)S(1)}, bf16[164,512]{1,0:T(8,128)(2,1)S(1)}, u32[]{:S(2)}, u32[]{:S(2)}) collective-permute-start(bf16[164,512]{1,0:T(8,128)(2,1)S(1)} %pad_maximum_fusion.3), channel_id=1, source_target_pairs={{0,2},{1,3},{2,0},{3,1},{4,6},{5,7},{6,4},{7,5},{8,10},{9,11},{10,... | collective-permute-start | bytes 503816 | tf_op jit(solution)/shard_map/ppermute | solution.py:540
  84.3 2.5 %collective-permute-start.11 = (bf16[164,512]{1,0:T(8,128)(2,1)S(1)}, bf16[164,512]{1,0:T(8,128)(2,1)S(1)}, u32[]{:S(2)}, u32[]{:S(2)}) collective-permute-start(bf16[164,512]{1,0:T(8,128)(2,1)S(1)} %pad_maximum_fusion.4), channel_id=1, source_target_pairs={{0,1},{1,0},{2,3},{3,2},{4,5},{5,4},{6,7},{7,6},{8,9},{9,8},{10,11... | collective-permute-start | bytes 503816 | tf_op jit(solution)/shard_map/ppermute | solution.py:540
  84.4 3.6 %collective-permute-start.12 = (bf16[160,512]{1,0:T(8,128)(2,1)S(1)}, bf16[160,512]{1,0:T(8,128)(2,1)S(1)}, u32[]{:S(2)}, u32[]{:S(2)}) collective-permute-start(bf16[160,512]{1,0:T(8,128)(2,1)S(1)} %slice.221.refs_1_), channel_id=1, source_target_pairs={{0,1},{1,0},{2,3},{3,2},{4,5},{5,4},{6,7},{7,6},{8,9},{9,8},{10,11... | collective-permute-start | bytes 491528 | tf_op jit(solution)/shard_map/ppermute | solution.py:540
  85.0 3.0 %collective-permute-start.13 = (bf16[160,512]{1,0:T(8,128)(2,1)S(1)}, bf16[160,512]{1,0:T(8,128)(2,1)S(1)}, u32[]{:S(2)}, u32[]{:S(2)}) collective-permute-start(bf16[160,512]{1,0:T(8,128)(2,1)S(1)} %slice.222.refs_2_), channel_id=1, source_target_pairs={{0,1},{1,0},{2,3},{3,2},{4,5},{5,4},{6,7},{7,6},{8,9},{9,8},{10,11... | collective-permute-start | bytes 491528 | tf_op jit(solution)/shard_map/ppermute | solution.py:540
  85.1 2.9 %collective-permute-start.14 = (bf16[160,512]{1,0:T(8,128)(2,1)S(1)}, bf16[160,512]{1,0:T(8,128)(2,1)S(1)}, u32[]{:S(2)}, u32[]{:S(2)}) collective-permute-start(bf16[160,512]{1,0:T(8,128)(2,1)S(1)} %slice.223.refs_3_), channel_id=1, source_target_pairs={{0,1},{1,0},{2,3},{3,2},{4,5},{5,4},{6,7},{7,6},{8,9},{9,8},{10,11... | collective-permute-start | bytes 491528 | tf_op jit(solution)/shard_map/ppermute | solution.py:540

commit v4 on v3

--- a/solution.py
+++ b/solution.py
@@ -13,6 +13,8 @@
 
 AXES = ("blk", "rep")
 LANES = 128
+EIGHTHS = 8
+ONES = 16
 f32 = jnp.float32
 bf16 = jnp.bfloat16
 NT = (((1,), (1,)), ((), ()))
@@ -254,46 +256,51 @@
 
 
 def half_copies(half, big_any, dense_t, h1, sems):
-    each, packed = dense_t.shape[0], h1.shape[0] // 2
-    copies = [
-        pltpu.make_async_copy(big_any.at[pl.ds(pl.multiple_of(half * each, each), each)], dense_t, sems.at[0])
-    ]
+    n1 = 2 * (h1.shape[0] - ONES)
+    each, packed = dense_t.shape[0] - ONES, n1 // 4
+    span = pl.ds(pl.multiple_of(half * each, each), each)
+    copies = [pltpu.make_async_copy(big_any.at[span], dense_t.at[pl.ds(0, each)], sems.at[0])]
     for side in range(2):
-        start = pl.multiple_of(2 * each + half * packed + side * 2 * packed, packed)
+        span = pl.ds(pl.multiple_of(2 * each + half * packed + side * 2 * packed, packed), packed)
         copies.append(
-            pltpu.make_async_copy(
-                big_any.at[pl.ds(start, packed)], h1.at[pl.ds(side * packed, packed)], sems.at[1 + side]
-            )
+            pltpu.make_async_copy(big_any.at[span], h1.at[pl.ds(side * packed, packed)], sems.at[1 + side])
         )
     return copies
 
 
 def half_gradients(residual, copies, s2, q, dense_t, h1, target):
-    rows, first = residual.shape[0], dense_t.shape[0] // 4
-    packed, width = h1.shape[0] // 8, s2.shape[0]
+    rows, first = residual.shape[0], (dense_t.shape[0] - ONES) // EIGHTHS
+    packed, width = (h1.shape[0] - ONES) // 2 // EIGHTHS, s2.shape[0]
     each = first + packed
-    dlogit = jnp.concatenate([residual[k : k + 1] for k in range(rows)], axis=1)
-    dlogit = dlogit.astype(bf16).astype(f32)
-    d_two = (s2[...].astype(f32) * dlogit).astype(bf16)
+    dense_t[EIGHTHS * first :, :] = jnp.ones((ONES, dense_t.shape[1]), bf16)
+    h1[2 * EIGHTHS * packed :, :] = jnp.ones((ONES, h1.shape[1]), bf16)
+    dlogit = jnp.concatenate([residual[k : k + 1] for k in range(rows)], axis=1).astype(bf16)
+    scale = dlogit.astype(f32)
+    d_two = (s2[...].astype(f32) * scale).astype(bf16)
     copies[1].wait()
     copies[2].wait()
-    second = dot(h1[...], d_two, NT).astype(bf16)
-    for k in range(4):
-        at = k * packed
+    second = dot(h1[...], d_two, NT)
+    b_two = second[2 * EIGHTHS * packed : 2 * EIGHTHS * packed + 1]
+    second = second.astype(bf16)
+    for k in range(EIGHTHS):
+        at, low = k * packed, (k + EIGHTHS) * packed
         target[k * each + first : (k + 1) * each, 0:width] = second[at : at + packed]
-        target[k * each + first : (k + 1) * each, width:] = second[4 * packed + at : 5 * packed + at]
-    d_one = (q[...].astype(f32) * dlogit).astype(bf16)
+        target[k * each + first : (k + 1) * each, width:] = second[low : low + packed]
+    d_one = (q[...].astype(f32) * scale).astype(bf16)
     copies[0].wait()
-    made = dot(dense_t[...], d_one, NT).astype(bf16)
-    for k in range(4):
+    made = dot(dense_t[...], d_one, NT)
+    b_one = made[EIGHTHS * first : EIGHTHS * first + 1]
+    made = made.astype(bf16)
+    for k in range(EIGHTHS):
         target[k * each : k * each + first, :] = made[k * first : (k + 1) * first]
+    return dlogit, b_one, b_two
 
 
 def half_scratch(big, n1):
     half = (big.shape[0] - n1 - n1 // 2) // 2
     return [
-        pltpu.VMEM((half, big.shape[1]), bf16),
-        pltpu.VMEM((n1 // 2, big.shape[1]), bf16),
+        pltpu.VMEM((half + ONES, big.shape[1]), bf16),
+        pltpu.VMEM((n1 // 2 + ONES, big.shape[1]), bf16),
         pltpu.SemaphoreType.DMA((4,)),
     ]
 
@@ -338,10 +345,11 @@
         part = jnp.where(high[k : k + 1] == down, found[:, k * LANES : (k + 1) * LANES], 0.0)
         top, rest = split_two(jnp.sum(part, axis=0, keepdims=True))
         apart[me ^ k] = jnp.concatenate([top.astype(f32), rest.astype(f32)], axis=0)
-    for k in range(lists):
-        for side in range(2):
-            at = (k % 2) * 2 * LANES + side * LANES
-            slot_ref[k // 2 : k // 2 + 1, at : at + LANES] = apart[k, side : side + 1, :]
+    lines = [
+        jnp.concatenate([apart[k + c, s : s + 1, :] for c in range(2) for s in range(2)], axis=1)
+        for k in range(0, lists, 2)
+    ]
+    slot_ref[...] = jnp.concatenate(lines, axis=0).astype(bf16)
 
 
 def residuals(logits, example, deep, labels, marks, s2, q, big):
@@ -355,7 +363,7 @@
             jax.ShapeDtypeStruct((rows, LANES), f32),
             jax.ShapeDtypeStruct((rows, LANES), f32),
             jax.ShapeDtypeStruct((half, n1), bf16),
-            jax.ShapeDtypeStruct((lists // 2, 4 * LANES), f32),
+            jax.ShapeDtypeStruct((lists // 2, 4 * LANES), bf16),
         ),
         in_specs=[ANY] + [VM] * 6 + [HBM],
         out_specs=[VM, VM, VM, VM],
@@ -366,12 +374,18 @@
     )(logits, example, deep, labels.reshape(rows, LANES), marks, s2, q, big)
 
 
-def gradient_kernel(residual_ref, s2, q, big_any, keep_ref, dense_t, h1, sems):
+def gradient_kernel(residual_ref, s2, q, big_any, keep_ref, small_ref, h2, dense_t, h1, sems):
     core = lax.axis_index("rep") & 1
-    copies = half_copies(core, big_any, dense_t, h1, sems)
+    span = pl.ds(big_any.shape[0] - h2.shape[0], h2.shape[0])
+    copies = [pltpu.make_async_copy(big_any.at[span], h2, sems.at[3])]
+    copies = half_copies(core, big_any, dense_t, h1, sems) + copies
     for copy in copies:
         copy.start()
-    half_gradients(residual_ref[...], copies, s2, q, dense_t, h1, keep_ref)
+    dlogit, b_one, b_two = half_gradients(residual_ref[...], copies, s2, q, dense_t, h1, keep_ref)
+    copies[3].wait()
+    head = dot(jnp.broadcast_to(dlogit, (ONES, dlogit.shape[1])), h2[...], NT)[0:1]
+    small = jnp.concatenate([b_one, jnp.concatenate([b_two, head], axis=1)], axis=0)
+    small_ref[...] = jnp.concatenate(split_two(small), axis=0)
 
 
 def gradients(residual, s2, q, big):
@@ -379,67 +393,13 @@
     half = (big.shape[0] - n1 - s2.shape[0]) // 2 + n1 // 4
     return pl.pallas_call(
         gradient_kernel,
-        out_shape=jax.ShapeDtypeStruct((half, n1), bf16),
+        out_shape=(jax.ShapeDtypeStruct((half, n1), bf16), jax.ShapeDtypeStruct((4, n1), bf16)),
         in_specs=[VM] * 3 + [HBM],
-        out_specs=VM,
-        scratch_shapes=half_scratch(big, n1),
+        out_specs=[VM, VM],
+        scratch_shapes=[pltpu.VMEM(s2.shape, bf16)] + half_scratch(big, n1),
         compiler_params=params(49),
         cost_estimate=pl.CostEstimate(flops=2 * half * n1 * ex, bytes_accessed=6 << 20, transcendentals=0),
         name="gradients",
-    )(residual, s2, q, big)
-
-
-def small_kernel(residual_ref, s2_any, q_any, big_any, out_ref, s2, q, h2, sems):
-    h2_any = big_any.at[pl.ds(big_any.shape[0] - h2.shape[0], h2.shape[0])]
-    copies = [
-        pltpu.make_async_copy(src, dst, sems.at[k])
-        for k, (src, dst) in enumerate(((q_any, q), (s2_any, s2), (h2_any, h2)))
-    ]
-    for copy in copies:
-        copy.start()
-    residual = residual_ref[...]
-    rows = residual.shape[0]
-    dlogit = jnp.concatenate([residual[k : k + 1] for k in range(rows)], axis=1)
-    dlogit = dlogit.astype(bf16).astype(f32)
-
-    def fold(a):
-        return functools.reduce(
-            jnp.add, [a[:, k * LANES : (k + 1) * LANES].astype(f32) for k in range(rows)]
-        )
-
-    for copy in copies:
-        copy.wait()
-    small = jnp.concatenate(
-        [
-            fold((q[...].astype(f32) * dlogit).astype(bf16)),
-            fold((s2[...].astype(f32) * dlogit).astype(bf16)),
-            fold(h2[...].astype(f32) * dlogit),
-        ],
-        axis=0,
-    )
-    ones = jnp.ones((16, 2 * LANES), bf16)
-    sums = dot(ones, jnp.concatenate(split_two(small), axis=1), NT)[0:1]
-    width = out_ref.shape[1]
-    sums = jnp.concatenate([sums[:, k * width : (k + 1) * width] for k in range(sums.shape[1] // width)], axis=0)
-    out_ref[...] = jnp.concatenate(split_two(sums), axis=0).astype(f32)
-
-
-def small_gradients(residual, s2, q, big):
-    count = (q.shape[0] + 2 * s2.shape[0]) // q.shape[0]
-    return pl.pallas_call(
-        small_kernel,
-        out_shape=jax.ShapeDtypeStruct((2 * count, q.shape[0]), f32),
-        in_specs=[VM] + [HBM] * 3,
-        out_specs=VM,
-        scratch_shapes=[
-            pltpu.VMEM(s2.shape, bf16),
-            pltpu.VMEM(q.shape, bf16),
-            pltpu.VMEM(s2.shape, bf16),
-            pltpu.SemaphoreType.DMA((3,)),
-        ],
-        compiler_params=params(60),
-        cost_estimate=pl.CostEstimate(flops=8 * q.size, bytes_accessed=8 << 20, transcendentals=0),
-        name="small_gradients",
     )(residual, s2, q, big)
 
 
@@ -480,54 +440,61 @@
     )(got, res, z, n)
 
 
-def place_half(half, quad, parts, w1_any, w2_any, wide, narrow, sems):
-    each, width = parts[0].shape
-    first, packed = wide.shape[0] // 4, narrow.shape[1] // 4
-    copies = []
+def place_kernel(swapped, *refs):
+    parts, refs = refs[:4], refs[4:]
+    before, refs = (refs[:3], refs[3:]) if swapped else (None, refs)
+    w1_any, w2_any, *outs = refs[:-3]
+    wide, narrow, sems = refs[-3:]
+    me = position()
+    half, quad = (me & 1) ^ swapped, (me >> 1) & 3
+    first, packed = wide.shape[0] // EIGHTHS, narrow.shape[1] // EIGHTHS
+    each, width = first + packed, parts[0].shape[1]
+    copies, total = [], before[2][...] if swapped else 0.0
     for k, part in enumerate(parts):
-        quarter = quad ^ k
-        span = pl.ds(k * first, first)
-        wide[span, :] = part[0:first, :].astype(f32)
-        start = pl.multiple_of((half * 4 + quarter) * first, first)
-        copies.append(pltpu.make_async_copy(wide.at[span], w1_any.at[pl.ds(start, first)], sems.at[3 * k]))
-        copies[-1].start()
-        for side in range(2):
-            span = pl.ds(k * packed, packed)
-            narrow[side, span, :] = part[first:each, side * (width // 2) : (side + 1) * (width // 2)].astype(f32)
-            start = pl.multiple_of((side * 8 + half * 4 + quarter) * packed, packed)
-            copies.append(
-                pltpu.make_async_copy(narrow.at[side, span], w2_any.at[pl.ds(start, packed)], sems.at[3 * k + 1 + side])
-            )
+        for t in range(2):
+            at, slot = t * each, 2 * k + t
+            place = (half * 4 + (quad ^ k)) * 2 + t
+            span = pl.ds(slot * first, first)
+            wide[span, :] = part[at : at + first, :].astype(f32)
+            target = w1_any.at[pl.ds(pl.multiple_of(place * first, first), first)]
+            copies.append(pltpu.make_async_copy(wide.at[span], target, sems.at[3 * slot]))
             copies[-1].start()
+            for c in range(2):
+                span = pl.ds(slot * packed, packed)
+                lanes = slice(c * (width // 2), (c + 1) * (width // 2))
+                narrow[c, span, :] = part[at + first : at + each, lanes].astype(f32)
+                target = w2_any.at[pl.ds(pl.multiple_of((c * 2 * EIGHTHS + place) * packed, packed), packed)]
+                copies.append(pltpu.make_async_copy(narrow.at[c, span], target, sems.at[3 * slot + 1 + c]))
+                copies[-1].start()
+        extra = part[2 * each :, :].astype(f32)
+        total = total + sum(extra[r : r + 2] for r in range(0, extra.shape[0], 2))
+    if swapped:
+        outs[0][...] = total[0:1]
+        outs[1][...] = total[1:2, 0 : width // 2]
+        outs[2][...] = total[1:2, width // 2 :]
+    else:
+        outs[0][...] = total
     for copy in copies:
         copy.wait()
 
 
-def place_kernel(swapped, *refs):
-    parts, (w1_any, w2_any, wide, narrow, sems) = refs[:4], refs[-5:]
-    me = position()
-    place_half((me & 1) ^ swapped, (me >> 1) & 3, parts, w1_any, w2_any, wide, narrow, sems)
-
-
 def place(swapped, parts, first, packed, before=()):
     width = parts[0].shape[1]
-    shapes = (
-        jax.ShapeDtypeStruct((8 * first, width), f32),
-        jax.ShapeDtypeStruct((16 * packed, width // 2), f32),
-    )
+    shapes = [(2 * EIGHTHS * first, width), (4 * EIGHTHS * packed, width // 2)]
+    tail = [(1, width), (1, width // 2), (1, width // 2)] if swapped else [(2, width)]
     return pl.pallas_call(
         functools.partial(place_kernel, swapped),
-        out_shape=shapes,
-        in_specs=[VM] * 4 + [ANY] * len(before),
-        out_specs=[ANY, ANY],
-        input_output_aliases={4 + k: k for k in range(len(before))},
+        out_shape=[jax.ShapeDtypeStruct(t, f32) for t in shapes + tail],
+        in_specs=[VM] * 4 + [ANY, ANY, VM] * swapped,
+        out_specs=[ANY, ANY] + [VM] * len(tail),
+        input_output_aliases={4: 0, 5: 1} if swapped else {},
         scratch_shapes=[
-            pltpu.VMEM((4 * first, width), f32),
-            pltpu.VMEM((2, 4 * packed, width // 2), f32),
-            pltpu.SemaphoreType.DMA((12,)),
+            pltpu.VMEM((EIGHTHS * first, width), f32),
+            pltpu.VMEM((2, EIGHTHS * packed, width // 2), f32),
+            pltpu.SemaphoreType.DMA((3 * EIGHTHS,)),
         ],
         compiler_params=params(16),
-        cost_estimate=pl.CostEstimate(flops=first * width, bytes_accessed=40 * first * width, transcendentals=0),
+        cost_estimate=pl.CostEstimate(flops=first * width, bytes_accessed=80 * first * width, transcendentals=0),
         name="place_other" if swapped else "place_own",
     )(*parts, *before)
 
@@ -553,9 +520,8 @@
     return lax.optimization_barrier(values)
 
 
-def pair(x):
-    top = lax.reduce_precision(x, 8, 7)
-    return jnp.concatenate([top, x - top], axis=0).astype(bf16)
+def join(*parts):
+    return jnp.concatenate(parts, axis=0)
 
 
 def whole(p):
@@ -563,47 +529,51 @@
     return p[:rows].astype(f32) + p[rows:].astype(f32)
 
 
-def sum_everywhere(x, slots, me, devices, small, states):
+def sum_everywhere(x, slots, extra, me, devices, states):
     bits = [1 << k for k in range(1, devices.bit_length() - 1)]
     quad, inner, last = bits[:2], bits[2:-1], bits[-1]
     at = (me // quad[0]) % 4
     others = [(3, quad[0] + quad[1]), (1, quad[0]), (2, quad[1])]
-    join = lambda *parts: jnp.concatenate(parts, axis=0)
     wide = x.shape[1]
-    slots = slots.astype(bf16).reshape(-1, 4, wide)
-    rows = x.shape[0] // 4
-    quarter = lambda k: lax.dynamic_slice_in_dim(x, (at ^ k) * rows, rows, 0)
-    sums = small(x)
-    got = {k: swap(join(quarter(k), slots[:, k]), bit, devices) for k, bit in others}
-    slots = jnp.stack([slots[:, 0]] + [got[k][rows:] for k in (1, 2, 3)], axis=1)
-    x = add(quarter(0), *[got[k][:rows] for k in (1, 2, 3)])
-    x, sums = hold(x, sums)
-    sums = whole(sums)
+    slots = slots.reshape(-1, 4, wide)
+    rows = x.shape[0] // EIGHTHS
+    side = (me // inner[0]) % 2
+    quarters = lambda v: [v] + [swap(v, bit, devices) for k, bit in sorted(others)]
+    eighth = lambda k, t: lax.dynamic_slice_in_dim(x, ((at ^ k) * 2 + t) * rows, rows, 0)
+    away = {k: swap(join(eighth(k, 1 - side), slots[:, k]), bit, devices) for k, bit in others}
+    stay = {k: swap(eighth(k, side), bit, devices) for k, bit in others}
+    slots = jnp.stack([slots[:, 0]] + [away[k][rows:] for k in (1, 2, 3)], axis=1)
+    mine = None
+    theirs = add(eighth(0, 1 - side), *[away[k][:rows] for k in (1, 2, 3)])
     for bit in inner + [last]:
-        side = (me // bit) % 2
-        mine, theirs = (x, x) if bit == last else (halves(x, side), halves(x, 1 - side))
+        if bit == last:
+            mine = theirs = x
+        elif bit != inner[0]:
+            side_now = (me // bit) % 2
+            mine, theirs = halves(x, side_now), halves(x, 1 - side_now)
         slots = slots.reshape(slots.shape[0] // 2, 2, -1, wide)
-        ride, extra = slots[:, 1].reshape(-1, wide), pair(sums)
-        got = swap(join(theirs, ride, extra), bit, devices)
+        ride = slots[:, 1].reshape(-1, wide)
         n, m = theirs.shape[0], ride.shape[0]
+        got = swap(join(theirs, ride, *([extra] if bit == last else [])), bit, devices)
+        if bit == inner[0]:
+            mine = add(eighth(0, side), *[stay[k] for k in (1, 2, 3)])
         x = add(mine, got[:n])
         slots = jnp.stack([slots[:, 0], got[n : n + m].reshape(slots[:, 0].shape)], axis=1)
         slots = slots.reshape(slots.shape[0], -1, wide)
-        sums = sums + whole(got[n + m :])
+    extra = join(extra, got[n + m :])
     slots = slots.reshape(-1, 2, wide // 2)
     far = swap(slots[:, 1], 1, devices)
     made = states(whole(jnp.stack([*jnp.split(join(slots[:, 0], far), 2, axis=1)]).reshape(-1, wide // 4)))
     for bit in reversed(inner):
-        side = (me // bit) % 2
-        other = swap(x, bit, devices)
-        x = join(jnp.where(side == 0, x, other), jnp.where(side == 0, other, x))
-    n = x.shape[0]
-    message = join(x, pair(sums))
-    got = {k: swap(message, bit, devices) for k, bit in others}
-    parts = [x] + [got[k][:n] for k in (1, 2, 3)]
-    sums = sums + sum(whole(got[k][n:]) for k in (1, 2, 3))
+        side_now = (me // bit) % 2
+        got = swap(join(x, extra), bit, devices)
+        n = x.shape[0]
+        other = got[:n]
+        x = join(jnp.where(side_now == 0, x, other), jnp.where(side_now == 0, other, x))
+        extra = join(extra, got[n:])
+    parts = quarters(join(x, extra))
     parts[0], *made = hold(parts[0], *made)
-    return parts, sums, made
+    return parts, made
 
 
 def per_device(
@@ -627,41 +597,34 @@
     me = lax.axis_index(AXES)
     got = every_to_every(pack(tile_values, tile_block, tile_count))
     big, s2, q, deep = tower(dense, w_one, b_one, w_two, b_two, head)
-    wcat = weights(z_state, n_state)
-    got, deep = lax.optimization_barrier((got, deep))
+    deep, z_then, n_then = hold(deep, z_state, n_state)
+    wcat = weights(z_then, n_then)
+    got, deep = hold(got, deep)
     logits = slot_logits(got, wcat)
     logits, example = hold(logits, tile_example)
     marks = example_marks(example)
     logits = every_to_every(logits)
     prob, residual, send, slots = residuals(logits, tile_example, deep, labels, marks, s2, q, big)
-    keep = gradients(residual, s2, q, big)
+    keep, small = gradients(residual, s2, q, big)
     own = add(keep, swap(send, 1, devices))
-
-    def small(x):
-        return small_gradients(hold(x, residual)[1], s2, q, big)
 
     def states(res):
         return new_states(got, res, z_state, n_state)
 
-    parts, sums, (z_new, n_new) = sum_everywhere(own, slots, me, devices, small, states)
-    first, packed = din // 8, n1 // 16
-    order = (3, 1, 2, 0)
-    others = {k: swap(parts[k], 1, devices) for k in order[:-1]}
-    rows = parts[0].shape[0]
-    final = swap(jnp.concatenate([parts[0], pair(sums)], axis=0), 1, devices)
-    sums = (sums + whole(final[rows:])).reshape(-1)
-    others[0] = final[:rows]
+    parts, (z_new, n_new) = sum_everywhere(own, slots, small, me, devices, states)
+    first, packed = din // 2 // EIGHTHS, n1 // 4 // EIGHTHS
+    others = [swap(part, 1, devices) for part in parts]
     placed = place(0, parts, first, packed)
-    grad_w_one, grad_w_two = place(1, [others[k] for k in range(4)], first, packed, placed)
+    grad_w_one, grad_w_two, grad_b_one, grad_b_two, grad_head = place(1, others, first, packed, placed)
     return (
         prob.reshape(-1),
         z_new,
         n_new,
         grad_w_one,
-        sums[:n1],
+        grad_b_one.reshape(-1),
         grad_w_two,
-        sums[n1 : n1 + n2],
-        sums[n1 + n2 :],
+        grad_b_two.reshape(-1),
+        grad_head.reshape(-1),
     )
 
 

time: 89.9 us -> 85.6 us (0.952)
  waiting for transfers between devices: 34.6 us -> 30.2 us
  starting transfers between devices: 20.8 us -> 24.5 us
  Pallas kernels: 28.2 us -> 25.5 us
  other arithmetic: 2.13 us -> 0.45 us
  local copies, waits for them, and re-layouts: 2.22 us -> 3.23 us
    ppermute x15 -> x18, starting transfers between devices: 9.98 us -> 13.7 us  [swap(): return lax.ppermute(x, AXES, [(i, i ^ bit) for i in range(devices)])]
    pallas_call x4 -> x3, Pallas kernels: 8.83 us -> 6.2 us  [the longest x2 3.11 us: place(): pl.pallas_call(functools.partial(place_kernel, swapped), out_shape=[jax.S...]
    ppermute x15 -> x18, waiting for transfers between devices: 20.4 us -> 18.1 us  [swap(): return lax.ppermute(x, AXES, [(i, i ^ bit) for i in range(devices)])]
    unnamed x31 -> x28, local copies, waits for them, and re-layouts: 0.12 us -> 2.29 us
    all_to_all x2, waiting for transfers between devices: 14.3 us -> 12.2 us  [every_to_every(): return lax.all_to_all(x, AXES, split_axis=0, concat_axis=0, tiled=True)]
    another operation x7 -> x0, other arithmetic: 1.61 us -> none
    slice x10 -> x7, local copies, waits for them, and re-layouts: 1.22 us -> 0.08 us  [the longest x1 0.05 us: sum_everywhere(): slots[:, k]]
  transfers between devices with their start and end apart: 17 -> 20, of which waited for: 11 -> 11; matrix products, arithmetic and copies ran while one was open for 2% -> 1% of each run, Pallas kernels for 22% -> 19%
where the time goes in v4:
time: 85.6 us; the launch traced here: 85.2 us
  waiting for transfers between devices  30.2 us (35%)
  Pallas kernels  25.5 us (30%)
  starting transfers between devices  24.5 us (29%)
  local copies, waits for them, and re-layouts  3.23 us (4%)
  between operations  1.33 us (2%)
    ppermute x18, waiting for transfers between devices, swap(): return lax.ppermute(x, AXES, [(i, i ^ bit) for i in range(devices)])  18.1 us
    ppermute x18, starting transfers between devices, swap(): return lax.ppermute(x, AXES, [(i, i ^ bit) for i in range(devices)])  13.7 us
    all_to_all x2, waiting for transfers between devices, every_to_every(): return lax.all_to_all(x, AXES, split_axis=0, concat_axis=0, tiled=True)  12.2 us
    all_to_all x2, starting transfers between devices, every_to_every(): return lax.all_to_all(x, AXES, split_axis=0, concat_axis=0, tiled=True)  10.8 us
    pallas_call x1, Pallas kernels, tower(): pl.pallas_call(tower_kernel, grid=(steps,), out_shape=(jax.ShapeDtypeStru...  7.86 us
    pallas_call x1, Pallas kernels, residuals(): pl.pallas_call(residual_kernel, out_shape=(jax.ShapeDtypeStruct((rows, LA...  3.87 us
    pallas_call x2, Pallas kernels, place(): pl.pallas_call(functools.partial(place_kernel, swapped), out_shape=[jax.S...  3.11 us
    pallas_call x1, Pallas kernels, gradients(): pl.pallas_call(gradient_kernel, out_shape=(jax.ShapeDtypeStruct((half, n1...  3.09 us
  transfers between devices with their start and end apart: 20, of which 11 were waited for; matrix products, arithmetic and copies ran while one was open for 1% of the time, Pallas kernels for 19%

profile of v4, /device:TPU:0, one launch (start us, length us, event | category | flops | bytes accessed | tf_op | source)
XLA Modules:
  0.0 85.2 jit_solution(12683346686541693832)
XLA Ops:
  0.6 1.9 %pack.1 = bf16[32,72,128]{2,1,0:T(8,128)(2,1)} custom-call(bf16[32,64,128]{2,1,0:T(8,128)(2,1)} %values_any.1, s32[32,64]{1,0:T(8,128)} %block_any.1, s32[1,32]{1,0:T(1,128)} %bitcast.37), custom_call_target="tpu_custom_call" | custom-call | tf_op jit(solution)/shard_map/pack/pallas_call | solution.py:98
  2.5 7.3 %all-to-all-start = ((bf16[32,72,128]{2,1,0:T(8,128)(2,1)}), bf16[32,72,128]{2,1,0:T(8,128)(2,1)S(1)}, u32[]{:S(2)}, u32[]{:S(2)}) async-start(bf16[32,72,128]{2,1,0:T(8,128)(2,1)} %pack.1), calls=%async_computation | async-start | bytes 1179648 | tf_op jit(solution)/shard_map/all_to_all | solution.py:503
  9.8 0.6 reshape.62.head_ref
  10.4 7.9 %tower.1 = (bf16[1792,1024]{1,0:T(8,128)(2,1)}, bf16[256,1024]{1,0:T(8,128)(2,1)}, bf16[512,1024]{1,0:T(8,128)(2,1)}, f32[1,1024]{1,0:T(1,128)}) custom-call(bf16[1024,1024]{1,0:T(8,128)(2,1)} %dense_ref.1, bf16[1024,512]{1,0:T(8,128)(2,1)} %w1_ref.1, f32[1,512]{1,0:T(1,128)} %bitcast.39, bf16[512,256]{1,0:T(8,128)(2,1)} %w2_ref.1, f32[1,256]{1,0:T(1,128)} %bitcast.41, ...), custom_call_target="tpu_custom_call" | custom-call | flops 1610612736 | bytes 12582912 | tf_op jit(solution)/shard_map/tower/pallas_call | solution.py:156
  18.3 1.1 %copy-done.2 = f32[1024,128]{1,0:T(8,128)S(1)} copy-done((f32[1024,128]{1,0:T(8,128)S(1)}, f32[1024,128]{1,0:T(8,128)}, u32[]{:S(2)}) %copy-start.2) | copy-done | bytes 524312
  19.4 1.0 %copy-done.4 = f32[1024,128]{1,0:T(8,128)S(1)} copy-done((f32[1024,128]{1,0:T(8,128)S(1)}, f32[1024,128]{1,0:T(8,128)}, u32[]{:S(2)}) %copy-start.4) | copy-done | bytes 524312
  20.9 5.6 %all-to-all-done.got_ref = bf16[32,72,128]{2,1,0:T(8,128)(2,1)S(1)} async-done(((bf16[32,72,128]{2,1,0:T(8,128)(2,1)}), bf16[32,72,128]{2,1,0:T(8,128)(2,1)S(1)}, u32[]{:S(2)}, u32[]{:S(2)}) %all-to-all-start) | async-done | bytes 589856 | tf_op jit(solution)/shard_map/all_to_all | solution.py:503
  26.6 1.9 %slot_logits.1 = f32[32,1,128]{2,1,0:T(1,128)} custom-call(bf16[32,72,128]{2,1,0:T(8,128)(2,1)S(1)} %all-to-all-done.got_ref, bf16[1024,256]{1,0:T(8,128)(2,1)S(1)} %weights.1.wcat_ref), custom_call_target="tpu_custom_call" | custom-call | tf_op jit(solution)/shard_map/slot_logits/pallas_call | solution.py:220
  28.5 3.5 %all-to-all-start.1 = ((f32[32,1,128]{2,1,0:T(1,128)}), f32[32,1,128]{2,1,0:T(1,128)S(1)}, u32[]{:S(2)}, u32[]{:S(2)}) async-start(f32[32,1,128]{2,1,0:T(1,128)} %slot_logits.1), calls=%async_computation.1 | async-start | bytes 32768 | tf_op jit(solution)/shard_map/all_to_all | solution.py:503
  32.4 6.5 %all-to-all-done.1.logit_any = f32[32,1,128]{2,1,0:T(1,128)S(1)} async-done(((f32[32,1,128]{2,1,0:T(1,128)}), f32[32,1,128]{2,1,0:T(1,128)S(1)}, u32[]{:S(2)}, u32[]{:S(2)}) %all-to-all-start.1) | async-done | bytes 16416 | tf_op jit(solution)/shard_map/all_to_all | solution.py:503
  38.9 3.9 %residuals.1 = (f32[8,128]{1,0:T(8,128)}, f32[8,128]{1,0:T(8,128)S(1)}, bf16[640,512]{1,0:T(8,128)(2,1)}, bf16[16,512]{1,0:T(8,128)(2,1)S(1)}) custom-call(f32[32,1,128]{2,1,0:T(1,128)S(1)} %all-to-all-done.1.logit_any, s32[32,64]{1,0:T(8,128)S(1)} %copy-done.6, f32[1,1024]{1,0:T(1,128)S(1)} %copy-done.8, s32[8,128]{1,0:T(8,128)S(1)} %bitcast.31, ...), custom_call_target="tpu_custom_call" | custom-call | tf_op jit(solution)/shard_map/residuals/pallas_call | solution.py:360
  43.1 3.1 %gradients.1 = (bf16[640,512]{1,0:T(8,128)(2,1)S(1)}, bf16[4,512]{1,0:T(4,128)(2,1)S(1)}) custom-call(f32[8,128]{1,0:T(8,128)S(1)} %get-tuple-element.50.residual_ref, bf16[256,1024]{1,0:T(8,128)(2,1)S(1)} %copy-done.1, bf16[512,1024]{1,0:T(8,128)(2,1)S(1)} %copy-done, bf16[1792,1024]{1,0:T(8,128)(2,1)} %get-tuple-element.48.big_any), custom_call_target="tpu_custom_call" | custom-call | flops 671088640 | bytes 6291456 | tf_op jit(solution)/shard_map/gradients/pallas_call | solution.py:394
  46.5 0.6 collective-permute-start.4
  47.1 0.7 collective-permute-start.5
  47.8 2.4 %collective-permute-start.6 = (bf16[84,512]{1,0:T(8,128)(2,1)S(1)}, bf16[84,512]{1,0:T(8,128)(2,1)S(1)}, u32[]{:S(2)}, u32[]{:S(2)}) collective-permute-start(bf16[84,512]{1,0:T(8,128)(2,1)S(1)} %pad_maximum_fusion.3), channel_id=1, source_target_pairs={{0,6},{1,7},{2,4},{3,5},{4,2},{5,3},{6,0},{7,1},{8,14},{9,15},{10,... | collective-permute-start | bytes 258056 | tf_op jit(solution)/shard_map/ppermute | solution.py:507
  50.2 1.6 %collective-permute-done.4 = bf16[84,512]{1,0:T(8,128)(2,1)S(1)} collective-permute-done((bf16[84,512]{1,0:T(8,128)(2,1)S(1)}, bf16[84,512]{1,0:T(8,128)(2,1)S(1)}, u32[]{:S(2)}, u32[]{:S(2)}) %collective-permute-start.4) | collective-permute-done | bytes 86048 | tf_op jit(solution)/shard_map/ppermute | solution.py:507
  51.8 1.9 %collective-permute-done.5 = bf16[84,512]{1,0:T(8,128)(2,1)S(1)} collective-permute-done((bf16[84,512]{1,0:T(8,128)(2,1)S(1)}, bf16[84,512]{1,0:T(8,128)(2,1)S(1)}, u32[]{:S(2)}, u32[]{:S(2)}) %collective-permute-start.5) | collective-permute-done | bytes 86048 | tf_op jit(solution)/shard_map/ppermute | solution.py:507
  54.0 0.6 collective-permute-start.7
  54.6 1.9 %collective-permute-start.3 = (bf16[80,512]{1,0:T(8,128)(2,1)S(1)}, bf16[80,512]{1,0:T(8,128)(2,1)S(1)}, u32[]{:S(2)}, u32[]{:S(2)}) collective-permute-start(bf16[80,512]{1,0:T(8,128)(2,1)S(1)} %get-tuple-element.71), channel_id=1, source_target_pairs={{0,6},{1,7},{2,4},{3,5},{4,2},{5,3},{6,0},{7,1},{8,14},{9,15},{10,... | collective-permute-start | bytes 245768 | tf_op jit(solution)/shard_map/ppermute | solution.py:507
  56.5 1.1 %collective-permute-start.2 = (bf16[80,512]{1,0:T(8,128)(2,1)S(1)}, bf16[80,512]{1,0:T(8,128)(2,1)S(1)}, u32[]{:S(2)}, u32[]{:S(2)}) collective-permute-start(bf16[80,512]{1,0:T(8,128)(2,1)S(1)} %get-tuple-element.72), channel_id=1, source_target_pairs={{0,4},{1,5},{2,6},{3,7},{4,0},{5,1},{6,2},{7,3},{8,12},{9,13},{10,... | collective-permute-start | bytes 245768 | tf_op jit(solution)/shard_map/ppermute | solution.py:507
  58.7 1.4 %collective-permute-done.3 = bf16[80,512]{1,0:T(8,128)(2,1)S(1)} collective-permute-done((bf16[80,512]{1,0:T(8,128)(2,1)S(1)}, bf16[80,512]{1,0:T(8,128)(2,1)S(1)}, u32[]{:S(2)}, u32[]{:S(2)}) %collective-permute-start.3) | collective-permute-done | bytes 81952 | tf_op jit(solution)/shard_map/ppermute | solution.py:507
  60.1 0.9 %collective-permute-done.2 = bf16[80,512]{1,0:T(8,128)(2,1)S(1)} collective-permute-done((bf16[80,512]{1,0:T(8,128)(2,1)S(1)}, bf16[80,512]{1,0:T(8,128)(2,1)S(1)}, u32[]{:S(2)}, u32[]{:S(2)}) %collective-permute-start.2) | collective-permute-done | bytes 81952 | tf_op jit(solution)/shard_map/ppermute | solution.py:507
  61.0 1.0 %collective-permute-done.1 = bf16[80,512]{1,0:T(8,128)(2,1)S(1)} collective-permute-done((bf16[80,512]{1,0:T(8,128)(2,1)S(1)}, bf16[80,512]{1,0:T(8,128)(2,1)S(1)}, u32[]{:S(2)}, u32[]{:S(2)}) %collective-permute-start.1) | collective-permute-done | bytes 81952 | tf_op jit(solution)/shard_map/ppermute | solution.py:507
  62.1 0.6 collective-permute-start.8
  62.7 6.0 %collective-permute-done.8 = bf16[92,512]{1,0:T(8,128)(2,1)S(1)} collective-permute-done((bf16[92,512]{1,0:T(8,128)(2,1)S(1)}, bf16[92,512]{1,0:T(8,128)(2,1)S(1)}, u32[]{:S(2)}, u32[]{:S(2)}) %collective-permute-start.8) | collective-permute-done | bytes 94240 | tf_op jit(solution)/shard_map/ppermute | solution.py:507
  69.5 3.9 %collective-permute-done.9 = bf16[88,512]{1,0:T(8,128)(2,1)S(1)} collective-permute-done((bf16[88,512]{1,0:T(8,128)(2,1)S(1)}, bf16[88,512]{1,0:T(8,128)(2,1)S(1)}, u32[]{:S(2)}, u32[]{:S(2)}) %collective-permute-start.9) | collective-permute-done | bytes 90144 | tf_op jit(solution)/shard_map/ppermute | solution.py:507
  73.5 0.8 collective-permute-start.14
  74.3 2.7 %collective-permute-start.16 = (bf16[176,512]{1,0:T(8,128)(2,1)S(1)}, bf16[176,512]{1,0:T(8,128)(2,1)S(1)}, u32[]{:S(2)}, u32[]{:S(2)}) collective-permute-start(bf16[176,512]{1,0:T(8,128)(2,1)S(1)} %concatenate.34.refs_0_), channel_id=1, source_target_pairs={{0,6},{1,7},{2,4},{3,5},{4,2},{5,3},{6,0},{7,1},{8,14},{9,15},{10,... | collective-permute-start | bytes 540680 | tf_op jit(solution)/shard_map/ppermute | solution.py:507
  77.0 2.9 %new_states.1 = (f32[1024,128]{1,0:T(8,128)}, f32[1024,128]{1,0:T(8,128)}) custom-call(bf16[32,72,128]{2,1,0:T(8,128)(2,1)S(1)} %all-to-all-done.got_ref, f32[32,128]{1,0:T(8,128)S(1)} %convert_add_fusion.res_ref, f32[1024,128]{1,0:T(8,128)S(1)} %copy-done.3, f32[1024,128]{1,0:T(8,128)S(1)} %copy-done.5), custom_call_target="tpu_custom_call" | custom-call | flops 1073741824 | bytes 4194304 | tf_op jit(solution)/shard_map/new_states/pallas_call | solution.py:430
  80.5 0.9 %collective-permute-done.14.refs_2_ = bf16[176,512]{1,0:T(8,128)(2,1)S(1)} collective-permute-done((bf16[176,512]{1,0:T(8,128)(2,1)S(1)}, bf16[176,512]{1,0:T(8,128)(2,1)S(1)}, u32[]{:S(2)}, u32[]{:S(2)}) %collective-permute-start.14) | collective-permute-done | bytes 180256 | tf_op jit(solution)/shard_map/ppermute | solution.py:507
  81.9 1.3 %place_own.1 = (f32[1024,512]{1,0:T(8,128)}, f32[512,256]{1,0:T(8,128)}, f32[2,512]{1,0:T(2,128)S(1)}) custom-call(bf16[176,512]{1,0:T(8,128)(2,1)S(1)} %concatenate.34.refs_0_, bf16[176,512]{1,0:T(8,128)(2,1)S(1)} %collective-permute-done.12.refs_1_, bf16[176,512]{1,0:T(8,128)(2,1)S(1)} %collective-permute-done.14.refs_2_, ...), custom_call_target="tpu_custom_call" | custom-call | flops 32768 | bytes 2621440 | tf_op jit(solution)/shard_map/place_own/pallas_call | solution.py:485
  83.2 1.9 %place_other.1 = (f32[1024,512]{1,0:T(8,128)}, f32[512,256]{1,0:T(8,128)}, f32[1,512]{1,0:T(1,128)}, f32[1,256]{1,0:T(1,128)}, f32[1,256]{1,0:T(1,128)}) custom-call(bf16[176,512]{1,0:T(8,128)(2,1)S(1)} %collective-permute-done.11.refs_0_, bf16[176,512]{1,0:T(8,128)(2,1)S(1)} %collective-permute-done.13.refs_1_, ...), custom_call_target="tpu_custom_call", output_to_operand_aliasing={{0}: (4, {}), {1}: (5, {})} | custom-call | flops 32768 | bytes 2621440 | tf_op jit(solution)/shard_map/place_other/pallas_call | solution.py:485
  (87 shorter events, 4.5 us)
Async XLA Ops:
  0.6 9.2 %copy-start.9 = (bf16[256]{0:T(256)(128)(2,1)S(1)}, bf16[256]{0:T(256)(128)(2,1)}, u32[]{:S(2)}) copy-start(bf16[256]{0:T(256)(128)(2,1)} %param.25) | copy-start | bytes 1540
  2.5 24.0 %all-to-all-start = ((bf16[32,72,128]{2,1,0:T(8,128)(2,1)}), bf16[32,72,128]{2,1,0:T(8,128)(2,1)S(1)}, u32[]{:S(2)}, u32[]{:S(2)}) async-start(bf16[32,72,128]{2,1,0:T(8,128)(2,1)} %pack.1), calls=%async_computation | async-start | bytes 1179648 | tf_op jit(solution)/shard_map/all_to_all | solution.py:503
  18.3 20.6 %copy-start = (bf16[512,1024]{1,0:T(8,128)(2,1)S(1)}, bf16[512,1024]{1,0:T(8,128)(2,1)}, u32[]{:S(2)}) copy-start(bf16[512,1024]{1,0:T(8,128)(2,1)} %get-tuple-element.47.q) | copy-start | bytes 3145732
  18.3 20.6 %copy-start.1 = (bf16[256,1024]{1,0:T(8,128)(2,1)S(1)}, bf16[256,1024]{1,0:T(8,128)(2,1)}, u32[]{:S(2)}) copy-start(bf16[256,1024]{1,0:T(8,128)(2,1)} %get-tuple-element.46.s2) | copy-start | bytes 1572868
  18.3 1.2 %copy-start.2 = (f32[1024,128]{1,0:T(8,128)S(1)}, f32[1024,128]{1,0:T(8,128)}, u32[]{:S(2)}) copy-start(f32[1024,128]{1,0:T(8,128)} %z_ref.2) | copy-start | bytes 1572868
  19.4 1.0 %copy-start.4 = (f32[1024,128]{1,0:T(8,128)S(1)}, f32[1024,128]{1,0:T(8,128)}, u32[]{:S(2)}) copy-start(f32[1024,128]{1,0:T(8,128)} %n_ref.2) | copy-start | bytes 1572868
  20.5 11.5 %copy-start.6 = (s32[32,64]{1,0:T(8,128)S(1)}, s32[32,64]{1,0:T(8,128)}, u32[]{:S(2)}) copy-start(s32[32,64]{1,0:T(8,128)} %example_ref.2) | copy-start | bytes 24580
  20.5 18.4 %copy-start.7 = (s32[1024]{0:T(1024)S(1)}, s32[1024]{0:T(1024)}, u32[]{:S(2)}) copy-start(s32[1024]{0:T(1024)} %param.14) | copy-start | bytes 12292
  20.5 18.4 %copy-start.8 = (f32[1,1024]{1,0:T(1,128)S(1)}, f32[1,1024]{1,0:T(1,128)}, u32[]{:S(2)}) copy-start(f32[1,1024]{1,0:T(1,128)} %get-tuple-element.44.deep_ref) | copy-start | bytes 12292
  28.5 10.4 %all-to-all-start.1 = ((f32[32,1,128]{2,1,0:T(1,128)}), f32[32,1,128]{2,1,0:T(1,128)S(1)}, u32[]{:S(2)}, u32[]{:S(2)}) async-start(f32[32,1,128]{2,1,0:T(1,128)} %slot_logits.1), calls=%async_computation.1 | async-start | bytes 32768 | tf_op jit(solution)/shard_map/all_to_all | solution.py:503
  42.8 3.4 %collective-permute-start = (bf16[640,512]{1,0:T(8,128)(2,1)}, bf16[640,512]{1,0:T(8,128)(2,1)S(1)}, u32[]{:S(2)}, u32[]{:S(2)}) collective-permute-start(bf16[640,512]{1,0:T(8,128)(2,1)} %get-tuple-element.52), channel_id=1, source_target_pairs={{0,1},{1,0},{2,3},{3,2},{4,5},{5,4},{6,7},{7,6},{8,9},{9,8},{10,11... | collective-permute-start | bytes 1966088 | tf_op jit(solution)/shard_map/ppermute | solution.py:507
  46.4 30.6 %copy-start.3 = (f32[1024,128]{1,0:T(8,128)S(1)}, f32[1024,128]{1,0:T(8,128)}, u32[]{:S(2)}) copy-start(f32[1024,128]{1,0:T(8,128)} %z_ref.2) | copy-start | bytes 1572868
  46.4 30.6 %copy-start.5 = (f32[1024,128]{1,0:T(8,128)S(1)}, f32[1024,128]{1,0:T(8,128)}, u32[]{:S(2)}) copy-start(f32[1024,128]{1,0:T(8,128)} %n_ref.2) | copy-start | bytes 1572868
  46.5 5.3 %collective-permute-start.4 = (bf16[84,512]{1,0:T(8,128)(2,1)S(1)}, bf16[84,512]{1,0:T(8,128)(2,1)S(1)}, u32[]{:S(2)}, u32[]{:S(2)}) collective-permute-start(bf16[84,512]{1,0:T(8,128)(2,1)S(1)} %pad_maximum_fusion.1), channel_id=1, source_target_pairs={{0,2},{1,3},{2,0},{3,1},{4,6},{5,7},{6,4},{7,5},{8,10},{9,11},{10,... | collective-permute-start | bytes 258056 | tf_op jit(solution)/shard_map/ppermute | solution.py:507
  47.1 6.6 %collective-permute-start.5 = (bf16[84,512]{1,0:T(8,128)(2,1)S(1)}, bf16[84,512]{1,0:T(8,128)(2,1)S(1)}, u32[]{:S(2)}, u32[]{:S(2)}) collective-permute-start(bf16[84,512]{1,0:T(8,128)(2,1)S(1)} %pad_maximum_fusion.2), channel_id=1, source_target_pairs={{0,4},{1,5},{2,6},{3,7},{4,0},{5,1},{6,2},{7,3},{8,12},{9,13},{10,... | collective-permute-start | bytes 258056 | tf_op jit(solution)/shard_map/ppermute | solution.py:507
  47.8 5.9 %collective-permute-start.6 = (bf16[84,512]{1,0:T(8,128)(2,1)S(1)}, bf16[84,512]{1,0:T(8,128)(2,1)S(1)}, u32[]{:S(2)}, u32[]{:S(2)}) collective-permute-start(bf16[84,512]{1,0:T(8,128)(2,1)S(1)} %pad_maximum_fusion.3), channel_id=1, source_target_pairs={{0,6},{1,7},{2,4},{3,5},{4,2},{5,3},{6,0},{7,1},{8,14},{9,15},{10,... | collective-permute-start | bytes 258056 | tf_op jit(solution)/shard_map/ppermute | solution.py:507
  54.0 4.6 %collective-permute-start.7 = (bf16[88,512]{1,0:T(8,128)(2,1)S(1)}, bf16[88,512]{1,0:T(8,128)(2,1)S(1)}, u32[]{:S(2)}, u32[]{:S(2)}) collective-permute-start(bf16[88,512]{1,0:T(8,128)(2,1)S(1)} %pad_maximum_fusion.4), channel_id=1, source_target_pairs={{0,8},{1,9},{2,10},{3,11},{4,12},{5,13},{6,14},{7,15},{8,0},{9,1},... | collective-permute-start | bytes 270344 | tf_op jit(solution)/shard_map/ppermute | solution.py:507
  54.6 5.5 %collective-permute-start.3 = (bf16[80,512]{1,0:T(8,128)(2,1)S(1)}, bf16[80,512]{1,0:T(8,128)(2,1)S(1)}, u32[]{:S(2)}, u32[]{:S(2)}) collective-permute-start(bf16[80,512]{1,0:T(8,128)(2,1)S(1)} %get-tuple-element.71), channel_id=1, source_target_pairs={{0,6},{1,7},{2,4},{3,5},{4,2},{5,3},{6,0},{7,1},{8,14},{9,15},{10,... | collective-permute-start | bytes 245768 | tf_op jit(solution)/shard_map/ppermute | solution.py:507
  56.5 4.5 %collective-permute-start.2 = (bf16[80,512]{1,0:T(8,128)(2,1)S(1)}, bf16[80,512]{1,0:T(8,128)(2,1)S(1)}, u32[]{:S(2)}, u32[]{:S(2)}) collective-permute-start(bf16[80,512]{1,0:T(8,128)(2,1)S(1)} %get-tuple-element.72), channel_id=1, source_target_pairs={{0,4},{1,5},{2,6},{3,7},{4,0},{5,1},{6,2},{7,3},{8,12},{9,13},{10,... | collective-permute-start | bytes 245768 | tf_op jit(solution)/shard_map/ppermute | solution.py:507
  57.6 4.4 %collective-permute-start.1 = (bf16[80,512]{1,0:T(8,128)(2,1)S(1)}, bf16[80,512]{1,0:T(8,128)(2,1)S(1)}, u32[]{:S(2)}, u32[]{:S(2)}) collective-permute-start(bf16[80,512]{1,0:T(8,128)(2,1)S(1)} %get-tuple-element.73), channel_id=1, source_target_pairs={{0,2},{1,3},{2,0},{3,1},{4,6},{5,7},{6,4},{7,5},{8,10},{9,11},{10,... | collective-permute-start | bytes 245768 | tf_op jit(solution)/shard_map/ppermute | solution.py:507
  62.1 6.6 %collective-permute-start.8 = (bf16[92,512]{1,0:T(8,128)(2,1)S(1)}, bf16[92,512]{1,0:T(8,128)(2,1)S(1)}, u32[]{:S(2)}, u32[]{:S(2)}) collective-permute-start(bf16[92,512]{1,0:T(8,128)(2,1)S(1)} %pad_maximum_fusion), channel_id=1, source_target_pairs={{0,16},{1,17},{2,18},{3,19},{4,20},{5,21},{6,22},{7,23},{8,24},{9,... | collective-permute-start | bytes 282632 | tf_op jit(solution)/shard_map/ppermute | solution.py:507
  68.8 4.6 %collective-permute-start.9 = (bf16[88,512]{1,0:T(8,128)(2,1)S(1)}, bf16[88,512]{1,0:T(8,128)(2,1)S(1)}, u32[]{:S(2)}, u32[]{:S(2)}) collective-permute-start(bf16[88,512]{1,0:T(8,128)(2,1)S(1)} %pad_maximum_fusion.5), channel_id=1, source_target_pairs={{0,8},{1,9},{2,10},{3,11},{4,12},{5,13},{6,14},{7,15},{8,0},{9,1},... | collective-permute-start | bytes 270344 | tf_op jit(solution)/shard_map/ppermute | solution.py:507
  69.4 7.6 %collective-permute-start.10 = (bf16[16,256]{1,0:T(8,128)(2,1)S(1)}, bf16[16,256]{1,0:T(8,128)(2,1)S(1)}, u32[]{:S(2)}, u32[]{:S(2)}) collective-permute-start(bf16[16,256]{1,0:T(8,128)(2,1)S(1)} %bitcast.36), channel_id=1, source_target_pairs={{0,1},{1,0},{2,3},{3,2},{4,5},{5,4},{6,7},{7,6},{8,9},{9,8},{10,11... | collective-permute-start | bytes 24584 | tf_op jit(solution)/shard_map/ppermute | solution.py:507
  73.4 6.5 %collective-permute-start.12 = (bf16[176,512]{1,0:T(8,128)(2,1)S(1)}, bf16[176,512]{1,0:T(8,128)(2,1)S(1)}, u32[]{:S(2)}, u32[]{:S(2)}) collective-permute-start(bf16[176,512]{1,0:T(8,128)(2,1)S(1)} %concatenate.34.refs_0_), channel_id=1, source_target_pairs={{0,2},{1,3},{2,0},{3,1},{4,6},{5,7},{6,4},{7,5},{8,10},{9,11},{10,... | collective-permute-start | bytes 540680 | tf_op jit(solution)/shard_map/ppermute | solution.py:507
  73.5 7.9 %collective-permute-start.14 = (bf16[176,512]{1,0:T(8,128)(2,1)S(1)}, bf16[176,512]{1,0:T(8,128)(2,1)S(1)}, u32[]{:S(2)}, u32[]{:S(2)}) collective-permute-start(bf16[176,512]{1,0:T(8,128)(2,1)S(1)} %concatenate.34.refs_0_), channel_id=1, source_target_pairs={{0,4},{1,5},{2,6},{3,7},{4,0},{5,1},{6,2},{7,3},{8,12},{9,13},{10,... | collective-permute-start | bytes 540680 | tf_op jit(solution)/shard_map/ppermute | solution.py:507
  74.3 7.1 %collective-permute-start.16 = (bf16[176,512]{1,0:T(8,128)(2,1)S(1)}, bf16[176,512]{1,0:T(8,128)(2,1)S(1)}, u32[]{:S(2)}, u32[]{:S(2)}) collective-permute-start(bf16[176,512]{1,0:T(8,128)(2,1)S(1)} %concatenate.34.refs_0_), channel_id=1, source_target_pairs={{0,6},{1,7},{2,4},{3,5},{4,2},{5,3},{6,0},{7,1},{8,14},{9,15},{10,... | collective-permute-start | bytes 540680 | tf_op jit(solution)/shard_map/ppermute | solution.py:507
  80.0 3.2 %collective-permute-start.11 = (bf16[176,512]{1,0:T(8,128)(2,1)S(1)}, bf16[176,512]{1,0:T(8,128)(2,1)S(1)}, u32[]{:S(2)}, u32[]{:S(2)}) collective-permute-start(bf16[176,512]{1,0:T(8,128)(2,1)S(1)} %concatenate.34.refs_0_), channel_id=1, source_target_pairs={{0,1},{1,0},{2,3},{3,2},{4,5},{5,4},{6,7},{7,6},{8,9},{9,8},{10,11... | collective-permute-start | bytes 540680 | tf_op jit(solution)/shard_map/ppermute | solution.py:507
  80.0 3.2 %collective-permute-start.13 = (bf16[176,512]{1,0:T(8,128)(2,1)S(1)}, bf16[176,512]{1,0:T(8,128)(2,1)S(1)}, u32[]{:S(2)}, u32[]{:S(2)}) collective-permute-start(bf16[176,512]{1,0:T(8,128)(2,1)S(1)} %collective-permute-done.12.refs_1_), channel_id=1, source_target_pairs={{0,1},{1,0},{2,3},{3,2},{4,5},{5,4},{6,7},{7,6},{8,9},{9,8},{10,11... | collective-permute-start | bytes 540680 | tf_op jit(solution)/shard_map/ppermute | solution.py:507
  81.4 1.8 %collective-permute-start.15 = (bf16[176,512]{1,0:T(8,128)(2,1)S(1)}, bf16[176,512]{1,0:T(8,128)(2,1)S(1)}, u32[]{:S(2)}, u32[]{:S(2)}) collective-permute-start(bf16[176,512]{1,0:T(8,128)(2,1)S(1)} %collective-permute-done.14.refs_2_), channel_id=1, source_target_pairs={{0,1},{1,0},{2,3},{3,2},{4,5},{5,4},{6,7},{7,6},{8,9},{9,8},{10,11... | collective-permute-start | bytes 540680 | tf_op jit(solution)/shard_map/ppermute | solution.py:507
  81.4 1.8 %collective-permute-start.17 = (bf16[176,512]{1,0:T(8,128)(2,1)S(1)}, bf16[176,512]{1,0:T(8,128)(2,1)S(1)}, u32[]{:S(2)}, u32[]{:S(2)}) collective-permute-start(bf16[176,512]{1,0:T(8,128)(2,1)S(1)} %collective-permute-done.16.refs_3_), channel_id=1, source_target_pairs={{0,1},{1,0},{2,3},{3,2},{4,5},{5,4},{6,7},{7,6},{8,9},{9,8},{10,11... | collective-permute-start | bytes 540680 | tf_op jit(solution)/shard_map/ppermute | solution.py:507

commit v5 on v4

--- a/solution.py
+++ b/solution.py
@@ -15,6 +15,7 @@
 LANES = 128
 EIGHTHS = 8
 ONES = 16
+PIECES = 2
 f32 = jnp.float32
 bf16 = jnp.bfloat16
 NT = (((1,), (1,)), ((), ()))
@@ -117,7 +118,7 @@
 
 def tower_kernel(
     dense_ref, w1_ref, b1_ref, w2_ref, b2_ref, head_ref,
-    big_ref, s2_ref, q_ref, deep_ref,
+    big_ref, h2_ref, s2_ref, q_ref, deep_ref,
     w1t, w2t,
 ):
     @pl.when(pl.program_id(0) == 0)
@@ -132,11 +133,12 @@
     gate1 = jax.nn.sigmoid(pre1)
     h1 = (pre1 * gate1).astype(bf16)
     big_ref[din : din + n1, :] = h1
+    big_ref[din + n1 :, :] = jnp.zeros((n2, big_ref.shape[1]), bf16)
     slope1 = gate1 * (1.0 + pre1 * (1.0 - gate1))
     pre2 = dot(w2t[...], h1) + to_column(b2_ref[...])
     gate2 = jax.nn.sigmoid(pre2)
     h2 = (pre2 * gate2).astype(bf16)
-    big_ref[din + n1 : din + n1 + n2, :] = h2
+    h2_ref[...] = h2
     head = head_ref[...]
     deep_ref[...] = dot(jnp.broadcast_to(head, (16, head.shape[1])), h2)[0:1]
     s2 = to_column(head.astype(f32)) * (gate2 * (1.0 + pre2 * (1.0 - gate2)))
@@ -159,6 +161,7 @@
         out_shape=(
             jax.ShapeDtypeStruct((din + h1 + h2, ex), bf16),
             jax.ShapeDtypeStruct((h2, ex), bf16),
+            jax.ShapeDtypeStruct((h2, ex), bf16),
             jax.ShapeDtypeStruct((h1, ex), bf16),
             jax.ShapeDtypeStruct((1, ex), f32),
         ),
@@ -166,7 +169,7 @@
             pl.BlockSpec((be, din), lambda i: (i, 0)),
             whole(w1), whole(b1), whole(w2), whole(b2), whole(head),
         ],
-        out_specs=(cols(din + h1 + h2), cols(h2), cols(h1), cols(1)),
+        out_specs=(cols(din + h1 + h2), cols(h2), cols(h2), cols(h1), cols(1)),
         scratch_shapes=[pltpu.VMEM((h1, din), bf16), pltpu.VMEM((h2, h1), bf16)],
         compiler_params=params(62),
         cost_estimate=pl.CostEstimate(
@@ -227,26 +230,25 @@
     )(got, wcat)
 
 
-def doubled(example_ref):
-    example = jnp.concatenate([example_ref[...], example_ref[...]], axis=1)
-    return example >> 7, example & (LANES - 1)
-
-
-def mark(low, marks):
+def paired(example_ref):
+    lists = example_ref.shape[0]
+    example = [
+        jnp.concatenate([example_ref[k : k + 1], example_ref[k + 1 : k + 2]], axis=1) for k in range(0, lists, 2)
+    ]
+    return [e >> 7 for e in example], [e & (LANES - 1) for e in example]
+
+
+def marks_kernel(example_ref, marks_ref):
     down = iota((LANES, LANES), 0)
-    for k in range(low.shape[0]):
-        marks[:, k * LANES : (k + 1) * LANES] = jnp.where(low[k : k + 1] == down, 1.0, 0.0).astype(bf16)
-
-
-def marks_kernel(example_ref, marks_ref):
-    mark(doubled(example_ref)[1], marks_ref)
+    for k, low in enumerate(paired(example_ref)[1]):
+        marks_ref[:, k * LANES : (k + 1) * LANES] = jnp.where(low == down, 1.0, 0.0).astype(bf16)
 
 
 def example_marks(example):
-    lists = example.shape[0]
+    lists, cap = example.shape
     return pl.pallas_call(
         marks_kernel,
-        out_shape=jax.ShapeDtypeStruct((LANES, lists * LANES), bf16),
+        out_shape=jax.ShapeDtypeStruct((LANES, lists * cap), bf16),
         in_specs=[VM],
         out_specs=VM,
         compiler_params=params(8),
@@ -258,13 +260,14 @@
 def half_copies(half, big_any, dense_t, h1, sems):
     n1 = 2 * (h1.shape[0] - ONES)
     each, packed = dense_t.shape[0] - ONES, n1 // 4
-    span = pl.ds(pl.multiple_of(half * each, each), each)
-    copies = [pltpu.make_async_copy(big_any.at[span], dense_t.at[pl.ds(0, each)], sems.at[0])]
+    copies = []
     for side in range(2):
         span = pl.ds(pl.multiple_of(2 * each + half * packed + side * 2 * packed, packed), packed)
-        copies.append(
-            pltpu.make_async_copy(big_any.at[span], h1.at[pl.ds(side * packed, packed)], sems.at[1 + side])
-        )
+        copies.append(pltpu.make_async_copy(big_any.at[span], h1.at[pl.ds(side * packed, packed)], sems.at[side]))
+    rows = each // PIECES
+    for k in range(PIECES):
+        span = pl.ds(pl.multiple_of(half * each + k * rows, rows), rows)
+        copies.append(pltpu.make_async_copy(big_any.at[span], dense_t.at[pl.ds(k * rows, rows)], sems.at[2 + k]))
     return copies
 
 
@@ -277,8 +280,9 @@
     dlogit = jnp.concatenate([residual[k : k + 1] for k in range(rows)], axis=1).astype(bf16)
     scale = dlogit.astype(f32)
     d_two = (s2[...].astype(f32) * scale).astype(bf16)
+    d_one = (q[...].astype(f32) * scale).astype(bf16)
+    copies[0].wait()
     copies[1].wait()
-    copies[2].wait()
     second = dot(h1[...], d_two, NT)
     b_two = second[2 * EIGHTHS * packed : 2 * EIGHTHS * packed + 1]
     second = second.astype(bf16)
@@ -286,8 +290,8 @@
         at, low = k * packed, (k + EIGHTHS) * packed
         target[k * each + first : (k + 1) * each, 0:width] = second[at : at + packed]
         target[k * each + first : (k + 1) * each, width:] = second[low : low + packed]
-    d_one = (q[...].astype(f32) * scale).astype(bf16)
-    copies[0].wait()
+    for copy in copies[2:]:
+        copy.wait()
     made = dot(dense_t[...], d_one, NT)
     b_one = made[EIGHTHS * first : EIGHTHS * first + 1]
     made = made.astype(bf16)
@@ -301,7 +305,7 @@
     return [
         pltpu.VMEM((half + ONES, big.shape[1]), bf16),
         pltpu.VMEM((n1 // 2 + ONES, big.shape[1]), bf16),
-        pltpu.SemaphoreType.DMA((4,)),
+        pltpu.SemaphoreType.DMA((4 + PIECES,)),
     ]
 
 
@@ -318,18 +322,20 @@
     rows = label_ref.shape[0]
     me = position()
     core = me & 1
-    first = pltpu.make_async_copy(logit_any, logit_ref, sems.at[3])
+    first = pltpu.make_async_copy(logit_any, logit_ref, sems.at[2 + PIECES])
     first.start()
     copies = half_copies(1 - core, big_any, dense_t, h1, sems)
     for copy in copies:
         copy.start()
-    high = doubled(example_ref)[0]
-    mine = (iota((lists, LANES), 1) >= cap) == (core == 1)
-    high_mine = jnp.where(mine, high, -1)
+    high = paired(example_ref)[0]
+    left = iota((1, LANES), 1) < cap
     down = iota((rows, LANES), 0)
+    turned = lambda v: pltpu.roll(v, cap, 1)
     first.wait()
-    for k in range(lists):
-        part = jnp.where(high_mine[k : k + 1] == down, logit_ref[k], 0.0)
+    for k in range(lists // 2):
+        even, odd = logit_ref[2 * k], logit_ref[2 * k + 1]
+        pair = jnp.where(core == 0, jnp.where(left, even, turned(odd)), jnp.where(left, turned(even), odd))
+        part = jnp.where(high[k] == down, pair, 0.0)
         spread[:, k * LANES : (k + 1) * LANES] = jnp.concatenate(split_two(part), axis=0)
     wide = dot(spread[...], marks[...], NT)
     wide = wide[0:rows] + wide[rows:]
@@ -338,18 +344,21 @@
     prob_ref[...] = prob
     residual = prob - label_ref[...].astype(f32)
     residual_ref[...] = residual
-    half_gradients(residual, copies, s2, q, dense_t, h1, send_ref)
     found = dot(jnp.concatenate(split_two(residual), axis=0), marks[...])
     found = found[0:rows] + found[rows:]
-    for k in range(lists):
-        part = jnp.where(high[k : k + 1] == down, found[:, k * LANES : (k + 1) * LANES], 0.0)
-        top, rest = split_two(jnp.sum(part, axis=0, keepdims=True))
-        apart[me ^ k] = jnp.concatenate([top.astype(f32), rest.astype(f32)], axis=0)
+    for k in range(lists // 2):
+        part = jnp.where(high[k] == down, found[:, k * LANES : (k + 1) * LANES], 0.0)
+        both = jnp.sum(part, axis=0, keepdims=True)
+        swapped = turned(both)
+        for c, one in enumerate((jnp.where(left, both, swapped), jnp.where(left, swapped, both))):
+            top, rest = split_two(one)
+            apart[me ^ (2 * k + c)] = jnp.concatenate([top.astype(f32), rest.astype(f32)], axis=0)
     lines = [
         jnp.concatenate([apart[k + c, s : s + 1, :] for c in range(2) for s in range(2)], axis=1)
         for k in range(0, lists, 2)
     ]
     slot_ref[...] = jnp.concatenate(lines, axis=0).astype(bf16)
+    half_gradients(residual, copies, s2, q, dense_t, h1, send_ref)
 
 
 def residuals(logits, example, deep, labels, marks, s2, q, big):
@@ -367,24 +376,20 @@
         ),
         in_specs=[ANY] + [VM] * 6 + [HBM],
         out_specs=[VM, VM, VM, VM],
-        scratch_shapes=[pltpu.VMEM((2 * rows, lists * LANES), bf16), pltpu.VMEM(logits.shape, f32), pltpu.VMEM((lists, 2, LANES), f32)]
+        scratch_shapes=[pltpu.VMEM((2 * rows, marks.shape[1]), bf16), pltpu.VMEM(logits.shape, f32), pltpu.VMEM((lists, 2, LANES), f32)]
         + half_scratch(big, n1),
         compiler_params=params(49),
         name="residuals",
     )(logits, example, deep, labels.reshape(rows, LANES), marks, s2, q, big)
 
 
-def gradient_kernel(residual_ref, s2, q, big_any, keep_ref, small_ref, h2, dense_t, h1, sems):
+def gradient_kernel(residual_ref, s2, q, big_any, keep_ref, small_ref, dense_t, h1, sems):
     core = lax.axis_index("rep") & 1
-    span = pl.ds(big_any.shape[0] - h2.shape[0], h2.shape[0])
-    copies = [pltpu.make_async_copy(big_any.at[span], h2, sems.at[3])]
-    copies = half_copies(core, big_any, dense_t, h1, sems) + copies
+    copies = half_copies(core, big_any, dense_t, h1, sems)
     for copy in copies:
         copy.start()
-    dlogit, b_one, b_two = half_gradients(residual_ref[...], copies, s2, q, dense_t, h1, keep_ref)
-    copies[3].wait()
-    head = dot(jnp.broadcast_to(dlogit, (ONES, dlogit.shape[1])), h2[...], NT)[0:1]
-    small = jnp.concatenate([b_one, jnp.concatenate([b_two, head], axis=1)], axis=0)
+    _, b_one, b_two = half_gradients(residual_ref[...], copies, s2, q, dense_t, h1, keep_ref)
+    small = jnp.concatenate([b_one, jnp.concatenate([b_two, jnp.zeros_like(b_two)], axis=1)], axis=0)
     small_ref[...] = jnp.concatenate(split_two(small), axis=0)
 
 
@@ -396,11 +401,32 @@
         out_shape=(jax.ShapeDtypeStruct((half, n1), bf16), jax.ShapeDtypeStruct((4, n1), bf16)),
         in_specs=[VM] * 3 + [HBM],
         out_specs=[VM, VM],
-        scratch_shapes=[pltpu.VMEM(s2.shape, bf16)] + half_scratch(big, n1),
+        scratch_shapes=half_scratch(big, n1),
         compiler_params=params(49),
         cost_estimate=pl.CostEstimate(flops=2 * half * n1 * ex, bytes_accessed=6 << 20, transcendentals=0),
         name="gradients",
     )(residual, s2, q, big)
+
+
+def head_kernel(residual_ref, small, h2, out_ref):
+    residual = residual_ref[...]
+    dlogit = jnp.concatenate([residual[k : k + 1] for k in range(residual.shape[0])], axis=1).astype(bf16)
+    head = dot(jnp.broadcast_to(dlogit, (ONES, dlogit.shape[1])), h2[...], NT)[0:1]
+    top, rest = split_two(jnp.concatenate([jnp.zeros_like(head), head], axis=1))
+    zero = jnp.zeros_like(top)
+    out_ref[...] = small[...] + jnp.concatenate([zero, top, zero, rest], axis=0)
+
+
+def head_gradient(residual, small, h2):
+    return pl.pallas_call(
+        head_kernel,
+        out_shape=jax.ShapeDtypeStruct(small.shape, bf16),
+        in_specs=[VM] * 3,
+        out_specs=VM,
+        compiler_params=params(8),
+        cost_estimate=pl.CostEstimate(flops=32 * h2.size, bytes_accessed=2 << 20, transcendentals=0),
+        name="head_gradient",
+    )(residual, small, h2)
 
 
 def state_kernel(got_ref, res_ref, z_ref, n_ref, z_out, n_out):
@@ -440,35 +466,35 @@
     )(got, res, z, n)
 
 
-def place_kernel(swapped, *refs):
-    parts, refs = refs[:4], refs[4:]
-    before, refs = (refs[:3], refs[3:]) if swapped else (None, refs)
+def place_kernel(items, follows, *refs):
+    parts, refs = refs[: len(items)], refs[len(items) :]
+    before, refs = (refs[:3], refs[3:]) if follows else (None, refs)
     w1_any, w2_any, *outs = refs[:-3]
     wide, narrow, sems = refs[-3:]
     me = position()
-    half, quad = (me & 1) ^ swapped, (me >> 1) & 3
-    first, packed = wide.shape[0] // EIGHTHS, narrow.shape[1] // EIGHTHS
+    quad = (me >> 1) & 3
+    first, packed = wide.shape[1] // 2, narrow.shape[2] // 2
     each, width = first + packed, parts[0].shape[1]
-    copies, total = [], before[2][...] if swapped else 0.0
-    for k, part in enumerate(parts):
+    copies, total = [], before[2][...] if follows else 0.0
+    for k, ((apart, swapped), part) in enumerate(zip(items, parts)):
+        quarter = ((me & 1) ^ swapped) * 4 + (quad ^ apart)
         for t in range(2):
-            at, slot = t * each, 2 * k + t
-            place = (half * 4 + (quad ^ k)) * 2 + t
-            span = pl.ds(slot * first, first)
-            wide[span, :] = part[at : at + first, :].astype(f32)
-            target = w1_any.at[pl.ds(pl.multiple_of(place * first, first), first)]
-            copies.append(pltpu.make_async_copy(wide.at[span], target, sems.at[3 * slot]))
-            copies[-1].start()
+            at = t * each
+            wide[k, t * first : (t + 1) * first, :] = part[at : at + first, :].astype(f32)
             for c in range(2):
-                span = pl.ds(slot * packed, packed)
                 lanes = slice(c * (width // 2), (c + 1) * (width // 2))
-                narrow[c, span, :] = part[at + first : at + each, lanes].astype(f32)
-                target = w2_any.at[pl.ds(pl.multiple_of((c * 2 * EIGHTHS + place) * packed, packed), packed)]
-                copies.append(pltpu.make_async_copy(narrow.at[c, span], target, sems.at[3 * slot + 1 + c]))
-                copies[-1].start()
+                narrow[k, c, t * packed : (t + 1) * packed, :] = part[at + first : at + each, lanes].astype(f32)
+        start = pl.multiple_of(quarter * 2 * first, 2 * first)
+        copies.append(pltpu.make_async_copy(wide.at[k], w1_any.at[pl.ds(start, 2 * first)], sems.at[3 * k]))
+        for c in range(2):
+            start = pl.multiple_of((c * EIGHTHS + quarter) * 2 * packed, 2 * packed)
+            target = w2_any.at[pl.ds(start, 2 * packed)]
+            copies.append(pltpu.make_async_copy(narrow.at[k, c], target, sems.at[3 * k + 1 + c]))
+        for copy in copies[-3:]:
+            copy.start()
         extra = part[2 * each :, :].astype(f32)
         total = total + sum(extra[r : r + 2] for r in range(0, extra.shape[0], 2))
-    if swapped:
+    if len(outs) > 1:
         outs[0][...] = total[0:1]
         outs[1][...] = total[1:2, 0 : width // 2]
         outs[2][...] = total[1:2, width // 2 :]
@@ -478,24 +504,26 @@
         copy.wait()
 
 
-def place(swapped, parts, first, packed, before=()):
-    width = parts[0].shape[1]
+def place(items, parts, first, packed, before=(), final=False):
+    width, count = parts[0].shape[1], len(items)
     shapes = [(2 * EIGHTHS * first, width), (4 * EIGHTHS * packed, width // 2)]
-    tail = [(1, width), (1, width // 2), (1, width // 2)] if swapped else [(2, width)]
-    return pl.pallas_call(
-        functools.partial(place_kernel, swapped),
+    tail = [(1, width), (1, width // 2), (1, width // 2)] if final else [(2, width)]
+    return pl.pallas_call(
+        functools.partial(place_kernel, items, bool(before)),
         out_shape=[jax.ShapeDtypeStruct(t, f32) for t in shapes + tail],
-        in_specs=[VM] * 4 + [ANY, ANY, VM] * swapped,
+        in_specs=[VM] * count + ([ANY, ANY, VM] if before else []),
         out_specs=[ANY, ANY] + [VM] * len(tail),
-        input_output_aliases={4: 0, 5: 1} if swapped else {},
+        input_output_aliases={count: 0, count + 1: 1} if before else {},
         scratch_shapes=[
-            pltpu.VMEM((EIGHTHS * first, width), f32),
-            pltpu.VMEM((2, EIGHTHS * packed, width // 2), f32),
-            pltpu.SemaphoreType.DMA((3 * EIGHTHS,)),
+            pltpu.VMEM((count, 2 * first, width), f32),
+            pltpu.VMEM((count, 2, 2 * packed, width // 2), f32),
+            pltpu.SemaphoreType.DMA((3 * count,)),
         ],
         compiler_params=params(16),
-        cost_estimate=pl.CostEstimate(flops=first * width, bytes_accessed=80 * first * width, transcendentals=0),
-        name="place_other" if swapped else "place_own",
+        cost_estimate=pl.CostEstimate(
+            flops=count * first * width, bytes_accessed=16 * count * first * width, transcendentals=0
+        ),
+        name="place",
     )(*parts, *before)
 
 
@@ -596,7 +624,7 @@
     din = dense.shape[1]
     me = lax.axis_index(AXES)
     got = every_to_every(pack(tile_values, tile_block, tile_count))
-    big, s2, q, deep = tower(dense, w_one, b_one, w_two, b_two, head)
+    big, h2, s2, q, deep = tower(dense, w_one, b_one, w_two, b_two, head)
     deep, z_then, n_then = hold(deep, z_state, n_state)
     wcat = weights(z_then, n_then)
     got, deep = hold(got, deep)
@@ -608,14 +636,19 @@
     keep, small = gradients(residual, s2, q, big)
     own = add(keep, swap(send, 1, devices))
 
+    own, small, seen = hold(own, small, residual)
+    small = head_gradient(seen, small, h2)
+
     def states(res):
         return new_states(got, res, z_state, n_state)
 
     parts, (z_new, n_new) = sum_everywhere(own, slots, small, me, devices, states)
     first, packed = din // 2 // EIGHTHS, n1 // 4 // EIGHTHS
     others = [swap(part, 1, devices) for part in parts]
-    placed = place(0, parts, first, packed)
-    grad_w_one, grad_w_two, grad_b_one, grad_b_two, grad_head = place(1, others, first, packed, placed)
+    placed = place([(k, 0) for k in range(4)], parts, first, packed)
+    grad_w_one, grad_w_two, grad_b_one, grad_b_two, grad_head = place(
+        [(k, 1) for k in range(4)], others, first, packed, placed, True
+    )
     return (
         prob.reshape(-1),
         z_new,

time: 85.6 us -> 84.2 us (0.984)
  Pallas kernels: 25.5 us -> 24.4 us
    pallas_call x2 -> x3, Pallas kernels: 3.11 us -> 3.16 us  [the longest x2 2.9 us: place(): pl.pallas_call(functools.partial(place_kernel, items, bool(before)), out_...]
    unnamed x28 -> x30, local copies, waits for them, and re-layouts: 2.29 us -> 2.29 us
  transfers between devices with their start and end apart: 20 -> 20, of which waited for: 11 -> 11; matrix products, arithmetic and copies ran while one was open for 1% -> 1% of each run, Pallas kernels for 19% -> 18%
where the time goes in v5:
time: 84.2 us; the launch traced here: 83.8 us
  waiting for transfers between devices  30.2 us (36%)
  Pallas kernels  24.4 us (29%)
  starting transfers between devices  24.3 us (29%)
  local copies, waits for them, and re-layouts  3.24 us (4%)
  between operations  1.18 us (1%)
    ppermute x18, waiting for transfers between devices, swap(): return lax.ppermute(x, AXES, [(i, i ^ bit) for i in range(devices)])  17.8 us
    ppermute x18, starting transfers between devices, swap(): return lax.ppermute(x, AXES, [(i, i ^ bit) for i in range(devices)])  13.7 us
    all_to_all x2, waiting for transfers between devices, every_to_every(): return lax.all_to_all(x, AXES, split_axis=0, concat_axis=0, tiled=True)  12.4 us
    all_to_all x2, starting transfers between devices, every_to_every(): return lax.all_to_all(x, AXES, split_axis=0, concat_axis=0, tiled=True)  10.6 us
    pallas_call x1, Pallas kernels, tower(): pl.pallas_call(tower_kernel, grid=(steps,), out_shape=(jax.ShapeDtypeStru...  7.88 us
    pallas_call x1, Pallas kernels, residuals(): pl.pallas_call(residual_kernel, out_shape=(jax.ShapeDtypeStruct((rows, LA...  3.44 us
    pallas_call x1, Pallas kernels, new_states(): pl.pallas_call(state_kernel, out_shape=(jax.ShapeDtypeStruct(z.shape, f32...  2.94 us
    pallas_call x2, Pallas kernels, place(): pl.pallas_call(functools.partial(place_kernel, items, bool(before)), out_...  2.9 us
  transfers between devices with their start and end apart: 20, of which 11 were waited for; matrix products, arithmetic and copies ran while one was open for 1% of the time, Pallas kernels for 18%

profile of v5, /device:TPU:0, one launch (start us, length us, event | category | flops | bytes accessed | tf_op | source)
XLA Modules:
  0.0 83.8 jit_solution(4838695789652593217)
XLA Ops:
  0.6 1.9 %pack.1 = bf16[32,72,128]{2,1,0:T(8,128)(2,1)} custom-call(bf16[32,64,128]{2,1,0:T(8,128)(2,1)} %values_any.1, s32[32,64]{1,0:T(8,128)} %block_any.1, s32[1,32]{1,0:T(1,128)} %bitcast.37), custom_call_target="tpu_custom_call" | custom-call | tf_op jit(solution)/shard_map/pack/pallas_call | solution.py:99
  2.5 7.3 %all-to-all-start = ((bf16[32,72,128]{2,1,0:T(8,128)(2,1)}), bf16[32,72,128]{2,1,0:T(8,128)(2,1)S(1)}, u32[]{:S(2)}, u32[]{:S(2)}) async-start(bf16[32,72,128]{2,1,0:T(8,128)(2,1)} %pack.1), calls=%async_computation | async-start | bytes 1179648 | tf_op jit(solution)/shard_map/all_to_all | solution.py:531
  10.4 7.9 %tower.1 = (bf16[1792,1024]{1,0:T(8,128)(2,1)}, bf16[256,1024]{1,0:T(8,128)(2,1)}, bf16[256,1024]{1,0:T(8,128)(2,1)}, bf16[512,1024]{1,0:T(8,128)(2,1)}, f32[1,1024]{1,0:T(1,128)}) custom-call(bf16[1024,1024]{1,0:T(8,128)(2,1)} %dense_ref.1, bf16[1024,512]{1,0:T(8,128)(2,1)} %w1_ref.1, f32[1,512]{1,0:T(1,128)} %bitcast.39, bf16[512,256]{1,0:T(8,128)(2,1)} %w2_ref.1, ...), custom_call_target="tpu_custom_call" | custom-call | flops 1610612736 | bytes 12582912 | tf_op jit(solution)/shard_map/tower/pallas_call | solution.py:158
  18.3 1.1 %copy-done.2 = f32[1024,128]{1,0:T(8,128)S(1)} copy-done((f32[1024,128]{1,0:T(8,128)S(1)}, f32[1024,128]{1,0:T(8,128)}, u32[]{:S(2)}) %copy-start.2) | copy-done | bytes 524312
  19.5 1.0 %copy-done.4 = f32[1024,128]{1,0:T(8,128)S(1)} copy-done((f32[1024,128]{1,0:T(8,128)S(1)}, f32[1024,128]{1,0:T(8,128)}, u32[]{:S(2)}) %copy-start.4) | copy-done | bytes 524312
  21.0 5.6 %all-to-all-done.got_ref = bf16[32,72,128]{2,1,0:T(8,128)(2,1)S(1)} async-done(((bf16[32,72,128]{2,1,0:T(8,128)(2,1)}), bf16[32,72,128]{2,1,0:T(8,128)(2,1)S(1)}, u32[]{:S(2)}, u32[]{:S(2)}) %all-to-all-start) | async-done | bytes 589856 | tf_op jit(solution)/shard_map/all_to_all | solution.py:531
  26.6 2.0 %slot_logits.1 = f32[32,1,128]{2,1,0:T(1,128)} custom-call(bf16[32,72,128]{2,1,0:T(8,128)(2,1)S(1)} %all-to-all-done.got_ref, bf16[1024,256]{1,0:T(8,128)(2,1)S(1)} %weights.1.wcat_ref), custom_call_target="tpu_custom_call" | custom-call | tf_op jit(solution)/shard_map/slot_logits/pallas_call | solution.py:223
  28.5 3.3 %all-to-all-start.1 = ((f32[32,1,128]{2,1,0:T(1,128)}), f32[32,1,128]{2,1,0:T(1,128)S(1)}, u32[]{:S(2)}, u32[]{:S(2)}) async-start(f32[32,1,128]{2,1,0:T(1,128)} %slot_logits.1), calls=%async_computation.1 | async-start | bytes 32768 | tf_op jit(solution)/shard_map/all_to_all | solution.py:531
  32.1 6.8 %all-to-all-done.1.logit_any = f32[32,1,128]{2,1,0:T(1,128)S(1)} async-done(((f32[32,1,128]{2,1,0:T(1,128)}), f32[32,1,128]{2,1,0:T(1,128)S(1)}, u32[]{:S(2)}, u32[]{:S(2)}) %all-to-all-start.1) | async-done | bytes 16416 | tf_op jit(solution)/shard_map/all_to_all | solution.py:531
  38.9 3.4 %residuals.1 = (f32[8,128]{1,0:T(8,128)}, f32[8,128]{1,0:T(8,128)S(1)}, bf16[640,512]{1,0:T(8,128)(2,1)}, bf16[16,512]{1,0:T(8,128)(2,1)S(1)}) custom-call(f32[32,1,128]{2,1,0:T(1,128)S(1)} %all-to-all-done.1.logit_any, s32[32,64]{1,0:T(8,128)S(1)} %copy-done.7, f32[1,1024]{1,0:T(1,128)S(1)} %copy-done.9, s32[8,128]{1,0:T(8,128)S(1)} %bitcast.31, ...), custom_call_target="tpu_custom_call" | custom-call | tf_op jit(solution)/shard_map/residuals/pallas_call | solution.py:369
  42.7 2.5 %gradients.1 = (bf16[640,512]{1,0:T(8,128)(2,1)S(1)}, bf16[4,512]{1,0:T(4,128)(2,1)S(1)}) custom-call(f32[8,128]{1,0:T(8,128)S(1)} %get-tuple-element.60.residual_ref, bf16[256,1024]{1,0:T(8,128)(2,1)S(1)} %copy-done.1, bf16[512,1024]{1,0:T(8,128)(2,1)S(1)} %copy-done, bf16[1792,1024]{1,0:T(8,128)(2,1)} %get-tuple-element.52.big_any), custom_call_target="tpu_custom_call" | custom-call | flops 671088640 | bytes 6291456 | tf_op jit(solution)/shard_map/gradients/pallas_call | solution.py:399
  45.5 0.6 collective-permute-start.4
  46.1 0.7 collective-permute-start.5
  46.8 2.4 %collective-permute-start.6 = (bf16[84,512]{1,0:T(8,128)(2,1)S(1)}, bf16[84,512]{1,0:T(8,128)(2,1)S(1)}, u32[]{:S(2)}, u32[]{:S(2)}) collective-permute-start(bf16[84,512]{1,0:T(8,128)(2,1)S(1)} %pad_maximum_fusion.3), channel_id=1, source_target_pairs={{0,6},{1,7},{2,4},{3,5},{4,2},{5,3},{6,0},{7,1},{8,14},{9,15},{10,... | collective-permute-start | bytes 258056 | tf_op jit(solution)/shard_map/ppermute | solution.py:535
  49.2 1.6 %collective-permute-done.4 = bf16[84,512]{1,0:T(8,128)(2,1)S(1)} collective-permute-done((bf16[84,512]{1,0:T(8,128)(2,1)S(1)}, bf16[84,512]{1,0:T(8,128)(2,1)S(1)}, u32[]{:S(2)}, u32[]{:S(2)}) %collective-permute-start.4) | collective-permute-done | bytes 86048 | tf_op jit(solution)/shard_map/ppermute | solution.py:535
  50.8 1.9 %collective-permute-done.5 = bf16[84,512]{1,0:T(8,128)(2,1)S(1)} collective-permute-done((bf16[84,512]{1,0:T(8,128)(2,1)S(1)}, bf16[84,512]{1,0:T(8,128)(2,1)S(1)}, u32[]{:S(2)}, u32[]{:S(2)}) %collective-permute-start.5) | collective-permute-done | bytes 86048 | tf_op jit(solution)/shard_map/ppermute | solution.py:535
  52.9 0.6 collective-permute-start.7
  53.6 1.9 %collective-permute-start.3 = (bf16[80,512]{1,0:T(8,128)(2,1)S(1)}, bf16[80,512]{1,0:T(8,128)(2,1)S(1)}, u32[]{:S(2)}, u32[]{:S(2)}) collective-permute-start(bf16[80,512]{1,0:T(8,128)(2,1)S(1)} %get-tuple-element.79), channel_id=1, source_target_pairs={{0,6},{1,7},{2,4},{3,5},{4,2},{5,3},{6,0},{7,1},{8,14},{9,15},{10,... | collective-permute-start | bytes 245768 | tf_op jit(solution)/shard_map/ppermute | solution.py:535
  55.5 1.1 %collective-permute-start.2 = (bf16[80,512]{1,0:T(8,128)(2,1)S(1)}, bf16[80,512]{1,0:T(8,128)(2,1)S(1)}, u32[]{:S(2)}, u32[]{:S(2)}) collective-permute-start(bf16[80,512]{1,0:T(8,128)(2,1)S(1)} %get-tuple-element.80), channel_id=1, source_target_pairs={{0,4},{1,5},{2,6},{3,7},{4,0},{5,1},{6,2},{7,3},{8,12},{9,13},{10,... | collective-permute-start | bytes 245768 | tf_op jit(solution)/shard_map/ppermute | solution.py:535
  57.7 1.4 %collective-permute-done.3 = bf16[80,512]{1,0:T(8,128)(2,1)S(1)} collective-permute-done((bf16[80,512]{1,0:T(8,128)(2,1)S(1)}, bf16[80,512]{1,0:T(8,128)(2,1)S(1)}, u32[]{:S(2)}, u32[]{:S(2)}) %collective-permute-start.3) | collective-permute-done | bytes 81952 | tf_op jit(solution)/shard_map/ppermute | solution.py:535
  59.1 0.9 %collective-permute-done.2 = bf16[80,512]{1,0:T(8,128)(2,1)S(1)} collective-permute-done((bf16[80,512]{1,0:T(8,128)(2,1)S(1)}, bf16[80,512]{1,0:T(8,128)(2,1)S(1)}, u32[]{:S(2)}, u32[]{:S(2)}) %collective-permute-start.2) | collective-permute-done | bytes 81952 | tf_op jit(solution)/shard_map/ppermute | solution.py:535
  60.0 1.0 %collective-permute-done.1 = bf16[80,512]{1,0:T(8,128)(2,1)S(1)} collective-permute-done((bf16[80,512]{1,0:T(8,128)(2,1)S(1)}, bf16[80,512]{1,0:T(8,128)(2,1)S(1)}, u32[]{:S(2)}, u32[]{:S(2)}) %collective-permute-start.1) | collective-permute-done | bytes 81952 | tf_op jit(solution)/shard_map/ppermute | solution.py:535
  61.1 0.6 collective-permute-start.8
  61.7 6.0 %collective-permute-done.8 = bf16[92,512]{1,0:T(8,128)(2,1)S(1)} collective-permute-done((bf16[92,512]{1,0:T(8,128)(2,1)S(1)}, bf16[92,512]{1,0:T(8,128)(2,1)S(1)}, u32[]{:S(2)}, u32[]{:S(2)}) %collective-permute-start.8) | collective-permute-done | bytes 94240 | tf_op jit(solution)/shard_map/ppermute | solution.py:535
  67.8 0.6 collective-permute-start.9
  68.5 3.9 %collective-permute-done.9 = bf16[88,512]{1,0:T(8,128)(2,1)S(1)} collective-permute-done((bf16[88,512]{1,0:T(8,128)(2,1)S(1)}, bf16[88,512]{1,0:T(8,128)(2,1)S(1)}, u32[]{:S(2)}, u32[]{:S(2)}) %collective-permute-start.9) | collective-permute-done | bytes 90144 | tf_op jit(solution)/shard_map/ppermute | solution.py:535
  72.5 0.8 collective-permute-start.14
  73.2 2.7 %collective-permute-start.16 = (bf16[176,512]{1,0:T(8,128)(2,1)S(1)}, bf16[176,512]{1,0:T(8,128)(2,1)S(1)}, u32[]{:S(2)}, u32[]{:S(2)}) collective-permute-start(bf16[176,512]{1,0:T(8,128)(2,1)S(1)} %concatenate.34.refs_0_), channel_id=1, source_target_pairs={{0,6},{1,7},{2,4},{3,5},{4,2},{5,3},{6,0},{7,1},{8,14},{9,15},{10,... | collective-permute-start | bytes 540680 | tf_op jit(solution)/shard_map/ppermute | solution.py:535
  76.0 2.9 %new_states.1 = (f32[1024,128]{1,0:T(8,128)}, f32[1024,128]{1,0:T(8,128)}) custom-call(bf16[32,72,128]{2,1,0:T(8,128)(2,1)S(1)} %all-to-all-done.got_ref, f32[32,128]{1,0:T(8,128)S(1)} %convert_add_fusion.res_ref, f32[1024,128]{1,0:T(8,128)S(1)} %copy-done.3, f32[1024,128]{1,0:T(8,128)S(1)} %copy-done.5), custom_call_target="tpu_custom_call" | custom-call | flops 1073741824 | bytes 4194304 | tf_op jit(solution)/shard_map/new_states/pallas_call | solution.py:456
  79.4 0.9 %collective-permute-done.14.refs_2_ = bf16[176,512]{1,0:T(8,128)(2,1)S(1)} collective-permute-done((bf16[176,512]{1,0:T(8,128)(2,1)S(1)}, bf16[176,512]{1,0:T(8,128)(2,1)S(1)}, u32[]{:S(2)}, u32[]{:S(2)}) %collective-permute-start.14) | collective-permute-done | bytes 180256 | tf_op jit(solution)/shard_map/ppermute | solution.py:535
  80.9 1.2 %place.2 = (f32[1024,512]{1,0:T(8,128)}, f32[512,256]{1,0:T(8,128)}, f32[2,512]{1,0:T(2,128)S(1)}) custom-call(bf16[176,512]{1,0:T(8,128)(2,1)S(1)} %concatenate.34.refs_0_, bf16[176,512]{1,0:T(8,128)(2,1)S(1)} %collective-permute-done.12.refs_1_, bf16[176,512]{1,0:T(8,128)(2,1)S(1)} %collective-permute-done.14.refs_2_, ...), custom_call_target="tpu_custom_call" | custom-call | flops 131072 | bytes 2097152 | tf_op jit(solution)/shard_map/place/pallas_call | solution.py:511
  82.1 1.7 %place.3 = (f32[1024,512]{1,0:T(8,128)}, f32[512,256]{1,0:T(8,128)}, f32[1,512]{1,0:T(1,128)}, f32[1,256]{1,0:T(1,128)}, f32[1,256]{1,0:T(1,128)}) custom-call(bf16[176,512]{1,0:T(8,128)(2,1)S(1)} %collective-permute-done.11.refs_0_, bf16[176,512]{1,0:T(8,128)(2,1)S(1)} %collective-permute-done.13.refs_1_, ...), custom_call_target="tpu_custom_call", output_to_operand_aliasing={{0}: (4, {}), {1}: (5, {})} | custom-call | flops 131072 | bytes 2097152 | tf_op jit(solution)/shard_map/place/pallas_call | solution.py:511
  (90 shorter events, 4.4 us)
Async XLA Ops:
  0.6 9.2 %copy-start.10 = (bf16[256]{0:T(256)(128)(2,1)S(1)}, bf16[256]{0:T(256)(128)(2,1)}, u32[]{:S(2)}) copy-start(bf16[256]{0:T(256)(128)(2,1)} %param.25) | copy-start | bytes 1540
  2.5 24.0 %all-to-all-start = ((bf16[32,72,128]{2,1,0:T(8,128)(2,1)}), bf16[32,72,128]{2,1,0:T(8,128)(2,1)S(1)}, u32[]{:S(2)}, u32[]{:S(2)}) async-start(bf16[32,72,128]{2,1,0:T(8,128)(2,1)} %pack.1), calls=%async_computation | async-start | bytes 1179648 | tf_op jit(solution)/shard_map/all_to_all | solution.py:531
  18.3 20.6 %copy-start = (bf16[512,1024]{1,0:T(8,128)(2,1)S(1)}, bf16[512,1024]{1,0:T(8,128)(2,1)}, u32[]{:S(2)}) copy-start(bf16[512,1024]{1,0:T(8,128)(2,1)} %get-tuple-element.51.q) | copy-start | bytes 3145732
  18.3 20.6 %copy-start.1 = (bf16[256,1024]{1,0:T(8,128)(2,1)S(1)}, bf16[256,1024]{1,0:T(8,128)(2,1)}, u32[]{:S(2)}) copy-start(bf16[256,1024]{1,0:T(8,128)(2,1)} %get-tuple-element.50.s2) | copy-start | bytes 1572868
  18.3 1.2 %copy-start.2 = (f32[1024,128]{1,0:T(8,128)S(1)}, f32[1024,128]{1,0:T(8,128)}, u32[]{:S(2)}) copy-start(f32[1024,128]{1,0:T(8,128)} %z_ref.2) | copy-start | bytes 1572868
  19.5 1.0 %copy-start.4 = (f32[1024,128]{1,0:T(8,128)S(1)}, f32[1024,128]{1,0:T(8,128)}, u32[]{:S(2)}) copy-start(f32[1024,128]{1,0:T(8,128)} %n_ref.2) | copy-start | bytes 1572868
  20.5 11.3 %copy-start.7 = (s32[32,64]{1,0:T(8,128)S(1)}, s32[32,64]{1,0:T(8,128)}, u32[]{:S(2)}) copy-start(s32[32,64]{1,0:T(8,128)} %example_ref.2) | copy-start | bytes 24580
  20.5 18.4 %copy-start.8 = (s32[1024]{0:T(1024)S(1)}, s32[1024]{0:T(1024)}, u32[]{:S(2)}) copy-start(s32[1024]{0:T(1024)} %param.14) | copy-start | bytes 12292
  20.5 18.4 %copy-start.9 = (f32[1,1024]{1,0:T(1,128)S(1)}, f32[1,1024]{1,0:T(1,128)}, u32[]{:S(2)}) copy-start(f32[1,1024]{1,0:T(1,128)} %get-tuple-element.48.deep_ref) | copy-start | bytes 12292
  28.5 10.4 %all-to-all-start.1 = ((f32[32,1,128]{2,1,0:T(1,128)}), f32[32,1,128]{2,1,0:T(1,128)S(1)}, u32[]{:S(2)}, u32[]{:S(2)}) async-start(f32[32,1,128]{2,1,0:T(1,128)} %slot_logits.1), calls=%async_computation.1 | async-start | bytes 32768 | tf_op jit(solution)/shard_map/all_to_all | solution.py:531
  42.4 2.8 %collective-permute-start = (bf16[640,512]{1,0:T(8,128)(2,1)}, bf16[640,512]{1,0:T(8,128)(2,1)S(1)}, u32[]{:S(2)}, u32[]{:S(2)}) collective-permute-start(bf16[640,512]{1,0:T(8,128)(2,1)} %get-tuple-element.56), channel_id=1, source_target_pairs={{0,1},{1,0},{2,3},{3,2},{4,5},{5,4},{6,7},{7,6},{8,9},{9,8},{10,11... | collective-permute-start | bytes 1966088 | tf_op jit(solution)/shard_map/ppermute | solution.py:535
  45.2 11.9 %copy-start.6 = (bf16[256,1024]{1,0:T(8,128)(2,1)S(1)}, bf16[256,1024]{1,0:T(8,128)(2,1)}, u32[]{:S(2)}) copy-start(bf16[256,1024]{1,0:T(8,128)(2,1)} %get-tuple-element.62.h2) | copy-start | bytes 1572868
  45.4 30.6 %copy-start.3 = (f32[1024,128]{1,0:T(8,128)S(1)}, f32[1024,128]{1,0:T(8,128)}, u32[]{:S(2)}) copy-start(f32[1024,128]{1,0:T(8,128)} %z_ref.2) | copy-start | bytes 1572868
  45.4 30.5 %copy-start.5 = (f32[1024,128]{1,0:T(8,128)S(1)}, f32[1024,128]{1,0:T(8,128)}, u32[]{:S(2)}) copy-start(f32[1024,128]{1,0:T(8,128)} %n_ref.2) | copy-start | bytes 1572868
  45.5 5.3 %collective-permute-start.4 = (bf16[84,512]{1,0:T(8,128)(2,1)S(1)}, bf16[84,512]{1,0:T(8,128)(2,1)S(1)}, u32[]{:S(2)}, u32[]{:S(2)}) collective-permute-start(bf16[84,512]{1,0:T(8,128)(2,1)S(1)} %pad_maximum_fusion.1), channel_id=1, source_target_pairs={{0,2},{1,3},{2,0},{3,1},{4,6},{5,7},{6,4},{7,5},{8,10},{9,11},{10,... | collective-permute-start | bytes 258056 | tf_op jit(solution)/shard_map/ppermute | solution.py:535
  46.1 6.6 %collective-permute-start.5 = (bf16[84,512]{1,0:T(8,128)(2,1)S(1)}, bf16[84,512]{1,0:T(8,128)(2,1)S(1)}, u32[]{:S(2)}, u32[]{:S(2)}) collective-permute-start(bf16[84,512]{1,0:T(8,128)(2,1)S(1)} %pad_maximum_fusion.2), channel_id=1, source_target_pairs={{0,4},{1,5},{2,6},{3,7},{4,0},{5,1},{6,2},{7,3},{8,12},{9,13},{10,... | collective-permute-start | bytes 258056 | tf_op jit(solution)/shard_map/ppermute | solution.py:535
  46.8 5.9 %collective-permute-start.6 = (bf16[84,512]{1,0:T(8,128)(2,1)S(1)}, bf16[84,512]{1,0:T(8,128)(2,1)S(1)}, u32[]{:S(2)}, u32[]{:S(2)}) collective-permute-start(bf16[84,512]{1,0:T(8,128)(2,1)S(1)} %pad_maximum_fusion.3), channel_id=1, source_target_pairs={{0,6},{1,7},{2,4},{3,5},{4,2},{5,3},{6,0},{7,1},{8,14},{9,15},{10,... | collective-permute-start | bytes 258056 | tf_op jit(solution)/shard_map/ppermute | solution.py:535
  52.9 4.6 %collective-permute-start.7 = (bf16[88,512]{1,0:T(8,128)(2,1)S(1)}, bf16[88,512]{1,0:T(8,128)(2,1)S(1)}, u32[]{:S(2)}, u32[]{:S(2)}) collective-permute-start(bf16[88,512]{1,0:T(8,128)(2,1)S(1)} %pad_maximum_fusion.4), channel_id=1, source_target_pairs={{0,8},{1,9},{2,10},{3,11},{4,12},{5,13},{6,14},{7,15},{8,0},{9,1},... | collective-permute-start | bytes 270344 | tf_op jit(solution)/shard_map/ppermute | solution.py:535
  53.6 5.5 %collective-permute-start.3 = (bf16[80,512]{1,0:T(8,128)(2,1)S(1)}, bf16[80,512]{1,0:T(8,128)(2,1)S(1)}, u32[]{:S(2)}, u32[]{:S(2)}) collective-permute-start(bf16[80,512]{1,0:T(8,128)(2,1)S(1)} %get-tuple-element.79), channel_id=1, source_target_pairs={{0,6},{1,7},{2,4},{3,5},{4,2},{5,3},{6,0},{7,1},{8,14},{9,15},{10,... | collective-permute-start | bytes 245768 | tf_op jit(solution)/shard_map/ppermute | solution.py:535
  55.5 4.5 %collective-permute-start.2 = (bf16[80,512]{1,0:T(8,128)(2,1)S(1)}, bf16[80,512]{1,0:T(8,128)(2,1)S(1)}, u32[]{:S(2)}, u32[]{:S(2)}) collective-permute-start(bf16[80,512]{1,0:T(8,128)(2,1)S(1)} %get-tuple-element.80), channel_id=1, source_target_pairs={{0,4},{1,5},{2,6},{3,7},{4,0},{5,1},{6,2},{7,3},{8,12},{9,13},{10,... | collective-permute-start | bytes 245768 | tf_op jit(solution)/shard_map/ppermute | solution.py:535
  56.5 4.4 %collective-permute-start.1 = (bf16[80,512]{1,0:T(8,128)(2,1)S(1)}, bf16[80,512]{1,0:T(8,128)(2,1)S(1)}, u32[]{:S(2)}, u32[]{:S(2)}) collective-permute-start(bf16[80,512]{1,0:T(8,128)(2,1)S(1)} %get-tuple-element.81), channel_id=1, source_target_pairs={{0,2},{1,3},{2,0},{3,1},{4,6},{5,7},{6,4},{7,5},{8,10},{9,11},{10,... | collective-permute-start | bytes 245768 | tf_op jit(solution)/shard_map/ppermute | solution.py:535
  61.1 6.6 %collective-permute-start.8 = (bf16[92,512]{1,0:T(8,128)(2,1)S(1)}, bf16[92,512]{1,0:T(8,128)(2,1)S(1)}, u32[]{:S(2)}, u32[]{:S(2)}) collective-permute-start(bf16[92,512]{1,0:T(8,128)(2,1)S(1)} %pad_maximum_fusion), channel_id=1, source_target_pairs={{0,16},{1,17},{2,18},{3,19},{4,20},{5,21},{6,22},{7,23},{8,24},{9,... | collective-permute-start | bytes 282632 | tf_op jit(solution)/shard_map/ppermute | solution.py:535
  67.8 4.6 %collective-permute-start.9 = (bf16[88,512]{1,0:T(8,128)(2,1)S(1)}, bf16[88,512]{1,0:T(8,128)(2,1)S(1)}, u32[]{:S(2)}, u32[]{:S(2)}) collective-permute-start(bf16[88,512]{1,0:T(8,128)(2,1)S(1)} %pad_maximum_fusion.5), channel_id=1, source_target_pairs={{0,8},{1,9},{2,10},{3,11},{4,12},{5,13},{6,14},{7,15},{8,0},{9,1},... | collective-permute-start | bytes 270344 | tf_op jit(solution)/shard_map/ppermute | solution.py:535
  68.4 7.6 %collective-permute-start.10 = (bf16[16,256]{1,0:T(8,128)(2,1)S(1)}, bf16[16,256]{1,0:T(8,128)(2,1)S(1)}, u32[]{:S(2)}, u32[]{:S(2)}) collective-permute-start(bf16[16,256]{1,0:T(8,128)(2,1)S(1)} %bitcast.36), channel_id=1, source_target_pairs={{0,1},{1,0},{2,3},{3,2},{4,5},{5,4},{6,7},{7,6},{8,9},{9,8},{10,11... | collective-permute-start | bytes 24584 | tf_op jit(solution)/shard_map/ppermute | solution.py:535
  72.4 6.5 %collective-permute-start.12 = (bf16[176,512]{1,0:T(8,128)(2,1)S(1)}, bf16[176,512]{1,0:T(8,128)(2,1)S(1)}, u32[]{:S(2)}, u32[]{:S(2)}) collective-permute-start(bf16[176,512]{1,0:T(8,128)(2,1)S(1)} %concatenate.34.refs_0_), channel_id=1, source_target_pairs={{0,2},{1,3},{2,0},{3,1},{4,6},{5,7},{6,4},{7,5},{8,10},{9,11},{10,... | collective-permute-start | bytes 540680 | tf_op jit(solution)/shard_map/ppermute | solution.py:535
  72.5 7.9 %collective-permute-start.14 = (bf16[176,512]{1,0:T(8,128)(2,1)S(1)}, bf16[176,512]{1,0:T(8,128)(2,1)S(1)}, u32[]{:S(2)}, u32[]{:S(2)}) collective-permute-start(bf16[176,512]{1,0:T(8,128)(2,1)S(1)} %concatenate.34.refs_0_), channel_id=1, source_target_pairs={{0,4},{1,5},{2,6},{3,7},{4,0},{5,1},{6,2},{7,3},{8,12},{9,13},{10,... | collective-permute-start | bytes 540680 | tf_op jit(solution)/shard_map/ppermute | solution.py:535
  73.2 7.1 %collective-permute-start.16 = (bf16[176,512]{1,0:T(8,128)(2,1)S(1)}, bf16[176,512]{1,0:T(8,128)(2,1)S(1)}, u32[]{:S(2)}, u32[]{:S(2)}) collective-permute-start(bf16[176,512]{1,0:T(8,128)(2,1)S(1)} %concatenate.34.refs_0_), channel_id=1, source_target_pairs={{0,6},{1,7},{2,4},{3,5},{4,2},{5,3},{6,0},{7,1},{8,14},{9,15},{10,... | collective-permute-start | bytes 540680 | tf_op jit(solution)/shard_map/ppermute | solution.py:535
  78.9 3.1 %collective-permute-start.11 = (bf16[176,512]{1,0:T(8,128)(2,1)S(1)}, bf16[176,512]{1,0:T(8,128)(2,1)S(1)}, u32[]{:S(2)}, u32[]{:S(2)}) collective-permute-start(bf16[176,512]{1,0:T(8,128)(2,1)S(1)} %concatenate.34.refs_0_), channel_id=1, source_target_pairs={{0,1},{1,0},{2,3},{3,2},{4,5},{5,4},{6,7},{7,6},{8,9},{9,8},{10,11... | collective-permute-start | bytes 540680 | tf_op jit(solution)/shard_map/ppermute | solution.py:535
  78.9 3.1 %collective-permute-start.13 = (bf16[176,512]{1,0:T(8,128)(2,1)S(1)}, bf16[176,512]{1,0:T(8,128)(2,1)S(1)}, u32[]{:S(2)}, u32[]{:S(2)}) collective-permute-start(bf16[176,512]{1,0:T(8,128)(2,1)S(1)} %collective-permute-done.12.refs_1_), channel_id=1, source_target_pairs={{0,1},{1,0},{2,3},{3,2},{4,5},{5,4},{6,7},{7,6},{8,9},{9,8},{10,11... | collective-permute-start | bytes 540680 | tf_op jit(solution)/shard_map/ppermute | solution.py:535
  80.4 1.7 %collective-permute-start.15 = (bf16[176,512]{1,0:T(8,128)(2,1)S(1)}, bf16[176,512]{1,0:T(8,128)(2,1)S(1)}, u32[]{:S(2)}, u32[]{:S(2)}) collective-permute-start(bf16[176,512]{1,0:T(8,128)(2,1)S(1)} %collective-permute-done.14.refs_2_), channel_id=1, source_target_pairs={{0,1},{1,0},{2,3},{3,2},{4,5},{5,4},{6,7},{7,6},{8,9},{9,8},{10,11... | collective-permute-start | bytes 540680 | tf_op jit(solution)/shard_map/ppermute | solution.py:535
  80.4 1.7 %collective-permute-start.17 = (bf16[176,512]{1,0:T(8,128)(2,1)S(1)}, bf16[176,512]{1,0:T(8,128)(2,1)S(1)}, u32[]{:S(2)}, u32[]{:S(2)}) collective-permute-start(bf16[176,512]{1,0:T(8,128)(2,1)S(1)} %collective-permute-done.16.refs_3_), channel_id=1, source_target_pairs={{0,1},{1,0},{2,3},{3,2},{4,5},{5,4},{6,7},{7,6},{8,9},{9,8},{10,11... | collective-permute-start | bytes 540680 | tf_op jit(solution)/shard_map/ppermute | solution.py:535

commit v6 on v5

--- a/solution.py
+++ b/solution.py
@@ -238,25 +238,6 @@
     return [e >> 7 for e in example], [e & (LANES - 1) for e in example]
 
 
-def marks_kernel(example_ref, marks_ref):
-    down = iota((LANES, LANES), 0)
-    for k, low in enumerate(paired(example_ref)[1]):
-        marks_ref[:, k * LANES : (k + 1) * LANES] = jnp.where(low == down, 1.0, 0.0).astype(bf16)
-
-
-def example_marks(example):
-    lists, cap = example.shape
-    return pl.pallas_call(
-        marks_kernel,
-        out_shape=jax.ShapeDtypeStruct((LANES, lists * cap), bf16),
-        in_specs=[VM],
-        out_specs=VM,
-        compiler_params=params(8),
-        cost_estimate=pl.CostEstimate(flops=2 << 20, bytes_accessed=4 << 20, transcendentals=0),
-        name="example_marks",
-    )(example)
-
-
 def half_copies(half, big_any, dense_t, h1, sems):
     n1 = 2 * (h1.shape[0] - ONES)
     each, packed = dense_t.shape[0] - ONES, n1 // 4
@@ -314,9 +295,9 @@
 
 
 def residual_kernel(
-    logit_any, example_ref, deep_ref, label_ref, marks, s2, q, big_any,
+    logit_any, example_ref, deep_ref, label_ref, s2, q, big_any,
     prob_ref, residual_ref, send_ref, slot_ref,
-    spread, logit_ref, apart, dense_t, h1, sems,
+    spread, marks, logit_ref, apart, dense_t, h1, sems,
 ):
     lists, cap = example_ref.shape
     rows = label_ref.shape[0]
@@ -327,7 +308,10 @@
     copies = half_copies(1 - core, big_any, dense_t, h1, sems)
     for copy in copies:
         copy.start()
-    high = paired(example_ref)[0]
+    high, low = paired(example_ref)
+    down_all = iota((LANES, LANES), 0)
+    for k in range(lists // 2):
+        marks[:, k * LANES : (k + 1) * LANES] = jnp.where(low[k] == down_all, 1.0, 0.0).astype(bf16)
     left = iota((1, LANES), 1) < cap
     down = iota((rows, LANES), 0)
     turned = lambda v: pltpu.roll(v, cap, 1)
@@ -361,8 +345,8 @@
     half_gradients(residual, copies, s2, q, dense_t, h1, send_ref)
 
 
-def residuals(logits, example, deep, labels, marks, s2, q, big):
-    lists = example.shape[0]
+def residuals(logits, example, deep, labels, s2, q, big):
+    lists, cap = example.shape
     rows = deep.shape[1] // LANES
     n1 = q.shape[0]
     half = (big.shape[0] - n1 - s2.shape[0]) // 2 + n1 // 4
@@ -374,13 +358,18 @@
             jax.ShapeDtypeStruct((half, n1), bf16),
             jax.ShapeDtypeStruct((lists // 2, 4 * LANES), bf16),
         ),
-        in_specs=[ANY] + [VM] * 6 + [HBM],
+        in_specs=[ANY] + [VM] * 5 + [HBM],
         out_specs=[VM, VM, VM, VM],
-        scratch_shapes=[pltpu.VMEM((2 * rows, marks.shape[1]), bf16), pltpu.VMEM(logits.shape, f32), pltpu.VMEM((lists, 2, LANES), f32)]
+        scratch_shapes=[
+            pltpu.VMEM((2 * rows, lists * cap), bf16),
+            pltpu.VMEM((LANES, lists * cap), bf16),
+            pltpu.VMEM(logits.shape, f32),
+            pltpu.VMEM((lists, 2, LANES), f32),
+        ]
         + half_scratch(big, n1),
         compiler_params=params(49),
         name="residuals",
-    )(logits, example, deep, labels.reshape(rows, LANES), marks, s2, q, big)
+    )(logits, example, deep, labels.reshape(rows, LANES), s2, q, big)
 
 
 def gradient_kernel(residual_ref, s2, q, big_any, keep_ref, small_ref, dense_t, h1, sems):
@@ -469,8 +458,8 @@
 def place_kernel(items, follows, *refs):
     parts, refs = refs[: len(items)], refs[len(items) :]
     before, refs = (refs[:3], refs[3:]) if follows else (None, refs)
-    w1_any, w2_any, *outs = refs[:-3]
-    wide, narrow, sems = refs[-3:]
+    w1_any, w2_any, *outs = refs[:-4]
+    wide, narrow, small, sems = refs[-4:]
     me = position()
     quad = (me >> 1) & 3
     first, packed = wide.shape[1] // 2, narrow.shape[2] // 2
@@ -495,9 +484,15 @@
         extra = part[2 * each :, :].astype(f32)
         total = total + sum(extra[r : r + 2] for r in range(0, extra.shape[0], 2))
     if len(outs) > 1:
-        outs[0][...] = total[0:1]
-        outs[1][...] = total[1:2, 0 : width // 2]
-        outs[2][...] = total[1:2, width // 2 :]
+        small[0:1, :] = total[0:1]
+        small[8:9, :] = total[1:2]
+        small[16:17, 0 : width // 2] = total[1:2, width // 2 :]
+        spans = ((0, width), (8, width // 2), (16, width // 2))
+        for n, (out, (row, size)) in enumerate(zip(outs, spans)):
+            copies.append(
+                pltpu.make_async_copy(small.at[pl.ds(row, 1), pl.ds(0, size)], out, sems.at[3 * len(items) + n])
+            )
+            copies[-1].start()
     else:
         outs[0][...] = total
     for copy in copies:
@@ -512,12 +507,13 @@
         functools.partial(place_kernel, items, bool(before)),
         out_shape=[jax.ShapeDtypeStruct(t, f32) for t in shapes + tail],
         in_specs=[VM] * count + ([ANY, ANY, VM] if before else []),
-        out_specs=[ANY, ANY] + [VM] * len(tail),
+        out_specs=[ANY, ANY] + [ANY if final else VM] * len(tail),
         input_output_aliases={count: 0, count + 1: 1} if before else {},
         scratch_shapes=[
             pltpu.VMEM((count, 2 * first, width), f32),
             pltpu.VMEM((count, 2, 2 * packed, width // 2), f32),
-            pltpu.SemaphoreType.DMA((3 * count,)),
+            pltpu.VMEM((24, width), f32),
+            pltpu.SemaphoreType.DMA((3 * count + 3,)),
         ],
         compiler_params=params(16),
         cost_estimate=pl.CostEstimate(
@@ -629,10 +625,8 @@
     wcat = weights(z_then, n_then)
     got, deep = hold(got, deep)
     logits = slot_logits(got, wcat)
-    logits, example = hold(logits, tile_example)
-    marks = example_marks(example)
     logits = every_to_every(logits)
-    prob, residual, send, slots = residuals(logits, tile_example, deep, labels, marks, s2, q, big)
+    prob, residual, send, slots = residuals(logits, tile_example, deep, labels, s2, q, big)
     keep, small = gradients(residual, s2, q, big)
     own = add(keep, swap(send, 1, devices))
 

time: 84.2 us -> 82.3 us (0.977)
  blocking collectives: 0 us -> 10.3 us
  waiting for transfers between devices: 30.2 us -> 23.4 us
  starting transfers between devices: 24.3 us -> 21 us
  Pallas kernels: 24.4 us -> 22.3 us
    all_to_all x0 -> x1, blocking collectives: none -> 10.3 us  [every_to_every(): return lax.all_to_all(x, AXES, split_axis=0, concat_axis=0, tiled=True)]
    all_to_all x2 -> x1, waiting for transfers between devices: 12.4 us -> 5.61 us  [every_to_every(): return lax.all_to_all(x, AXES, split_axis=0, concat_axis=0, tiled=True)]
    all_to_all x2 -> x1, starting transfers between devices: 10.6 us -> 7.3 us  [every_to_every(): return lax.all_to_all(x, AXES, split_axis=0, concat_axis=0, tiled=True)]
  transfers between devices with their start and end apart: 20 -> 19, of which waited for: 11 -> 10; matrix products, arithmetic and copies ran while one was open for 1% -> 1% of each run, Pallas kernels for 18% -> 19%
where the time goes in v6:
time: 82.3 us; the launch traced here: 81.9 us
  waiting for transfers between devices  23.4 us (28%)
  Pallas kernels  22.3 us (27%)
  starting transfers between devices  21 us (26%)
  blocking collectives  10.3 us (13%)
  local copies, waits for them, and re-layouts  3.24 us (4%)
  between operations  1.17 us (1%)
    ppermute x18, waiting for transfers between devices, swap(): return lax.ppermute(x, AXES, [(i, i ^ bit) for i in range(devices)])  17.8 us
    ppermute x18, starting transfers between devices, swap(): return lax.ppermute(x, AXES, [(i, i ^ bit) for i in range(devices)])  13.7 us
    all_to_all x1, blocking collectives, every_to_every(): return lax.all_to_all(x, AXES, split_axis=0, concat_axis=0, tiled=True)  10.3 us
    pallas_call x1, Pallas kernels, tower(): pl.pallas_call(tower_kernel, grid=(steps,), out_shape=(jax.ShapeDtypeStru...  7.88 us
    all_to_all x1, starting transfers between devices, every_to_every(): return lax.all_to_all(x, AXES, split_axis=0, concat_axis=0, tiled=True)  7.3 us
    all_to_all x1, waiting for transfers between devices, every_to_every(): return lax.all_to_all(x, AXES, split_axis=0, concat_axis=0, tiled=True)  5.61 us
    pallas_call x1, Pallas kernels, new_states(): pl.pallas_call(state_kernel, out_shape=(jax.ShapeDtypeStruct(z.shape, f32...  2.94 us
    pallas_call x1, Pallas kernels, residuals(): pl.pallas_call(residual_kernel, out_shape=(jax.ShapeDtypeStruct((rows, LA...  2.75 us
  transfers between devices with their start and end apart: 19, of which 10 were waited for; matrix products, arithmetic and copies ran while one was open for 1% of the time, Pallas kernels for 19%

profile of v6, /device:TPU:0, one launch (start us, length us, event | category | flops | bytes accessed | tf_op | source)
XLA Modules:
  0.0 81.9 jit_solution(8990232764048149887)
XLA Ops:
  0.6 1.9 %pack.1 = bf16[32,72,128]{2,1,0:T(8,128)(2,1)} custom-call(bf16[32,64,128]{2,1,0:T(8,128)(2,1)} %values_any.1, s32[32,64]{1,0:T(8,128)} %block_any.1, s32[1,32]{1,0:T(1,128)} %bitcast.37), custom_call_target="tpu_custom_call" | custom-call | tf_op jit(solution)/shard_map/pack/pallas_call | solution.py:99
  2.5 7.3 %all-to-all-start = ((bf16[32,72,128]{2,1,0:T(8,128)(2,1)}), bf16[32,72,128]{2,1,0:T(8,128)(2,1)S(1)}, u32[]{:S(2)}, u32[]{:S(2)}) async-start(bf16[32,72,128]{2,1,0:T(8,128)(2,1)} %pack.1), calls=%async_computation | async-start | bytes 1179648 | tf_op jit(solution)/shard_map/all_to_all | solution.py:527
  9.8 0.6 reshape.62.head_ref
  10.4 7.9 %tower.1 = (bf16[1792,1024]{1,0:T(8,128)(2,1)}, bf16[256,1024]{1,0:T(8,128)(2,1)}, bf16[256,1024]{1,0:T(8,128)(2,1)}, bf16[512,1024]{1,0:T(8,128)(2,1)}, f32[1,1024]{1,0:T(1,128)}) custom-call(bf16[1024,1024]{1,0:T(8,128)(2,1)} %dense_ref.1, bf16[1024,512]{1,0:T(8,128)(2,1)} %w1_ref.1, f32[1,512]{1,0:T(1,128)} %bitcast.39, bf16[512,256]{1,0:T(8,128)(2,1)} %w2_ref.1, ...), custom_call_target="tpu_custom_call" | custom-call | flops 1610612736 | bytes 12582912 | tf_op jit(solution)/shard_map/tower/pallas_call | solution.py:158
  18.3 1.1 %copy-done.2 = f32[1024,128]{1,0:T(8,128)S(1)} copy-done((f32[1024,128]{1,0:T(8,128)S(1)}, f32[1024,128]{1,0:T(8,128)}, u32[]{:S(2)}) %copy-start.2) | copy-done | bytes 524312
  19.5 1.0 %copy-done.4 = f32[1024,128]{1,0:T(8,128)S(1)} copy-done((f32[1024,128]{1,0:T(8,128)S(1)}, f32[1024,128]{1,0:T(8,128)}, u32[]{:S(2)}) %copy-start.4) | copy-done | bytes 524312
  21.0 5.6 %all-to-all-done.got_ref = bf16[32,72,128]{2,1,0:T(8,128)(2,1)S(1)} async-done(((bf16[32,72,128]{2,1,0:T(8,128)(2,1)}), bf16[32,72,128]{2,1,0:T(8,128)(2,1)S(1)}, u32[]{:S(2)}, u32[]{:S(2)}) %all-to-all-start) | async-done | bytes 589856 | tf_op jit(solution)/shard_map/all_to_all | solution.py:527
  26.6 1.3 %slot_logits.1 = f32[32,1,128]{2,1,0:T(1,128)S(1)} custom-call(bf16[32,72,128]{2,1,0:T(8,128)(2,1)S(1)} %all-to-all-done.got_ref, bf16[1024,256]{1,0:T(8,128)(2,1)S(1)} %weights.1.wcat_ref), custom_call_target="tpu_custom_call" | custom-call | tf_op jit(solution)/shard_map/slot_logits/pallas_call | solution.py:223
  27.9 10.3 %all_to_all.10.logit_any = f32[32,1,128]{2,1,0:T(1,128)S(1)} all-to-all(f32[32,1,128]{2,1,0:T(1,128)S(1)} %slot_logits.1), channel_id=1, replica_groups=mesh['blk'=8,'rep'=4] {'blk','rep'}, dimensions={0} | all-to-all | bytes 32768 | tf_op jit(solution)/shard_map/all_to_all | solution.py:527
  38.2 2.7 %residuals.1 = (f32[8,128]{1,0:T(8,128)}, f32[8,128]{1,0:T(8,128)S(1)}, bf16[640,512]{1,0:T(8,128)(2,1)S(1)}, bf16[16,512]{1,0:T(8,128)(2,1)S(1)}) custom-call(f32[32,1,128]{2,1,0:T(1,128)S(1)} %all_to_all.10.logit_any, s32[32,64]{1,0:T(8,128)S(1)} %copy-done.7, f32[1,1024]{1,0:T(1,128)S(1)} %copy-done.9, s32[8,128]{1,0:T(8,128)S(1)} %bitcast.31, ...), custom_call_target="tpu_custom_call" | custom-call | tf_op jit(solution)/shard_map/residuals/pallas_call | solution.py:353
  41.3 2.5 %gradients.1 = (bf16[640,512]{1,0:T(8,128)(2,1)S(1)}, bf16[4,512]{1,0:T(4,128)(2,1)S(1)}) custom-call(f32[8,128]{1,0:T(8,128)S(1)} %get-tuple-element.56.residual_ref, bf16[256,1024]{1,0:T(8,128)(2,1)S(1)} %copy-done.1, bf16[512,1024]{1,0:T(8,128)(2,1)S(1)} %copy-done, bf16[1792,1024]{1,0:T(8,128)(2,1)} %get-tuple-element.48.big_any), custom_call_target="tpu_custom_call" | custom-call | flops 671088640 | bytes 6291456 | tf_op jit(solution)/shard_map/gradients/pallas_call | solution.py:388
  44.1 0.6 collective-permute-start.4
  44.7 0.7 collective-permute-start.5
  45.4 2.4 %collective-permute-start.6 = (bf16[84,512]{1,0:T(8,128)(2,1)S(1)}, bf16[84,512]{1,0:T(8,128)(2,1)S(1)}, u32[]{:S(2)}, u32[]{:S(2)}) collective-permute-start(bf16[84,512]{1,0:T(8,128)(2,1)S(1)} %pad_maximum_fusion.3), channel_id=1, source_target_pairs={{0,6},{1,7},{2,4},{3,5},{4,2},{5,3},{6,0},{7,1},{8,14},{9,15},{10,... | collective-permute-start | bytes 258056 | tf_op jit(solution)/shard_map/ppermute | solution.py:531
  47.8 1.6 %collective-permute-done.4 = bf16[84,512]{1,0:T(8,128)(2,1)S(1)} collective-permute-done((bf16[84,512]{1,0:T(8,128)(2,1)S(1)}, bf16[84,512]{1,0:T(8,128)(2,1)S(1)}, u32[]{:S(2)}, u32[]{:S(2)}) %collective-permute-start.4) | collective-permute-done | bytes 86048 | tf_op jit(solution)/shard_map/ppermute | solution.py:531
  49.4 1.9 %collective-permute-done.5 = bf16[84,512]{1,0:T(8,128)(2,1)S(1)} collective-permute-done((bf16[84,512]{1,0:T(8,128)(2,1)S(1)}, bf16[84,512]{1,0:T(8,128)(2,1)S(1)}, u32[]{:S(2)}, u32[]{:S(2)}) %collective-permute-start.5) | collective-permute-done | bytes 86048 | tf_op jit(solution)/shard_map/ppermute | solution.py:531
  51.5 0.7 collective-permute-start.7
  52.2 1.9 %collective-permute-start.3 = (bf16[80,512]{1,0:T(8,128)(2,1)S(1)}, bf16[80,512]{1,0:T(8,128)(2,1)S(1)}, u32[]{:S(2)}, u32[]{:S(2)}) collective-permute-start(bf16[80,512]{1,0:T(8,128)(2,1)S(1)} %get-tuple-element.75), channel_id=1, source_target_pairs={{0,6},{1,7},{2,4},{3,5},{4,2},{5,3},{6,0},{7,1},{8,14},{9,15},{10,... | collective-permute-start | bytes 245768 | tf_op jit(solution)/shard_map/ppermute | solution.py:531
  54.1 1.1 %collective-permute-start.2 = (bf16[80,512]{1,0:T(8,128)(2,1)S(1)}, bf16[80,512]{1,0:T(8,128)(2,1)S(1)}, u32[]{:S(2)}, u32[]{:S(2)}) collective-permute-start(bf16[80,512]{1,0:T(8,128)(2,1)S(1)} %get-tuple-element.76), channel_id=1, source_target_pairs={{0,4},{1,5},{2,6},{3,7},{4,0},{5,1},{6,2},{7,3},{8,12},{9,13},{10,... | collective-permute-start | bytes 245768 | tf_op jit(solution)/shard_map/ppermute | solution.py:531
  56.3 1.4 %collective-permute-done.3 = bf16[80,512]{1,0:T(8,128)(2,1)S(1)} collective-permute-done((bf16[80,512]{1,0:T(8,128)(2,1)S(1)}, bf16[80,512]{1,0:T(8,128)(2,1)S(1)}, u32[]{:S(2)}, u32[]{:S(2)}) %collective-permute-start.3) | collective-permute-done | bytes 81952 | tf_op jit(solution)/shard_map/ppermute | solution.py:531
  57.7 0.9 %collective-permute-done.2 = bf16[80,512]{1,0:T(8,128)(2,1)S(1)} collective-permute-done((bf16[80,512]{1,0:T(8,128)(2,1)S(1)}, bf16[80,512]{1,0:T(8,128)(2,1)S(1)}, u32[]{:S(2)}, u32[]{:S(2)}) %collective-permute-start.2) | collective-permute-done | bytes 81952 | tf_op jit(solution)/shard_map/ppermute | solution.py:531
  58.6 1.0 %collective-permute-done.1 = bf16[80,512]{1,0:T(8,128)(2,1)S(1)} collective-permute-done((bf16[80,512]{1,0:T(8,128)(2,1)S(1)}, bf16[80,512]{1,0:T(8,128)(2,1)S(1)}, u32[]{:S(2)}, u32[]{:S(2)}) %collective-permute-start.1) | collective-permute-done | bytes 81952 | tf_op jit(solution)/shard_map/ppermute | solution.py:531
  59.7 0.6 collective-permute-start.8
  60.3 6.0 %collective-permute-done.8 = bf16[92,512]{1,0:T(8,128)(2,1)S(1)} collective-permute-done((bf16[92,512]{1,0:T(8,128)(2,1)S(1)}, bf16[92,512]{1,0:T(8,128)(2,1)S(1)}, u32[]{:S(2)}, u32[]{:S(2)}) %collective-permute-start.8) | collective-permute-done | bytes 94240 | tf_op jit(solution)/shard_map/ppermute | solution.py:531
  66.3 0.6 collective-permute-start.9
  67.1 3.9 %collective-permute-done.9 = bf16[88,512]{1,0:T(8,128)(2,1)S(1)} collective-permute-done((bf16[88,512]{1,0:T(8,128)(2,1)S(1)}, bf16[88,512]{1,0:T(8,128)(2,1)S(1)}, u32[]{:S(2)}, u32[]{:S(2)}) %collective-permute-start.9) | collective-permute-done | bytes 90144 | tf_op jit(solution)/shard_map/ppermute | solution.py:531
  71.1 0.8 collective-permute-start.14
  71.9 2.7 %collective-permute-start.16 = (bf16[176,512]{1,0:T(8,128)(2,1)S(1)}, bf16[176,512]{1,0:T(8,128)(2,1)S(1)}, u32[]{:S(2)}, u32[]{:S(2)}) collective-permute-start(bf16[176,512]{1,0:T(8,128)(2,1)S(1)} %concatenate.34.refs_0_), channel_id=1, source_target_pairs={{0,6},{1,7},{2,4},{3,5},{4,2},{5,3},{6,0},{7,1},{8,14},{9,15},{10,... | collective-permute-start | bytes 540680 | tf_op jit(solution)/shard_map/ppermute | solution.py:531
  74.6 2.9 %new_states.1 = (f32[1024,128]{1,0:T(8,128)}, f32[1024,128]{1,0:T(8,128)}) custom-call(bf16[32,72,128]{2,1,0:T(8,128)(2,1)S(1)} %all-to-all-done.got_ref, f32[32,128]{1,0:T(8,128)S(1)} %convert_add_fusion.res_ref, f32[1024,128]{1,0:T(8,128)S(1)} %copy-done.3, f32[1024,128]{1,0:T(8,128)S(1)} %copy-done.5), custom_call_target="tpu_custom_call" | custom-call | flops 1073741824 | bytes 4194304 | tf_op jit(solution)/shard_map/new_states/pallas_call | solution.py:445
  78.0 0.9 %collective-permute-done.14.refs_2_ = bf16[176,512]{1,0:T(8,128)(2,1)S(1)} collective-permute-done((bf16[176,512]{1,0:T(8,128)(2,1)S(1)}, bf16[176,512]{1,0:T(8,128)(2,1)S(1)}, u32[]{:S(2)}, u32[]{:S(2)}) %collective-permute-start.14) | collective-permute-done | bytes 180256 | tf_op jit(solution)/shard_map/ppermute | solution.py:531
  79.5 1.2 %place.2 = (f32[1024,512]{1,0:T(8,128)}, f32[512,256]{1,0:T(8,128)}, f32[2,512]{1,0:T(2,128)S(1)}) custom-call(bf16[176,512]{1,0:T(8,128)(2,1)S(1)} %concatenate.34.refs_0_, bf16[176,512]{1,0:T(8,128)(2,1)S(1)} %collective-permute-done.12.refs_1_, bf16[176,512]{1,0:T(8,128)(2,1)S(1)} %collective-permute-done.14.refs_2_, ...), custom_call_target="tpu_custom_call" | custom-call | flops 131072 | bytes 2097152 | tf_op jit(solution)/shard_map/place/pallas_call | solution.py:506
  80.7 1.2 %place.3 = (f32[1024,512]{1,0:T(8,128)}, f32[512,256]{1,0:T(8,128)}, f32[1,512]{1,0:T(1,128)}, f32[1,256]{1,0:T(1,128)}, f32[1,256]{1,0:T(1,128)}) custom-call(bf16[176,512]{1,0:T(8,128)(2,1)S(1)} %collective-permute-done.11.refs_0_, bf16[176,512]{1,0:T(8,128)(2,1)S(1)} %collective-permute-done.13.refs_1_, ...), custom_call_target="tpu_custom_call", output_to_operand_aliasing={{0}: (4, {}), {1}: (5, {})} | custom-call | flops 131072 | bytes 2097152 | tf_op jit(solution)/shard_map/place/pallas_call | solution.py:506
  (88 shorter events, 3.6 us)
Async XLA Ops:
  0.6 9.2 %copy-start.10 = (bf16[256]{0:T(256)(128)(2,1)S(1)}, bf16[256]{0:T(256)(128)(2,1)}, u32[]{:S(2)}) copy-start(bf16[256]{0:T(256)(128)(2,1)} %param.25) | copy-start | bytes 1540
  2.5 24.0 %all-to-all-start = ((bf16[32,72,128]{2,1,0:T(8,128)(2,1)}), bf16[32,72,128]{2,1,0:T(8,128)(2,1)S(1)}, u32[]{:S(2)}, u32[]{:S(2)}) async-start(bf16[32,72,128]{2,1,0:T(8,128)(2,1)} %pack.1), calls=%async_computation | async-start | bytes 1179648 | tf_op jit(solution)/shard_map/all_to_all | solution.py:527
  18.3 19.9 %copy-start = (bf16[512,1024]{1,0:T(8,128)(2,1)S(1)}, bf16[512,1024]{1,0:T(8,128)(2,1)}, u32[]{:S(2)}) copy-start(bf16[512,1024]{1,0:T(8,128)(2,1)} %get-tuple-element.47.q) | copy-start | bytes 3145732
  18.3 19.9 %copy-start.1 = (bf16[256,1024]{1,0:T(8,128)(2,1)S(1)}, bf16[256,1024]{1,0:T(8,128)(2,1)}, u32[]{:S(2)}) copy-start(bf16[256,1024]{1,0:T(8,128)(2,1)} %get-tuple-element.46.s2) | copy-start | bytes 1572868
  18.3 1.2 %copy-start.2 = (f32[1024,128]{1,0:T(8,128)S(1)}, f32[1024,128]{1,0:T(8,128)}, u32[]{:S(2)}) copy-start(f32[1024,128]{1,0:T(8,128)} %z_ref.2) | copy-start | bytes 1572868
  19.5 1.0 %copy-start.4 = (f32[1024,128]{1,0:T(8,128)S(1)}, f32[1024,128]{1,0:T(8,128)}, u32[]{:S(2)}) copy-start(f32[1024,128]{1,0:T(8,128)} %n_ref.2) | copy-start | bytes 1572868
  20.5 17.7 %copy-start.7 = (s32[32,64]{1,0:T(8,128)S(1)}, s32[32,64]{1,0:T(8,128)}, u32[]{:S(2)}) copy-start(s32[32,64]{1,0:T(8,128)} %example_ref.1) | copy-start | bytes 24580
  20.5 17.7 %copy-start.8 = (s32[1024]{0:T(1024)S(1)}, s32[1024]{0:T(1024)}, u32[]{:S(2)}) copy-start(s32[1024]{0:T(1024)} %param.14) | copy-start | bytes 12292
  20.5 17.7 %copy-start.9 = (f32[1,1024]{1,0:T(1,128)S(1)}, f32[1,1024]{1,0:T(1,128)}, u32[]{:S(2)}) copy-start(f32[1,1024]{1,0:T(1,128)} %get-tuple-element.45.deep_ref) | copy-start | bytes 12292
  41.0 2.8 %collective-permute-start = (bf16[640,512]{1,0:T(8,128)(2,1)S(1)}, bf16[640,512]{1,0:T(8,128)(2,1)S(1)}, u32[]{:S(2)}, u32[]{:S(2)}) collective-permute-start(bf16[640,512]{1,0:T(8,128)(2,1)S(1)} %get-tuple-element.52), channel_id=1, source_target_pairs={{0,1},{1,0},{2,3},{3,2},{4,5},{5,4},{6,7},{7,6},{8,9},{9,8},{10,11... | collective-permute-start | bytes 1966088 | tf_op jit(solution)/shard_map/ppermute | solution.py:531
  43.8 11.9 %copy-start.6 = (bf16[256,1024]{1,0:T(8,128)(2,1)S(1)}, bf16[256,1024]{1,0:T(8,128)(2,1)}, u32[]{:S(2)}) copy-start(bf16[256,1024]{1,0:T(8,128)(2,1)} %get-tuple-element.58.h2) | copy-start | bytes 1572868
  44.0 30.6 %copy-start.3 = (f32[1024,128]{1,0:T(8,128)S(1)}, f32[1024,128]{1,0:T(8,128)}, u32[]{:S(2)}) copy-start(f32[1024,128]{1,0:T(8,128)} %z_ref.2) | copy-start | bytes 1572868
  44.0 30.5 %copy-start.5 = (f32[1024,128]{1,0:T(8,128)S(1)}, f32[1024,128]{1,0:T(8,128)}, u32[]{:S(2)}) copy-start(f32[1024,128]{1,0:T(8,128)} %n_ref.2) | copy-start | bytes 1572868
  44.1 5.3 %collective-permute-start.4 = (bf16[84,512]{1,0:T(8,128)(2,1)S(1)}, bf16[84,512]{1,0:T(8,128)(2,1)S(1)}, u32[]{:S(2)}, u32[]{:S(2)}) collective-permute-start(bf16[84,512]{1,0:T(8,128)(2,1)S(1)} %pad_maximum_fusion.1), channel_id=1, source_target_pairs={{0,2},{1,3},{2,0},{3,1},{4,6},{5,7},{6,4},{7,5},{8,10},{9,11},{10,... | collective-permute-start | bytes 258056 | tf_op jit(solution)/shard_map/ppermute | solution.py:531
  44.7 6.6 %collective-permute-start.5 = (bf16[84,512]{1,0:T(8,128)(2,1)S(1)}, bf16[84,512]{1,0:T(8,128)(2,1)S(1)}, u32[]{:S(2)}, u32[]{:S(2)}) collective-permute-start(bf16[84,512]{1,0:T(8,128)(2,1)S(1)} %pad_maximum_fusion.2), channel_id=1, source_target_pairs={{0,4},{1,5},{2,6},{3,7},{4,0},{5,1},{6,2},{7,3},{8,12},{9,13},{10,... | collective-permute-start | bytes 258056 | tf_op jit(solution)/shard_map/ppermute | solution.py:531
  45.4 5.9 %collective-permute-start.6 = (bf16[84,512]{1,0:T(8,128)(2,1)S(1)}, bf16[84,512]{1,0:T(8,128)(2,1)S(1)}, u32[]{:S(2)}, u32[]{:S(2)}) collective-permute-start(bf16[84,512]{1,0:T(8,128)(2,1)S(1)} %pad_maximum_fusion.3), channel_id=1, source_target_pairs={{0,6},{1,7},{2,4},{3,5},{4,2},{5,3},{6,0},{7,1},{8,14},{9,15},{10,... | collective-permute-start | bytes 258056 | tf_op jit(solution)/shard_map/ppermute | solution.py:531
  51.5 4.6 %collective-permute-start.7 = (bf16[88,512]{1,0:T(8,128)(2,1)S(1)}, bf16[88,512]{1,0:T(8,128)(2,1)S(1)}, u32[]{:S(2)}, u32[]{:S(2)}) collective-permute-start(bf16[88,512]{1,0:T(8,128)(2,1)S(1)} %pad_maximum_fusion.4), channel_id=1, source_target_pairs={{0,8},{1,9},{2,10},{3,11},{4,12},{5,13},{6,14},{7,15},{8,0},{9,1},... | collective-permute-start | bytes 270344 | tf_op jit(solution)/shard_map/ppermute | solution.py:531
  52.2 5.5 %collective-permute-start.3 = (bf16[80,512]{1,0:T(8,128)(2,1)S(1)}, bf16[80,512]{1,0:T(8,128)(2,1)S(1)}, u32[]{:S(2)}, u32[]{:S(2)}) collective-permute-start(bf16[80,512]{1,0:T(8,128)(2,1)S(1)} %get-tuple-element.75), channel_id=1, source_target_pairs={{0,6},{1,7},{2,4},{3,5},{4,2},{5,3},{6,0},{7,1},{8,14},{9,15},{10,... | collective-permute-start | bytes 245768 | tf_op jit(solution)/shard_map/ppermute | solution.py:531
  54.1 4.5 %collective-permute-start.2 = (bf16[80,512]{1,0:T(8,128)(2,1)S(1)}, bf16[80,512]{1,0:T(8,128)(2,1)S(1)}, u32[]{:S(2)}, u32[]{:S(2)}) collective-permute-start(bf16[80,512]{1,0:T(8,128)(2,1)S(1)} %get-tuple-element.76), channel_id=1, source_target_pairs={{0,4},{1,5},{2,6},{3,7},{4,0},{5,1},{6,2},{7,3},{8,12},{9,13},{10,... | collective-permute-start | bytes 245768 | tf_op jit(solution)/shard_map/ppermute | solution.py:531
  55.1 4.4 %collective-permute-start.1 = (bf16[80,512]{1,0:T(8,128)(2,1)S(1)}, bf16[80,512]{1,0:T(8,128)(2,1)S(1)}, u32[]{:S(2)}, u32[]{:S(2)}) collective-permute-start(bf16[80,512]{1,0:T(8,128)(2,1)S(1)} %get-tuple-element.77), channel_id=1, source_target_pairs={{0,2},{1,3},{2,0},{3,1},{4,6},{5,7},{6,4},{7,5},{8,10},{9,11},{10,... | collective-permute-start | bytes 245768 | tf_op jit(solution)/shard_map/ppermute | solution.py:531
  59.7 6.6 %collective-permute-start.8 = (bf16[92,512]{1,0:T(8,128)(2,1)S(1)}, bf16[92,512]{1,0:T(8,128)(2,1)S(1)}, u32[]{:S(2)}, u32[]{:S(2)}) collective-permute-start(bf16[92,512]{1,0:T(8,128)(2,1)S(1)} %pad_maximum_fusion), channel_id=1, source_target_pairs={{0,16},{1,17},{2,18},{3,19},{4,20},{5,21},{6,22},{7,23},{8,24},{9,... | collective-permute-start | bytes 282632 | tf_op jit(solution)/shard_map/ppermute | solution.py:531
  66.3 4.6 %collective-permute-start.9 = (bf16[88,512]{1,0:T(8,128)(2,1)S(1)}, bf16[88,512]{1,0:T(8,128)(2,1)S(1)}, u32[]{:S(2)}, u32[]{:S(2)}) collective-permute-start(bf16[88,512]{1,0:T(8,128)(2,1)S(1)} %pad_maximum_fusion.5), channel_id=1, source_target_pairs={{0,8},{1,9},{2,10},{3,11},{4,12},{5,13},{6,14},{7,15},{8,0},{9,1},... | collective-permute-start | bytes 270344 | tf_op jit(solution)/shard_map/ppermute | solution.py:531
  67.0 7.6 %collective-permute-start.10 = (bf16[16,256]{1,0:T(8,128)(2,1)S(1)}, bf16[16,256]{1,0:T(8,128)(2,1)S(1)}, u32[]{:S(2)}, u32[]{:S(2)}) collective-permute-start(bf16[16,256]{1,0:T(8,128)(2,1)S(1)} %bitcast.36), channel_id=1, source_target_pairs={{0,1},{1,0},{2,3},{3,2},{4,5},{5,4},{6,7},{7,6},{8,9},{9,8},{10,11... | collective-permute-start | bytes 24584 | tf_op jit(solution)/shard_map/ppermute | solution.py:531
  71.0 6.5 %collective-permute-start.12 = (bf16[176,512]{1,0:T(8,128)(2,1)S(1)}, bf16[176,512]{1,0:T(8,128)(2,1)S(1)}, u32[]{:S(2)}, u32[]{:S(2)}) collective-permute-start(bf16[176,512]{1,0:T(8,128)(2,1)S(1)} %concatenate.34.refs_0_), channel_id=1, source_target_pairs={{0,2},{1,3},{2,0},{3,1},{4,6},{5,7},{6,4},{7,5},{8,10},{9,11},{10,... | collective-permute-start | bytes 540680 | tf_op jit(solution)/shard_map/ppermute | solution.py:531
  71.1 7.9 %collective-permute-start.14 = (bf16[176,512]{1,0:T(8,128)(2,1)S(1)}, bf16[176,512]{1,0:T(8,128)(2,1)S(1)}, u32[]{:S(2)}, u32[]{:S(2)}) collective-permute-start(bf16[176,512]{1,0:T(8,128)(2,1)S(1)} %concatenate.34.refs_0_), channel_id=1, source_target_pairs={{0,4},{1,5},{2,6},{3,7},{4,0},{5,1},{6,2},{7,3},{8,12},{9,13},{10,... | collective-permute-start | bytes 540680 | tf_op jit(solution)/shard_map/ppermute | solution.py:531
  71.9 7.1 %collective-permute-start.16 = (bf16[176,512]{1,0:T(8,128)(2,1)S(1)}, bf16[176,512]{1,0:T(8,128)(2,1)S(1)}, u32[]{:S(2)}, u32[]{:S(2)}) collective-permute-start(bf16[176,512]{1,0:T(8,128)(2,1)S(1)} %concatenate.34.refs_0_), channel_id=1, source_target_pairs={{0,6},{1,7},{2,4},{3,5},{4,2},{5,3},{6,0},{7,1},{8,14},{9,15},{10,... | collective-permute-start | bytes 540680 | tf_op jit(solution)/shard_map/ppermute | solution.py:531
  77.5 3.2 %collective-permute-start.11 = (bf16[176,512]{1,0:T(8,128)(2,1)S(1)}, bf16[176,512]{1,0:T(8,128)(2,1)S(1)}, u32[]{:S(2)}, u32[]{:S(2)}) collective-permute-start(bf16[176,512]{1,0:T(8,128)(2,1)S(1)} %concatenate.34.refs_0_), channel_id=1, source_target_pairs={{0,1},{1,0},{2,3},{3,2},{4,5},{5,4},{6,7},{7,6},{8,9},{9,8},{10,11... | collective-permute-start | bytes 540680 | tf_op jit(solution)/shard_map/ppermute | solution.py:531
  77.5 3.2 %collective-permute-start.13 = (bf16[176,512]{1,0:T(8,128)(2,1)S(1)}, bf16[176,512]{1,0:T(8,128)(2,1)S(1)}, u32[]{:S(2)}, u32[]{:S(2)}) collective-permute-start(bf16[176,512]{1,0:T(8,128)(2,1)S(1)} %collective-permute-done.12.refs_1_), channel_id=1, source_target_pairs={{0,1},{1,0},{2,3},{3,2},{4,5},{5,4},{6,7},{7,6},{8,9},{9,8},{10,11... | collective-permute-start | bytes 540680 | tf_op jit(solution)/shard_map/ppermute | solution.py:531
  79.0 1.7 %collective-permute-start.15 = (bf16[176,512]{1,0:T(8,128)(2,1)S(1)}, bf16[176,512]{1,0:T(8,128)(2,1)S(1)}, u32[]{:S(2)}, u32[]{:S(2)}) collective-permute-start(bf16[176,512]{1,0:T(8,128)(2,1)S(1)} %collective-permute-done.14.refs_2_), channel_id=1, source_target_pairs={{0,1},{1,0},{2,3},{3,2},{4,5},{5,4},{6,7},{7,6},{8,9},{9,8},{10,11... | collective-permute-start | bytes 540680 | tf_op jit(solution)/shard_map/ppermute | solution.py:531
  79.0 1.7 %collective-permute-start.17 = (bf16[176,512]{1,0:T(8,128)(2,1)S(1)}, bf16[176,512]{1,0:T(8,128)(2,1)S(1)}, u32[]{:S(2)}, u32[]{:S(2)}) collective-permute-start(bf16[176,512]{1,0:T(8,128)(2,1)S(1)} %collective-permute-done.16.refs_3_), channel_id=1, source_target_pairs={{0,1},{1,0},{2,3},{3,2},{4,5},{5,4},{6,7},{7,6},{8,9},{9,8},{10,11... | collective-permute-start | bytes 540680 | tf_op jit(solution)/shard_map/ppermute | solution.py:531

commit v7 on v6

--- a/solution.py
+++ b/solution.py
@@ -143,8 +143,8 @@
     deep_ref[...] = dot(jnp.broadcast_to(head, (16, head.shape[1])), h2)[0:1]
     s2 = to_column(head.astype(f32)) * (gate2 * (1.0 + pre2 * (1.0 - gate2)))
     s2 = s2.astype(bf16)
-    s2_ref[...] = s2
-    q_ref[...] = (dot(w2_ref[...], s2) * slope1).astype(bf16)
+    s2_ref[...] = jnp.transpose(s2)
+    q_ref[...] = jnp.transpose((dot(w2_ref[...], s2) * slope1).astype(bf16))
 
 
 def tower(dense, w1, b1, w2, b2, head):
@@ -154,6 +154,7 @@
     be = ex // steps
     whole = lambda a: pl.BlockSpec(a.shape, lambda i: (0, 0))
     cols = lambda rows: pl.BlockSpec((rows, be), lambda i: (0, i))
+    down = lambda width: pl.BlockSpec((be, width), lambda i: (i, 0))
     b1, b2, head = b1.reshape(1, h1), b2.reshape(1, h2), head.reshape(1, h2)
     return pl.pallas_call(
         tower_kernel,
@@ -161,15 +162,15 @@
         out_shape=(
             jax.ShapeDtypeStruct((din + h1 + h2, ex), bf16),
             jax.ShapeDtypeStruct((h2, ex), bf16),
-            jax.ShapeDtypeStruct((h2, ex), bf16),
-            jax.ShapeDtypeStruct((h1, ex), bf16),
+            jax.ShapeDtypeStruct((ex, h2), bf16),
+            jax.ShapeDtypeStruct((ex, h1), bf16),
             jax.ShapeDtypeStruct((1, ex), f32),
         ),
         in_specs=[
             pl.BlockSpec((be, din), lambda i: (i, 0)),
             whole(w1), whole(b1), whole(w2), whole(b2), whole(head),
         ],
-        out_specs=(cols(din + h1 + h2), cols(h2), cols(h2), cols(h1), cols(1)),
+        out_specs=(cols(din + h1 + h2), cols(h2), down(h2), down(h1), cols(1)),
         scratch_shapes=[pltpu.VMEM((h1, din), bf16), pltpu.VMEM((h2, h1), bf16)],
         compiler_params=params(62),
         cost_estimate=pl.CostEstimate(
@@ -254,17 +255,22 @@
 
 def half_gradients(residual, copies, s2, q, dense_t, h1, target):
     rows, first = residual.shape[0], (dense_t.shape[0] - ONES) // EIGHTHS
-    packed, width = (h1.shape[0] - ONES) // 2 // EIGHTHS, s2.shape[0]
+    packed, width = (h1.shape[0] - ONES) // 2 // EIGHTHS, s2.shape[1]
     each = first + packed
     dense_t[EIGHTHS * first :, :] = jnp.ones((ONES, dense_t.shape[1]), bf16)
     h1[2 * EIGHTHS * packed :, :] = jnp.ones((ONES, h1.shape[1]), bf16)
-    dlogit = jnp.concatenate([residual[k : k + 1] for k in range(rows)], axis=1).astype(bf16)
-    scale = dlogit.astype(f32)
-    d_two = (s2[...].astype(f32) * scale).astype(bf16)
-    d_one = (q[...].astype(f32) * scale).astype(bf16)
+    scale = jnp.transpose(residual.astype(bf16).astype(f32))
+
+    def scaled(a):
+        parts = [
+            (a[k * LANES : (k + 1) * LANES, :].astype(f32) * scale[:, k : k + 1]).astype(bf16) for k in range(rows)
+        ]
+        return jnp.concatenate(parts, axis=0)
+
+    d_two, d_one = scaled(s2), scaled(q)
     copies[0].wait()
     copies[1].wait()
-    second = dot(h1[...], d_two, NT)
+    second = dot(h1[...], d_two)
     b_two = second[2 * EIGHTHS * packed : 2 * EIGHTHS * packed + 1]
     second = second.astype(bf16)
     for k in range(EIGHTHS):
@@ -273,12 +279,12 @@
         target[k * each + first : (k + 1) * each, width:] = second[low : low + packed]
     for copy in copies[2:]:
         copy.wait()
-    made = dot(dense_t[...], d_one, NT)
+    made = dot(dense_t[...], d_one)
     b_one = made[EIGHTHS * first : EIGHTHS * first + 1]
     made = made.astype(bf16)
     for k in range(EIGHTHS):
         target[k * each : k * each + first, :] = made[k * first : (k + 1) * first]
-    return dlogit, b_one, b_two
+    return b_one, b_two
 
 
 def half_scratch(big, n1):
@@ -348,8 +354,8 @@
 def residuals(logits, example, deep, labels, s2, q, big):
     lists, cap = example.shape
     rows = deep.shape[1] // LANES
-    n1 = q.shape[0]
-    half = (big.shape[0] - n1 - s2.shape[0]) // 2 + n1 // 4
+    n1 = q.shape[1]
+    half = (big.shape[0] - n1 - s2.shape[1]) // 2 + n1 // 4
     return pl.pallas_call(
         residual_kernel,
         out_shape=(
@@ -377,14 +383,14 @@
     copies = half_copies(core, big_any, dense_t, h1, sems)
     for copy in copies:
         copy.start()
-    _, b_one, b_two = half_gradients(residual_ref[...], copies, s2, q, dense_t, h1, keep_ref)
+    b_one, b_two = half_gradients(residual_ref[...], copies, s2, q, dense_t, h1, keep_ref)
     small = jnp.concatenate([b_one, jnp.concatenate([b_two, jnp.zeros_like(b_two)], axis=1)], axis=0)
     small_ref[...] = jnp.concatenate(split_two(small), axis=0)
 
 
 def gradients(residual, s2, q, big):
-    n1, ex = q.shape
-    half = (big.shape[0] - n1 - s2.shape[0]) // 2 + n1 // 4
+    ex, n1 = q.shape
+    half = (big.shape[0] - n1 - s2.shape[1]) // 2 + n1 // 4
     return pl.pallas_call(
         gradient_kernel,
         out_shape=(jax.ShapeDtypeStruct((half, n1), bf16), jax.ShapeDtypeStruct((4, n1), bf16)),

time: 82.3 us -> 82 us (level)
  no operation moved by 1% of the time
where the time goes in v7:
time: 82 us; the launch traced here: 81.7 us
  waiting for transfers between devices  23.3 us (28%)
  Pallas kernels  22.2 us (27%)
  starting transfers between devices  21 us (26%)
  blocking collectives  10.3 us (13%)
  local copies, waits for them, and re-layouts  3.24 us (4%)
  between operations  1.17 us (1%)
    ppermute x18, waiting for transfers between devices, swap(): return lax.ppermute(x, AXES, [(i, i ^ bit) for i in range(devices)])  17.8 us
    ppermute x18, starting transfers between devices, swap(): return lax.ppermute(x, AXES, [(i, i ^ bit) for i in range(devices)])  13.7 us
    all_to_all x1, blocking collectives, every_to_every(): return lax.all_to_all(x, AXES, split_axis=0, concat_axis=0, tiled=True)  10.3 us
    pallas_call x1, Pallas kernels, tower(): pl.pallas_call(tower_kernel, grid=(steps,), out_shape=(jax.ShapeDtypeStru...  8.06 us
    all_to_all x1, starting transfers between devices, every_to_every(): return lax.all_to_all(x, AXES, split_axis=0, concat_axis=0, tiled=True)  7.3 us
    all_to_all x1, waiting for transfers between devices, every_to_every(): return lax.all_to_all(x, AXES, split_axis=0, concat_axis=0, tiled=True)  5.42 us
    pallas_call x1, Pallas kernels, new_states(): pl.pallas_call(state_kernel, out_shape=(jax.ShapeDtypeStruct(z.shape, f32...  2.94 us
    pallas_call x1, Pallas kernels, residuals(): pl.pallas_call(residual_kernel, out_shape=(jax.ShapeDtypeStruct((rows, LA...  2.54 us
  transfers between devices with their start and end apart: 19, of which 10 were waited for; matrix products, arithmetic and copies ran while one was open for 1% of the time, Pallas kernels for 19%

profile of v7, /device:TPU:0, one launch (start us, length us, event | category | flops | bytes accessed | tf_op | source)
XLA Modules:
  0.0 81.7 jit_solution(6935848104385890509)
XLA Ops:
  0.6 1.9 %pack.1 = bf16[32,72,128]{2,1,0:T(8,128)(2,1)} custom-call(bf16[32,64,128]{2,1,0:T(8,128)(2,1)} %values_any.1, s32[32,64]{1,0:T(8,128)} %block_any.1, s32[1,32]{1,0:T(1,128)} %bitcast.37), custom_call_target="tpu_custom_call" | custom-call | tf_op jit(solution)/shard_map/pack/pallas_call | solution.py:99
  2.5 7.3 %all-to-all-start = ((bf16[32,72,128]{2,1,0:T(8,128)(2,1)}), bf16[32,72,128]{2,1,0:T(8,128)(2,1)S(1)}, u32[]{:S(2)}, u32[]{:S(2)}) async-start(bf16[32,72,128]{2,1,0:T(8,128)(2,1)} %pack.1), calls=%async_computation | async-start | bytes 1179648 | tf_op jit(solution)/shard_map/all_to_all | solution.py:533
  9.8 0.6 reshape.62.head_ref
  10.4 8.1 %tower.1 = (bf16[1792,1024]{1,0:T(8,128)(2,1)}, bf16[256,1024]{1,0:T(8,128)(2,1)}, bf16[1024,256]{1,0:T(8,128)(2,1)}, bf16[1024,512]{1,0:T(8,128)(2,1)}, f32[1,1024]{1,0:T(1,128)}) custom-call(bf16[1024,1024]{1,0:T(8,128)(2,1)} %dense_ref.1, bf16[1024,512]{1,0:T(8,128)(2,1)} %w1_ref.1, f32[1,512]{1,0:T(1,128)} %bitcast.39, bf16[512,256]{1,0:T(8,128)(2,1)} %w2_ref.1, ...), custom_call_target="tpu_custom_call" | custom-call | flops 1610612736 | bytes 12582912 | tf_op jit(solution)/shard_map/tower/pallas_call | solution.py:159
  18.5 1.1 %copy-done.2 = f32[1024,128]{1,0:T(8,128)S(1)} copy-done((f32[1024,128]{1,0:T(8,128)S(1)}, f32[1024,128]{1,0:T(8,128)}, u32[]{:S(2)}) %copy-start.2) | copy-done | bytes 524312
  19.7 1.0 %copy-done.4 = f32[1024,128]{1,0:T(8,128)S(1)} copy-done((f32[1024,128]{1,0:T(8,128)S(1)}, f32[1024,128]{1,0:T(8,128)}, u32[]{:S(2)}) %copy-start.4) | copy-done | bytes 524312
  21.1 5.4 %all-to-all-done.got_ref = bf16[32,72,128]{2,1,0:T(8,128)(2,1)S(1)} async-done(((bf16[32,72,128]{2,1,0:T(8,128)(2,1)}), bf16[32,72,128]{2,1,0:T(8,128)(2,1)S(1)}, u32[]{:S(2)}, u32[]{:S(2)}) %all-to-all-start) | async-done | bytes 589856 | tf_op jit(solution)/shard_map/all_to_all | solution.py:533
  26.6 1.3 %slot_logits.1 = f32[32,1,128]{2,1,0:T(1,128)S(1)} custom-call(bf16[32,72,128]{2,1,0:T(8,128)(2,1)S(1)} %all-to-all-done.got_ref, bf16[1024,256]{1,0:T(8,128)(2,1)S(1)} %weights.1.wcat_ref), custom_call_target="tpu_custom_call" | custom-call | tf_op jit(solution)/shard_map/slot_logits/pallas_call | solution.py:224
  27.9 10.3 %all_to_all.10.logit_any = f32[32,1,128]{2,1,0:T(1,128)S(1)} all-to-all(f32[32,1,128]{2,1,0:T(1,128)S(1)} %slot_logits.1), channel_id=1, replica_groups=mesh['blk'=8,'rep'=4] {'blk','rep'}, dimensions={0} | all-to-all | bytes 32768 | tf_op jit(solution)/shard_map/all_to_all | solution.py:533
  38.2 2.5 %residuals.1 = (f32[8,128]{1,0:T(8,128)}, f32[8,128]{1,0:T(8,128)S(1)}, bf16[640,512]{1,0:T(8,128)(2,1)S(1)}, bf16[16,512]{1,0:T(8,128)(2,1)S(1)}) custom-call(f32[32,1,128]{2,1,0:T(1,128)S(1)} %all_to_all.10.logit_any, s32[32,64]{1,0:T(8,128)S(1)} %copy-done.7, f32[1,1024]{1,0:T(1,128)S(1)} %copy-done.9, s32[8,128]{1,0:T(8,128)S(1)} %bitcast.31, ...), custom_call_target="tpu_custom_call" | custom-call | tf_op jit(solution)/shard_map/residuals/pallas_call | solution.py:359
  41.1 2.4 %gradients.1 = (bf16[640,512]{1,0:T(8,128)(2,1)S(1)}, bf16[4,512]{1,0:T(4,128)(2,1)S(1)}) custom-call(f32[8,128]{1,0:T(8,128)S(1)} %get-tuple-element.56.residual_ref, bf16[1024,256]{1,0:T(8,128)(2,1)S(1)} %copy-done.1, bf16[1024,512]{1,0:T(8,128)(2,1)S(1)} %copy-done, bf16[1792,1024]{1,0:T(8,128)(2,1)} %get-tuple-element.48.big_any), custom_call_target="tpu_custom_call" | custom-call | flops 671088640 | bytes 6291456 | tf_op jit(solution)/shard_map/gradients/pallas_call | solution.py:394
  43.8 0.6 collective-permute-start.4
  44.4 0.7 collective-permute-start.5
  45.1 2.4 %collective-permute-start.6 = (bf16[84,512]{1,0:T(8,128)(2,1)S(1)}, bf16[84,512]{1,0:T(8,128)(2,1)S(1)}, u32[]{:S(2)}, u32[]{:S(2)}) collective-permute-start(bf16[84,512]{1,0:T(8,128)(2,1)S(1)} %pad_maximum_fusion.3), channel_id=1, source_target_pairs={{0,6},{1,7},{2,4},{3,5},{4,2},{5,3},{6,0},{7,1},{8,14},{9,15},{10,... | collective-permute-start | bytes 258056 | tf_op jit(solution)/shard_map/ppermute | solution.py:537
  47.5 1.6 %collective-permute-done.4 = bf16[84,512]{1,0:T(8,128)(2,1)S(1)} collective-permute-done((bf16[84,512]{1,0:T(8,128)(2,1)S(1)}, bf16[84,512]{1,0:T(8,128)(2,1)S(1)}, u32[]{:S(2)}, u32[]{:S(2)}) %collective-permute-start.4) | collective-permute-done | bytes 86048 | tf_op jit(solution)/shard_map/ppermute | solution.py:537
  49.1 1.9 %collective-permute-done.5 = bf16[84,512]{1,0:T(8,128)(2,1)S(1)} collective-permute-done((bf16[84,512]{1,0:T(8,128)(2,1)S(1)}, bf16[84,512]{1,0:T(8,128)(2,1)S(1)}, u32[]{:S(2)}, u32[]{:S(2)}) %collective-permute-start.5) | collective-permute-done | bytes 86048 | tf_op jit(solution)/shard_map/ppermute | solution.py:537
  51.3 0.6 collective-permute-start.7
  51.9 1.9 %collective-permute-start.3 = (bf16[80,512]{1,0:T(8,128)(2,1)S(1)}, bf16[80,512]{1,0:T(8,128)(2,1)S(1)}, u32[]{:S(2)}, u32[]{:S(2)}) collective-permute-start(bf16[80,512]{1,0:T(8,128)(2,1)S(1)} %get-tuple-element.75), channel_id=1, source_target_pairs={{0,6},{1,7},{2,4},{3,5},{4,2},{5,3},{6,0},{7,1},{8,14},{9,15},{10,... | collective-permute-start | bytes 245768 | tf_op jit(solution)/shard_map/ppermute | solution.py:537
  53.8 1.1 %collective-permute-start.2 = (bf16[80,512]{1,0:T(8,128)(2,1)S(1)}, bf16[80,512]{1,0:T(8,128)(2,1)S(1)}, u32[]{:S(2)}, u32[]{:S(2)}) collective-permute-start(bf16[80,512]{1,0:T(8,128)(2,1)S(1)} %get-tuple-element.76), channel_id=1, source_target_pairs={{0,4},{1,5},{2,6},{3,7},{4,0},{5,1},{6,2},{7,3},{8,12},{9,13},{10,... | collective-permute-start | bytes 245768 | tf_op jit(solution)/shard_map/ppermute | solution.py:537
  56.0 1.4 %collective-permute-done.3 = bf16[80,512]{1,0:T(8,128)(2,1)S(1)} collective-permute-done((bf16[80,512]{1,0:T(8,128)(2,1)S(1)}, bf16[80,512]{1,0:T(8,128)(2,1)S(1)}, u32[]{:S(2)}, u32[]{:S(2)}) %collective-permute-start.3) | collective-permute-done | bytes 81952 | tf_op jit(solution)/shard_map/ppermute | solution.py:537
  57.4 0.9 %collective-permute-done.2 = bf16[80,512]{1,0:T(8,128)(2,1)S(1)} collective-permute-done((bf16[80,512]{1,0:T(8,128)(2,1)S(1)}, bf16[80,512]{1,0:T(8,128)(2,1)S(1)}, u32[]{:S(2)}, u32[]{:S(2)}) %collective-permute-start.2) | collective-permute-done | bytes 81952 | tf_op jit(solution)/shard_map/ppermute | solution.py:537
  58.3 1.0 %collective-permute-done.1 = bf16[80,512]{1,0:T(8,128)(2,1)S(1)} collective-permute-done((bf16[80,512]{1,0:T(8,128)(2,1)S(1)}, bf16[80,512]{1,0:T(8,128)(2,1)S(1)}, u32[]{:S(2)}, u32[]{:S(2)}) %collective-permute-start.1) | collective-permute-done | bytes 81952 | tf_op jit(solution)/shard_map/ppermute | solution.py:537
  59.4 0.6 collective-permute-start.8
  60.0 6.0 %collective-permute-done.8 = bf16[92,512]{1,0:T(8,128)(2,1)S(1)} collective-permute-done((bf16[92,512]{1,0:T(8,128)(2,1)S(1)}, bf16[92,512]{1,0:T(8,128)(2,1)S(1)}, u32[]{:S(2)}, u32[]{:S(2)}) %collective-permute-start.8) | collective-permute-done | bytes 94240 | tf_op jit(solution)/shard_map/ppermute | solution.py:537
  66.1 0.6 collective-permute-start.9
  66.8 3.9 %collective-permute-done.9 = bf16[88,512]{1,0:T(8,128)(2,1)S(1)} collective-permute-done((bf16[88,512]{1,0:T(8,128)(2,1)S(1)}, bf16[88,512]{1,0:T(8,128)(2,1)S(1)}, u32[]{:S(2)}, u32[]{:S(2)}) %collective-permute-start.9) | collective-permute-done | bytes 90144 | tf_op jit(solution)/shard_map/ppermute | solution.py:537
  70.8 0.8 collective-permute-start.14
  71.6 2.7 %collective-permute-start.16 = (bf16[176,512]{1,0:T(8,128)(2,1)S(1)}, bf16[176,512]{1,0:T(8,128)(2,1)S(1)}, u32[]{:S(2)}, u32[]{:S(2)}) collective-permute-start(bf16[176,512]{1,0:T(8,128)(2,1)S(1)} %concatenate.34.refs_0_), channel_id=1, source_target_pairs={{0,6},{1,7},{2,4},{3,5},{4,2},{5,3},{6,0},{7,1},{8,14},{9,15},{10,... | collective-permute-start | bytes 540680 | tf_op jit(solution)/shard_map/ppermute | solution.py:537
  74.3 2.9 %new_states.1 = (f32[1024,128]{1,0:T(8,128)}, f32[1024,128]{1,0:T(8,128)}) custom-call(bf16[32,72,128]{2,1,0:T(8,128)(2,1)S(1)} %all-to-all-done.got_ref, f32[32,128]{1,0:T(8,128)S(1)} %convert_add_fusion.res_ref, f32[1024,128]{1,0:T(8,128)S(1)} %copy-done.3, f32[1024,128]{1,0:T(8,128)S(1)} %copy-done.5), custom_call_target="tpu_custom_call" | custom-call | flops 1073741824 | bytes 4194304 | tf_op jit(solution)/shard_map/new_states/pallas_call | solution.py:451
  77.8 0.9 %collective-permute-done.14.refs_2_ = bf16[176,512]{1,0:T(8,128)(2,1)S(1)} collective-permute-done((bf16[176,512]{1,0:T(8,128)(2,1)S(1)}, bf16[176,512]{1,0:T(8,128)(2,1)S(1)}, u32[]{:S(2)}, u32[]{:S(2)}) %collective-permute-start.14) | collective-permute-done | bytes 180256 | tf_op jit(solution)/shard_map/ppermute | solution.py:537
  79.2 1.2 %place.2 = (f32[1024,512]{1,0:T(8,128)}, f32[512,256]{1,0:T(8,128)}, f32[2,512]{1,0:T(2,128)S(1)}) custom-call(bf16[176,512]{1,0:T(8,128)(2,1)S(1)} %concatenate.34.refs_0_, bf16[176,512]{1,0:T(8,128)(2,1)S(1)} %collective-permute-done.12.refs_1_, bf16[176,512]{1,0:T(8,128)(2,1)S(1)} %collective-permute-done.14.refs_2_, ...), custom_call_target="tpu_custom_call" | custom-call | flops 131072 | bytes 2097152 | tf_op jit(solution)/shard_map/place/pallas_call | solution.py:512
  80.5 1.2 %place.3 = (f32[1024,512]{1,0:T(8,128)}, f32[512,256]{1,0:T(8,128)}, f32[1,512]{1,0:T(1,128)}, f32[1,256]{1,0:T(1,128)}, f32[1,256]{1,0:T(1,128)}) custom-call(bf16[176,512]{1,0:T(8,128)(2,1)S(1)} %collective-permute-done.11.refs_0_, bf16[176,512]{1,0:T(8,128)(2,1)S(1)} %collective-permute-done.13.refs_1_, ...), custom_call_target="tpu_custom_call", output_to_operand_aliasing={{0}: (4, {}), {1}: (5, {})} | custom-call | flops 131072 | bytes 2097152 | tf_op jit(solution)/shard_map/place/pallas_call | solution.py:512
  (88 shorter events, 3.6 us)
Async XLA Ops:
  0.6 9.2 %copy-start.10 = (bf16[256]{0:T(256)(128)(2,1)S(1)}, bf16[256]{0:T(256)(128)(2,1)}, u32[]{:S(2)}) copy-start(bf16[256]{0:T(256)(128)(2,1)} %param.25) | copy-start | bytes 1540
  2.5 24.0 %all-to-all-start = ((bf16[32,72,128]{2,1,0:T(8,128)(2,1)}), bf16[32,72,128]{2,1,0:T(8,128)(2,1)S(1)}, u32[]{:S(2)}, u32[]{:S(2)}) async-start(bf16[32,72,128]{2,1,0:T(8,128)(2,1)} %pack.1), calls=%async_computation | async-start | bytes 1179648 | tf_op jit(solution)/shard_map/all_to_all | solution.py:533
  18.5 19.7 %copy-start = (bf16[1024,512]{1,0:T(8,128)(2,1)S(1)}, bf16[1024,512]{1,0:T(8,128)(2,1)}, u32[]{:S(2)}) copy-start(bf16[1024,512]{1,0:T(8,128)(2,1)} %get-tuple-element.47.q) | copy-start | bytes 3145732
  18.5 19.7 %copy-start.1 = (bf16[1024,256]{1,0:T(8,128)(2,1)S(1)}, bf16[1024,256]{1,0:T(8,128)(2,1)}, u32[]{:S(2)}) copy-start(bf16[1024,256]{1,0:T(8,128)(2,1)} %get-tuple-element.46.s2) | copy-start | bytes 1572868
  18.5 1.2 %copy-start.2 = (f32[1024,128]{1,0:T(8,128)S(1)}, f32[1024,128]{1,0:T(8,128)}, u32[]{:S(2)}) copy-start(f32[1024,128]{1,0:T(8,128)} %z_ref.2) | copy-start | bytes 1572868
  19.6 1.0 %copy-start.4 = (f32[1024,128]{1,0:T(8,128)S(1)}, f32[1024,128]{1,0:T(8,128)}, u32[]{:S(2)}) copy-start(f32[1024,128]{1,0:T(8,128)} %n_ref.2) | copy-start | bytes 1572868
  20.7 17.5 %copy-start.7 = (s32[32,64]{1,0:T(8,128)S(1)}, s32[32,64]{1,0:T(8,128)}, u32[]{:S(2)}) copy-start(s32[32,64]{1,0:T(8,128)} %example_ref.1) | copy-start | bytes 24580
  20.7 17.5 %copy-start.8 = (s32[1024]{0:T(1024)S(1)}, s32[1024]{0:T(1024)}, u32[]{:S(2)}) copy-start(s32[1024]{0:T(1024)} %param.14) | copy-start | bytes 12292
  20.7 17.5 %copy-start.9 = (f32[1,1024]{1,0:T(1,128)S(1)}, f32[1,1024]{1,0:T(1,128)}, u32[]{:S(2)}) copy-start(f32[1,1024]{1,0:T(1,128)} %get-tuple-element.45.deep_ref) | copy-start | bytes 12292
  40.8 2.7 %collective-permute-start = (bf16[640,512]{1,0:T(8,128)(2,1)S(1)}, bf16[640,512]{1,0:T(8,128)(2,1)S(1)}, u32[]{:S(2)}, u32[]{:S(2)}) collective-permute-start(bf16[640,512]{1,0:T(8,128)(2,1)S(1)} %get-tuple-element.52), channel_id=1, source_target_pairs={{0,1},{1,0},{2,3},{3,2},{4,5},{5,4},{6,7},{7,6},{8,9},{9,8},{10,11... | collective-permute-start | bytes 1966088 | tf_op jit(solution)/shard_map/ppermute | solution.py:537
  43.5 11.9 %copy-start.6 = (bf16[256,1024]{1,0:T(8,128)(2,1)S(1)}, bf16[256,1024]{1,0:T(8,128)(2,1)}, u32[]{:S(2)}) copy-start(bf16[256,1024]{1,0:T(8,128)(2,1)} %get-tuple-element.58.h2) | copy-start | bytes 1572868
  43.8 30.6 %copy-start.3 = (f32[1024,128]{1,0:T(8,128)S(1)}, f32[1024,128]{1,0:T(8,128)}, u32[]{:S(2)}) copy-start(f32[1024,128]{1,0:T(8,128)} %z_ref.2) | copy-start | bytes 1572868
  43.8 30.6 %copy-start.5 = (f32[1024,128]{1,0:T(8,128)S(1)}, f32[1024,128]{1,0:T(8,128)}, u32[]{:S(2)}) copy-start(f32[1024,128]{1,0:T(8,128)} %n_ref.2) | copy-start | bytes 1572868
  43.8 5.3 %collective-permute-start.4 = (bf16[84,512]{1,0:T(8,128)(2,1)S(1)}, bf16[84,512]{1,0:T(8,128)(2,1)S(1)}, u32[]{:S(2)}, u32[]{:S(2)}) collective-permute-start(bf16[84,512]{1,0:T(8,128)(2,1)S(1)} %pad_maximum_fusion.1), channel_id=1, source_target_pairs={{0,2},{1,3},{2,0},{3,1},{4,6},{5,7},{6,4},{7,5},{8,10},{9,11},{10,... | collective-permute-start | bytes 258056 | tf_op jit(solution)/shard_map/ppermute | solution.py:537
  44.4 6.6 %collective-permute-start.5 = (bf16[84,512]{1,0:T(8,128)(2,1)S(1)}, bf16[84,512]{1,0:T(8,128)(2,1)S(1)}, u32[]{:S(2)}, u32[]{:S(2)}) collective-permute-start(bf16[84,512]{1,0:T(8,128)(2,1)S(1)} %pad_maximum_fusion.2), channel_id=1, source_target_pairs={{0,4},{1,5},{2,6},{3,7},{4,0},{5,1},{6,2},{7,3},{8,12},{9,13},{10,... | collective-permute-start | bytes 258056 | tf_op jit(solution)/shard_map/ppermute | solution.py:537
  45.1 5.9 %collective-permute-start.6 = (bf16[84,512]{1,0:T(8,128)(2,1)S(1)}, bf16[84,512]{1,0:T(8,128)(2,1)S(1)}, u32[]{:S(2)}, u32[]{:S(2)}) collective-permute-start(bf16[84,512]{1,0:T(8,128)(2,1)S(1)} %pad_maximum_fusion.3), channel_id=1, source_target_pairs={{0,6},{1,7},{2,4},{3,5},{4,2},{5,3},{6,0},{7,1},{8,14},{9,15},{10,... | collective-permute-start | bytes 258056 | tf_op jit(solution)/shard_map/ppermute | solution.py:537
  51.3 4.6 %collective-permute-start.7 = (bf16[88,512]{1,0:T(8,128)(2,1)S(1)}, bf16[88,512]{1,0:T(8,128)(2,1)S(1)}, u32[]{:S(2)}, u32[]{:S(2)}) collective-permute-start(bf16[88,512]{1,0:T(8,128)(2,1)S(1)} %pad_maximum_fusion.4), channel_id=1, source_target_pairs={{0,8},{1,9},{2,10},{3,11},{4,12},{5,13},{6,14},{7,15},{8,0},{9,1},... | collective-permute-start | bytes 270344 | tf_op jit(solution)/shard_map/ppermute | solution.py:537
  51.9 5.5 %collective-permute-start.3 = (bf16[80,512]{1,0:T(8,128)(2,1)S(1)}, bf16[80,512]{1,0:T(8,128)(2,1)S(1)}, u32[]{:S(2)}, u32[]{:S(2)}) collective-permute-start(bf16[80,512]{1,0:T(8,128)(2,1)S(1)} %get-tuple-element.75), channel_id=1, source_target_pairs={{0,6},{1,7},{2,4},{3,5},{4,2},{5,3},{6,0},{7,1},{8,14},{9,15},{10,... | collective-permute-start | bytes 245768 | tf_op jit(solution)/shard_map/ppermute | solution.py:537
  53.8 4.5 %collective-permute-start.2 = (bf16[80,512]{1,0:T(8,128)(2,1)S(1)}, bf16[80,512]{1,0:T(8,128)(2,1)S(1)}, u32[]{:S(2)}, u32[]{:S(2)}) collective-permute-start(bf16[80,512]{1,0:T(8,128)(2,1)S(1)} %get-tuple-element.76), channel_id=1, source_target_pairs={{0,4},{1,5},{2,6},{3,7},{4,0},{5,1},{6,2},{7,3},{8,12},{9,13},{10,... | collective-permute-start | bytes 245768 | tf_op jit(solution)/shard_map/ppermute | solution.py:537
  54.9 4.4 %collective-permute-start.1 = (bf16[80,512]{1,0:T(8,128)(2,1)S(1)}, bf16[80,512]{1,0:T(8,128)(2,1)S(1)}, u32[]{:S(2)}, u32[]{:S(2)}) collective-permute-start(bf16[80,512]{1,0:T(8,128)(2,1)S(1)} %get-tuple-element.77), channel_id=1, source_target_pairs={{0,2},{1,3},{2,0},{3,1},{4,6},{5,7},{6,4},{7,5},{8,10},{9,11},{10,... | collective-permute-start | bytes 245768 | tf_op jit(solution)/shard_map/ppermute | solution.py:537
  59.4 6.6 %collective-permute-start.8 = (bf16[92,512]{1,0:T(8,128)(2,1)S(1)}, bf16[92,512]{1,0:T(8,128)(2,1)S(1)}, u32[]{:S(2)}, u32[]{:S(2)}) collective-permute-start(bf16[92,512]{1,0:T(8,128)(2,1)S(1)} %pad_maximum_fusion), channel_id=1, source_target_pairs={{0,16},{1,17},{2,18},{3,19},{4,20},{5,21},{6,22},{7,23},{8,24},{9,... | collective-permute-start | bytes 282632 | tf_op jit(solution)/shard_map/ppermute | solution.py:537
  66.1 4.6 %collective-permute-start.9 = (bf16[88,512]{1,0:T(8,128)(2,1)S(1)}, bf16[88,512]{1,0:T(8,128)(2,1)S(1)}, u32[]{:S(2)}, u32[]{:S(2)}) collective-permute-start(bf16[88,512]{1,0:T(8,128)(2,1)S(1)} %pad_maximum_fusion.5), channel_id=1, source_target_pairs={{0,8},{1,9},{2,10},{3,11},{4,12},{5,13},{6,14},{7,15},{8,0},{9,1},... | collective-permute-start | bytes 270344 | tf_op jit(solution)/shard_map/ppermute | solution.py:537
  66.7 7.6 %collective-permute-start.10 = (bf16[16,256]{1,0:T(8,128)(2,1)S(1)}, bf16[16,256]{1,0:T(8,128)(2,1)S(1)}, u32[]{:S(2)}, u32[]{:S(2)}) collective-permute-start(bf16[16,256]{1,0:T(8,128)(2,1)S(1)} %bitcast.36), channel_id=1, source_target_pairs={{0,1},{1,0},{2,3},{3,2},{4,5},{5,4},{6,7},{7,6},{8,9},{9,8},{10,11... | collective-permute-start | bytes 24584 | tf_op jit(solution)/shard_map/ppermute | solution.py:537
  70.8 6.5 %collective-permute-start.12 = (bf16[176,512]{1,0:T(8,128)(2,1)S(1)}, bf16[176,512]{1,0:T(8,128)(2,1)S(1)}, u32[]{:S(2)}, u32[]{:S(2)}) collective-permute-start(bf16[176,512]{1,0:T(8,128)(2,1)S(1)} %concatenate.34.refs_0_), channel_id=1, source_target_pairs={{0,2},{1,3},{2,0},{3,1},{4,6},{5,7},{6,4},{7,5},{8,10},{9,11},{10,... | collective-permute-start | bytes 540680 | tf_op jit(solution)/shard_map/ppermute | solution.py:537
  70.8 7.9 %collective-permute-start.14 = (bf16[176,512]{1,0:T(8,128)(2,1)S(1)}, bf16[176,512]{1,0:T(8,128)(2,1)S(1)}, u32[]{:S(2)}, u32[]{:S(2)}) collective-permute-start(bf16[176,512]{1,0:T(8,128)(2,1)S(1)} %concatenate.34.refs_0_), channel_id=1, source_target_pairs={{0,4},{1,5},{2,6},{3,7},{4,0},{5,1},{6,2},{7,3},{8,12},{9,13},{10,... | collective-permute-start | bytes 540680 | tf_op jit(solution)/shard_map/ppermute | solution.py:537
  71.6 7.1 %collective-permute-start.16 = (bf16[176,512]{1,0:T(8,128)(2,1)S(1)}, bf16[176,512]{1,0:T(8,128)(2,1)S(1)}, u32[]{:S(2)}, u32[]{:S(2)}) collective-permute-start(bf16[176,512]{1,0:T(8,128)(2,1)S(1)} %concatenate.34.refs_0_), channel_id=1, source_target_pairs={{0,6},{1,7},{2,4},{3,5},{4,2},{5,3},{6,0},{7,1},{8,14},{9,15},{10,... | collective-permute-start | bytes 540680 | tf_op jit(solution)/shard_map/ppermute | solution.py:537
  77.3 3.2 %collective-permute-start.11 = (bf16[176,512]{1,0:T(8,128)(2,1)S(1)}, bf16[176,512]{1,0:T(8,128)(2,1)S(1)}, u32[]{:S(2)}, u32[]{:S(2)}) collective-permute-start(bf16[176,512]{1,0:T(8,128)(2,1)S(1)} %concatenate.34.refs_0_), channel_id=1, source_target_pairs={{0,1},{1,0},{2,3},{3,2},{4,5},{5,4},{6,7},{7,6},{8,9},{9,8},{10,11... | collective-permute-start | bytes 540680 | tf_op jit(solution)/shard_map/ppermute | solution.py:537
  77.3 3.2 %collective-permute-start.13 = (bf16[176,512]{1,0:T(8,128)(2,1)S(1)}, bf16[176,512]{1,0:T(8,128)(2,1)S(1)}, u32[]{:S(2)}, u32[]{:S(2)}) collective-permute-start(bf16[176,512]{1,0:T(8,128)(2,1)S(1)} %collective-permute-done.12.refs_1_), channel_id=1, source_target_pairs={{0,1},{1,0},{2,3},{3,2},{4,5},{5,4},{6,7},{7,6},{8,9},{9,8},{10,11... | collective-permute-start | bytes 540680 | tf_op jit(solution)/shard_map/ppermute | solution.py:537
  78.7 1.7 %collective-permute-start.15 = (bf16[176,512]{1,0:T(8,128)(2,1)S(1)}, bf16[176,512]{1,0:T(8,128)(2,1)S(1)}, u32[]{:S(2)}, u32[]{:S(2)}) collective-permute-start(bf16[176,512]{1,0:T(8,128)(2,1)S(1)} %collective-permute-done.14.refs_2_), channel_id=1, source_target_pairs={{0,1},{1,0},{2,3},{3,2},{4,5},{5,4},{6,7},{7,6},{8,9},{9,8},{10,11... | collective-permute-start | bytes 540680 | tf_op jit(solution)/shard_map/ppermute | solution.py:537
  78.7 1.7 %collective-permute-start.17 = (bf16[176,512]{1,0:T(8,128)(2,1)S(1)}, bf16[176,512]{1,0:T(8,128)(2,1)S(1)}, u32[]{:S(2)}, u32[]{:S(2)}) collective-permute-start(bf16[176,512]{1,0:T(8,128)(2,1)S(1)} %collective-permute-done.16.refs_3_), channel_id=1, source_target_pairs={{0,1},{1,0},{2,3},{3,2},{4,5},{5,4},{6,7},{7,6},{8,9},{9,8},{10,11... | collective-permute-start | bytes 540680 | tf_op jit(solution)/shard_map/ppermute | solution.py:537

commit v8 on v7

--- a/solution.py
+++ b/solution.py
@@ -246,10 +246,13 @@
     for side in range(2):
         span = pl.ds(pl.multiple_of(2 * each + half * packed + side * 2 * packed, packed), packed)
         copies.append(pltpu.make_async_copy(big_any.at[span], h1.at[pl.ds(side * packed, packed)], sems.at[side]))
-    rows = each // PIECES
+    span = pl.ds(pl.multiple_of(half * each, each), each)
+    columns = dense_t.shape[1] // PIECES
     for k in range(PIECES):
-        span = pl.ds(pl.multiple_of(half * each + k * rows, rows), rows)
-        copies.append(pltpu.make_async_copy(big_any.at[span], dense_t.at[pl.ds(k * rows, rows)], sems.at[2 + k]))
+        lanes = pl.ds(k * columns, columns)
+        copies.append(
+            pltpu.make_async_copy(big_any.at[span, lanes], dense_t.at[pl.ds(0, each), lanes], sems.at[2 + k])
+        )
     return copies
 
 
@@ -277,9 +280,12 @@
         at, low = k * packed, (k + EIGHTHS) * packed
         target[k * each + first : (k + 1) * each, 0:width] = second[at : at + packed]
         target[k * each + first : (k + 1) * each, width:] = second[low : low + packed]
-    for copy in copies[2:]:
+    columns = dense_t.shape[1] // PIECES
+    made = 0.0
+    for k, copy in enumerate(copies[2:]):
         copy.wait()
-    made = dot(dense_t[...], d_one)
+        span = slice(k * columns, (k + 1) * columns)
+        made = made + dot(dense_t[:, span], d_one[span, :])
     b_one = made[EIGHTHS * first : EIGHTHS * first + 1]
     made = made.astype(bf16)
     for k in range(EIGHTHS):

time: 82 us -> 82 us (level)
  no operation moved by 1% of the time
where the time goes in v8:
time: 82 us; the launch traced here: 81.7 us
  waiting for transfers between devices  23.2 us (28%)
  Pallas kernels  22.3 us (27%)
  starting transfers between devices  21 us (26%)
  blocking collectives  10.3 us (13%)
  local copies, waits for them, and re-layouts  3.24 us (4%)
  between operations  1.17 us (1%)
    ppermute x18, waiting for transfers between devices, swap(): return lax.ppermute(x, AXES, [(i, i ^ bit) for i in range(devices)])  17.8 us
    ppermute x18, starting transfers between devices, swap(): return lax.ppermute(x, AXES, [(i, i ^ bit) for i in range(devices)])  13.7 us
    all_to_all x1, blocking collectives, every_to_every(): return lax.all_to_all(x, AXES, split_axis=0, concat_axis=0, tiled=True)  10.3 us
    pallas_call x1, Pallas kernels, tower(): pl.pallas_call(tower_kernel, grid=(steps,), out_shape=(jax.ShapeDtypeStru...  8.06 us
    all_to_all x1, starting transfers between devices, every_to_every(): return lax.all_to_all(x, AXES, split_axis=0, concat_axis=0, tiled=True)  7.3 us
    all_to_all x1, waiting for transfers between devices, every_to_every(): return lax.all_to_all(x, AXES, split_axis=0, concat_axis=0, tiled=True)  5.42 us
    pallas_call x1, Pallas kernels, new_states(): pl.pallas_call(state_kernel, out_shape=(jax.ShapeDtypeStruct(z.shape, f32...  2.94 us
    pallas_call x1, Pallas kernels, residuals(): pl.pallas_call(residual_kernel, out_shape=(jax.ShapeDtypeStruct((rows, LA...  2.57 us
  transfers between devices with their start and end apart: 19, of which 10 were waited for; matrix products, arithmetic and copies ran while one was open for 1% of the time, Pallas kernels for 19%

profile of v8, /device:TPU:0, one launch (start us, length us, event | category | flops | bytes accessed | tf_op | source)
XLA Modules:
  0.0 81.7 jit_solution(16411116545188366179)
XLA Ops:
  0.6 1.9 %pack.1 = bf16[32,72,128]{2,1,0:T(8,128)(2,1)} custom-call(bf16[32,64,128]{2,1,0:T(8,128)(2,1)} %values_any.1, s32[32,64]{1,0:T(8,128)} %block_any.1, s32[1,32]{1,0:T(1,128)} %bitcast.37), custom_call_target="tpu_custom_call" | custom-call | tf_op jit(solution)/shard_map/pack/pallas_call | solution.py:99
  2.5 7.3 %all-to-all-start = ((bf16[32,72,128]{2,1,0:T(8,128)(2,1)}), bf16[32,72,128]{2,1,0:T(8,128)(2,1)S(1)}, u32[]{:S(2)}, u32[]{:S(2)}) async-start(bf16[32,72,128]{2,1,0:T(8,128)(2,1)} %pack.1), calls=%async_computation | async-start | bytes 1179648 | tf_op jit(solution)/shard_map/all_to_all | solution.py:539
  9.8 0.6 reshape.62.head_ref
  10.4 8.1 %tower.1 = (bf16[1792,1024]{1,0:T(8,128)(2,1)}, bf16[256,1024]{1,0:T(8,128)(2,1)}, bf16[1024,256]{1,0:T(8,128)(2,1)}, bf16[1024,512]{1,0:T(8,128)(2,1)}, f32[1,1024]{1,0:T(1,128)}) custom-call(bf16[1024,1024]{1,0:T(8,128)(2,1)} %dense_ref.1, bf16[1024,512]{1,0:T(8,128)(2,1)} %w1_ref.1, f32[1,512]{1,0:T(1,128)} %bitcast.39, bf16[512,256]{1,0:T(8,128)(2,1)} %w2_ref.1, ...), custom_call_target="tpu_custom_call" | custom-call | flops 1610612736 | bytes 12582912 | tf_op jit(solution)/shard_map/tower/pallas_call | solution.py:159
  18.5 1.1 %copy-done.2 = f32[1024,128]{1,0:T(8,128)S(1)} copy-done((f32[1024,128]{1,0:T(8,128)S(1)}, f32[1024,128]{1,0:T(8,128)}, u32[]{:S(2)}) %copy-start.2) | copy-done | bytes 524312
  19.7 1.0 %copy-done.4 = f32[1024,128]{1,0:T(8,128)S(1)} copy-done((f32[1024,128]{1,0:T(8,128)S(1)}, f32[1024,128]{1,0:T(8,128)}, u32[]{:S(2)}) %copy-start.4) | copy-done | bytes 524312
  21.1 5.4 %all-to-all-done.got_ref = bf16[32,72,128]{2,1,0:T(8,128)(2,1)S(1)} async-done(((bf16[32,72,128]{2,1,0:T(8,128)(2,1)}), bf16[32,72,128]{2,1,0:T(8,128)(2,1)S(1)}, u32[]{:S(2)}, u32[]{:S(2)}) %all-to-all-start) | async-done | bytes 589856 | tf_op jit(solution)/shard_map/all_to_all | solution.py:539
  26.6 1.3 %slot_logits.1 = f32[32,1,128]{2,1,0:T(1,128)S(1)} custom-call(bf16[32,72,128]{2,1,0:T(8,128)(2,1)S(1)} %all-to-all-done.got_ref, bf16[1024,256]{1,0:T(8,128)(2,1)S(1)} %weights.1.wcat_ref), custom_call_target="tpu_custom_call" | custom-call | tf_op jit(solution)/shard_map/slot_logits/pallas_call | solution.py:224
  27.9 10.3 %all_to_all.10.logit_any = f32[32,1,128]{2,1,0:T(1,128)S(1)} all-to-all(f32[32,1,128]{2,1,0:T(1,128)S(1)} %slot_logits.1), channel_id=1, replica_groups=mesh['blk'=8,'rep'=4] {'blk','rep'}, dimensions={0} | all-to-all | bytes 32768 | tf_op jit(solution)/shard_map/all_to_all | solution.py:539
  38.2 2.6 %residuals.1 = (f32[8,128]{1,0:T(8,128)}, f32[8,128]{1,0:T(8,128)S(1)}, bf16[640,512]{1,0:T(8,128)(2,1)S(1)}, bf16[16,512]{1,0:T(8,128)(2,1)S(1)}) custom-call(f32[32,1,128]{2,1,0:T(1,128)S(1)} %all_to_all.10.logit_any, s32[32,64]{1,0:T(8,128)S(1)} %copy-done.7, f32[1,1024]{1,0:T(1,128)S(1)} %copy-done.9, s32[8,128]{1,0:T(8,128)S(1)} %bitcast.31, ...), custom_call_target="tpu_custom_call" | custom-call | tf_op jit(solution)/shard_map/residuals/pallas_call | solution.py:365
  41.1 2.5 %gradients.1 = (bf16[640,512]{1,0:T(8,128)(2,1)S(1)}, bf16[4,512]{1,0:T(4,128)(2,1)S(1)}) custom-call(f32[8,128]{1,0:T(8,128)S(1)} %get-tuple-element.56.residual_ref, bf16[1024,256]{1,0:T(8,128)(2,1)S(1)} %copy-done.1, bf16[1024,512]{1,0:T(8,128)(2,1)S(1)} %copy-done, bf16[1792,1024]{1,0:T(8,128)(2,1)} %get-tuple-element.48.big_any), custom_call_target="tpu_custom_call" | custom-call | flops 671088640 | bytes 6291456 | tf_op jit(solution)/shard_map/gradients/pallas_call | solution.py:400
  43.9 0.6 collective-permute-start.4
  44.5 0.7 collective-permute-start.5
  45.2 2.4 %collective-permute-start.6 = (bf16[84,512]{1,0:T(8,128)(2,1)S(1)}, bf16[84,512]{1,0:T(8,128)(2,1)S(1)}, u32[]{:S(2)}, u32[]{:S(2)}) collective-permute-start(bf16[84,512]{1,0:T(8,128)(2,1)S(1)} %pad_maximum_fusion.3), channel_id=1, source_target_pairs={{0,6},{1,7},{2,4},{3,5},{4,2},{5,3},{6,0},{7,1},{8,14},{9,15},{10,... | collective-permute-start | bytes 258056 | tf_op jit(solution)/shard_map/ppermute | solution.py:543
  47.6 1.6 %collective-permute-done.4 = bf16[84,512]{1,0:T(8,128)(2,1)S(1)} collective-permute-done((bf16[84,512]{1,0:T(8,128)(2,1)S(1)}, bf16[84,512]{1,0:T(8,128)(2,1)S(1)}, u32[]{:S(2)}, u32[]{:S(2)}) %collective-permute-start.4) | collective-permute-done | bytes 86048 | tf_op jit(solution)/shard_map/ppermute | solution.py:543
  49.2 1.9 %collective-permute-done.5 = bf16[84,512]{1,0:T(8,128)(2,1)S(1)} collective-permute-done((bf16[84,512]{1,0:T(8,128)(2,1)S(1)}, bf16[84,512]{1,0:T(8,128)(2,1)S(1)}, u32[]{:S(2)}, u32[]{:S(2)}) %collective-permute-start.5) | collective-permute-done | bytes 86048 | tf_op jit(solution)/shard_map/ppermute | solution.py:543
  51.3 0.6 collective-permute-start.7
  52.0 1.9 %collective-permute-start.3 = (bf16[80,512]{1,0:T(8,128)(2,1)S(1)}, bf16[80,512]{1,0:T(8,128)(2,1)S(1)}, u32[]{:S(2)}, u32[]{:S(2)}) collective-permute-start(bf16[80,512]{1,0:T(8,128)(2,1)S(1)} %get-tuple-element.75), channel_id=1, source_target_pairs={{0,6},{1,7},{2,4},{3,5},{4,2},{5,3},{6,0},{7,1},{8,14},{9,15},{10,... | collective-permute-start | bytes 245768 | tf_op jit(solution)/shard_map/ppermute | solution.py:543
  53.9 1.1 %collective-permute-start.2 = (bf16[80,512]{1,0:T(8,128)(2,1)S(1)}, bf16[80,512]{1,0:T(8,128)(2,1)S(1)}, u32[]{:S(2)}, u32[]{:S(2)}) collective-permute-start(bf16[80,512]{1,0:T(8,128)(2,1)S(1)} %get-tuple-element.76), channel_id=1, source_target_pairs={{0,4},{1,5},{2,6},{3,7},{4,0},{5,1},{6,2},{7,3},{8,12},{9,13},{10,... | collective-permute-start | bytes 245768 | tf_op jit(solution)/shard_map/ppermute | solution.py:543
  56.1 1.4 %collective-permute-done.3 = bf16[80,512]{1,0:T(8,128)(2,1)S(1)} collective-permute-done((bf16[80,512]{1,0:T(8,128)(2,1)S(1)}, bf16[80,512]{1,0:T(8,128)(2,1)S(1)}, u32[]{:S(2)}, u32[]{:S(2)}) %collective-permute-start.3) | collective-permute-done | bytes 81952 | tf_op jit(solution)/shard_map/ppermute | solution.py:543
  57.5 0.9 %collective-permute-done.2 = bf16[80,512]{1,0:T(8,128)(2,1)S(1)} collective-permute-done((bf16[80,512]{1,0:T(8,128)(2,1)S(1)}, bf16[80,512]{1,0:T(8,128)(2,1)S(1)}, u32[]{:S(2)}, u32[]{:S(2)}) %collective-permute-start.2) | collective-permute-done | bytes 81952 | tf_op jit(solution)/shard_map/ppermute | solution.py:543
  58.4 1.0 %collective-permute-done.1 = bf16[80,512]{1,0:T(8,128)(2,1)S(1)} collective-permute-done((bf16[80,512]{1,0:T(8,128)(2,1)S(1)}, bf16[80,512]{1,0:T(8,128)(2,1)S(1)}, u32[]{:S(2)}, u32[]{:S(2)}) %collective-permute-start.1) | collective-permute-done | bytes 81952 | tf_op jit(solution)/shard_map/ppermute | solution.py:543
  59.5 0.6 collective-permute-start.8
  60.1 6.0 %collective-permute-done.8 = bf16[92,512]{1,0:T(8,128)(2,1)S(1)} collective-permute-done((bf16[92,512]{1,0:T(8,128)(2,1)S(1)}, bf16[92,512]{1,0:T(8,128)(2,1)S(1)}, u32[]{:S(2)}, u32[]{:S(2)}) %collective-permute-start.8) | collective-permute-done | bytes 94240 | tf_op jit(solution)/shard_map/ppermute | solution.py:543
  66.2 0.6 collective-permute-start.9
  66.9 3.9 %collective-permute-done.9 = bf16[88,512]{1,0:T(8,128)(2,1)S(1)} collective-permute-done((bf16[88,512]{1,0:T(8,128)(2,1)S(1)}, bf16[88,512]{1,0:T(8,128)(2,1)S(1)}, u32[]{:S(2)}, u32[]{:S(2)}) %collective-permute-start.9) | collective-permute-done | bytes 90144 | tf_op jit(solution)/shard_map/ppermute | solution.py:543
  70.9 0.8 collective-permute-start.14
  71.7 2.7 %collective-permute-start.16 = (bf16[176,512]{1,0:T(8,128)(2,1)S(1)}, bf16[176,512]{1,0:T(8,128)(2,1)S(1)}, u32[]{:S(2)}, u32[]{:S(2)}) collective-permute-start(bf16[176,512]{1,0:T(8,128)(2,1)S(1)} %concatenate.34.refs_0_), channel_id=1, source_target_pairs={{0,6},{1,7},{2,4},{3,5},{4,2},{5,3},{6,0},{7,1},{8,14},{9,15},{10,... | collective-permute-start | bytes 540680 | tf_op jit(solution)/shard_map/ppermute | solution.py:543
  74.4 2.9 %new_states.1 = (f32[1024,128]{1,0:T(8,128)}, f32[1024,128]{1,0:T(8,128)}) custom-call(bf16[32,72,128]{2,1,0:T(8,128)(2,1)S(1)} %all-to-all-done.got_ref, f32[32,128]{1,0:T(8,128)S(1)} %convert_add_fusion.res_ref, f32[1024,128]{1,0:T(8,128)S(1)} %copy-done.3, f32[1024,128]{1,0:T(8,128)S(1)} %copy-done.5), custom_call_target="tpu_custom_call" | custom-call | flops 1073741824 | bytes 4194304 | tf_op jit(solution)/shard_map/new_states/pallas_call | solution.py:457
  77.8 0.9 %collective-permute-done.14.refs_2_ = bf16[176,512]{1,0:T(8,128)(2,1)S(1)} collective-permute-done((bf16[176,512]{1,0:T(8,128)(2,1)S(1)}, bf16[176,512]{1,0:T(8,128)(2,1)S(1)}, u32[]{:S(2)}, u32[]{:S(2)}) %collective-permute-start.14) | collective-permute-done | bytes 180256 | tf_op jit(solution)/shard_map/ppermute | solution.py:543
  79.3 1.2 %place.2 = (f32[1024,512]{1,0:T(8,128)}, f32[512,256]{1,0:T(8,128)}, f32[2,512]{1,0:T(2,128)S(1)}) custom-call(bf16[176,512]{1,0:T(8,128)(2,1)S(1)} %concatenate.34.refs_0_, bf16[176,512]{1,0:T(8,128)(2,1)S(1)} %collective-permute-done.12.refs_1_, bf16[176,512]{1,0:T(8,128)(2,1)S(1)} %collective-permute-done.14.refs_2_, ...), custom_call_target="tpu_custom_call" | custom-call | flops 131072 | bytes 2097152 | tf_op jit(solution)/shard_map/place/pallas_call | solution.py:518
  80.5 1.2 %place.3 = (f32[1024,512]{1,0:T(8,128)}, f32[512,256]{1,0:T(8,128)}, f32[1,512]{1,0:T(1,128)}, f32[1,256]{1,0:T(1,128)}, f32[1,256]{1,0:T(1,128)}) custom-call(bf16[176,512]{1,0:T(8,128)(2,1)S(1)} %collective-permute-done.11.refs_0_, bf16[176,512]{1,0:T(8,128)(2,1)S(1)} %collective-permute-done.13.refs_1_, ...), custom_call_target="tpu_custom_call", output_to_operand_aliasing={{0}: (4, {}), {1}: (5, {})} | custom-call | flops 131072 | bytes 2097152 | tf_op jit(solution)/shard_map/place/pallas_call | solution.py:518
  (88 shorter events, 3.6 us)
Async XLA Ops:
  0.6 9.2 %copy-start.10 = (bf16[256]{0:T(256)(128)(2,1)S(1)}, bf16[256]{0:T(256)(128)(2,1)}, u32[]{:S(2)}) copy-start(bf16[256]{0:T(256)(128)(2,1)} %param.25) | copy-start | bytes 1540
  2.5 24.0 %all-to-all-start = ((bf16[32,72,128]{2,1,0:T(8,128)(2,1)}), bf16[32,72,128]{2,1,0:T(8,128)(2,1)S(1)}, u32[]{:S(2)}, u32[]{:S(2)}) async-start(bf16[32,72,128]{2,1,0:T(8,128)(2,1)} %pack.1), calls=%async_computation | async-start | bytes 1179648 | tf_op jit(solution)/shard_map/all_to_all | solution.py:539
  18.5 19.7 %copy-start = (bf16[1024,512]{1,0:T(8,128)(2,1)S(1)}, bf16[1024,512]{1,0:T(8,128)(2,1)}, u32[]{:S(2)}) copy-start(bf16[1024,512]{1,0:T(8,128)(2,1)} %get-tuple-element.47.q) | copy-start | bytes 3145732
  18.5 19.7 %copy-start.1 = (bf16[1024,256]{1,0:T(8,128)(2,1)S(1)}, bf16[1024,256]{1,0:T(8,128)(2,1)}, u32[]{:S(2)}) copy-start(bf16[1024,256]{1,0:T(8,128)(2,1)} %get-tuple-element.46.s2) | copy-start | bytes 1572868
  18.5 1.2 %copy-start.2 = (f32[1024,128]{1,0:T(8,128)S(1)}, f32[1024,128]{1,0:T(8,128)}, u32[]{:S(2)}) copy-start(f32[1024,128]{1,0:T(8,128)} %z_ref.2) | copy-start | bytes 1572868
  19.6 1.0 %copy-start.4 = (f32[1024,128]{1,0:T(8,128)S(1)}, f32[1024,128]{1,0:T(8,128)}, u32[]{:S(2)}) copy-start(f32[1024,128]{1,0:T(8,128)} %n_ref.2) | copy-start | bytes 1572868
  20.7 17.5 %copy-start.7 = (s32[32,64]{1,0:T(8,128)S(1)}, s32[32,64]{1,0:T(8,128)}, u32[]{:S(2)}) copy-start(s32[32,64]{1,0:T(8,128)} %example_ref.1) | copy-start | bytes 24580
  20.7 17.5 %copy-start.8 = (s32[1024]{0:T(1024)S(1)}, s32[1024]{0:T(1024)}, u32[]{:S(2)}) copy-start(s32[1024]{0:T(1024)} %param.14) | copy-start | bytes 12292
  20.7 17.5 %copy-start.9 = (f32[1,1024]{1,0:T(1,128)S(1)}, f32[1,1024]{1,0:T(1,128)}, u32[]{:S(2)}) copy-start(f32[1,1024]{1,0:T(1,128)} %get-tuple-element.45.deep_ref) | copy-start | bytes 12292
  40.8 2.8 %collective-permute-start = (bf16[640,512]{1,0:T(8,128)(2,1)S(1)}, bf16[640,512]{1,0:T(8,128)(2,1)S(1)}, u32[]{:S(2)}, u32[]{:S(2)}) collective-permute-start(bf16[640,512]{1,0:T(8,128)(2,1)S(1)} %get-tuple-element.52), channel_id=1, source_target_pairs={{0,1},{1,0},{2,3},{3,2},{4,5},{5,4},{6,7},{7,6},{8,9},{9,8},{10,11... | collective-permute-start | bytes 1966088 | tf_op jit(solution)/shard_map/ppermute | solution.py:543
  43.6 11.9 %copy-start.6 = (bf16[256,1024]{1,0:T(8,128)(2,1)S(1)}, bf16[256,1024]{1,0:T(8,128)(2,1)}, u32[]{:S(2)}) copy-start(bf16[256,1024]{1,0:T(8,128)(2,1)} %get-tuple-element.58.h2) | copy-start | bytes 1572868
  43.8 30.6 %copy-start.3 = (f32[1024,128]{1,0:T(8,128)S(1)}, f32[1024,128]{1,0:T(8,128)}, u32[]{:S(2)}) copy-start(f32[1024,128]{1,0:T(8,128)} %z_ref.2) | copy-start | bytes 1572868
  43.8 30.5 %copy-start.5 = (f32[1024,128]{1,0:T(8,128)S(1)}, f32[1024,128]{1,0:T(8,128)}, u32[]{:S(2)}) copy-start(f32[1024,128]{1,0:T(8,128)} %n_ref.2) | copy-start | bytes 1572868
  43.9 5.3 %collective-permute-start.4 = (bf16[84,512]{1,0:T(8,128)(2,1)S(1)}, bf16[84,512]{1,0:T(8,128)(2,1)S(1)}, u32[]{:S(2)}, u32[]{:S(2)}) collective-permute-start(bf16[84,512]{1,0:T(8,128)(2,1)S(1)} %pad_maximum_fusion.1), channel_id=1, source_target_pairs={{0,2},{1,3},{2,0},{3,1},{4,6},{5,7},{6,4},{7,5},{8,10},{9,11},{10,... | collective-permute-start | bytes 258056 | tf_op jit(solution)/shard_map/ppermute | solution.py:543
  44.5 6.6 %collective-permute-start.5 = (bf16[84,512]{1,0:T(8,128)(2,1)S(1)}, bf16[84,512]{1,0:T(8,128)(2,1)S(1)}, u32[]{:S(2)}, u32[]{:S(2)}) collective-permute-start(bf16[84,512]{1,0:T(8,128)(2,1)S(1)} %pad_maximum_fusion.2), channel_id=1, source_target_pairs={{0,4},{1,5},{2,6},{3,7},{4,0},{5,1},{6,2},{7,3},{8,12},{9,13},{10,... | collective-permute-start | bytes 258056 | tf_op jit(solution)/shard_map/ppermute | solution.py:543
  45.2 5.9 %collective-permute-start.6 = (bf16[84,512]{1,0:T(8,128)(2,1)S(1)}, bf16[84,512]{1,0:T(8,128)(2,1)S(1)}, u32[]{:S(2)}, u32[]{:S(2)}) collective-permute-start(bf16[84,512]{1,0:T(8,128)(2,1)S(1)} %pad_maximum_fusion.3), channel_id=1, source_target_pairs={{0,6},{1,7},{2,4},{3,5},{4,2},{5,3},{6,0},{7,1},{8,14},{9,15},{10,... | collective-permute-start | bytes 258056 | tf_op jit(solution)/shard_map/ppermute | solution.py:543
  51.3 4.6 %collective-permute-start.7 = (bf16[88,512]{1,0:T(8,128)(2,1)S(1)}, bf16[88,512]{1,0:T(8,128)(2,1)S(1)}, u32[]{:S(2)}, u32[]{:S(2)}) collective-permute-start(bf16[88,512]{1,0:T(8,128)(2,1)S(1)} %pad_maximum_fusion.4), channel_id=1, source_target_pairs={{0,8},{1,9},{2,10},{3,11},{4,12},{5,13},{6,14},{7,15},{8,0},{9,1},... | collective-permute-start | bytes 270344 | tf_op jit(solution)/shard_map/ppermute | solution.py:543
  52.0 5.5 %collective-permute-start.3 = (bf16[80,512]{1,0:T(8,128)(2,1)S(1)}, bf16[80,512]{1,0:T(8,128)(2,1)S(1)}, u32[]{:S(2)}, u32[]{:S(2)}) collective-permute-start(bf16[80,512]{1,0:T(8,128)(2,1)S(1)} %get-tuple-element.75), channel_id=1, source_target_pairs={{0,6},{1,7},{2,4},{3,5},{4,2},{5,3},{6,0},{7,1},{8,14},{9,15},{10,... | collective-permute-start | bytes 245768 | tf_op jit(solution)/shard_map/ppermute | solution.py:543
  53.9 4.5 %collective-permute-start.2 = (bf16[80,512]{1,0:T(8,128)(2,1)S(1)}, bf16[80,512]{1,0:T(8,128)(2,1)S(1)}, u32[]{:S(2)}, u32[]{:S(2)}) collective-permute-start(bf16[80,512]{1,0:T(8,128)(2,1)S(1)} %get-tuple-element.76), channel_id=1, source_target_pairs={{0,4},{1,5},{2,6},{3,7},{4,0},{5,1},{6,2},{7,3},{8,12},{9,13},{10,... | collective-permute-start | bytes 245768 | tf_op jit(solution)/shard_map/ppermute | solution.py:543
  54.9 4.4 %collective-permute-start.1 = (bf16[80,512]{1,0:T(8,128)(2,1)S(1)}, bf16[80,512]{1,0:T(8,128)(2,1)S(1)}, u32[]{:S(2)}, u32[]{:S(2)}) collective-permute-start(bf16[80,512]{1,0:T(8,128)(2,1)S(1)} %get-tuple-element.77), channel_id=1, source_target_pairs={{0,2},{1,3},{2,0},{3,1},{4,6},{5,7},{6,4},{7,5},{8,10},{9,11},{10,... | collective-permute-start | bytes 245768 | tf_op jit(solution)/shard_map/ppermute | solution.py:543
  59.5 6.6 %collective-permute-start.8 = (bf16[92,512]{1,0:T(8,128)(2,1)S(1)}, bf16[92,512]{1,0:T(8,128)(2,1)S(1)}, u32[]{:S(2)}, u32[]{:S(2)}) collective-permute-start(bf16[92,512]{1,0:T(8,128)(2,1)S(1)} %pad_maximum_fusion), channel_id=1, source_target_pairs={{0,16},{1,17},{2,18},{3,19},{4,20},{5,21},{6,22},{7,23},{8,24},{9,... | collective-permute-start | bytes 282632 | tf_op jit(solution)/shard_map/ppermute | solution.py:543
  66.2 4.6 %collective-permute-start.9 = (bf16[88,512]{1,0:T(8,128)(2,1)S(1)}, bf16[88,512]{1,0:T(8,128)(2,1)S(1)}, u32[]{:S(2)}, u32[]{:S(2)}) collective-permute-start(bf16[88,512]{1,0:T(8,128)(2,1)S(1)} %pad_maximum_fusion.5), channel_id=1, source_target_pairs={{0,8},{1,9},{2,10},{3,11},{4,12},{5,13},{6,14},{7,15},{8,0},{9,1},... | collective-permute-start | bytes 270344 | tf_op jit(solution)/shard_map/ppermute | solution.py:543
  66.8 7.6 %collective-permute-start.10 = (bf16[16,256]{1,0:T(8,128)(2,1)S(1)}, bf16[16,256]{1,0:T(8,128)(2,1)S(1)}, u32[]{:S(2)}, u32[]{:S(2)}) collective-permute-start(bf16[16,256]{1,0:T(8,128)(2,1)S(1)} %bitcast.36), channel_id=1, source_target_pairs={{0,1},{1,0},{2,3},{3,2},{4,5},{5,4},{6,7},{7,6},{8,9},{9,8},{10,11... | collective-permute-start | bytes 24584 | tf_op jit(solution)/shard_map/ppermute | solution.py:543
  70.8 6.5 %collective-permute-start.12 = (bf16[176,512]{1,0:T(8,128)(2,1)S(1)}, bf16[176,512]{1,0:T(8,128)(2,1)S(1)}, u32[]{:S(2)}, u32[]{:S(2)}) collective-permute-start(bf16[176,512]{1,0:T(8,128)(2,1)S(1)} %concatenate.34.refs_0_), channel_id=1, source_target_pairs={{0,2},{1,3},{2,0},{3,1},{4,6},{5,7},{6,4},{7,5},{8,10},{9,11},{10,... | collective-permute-start | bytes 540680 | tf_op jit(solution)/shard_map/ppermute | solution.py:543
  70.9 7.9 %collective-permute-start.14 = (bf16[176,512]{1,0:T(8,128)(2,1)S(1)}, bf16[176,512]{1,0:T(8,128)(2,1)S(1)}, u32[]{:S(2)}, u32[]{:S(2)}) collective-permute-start(bf16[176,512]{1,0:T(8,128)(2,1)S(1)} %concatenate.34.refs_0_), channel_id=1, source_target_pairs={{0,4},{1,5},{2,6},{3,7},{4,0},{5,1},{6,2},{7,3},{8,12},{9,13},{10,... | collective-permute-start | bytes 540680 | tf_op jit(solution)/shard_map/ppermute | solution.py:543
  71.7 7.1 %collective-permute-start.16 = (bf16[176,512]{1,0:T(8,128)(2,1)S(1)}, bf16[176,512]{1,0:T(8,128)(2,1)S(1)}, u32[]{:S(2)}, u32[]{:S(2)}) collective-permute-start(bf16[176,512]{1,0:T(8,128)(2,1)S(1)} %concatenate.34.refs_0_), channel_id=1, source_target_pairs={{0,6},{1,7},{2,4},{3,5},{4,2},{5,3},{6,0},{7,1},{8,14},{9,15},{10,... | collective-permute-start | bytes 540680 | tf_op jit(solution)/shard_map/ppermute | solution.py:543
  77.3 3.2 %collective-permute-start.11 = (bf16[176,512]{1,0:T(8,128)(2,1)S(1)}, bf16[176,512]{1,0:T(8,128)(2,1)S(1)}, u32[]{:S(2)}, u32[]{:S(2)}) collective-permute-start(bf16[176,512]{1,0:T(8,128)(2,1)S(1)} %concatenate.34.refs_0_), channel_id=1, source_target_pairs={{0,1},{1,0},{2,3},{3,2},{4,5},{5,4},{6,7},{7,6},{8,9},{9,8},{10,11... | collective-permute-start | bytes 540680 | tf_op jit(solution)/shard_map/ppermute | solution.py:543
  77.3 3.2 %collective-permute-start.13 = (bf16[176,512]{1,0:T(8,128)(2,1)S(1)}, bf16[176,512]{1,0:T(8,128)(2,1)S(1)}, u32[]{:S(2)}, u32[]{:S(2)}) collective-permute-start(bf16[176,512]{1,0:T(8,128)(2,1)S(1)} %collective-permute-done.12.refs_1_), channel_id=1, source_target_pairs={{0,1},{1,0},{2,3},{3,2},{4,5},{5,4},{6,7},{7,6},{8,9},{9,8},{10,11... | collective-permute-start | bytes 540680 | tf_op jit(solution)/shard_map/ppermute | solution.py:543
  78.8 1.7 %collective-permute-start.15 = (bf16[176,512]{1,0:T(8,128)(2,1)S(1)}, bf16[176,512]{1,0:T(8,128)(2,1)S(1)}, u32[]{:S(2)}, u32[]{:S(2)}) collective-permute-start(bf16[176,512]{1,0:T(8,128)(2,1)S(1)} %collective-permute-done.14.refs_2_), channel_id=1, source_target_pairs={{0,1},{1,0},{2,3},{3,2},{4,5},{5,4},{6,7},{7,6},{8,9},{9,8},{10,11... | collective-permute-start | bytes 540680 | tf_op jit(solution)/shard_map/ppermute | solution.py:543
  78.8 1.7 %collective-permute-start.17 = (bf16[176,512]{1,0:T(8,128)(2,1)S(1)}, bf16[176,512]{1,0:T(8,128)(2,1)S(1)}, u32[]{:S(2)}, u32[]{:S(2)}) collective-permute-start(bf16[176,512]{1,0:T(8,128)(2,1)S(1)} %collective-permute-done.16.refs_3_), channel_id=1, source_target_pairs={{0,1},{1,0},{2,3},{3,2},{4,5},{5,4},{6,7},{7,6},{8,9},{9,8},{10,11... | collective-permute-start | bytes 540680 | tf_op jit(solution)/shard_map/ppermute | solution.py:543
